TPU v7x, 32 devices: a whole 2x2x4 slice. The times are simulated.
32 devices in a mesh: gx: 2 (over y), gy: 4 (over z), gz: 4 (over x, core).
Axes of the slice: x: 2, y: 2, z: 4, core: 2. Of those that a mesh axis runs over, the one named last changes fastest.
Arguments:
- velocity: float32 [3, 16, 128, 512], P(None, 'gx', 'gz', 'gy'), may hold values from -4 to 4
- pressure: float32 [16, 128, 512], P('gx', 'gz', 'gy'), may hold values from -4 to 4
- viscosity: float32 [16, 128, 512], P('gx', 'gz', 'gy'), may hold values from 0.1 to 10
- body_force: float32 [3, 16, 128, 512], P(None, 'gx', 'gz', 'gy'), may hold values from -6 to 6
Outputs:
- velocity_out: float32 [3, 16, 128, 512], P(None, 'gx', 'gz', 'gy')
- pressure_out: float32 [16, 128, 512], P('gx', 'gz', 'gy')
All inputs are finite; a program needn't handle non-finite values.
Results may differ from a plain program's by a relative error of at most 0.00002.
Values sent between devices are 32-bit elements; how exact they have to be, the bound alone decides.
No kernel may reach another device: no remote copies, remote signals or barrier semaphores. Data moves between devices by JAX's collectives and lax.ppermute only.
A program may use at most 128 MiB of HBM per device.

v0:
```python
import jax
import jax.numpy as jnp
from jax import lax
from jax.sharding import PartitionSpec as P

PRE = 2
COARSE = 4
POST = 2


relax_weight = 0.6
uzawa_step = 0.5


def padded_2(array, sides, width):
    for axis, dim in sides:
        count, length = (lax.axis_size(axis), array.shape[dim])
        up = [(i, (i + 1) % count) for i in range(count - 1)]
        down = [(j, i) for i, j in up]
        last = lax.slice_in_dim(array, length - width, length, axis=dim)
        first = lax.slice_in_dim(array, 0, width, axis=dim)
        before = lax.ppermute(last, axis, up)
        after = lax.ppermute(first, axis, down)
        array = jnp.concatenate([before, array, after], axis=dim)
    return array


def window(padded, spatial, offset):
    leading = padded.ndim - 3
    selection = [slice(None)] * leading
    for axis_id in range(3):
        extent = padded.shape[leading + axis_id]
        if axis_id == spatial:
            selection.append(slice(1 + offset, extent - 1 + offset))
        else:
            selection.append(slice(1, extent - 1))
    return padded[tuple(selection)]


def operator_terms(padded_fields, padded_visc, right_side, source, spacing):
    visc_cell = window(padded_visc, 0, 0)
    velocity = window(padded_fields[:3], 0, 0)
    inverse_sq = 1.0 / (spacing * spacing)
    half_inverse = 0.5 / spacing
    diagonal = jnp.zeros_like(visc_cell)
    viscous = jnp.zeros_like(velocity)
    divergence = jnp.zeros_like(visc_cell)
    gradients = []
    for spatial in range(3):
        for offset in (1, -1):
            face_visc = 0.5 * (visc_cell + window(padded_visc, spatial, offset))
            diagonal = diagonal + face_visc
            viscous = viscous + face_visc * (velocity - window(padded_fields[:3], spatial, offset))
        gradients.append(
            (window(padded_fields[3], spatial, 1) - window(padded_fields[3], spatial, -1))
            * half_inverse
        )
        divergence = (
            divergence
            + (
                window(padded_fields[spatial], spatial, 1)
                - window(padded_fields[spatial], spatial, -1)
            )
            * half_inverse
        )
    momentum = right_side - viscous * inverse_sq - jnp.stack(gradients)
    continuity = source - divergence
    return (momentum, continuity, diagonal * inverse_sq, visc_cell)


def relax_sweep(padded_fields, padded_visc, right_side, source, spacing):
    momentum, continuity, diagonal, visc_cell = operator_terms(
        padded_fields, padded_visc, right_side, source, spacing
    )
    velocity = window(padded_fields[:3], 0, 0)
    pressure = window(padded_fields[3], 0, 0)
    new_velocity = velocity + relax_weight * momentum / diagonal
    new_pressure = pressure + uzawa_step * visc_cell * continuity
    return jnp.concatenate([new_velocity, new_pressure[None]], axis=0)


def restrict(stacked):
    extents = stacked.shape
    blocks = stacked.reshape(extents[0], extents[1] // 2, 2, extents[2] // 2, 2, extents[3] // 2, 2)
    return blocks.mean(axis=(2, 4, 6))


def prolong(coarse_fields):
    return jnp.repeat(jnp.repeat(jnp.repeat(coarse_fields, 2, axis=1), 2, axis=2), 2, axis=3)


def fine_rim(fields):
    return padded_2(fields, (("gx", 1), ("gy", 3), ("gz", 2)), 1)


def zero_padded(coarse):
    return jnp.zeros(
        (4, coarse.shape[1] + 2, coarse.shape[2] + 2, coarse.shape[3] + 2), jnp.float32
    )


def local(velocity, pressure, viscosity, body_force):
    fields = jnp.concatenate([velocity, pressure[None]], axis=0)
    padded_visc = padded_2(viscosity, (("gx", 0), ("gy", 2), ("gz", 1)), 1)
    remaining = PRE
    for repeat_index in range(remaining):
        fields = relax_sweep(fine_rim(fields), padded_visc, body_force, 0.0, 1.0)
    momentum, continuity, diagonal, visc_cell = operator_terms(
        fine_rim(fields), padded_visc, body_force, 0.0, 1.0
    )
    packed = restrict(jnp.concatenate([momentum, continuity[None], viscosity[None]], axis=0))
    coarse = lax.all_gather(packed, "gx", axis=1, tiled=True)
    visc_rimmed = padded_2(coarse[4], (("gy", 2), ("gz", 1)), 1)
    coarse_visc = jnp.pad(visc_rimmed, ((1, 1), (0, 0), (0, 0)))
    correction = relax_sweep(zero_padded(coarse), coarse_visc, coarse[:3], coarse[3], 2.0)
    for repeat_index in range(COARSE - 1):
        rimmed = padded_2(correction, (("gy", 3), ("gz", 2)), 1)
        correction = relax_sweep(
            jnp.pad(rimmed, ((0, 0), (1, 1), (0, 0), (0, 0))),
            coarse_visc,
            coarse[:3],
            coarse[3],
            2.0,
        )
    share = packed.shape[1]
    own_part = lax.dynamic_slice_in_dim(correction, lax.axis_index("gx") * share, share, 1)
    fields = fields + prolong(own_part)
    for repeat_index in range(POST):
        fields = relax_sweep(fine_rim(fields), padded_visc, body_force, 0.0, 1.0)
    return (fields[:3], fields[3])


def solution(mesh):
    return jax.shard_map(
        local,
        mesh=mesh,
        in_specs=(
            P(None, "gx", "gz", "gy"),
            P("gx", "gz", "gy"),
            P("gx", "gz", "gy"),
            P(None, "gx", "gz", "gy"),
        ),
        out_specs=(P(None, "gx", "gz", "gy"), P("gx", "gz", "gy")),
        check_vma=False,
    )
```

profile of v0, /device:TPU:0, one launch (start us, length us, event | category | flops | bytes accessed | tf_op | source)
XLA Modules:
  0.0 309.7 jit_solution(3311332207650180916)
XLA Ops:
  2.8 4.9 %collective-permute-start.3 = (f32[4,1,32,128]{3,2,1,0:T(8,128)S(1)}, f32[4,1,32,128]{3,2,1,0:T(8,128)S(1)}, u32[]{:S(2)}, u32[]{:S(2)}) collective-permute-start(f32[4,1,32,128]{3,2,1,0:T(8,128)S(1)} %get-tuple-element.82), channel_id=1, source_target_pairs={{0,16},{1,17},{2,18},{3,19},{4,20},{5,21},{6,22},{7,23},{8,24},{9,... | collective-permute-start | bytes 196616 | tf_op jit(solution)/shard_map/ppermute | solution.py:22
  11.3 4.6 %collective-permute-start.7 = (f32[4,10,32,1]{2,0,3,1:T(4,128)S(1)}, f32[4,10,32,1]{2,0,3,1:T(4,128)S(1)}, u32[]{:S(2)}, u32[]{:S(2)}) collective-permute-start(f32[4,10,32,1]{2,0,3,1:T(4,128)S(1)} %copy.668), channel_id=1, source_target_pairs={{0,4},{4,8},{8,12},{1,5},{5,9},{9,13},{2,6},{6,10},{10,14},{3,7},{... | collective-permute-start | bytes 15368 | tf_op jit(solution)/shard_map/ppermute | solution.py:22
  17.5 4.3 %collective-permute-start.2 = (f32[1,32,128]{2,1,0:T(8,128)S(1)}, f32[1,32,128]{2,1,0:T(8,128)S(1)}, u32[]{:S(2)}, u32[]{:S(2)}) collective-permute-start(f32[1,32,128]{2,1,0:T(8,128)S(1)} %get-tuple-element.129), channel_id=1, source_target_pairs={{0,16},{1,17},{2,18},{3,19},{4,20},{5,21},{6,22},{7,23},{8,24},{9,... | collective-permute-start | bytes 49160 | tf_op jit(solution)/shard_map/ppermute | solution.py:22
  31.5 4.6 %collective-permute-start.4 = (f32[10,32,1]{2,1,0:T(8,128)S(1)}, f32[10,32,1]{2,1,0:T(8,128)S(1)}, u32[]{:S(2)}, u32[]{:S(2)}) collective-permute-start(f32[10,32,1]{2,1,0:T(8,128)S(1)} %get-tuple-element.125), channel_id=1, source_target_pairs={{0,4},{4,8},{8,12},{1,5},{5,9},{9,13},{2,6},{6,10},{10,14},{3,7},{... | collective-permute-start | bytes 3848 | tf_op jit(solution)/shard_map/ppermute | solution.py:22
  40.3 4.6 %collective-permute-done.5 = f32[10,32,1]{2,1,0:T(8,128)S(1)} collective-permute-done((f32[10,32,1]{2,1,0:T(8,128)S(1)}, f32[10,32,1]{2,1,0:T(8,128)S(1)}, u32[]{:S(2)}, u32[]{:S(2)}) %collective-permute-start.5) | collective-permute-done | bytes 1312 | tf_op jit(solution)/shard_map/ppermute | solution.py:23
  54.7 4.5 %collective-permute-start.13 = (f32[4,1,32,128]{3,2,1,0:T(8,128)S(1)}, f32[4,1,32,128]{3,2,1,0:T(8,128)S(1)}, u32[]{:S(2)}, u32[]{:S(2)}) collective-permute-start(f32[4,1,32,128]{3,2,1,0:T(8,128)S(1)} %get-tuple-element.80), channel_id=1, source_target_pairs={{0,16},{1,17},{2,18},{3,19},{4,20},{5,21},{6,22},{7,23},{8,24},{9,... | collective-permute-start | bytes 196616 | tf_op jit(solution)/shard_map/ppermute | solution.py:22
  82.5 4.5 %collective-permute-start.19 = (f32[4,1,32,128]{3,2,1,0:T(8,128)S(1)}, f32[4,1,32,128]{3,2,1,0:T(8,128)S(1)}, u32[]{:S(2)}, u32[]{:S(2)}) collective-permute-start(f32[4,1,32,128]{3,2,1,0:T(8,128)S(1)} %get-tuple-element.78), channel_id=1, source_target_pairs={{0,16},{1,17},{2,18},{3,19},{4,20},{5,21},{6,22},{7,23},{8,24},{9,... | collective-permute-start | bytes 196616 | tf_op jit(solution)/shard_map/ppermute | solution.py:22
  96.9 4.1 %collective-permute-done.21 = f32[4,10,32,1]{2,0,3,1:T(4,128)S(1)} collective-permute-done((f32[4,10,32,1]{2,0,3,1:T(4,128)S(1)}, f32[4,10,32,1]{2,0,3,1:T(4,128)S(1)}, u32[]{:S(2)}, u32[]{:S(2)}) %collective-permute-start.21) | collective-permute-done | bytes 5152 | tf_op jit(solution)/shard_map/ppermute | solution.py:23
  106.2 9.7 %concatenate.306 = f32[1,4,2,16,2,64,2]{6,5,4,3,2,1,0:T(8,128)} reshape(f32[8,32,128]{2,1,0:T(8,128)S(1)} %copy-done.2) | data formatting | bytes 262144 | tf_op jit(solution)/shard_map/concatenate | solution.py:111
  118.9 26.5 %concatenate.304 = f32[3,4,2,16,2,64,2]{6,5,4,3,2,1,0:T(8,128)} reshape(f32[3,8,32,128]{3,2,1,0:T(8,128)S(1)} %fusion.50) | data formatting | bytes 786432 | tf_op jit(solution)/shard_map/concatenate | solution.py:111
  145.7 9.8 %concatenate.305 = f32[1,4,2,16,2,64,2]{6,5,4,3,2,1,0:T(8,128)} reshape(f32[8,32,128]{2,1,0:T(8,128)S(1)} %fusion.200) | data formatting | bytes 262144 | tf_op jit(solution)/shard_map/concatenate | solution.py:111
  155.5 14.7 %maximum_reduce_fusion = f32[5,4,16,64]{3,2,1,0:T(8,128)S(1)} fusion(f32[1,4,2,16,2,64,2]{6,5,4,3,2,1,0:T(8,128)} %concatenate.306, f32[1,4,2,16,2,64,2]{6,5,4,3,2,1,0:T(8,128)} %concatenate.305, f32[3,4,2,16,2,64,2]{6,5,4,3,2,1,0:T(8,128)} %concatenate.304), kind=kLoop, calls=%fused_computation | loop fusion | flops 471040 | bytes 737280 | tf_op jit(solution)/shard_map/reduce_sum | solution.py:85
  170.3 6.3 %all_gather.3 = f32[5,8,16,64]{3,2,0,1:T(8,128)S(1)} all-gather(f32[5,4,16,64]{3,2,0,1:T(8,128)S(1)} %copy.637), channel_id=1, replica_groups=mesh['gx'=2,'gy'=4,'gz'=4] {'gx'}, dimensions={1}, use_global_device_ids=true | all-gather | bytes 245760 | tf_op jit(solution)/shard_map/all_gather | solution.py:112
  180.5 4.3 %collective-permute-done.25 = f32[8,16,1]{2,1,0:T(8,128)S(1)} collective-permute-done((f32[8,16,1]{2,1,0:T(8,128)S(1)}, f32[8,16,1]{2,1,0:T(8,128)S(1)}, u32[]{:S(2)}, u32[]{:S(2)}) %collective-permute-start.25) | collective-permute-done | bytes 544 | tf_op jit(solution)/shard_map/ppermute | solution.py:23
  189.8 4.5 %collective-permute-done.27 = f32[8,1,66]{2,1,0:T(1,128)S(1)} collective-permute-done((f32[8,1,66]{2,1,0:T(1,128)S(1)}, f32[8,1,66]{2,1,0:T(1,128)S(1)}, u32[]{:S(2)}, u32[]{:S(2)}) %collective-permute-start.27) | collective-permute-done | bytes 2144 | tf_op jit(solution)/shard_map/ppermute | solution.py:23
  202.3 4.7 %collective-permute-done.29 = f32[4,8,16,1]{3,2,1,0:T(8,128)S(1)} collective-permute-done((f32[4,8,16,1]{3,2,1,0:T(8,128)S(1)}, f32[4,8,16,1]{3,2,1,0:T(8,128)S(1)}, u32[]{:S(2)}, u32[]{:S(2)}) %collective-permute-start.29) | collective-permute-done | bytes 2080 | tf_op jit(solution)/shard_map/ppermute | solution.py:23
  217.7 4.3 %collective-permute-done.32 = f32[4,8,16,1]{3,2,1,0:T(8,128)S(1)} collective-permute-done((f32[4,8,16,1]{3,2,1,0:T(8,128)S(1)}, f32[4,8,16,1]{3,2,1,0:T(8,128)S(1)}, u32[]{:S(2)}, u32[]{:S(2)}) %collective-permute-start.32) | collective-permute-done | bytes 2080 | tf_op jit(solution)/shard_map/ppermute | solution.py:22
  222.1 4.7 %collective-permute-done.33 = f32[4,8,16,1]{3,2,1,0:T(8,128)S(1)} collective-permute-done((f32[4,8,16,1]{3,2,1,0:T(8,128)S(1)}, f32[4,8,16,1]{3,2,1,0:T(8,128)S(1)}, u32[]{:S(2)}, u32[]{:S(2)}) %collective-permute-start.33) | collective-permute-done | bytes 2080 | tf_op jit(solution)/shard_map/ppermute | solution.py:23
  237.1 4.3 %collective-permute-done.36 = f32[4,8,16,1]{3,2,1,0:T(8,128)S(1)} collective-permute-done((f32[4,8,16,1]{3,2,1,0:T(8,128)S(1)}, f32[4,8,16,1]{3,2,1,0:T(8,128)S(1)}, u32[]{:S(2)}, u32[]{:S(2)}) %collective-permute-start.36) | collective-permute-done | bytes 2080 | tf_op jit(solution)/shard_map/ppermute | solution.py:22
  241.5 4.7 %collective-permute-done.37 = f32[4,8,16,1]{3,2,1,0:T(8,128)S(1)} collective-permute-done((f32[4,8,16,1]{3,2,1,0:T(8,128)S(1)}, f32[4,8,16,1]{3,2,1,0:T(8,128)S(1)}, u32[]{:S(2)}, u32[]{:S(2)}) %collective-permute-start.37) | collective-permute-done | bytes 2080 | tf_op jit(solution)/shard_map/ppermute | solution.py:23
  260.0 4.5 %collective-permute-start.41 = (f32[4,1,32,128]{3,2,1,0:T(8,128)S(1)}, f32[4,1,32,128]{3,2,1,0:T(8,128)S(1)}, u32[]{:S(2)}, u32[]{:S(2)}) collective-permute-start(f32[4,1,32,128]{3,2,1,0:T(8,128)S(1)} %get-tuple-element.76), channel_id=1, source_target_pairs={{0,16},{1,17},{2,18},{3,19},{4,20},{5,21},{6,22},{7,23},{8,24},{9,... | collective-permute-start | bytes 196616 | tf_op jit(solution)/shard_map/ppermute | solution.py:22
  270.9 4.0 %collective-permute-done.43 = f32[4,10,32,1]{2,0,3,1:T(4,128)S(1)} collective-permute-done((f32[4,10,32,1]{2,0,3,1:T(4,128)S(1)}, f32[4,10,32,1]{2,0,3,1:T(4,128)S(1)}, u32[]{:S(2)}, u32[]{:S(2)}) %collective-permute-start.43) | collective-permute-done | bytes 5152 | tf_op jit(solution)/shard_map/ppermute | solution.py:23
  284.9 4.5 %collective-permute-start.47 = (f32[4,1,32,128]{3,2,1,0:T(8,128)S(1)}, f32[4,1,32,128]{3,2,1,0:T(8,128)S(1)}, u32[]{:S(2)}, u32[]{:S(2)}) collective-permute-start(f32[4,1,32,128]{3,2,1,0:T(8,128)S(1)} %get-tuple-element.74), channel_id=1, source_target_pairs={{0,16},{1,17},{2,18},{3,19},{4,20},{5,21},{6,22},{7,23},{8,24},{9,... | collective-permute-start | bytes 196616 | tf_op jit(solution)/shard_map/ppermute | solution.py:22
  296.2 4.0 %collective-permute-done.49 = f32[4,10,32,1]{2,0,3,1:T(4,128)S(1)} collective-permute-done((f32[4,10,32,1]{2,0,3,1:T(4,128)S(1)}, f32[4,10,32,1]{2,0,3,1:T(4,128)S(1)}, u32[]{:S(2)}, u32[]{:S(2)}) %collective-permute-start.49) | collective-permute-done | bytes 5152 | tf_op jit(solution)/shard_map/ppermute | solution.py:23
  (314 shorter events, 155.4 us)
Async XLA Ops:
  1.5 6.5 %collective-permute-start.1 = (f32[4,1,32,128]{3,2,1,0:T(8,128)S(1)}, f32[4,1,32,128]{3,2,1,0:T(8,128)S(1)}, u32[]{:S(2)}, u32[]{:S(2)}) collective-permute-start(f32[4,1,32,128]{3,2,1,0:T(8,128)S(1)} %get-tuple-element.83), channel_id=1, source_target_pairs={{16,0},{17,1},{18,2},{19,3},{20,4},{21,5},{22,6},{23,7},{24,8},{25... | collective-permute-start | bytes 196616 | tf_op jit(solution)/shard_map/ppermute | solution.py:23
  2.8 6.8 %collective-permute-start.3 = (f32[4,1,32,128]{3,2,1,0:T(8,128)S(1)}, f32[4,1,32,128]{3,2,1,0:T(8,128)S(1)}, u32[]{:S(2)}, u32[]{:S(2)}) collective-permute-start(f32[4,1,32,128]{3,2,1,0:T(8,128)S(1)} %get-tuple-element.82), channel_id=1, source_target_pairs={{0,16},{1,17},{2,18},{3,19},{4,20},{5,21},{6,22},{7,23},{8,24},{9,... | collective-permute-start | bytes 196616 | tf_op jit(solution)/shard_map/ppermute | solution.py:22
  11.3 11.8 %collective-permute-start.7 = (f32[4,10,32,1]{2,0,3,1:T(4,128)S(1)}, f32[4,10,32,1]{2,0,3,1:T(4,128)S(1)}, u32[]{:S(2)}, u32[]{:S(2)}) collective-permute-start(f32[4,10,32,1]{2,0,3,1:T(4,128)S(1)} %copy.668), channel_id=1, source_target_pairs={{0,4},{4,8},{8,12},{1,5},{5,9},{9,13},{2,6},{6,10},{10,14},{3,7},{... | collective-permute-start | bytes 15368 | tf_op jit(solution)/shard_map/ppermute | solution.py:22
  16.2 7.2 %collective-permute-start.8 = (f32[4,10,32,1]{2,0,3,1:T(4,128)S(1)}, f32[4,10,32,1]{2,0,3,1:T(4,128)S(1)}, u32[]{:S(2)}, u32[]{:S(2)}) collective-permute-start(f32[4,10,32,1]{2,0,3,1:T(4,128)S(1)} %copy.669), channel_id=1, source_target_pairs={{4,0},{8,4},{12,8},{5,1},{9,5},{13,9},{6,2},{10,6},{14,10},{7,3},{... | collective-permute-start | bytes 15368 | tf_op jit(solution)/shard_map/ppermute | solution.py:23
  17.5 10.9 %collective-permute-start.2 = (f32[1,32,128]{2,1,0:T(8,128)S(1)}, f32[1,32,128]{2,1,0:T(8,128)S(1)}, u32[]{:S(2)}, u32[]{:S(2)}) collective-permute-start(f32[1,32,128]{2,1,0:T(8,128)S(1)} %get-tuple-element.129), channel_id=1, source_target_pairs={{0,16},{1,17},{2,18},{3,19},{4,20},{5,21},{6,22},{7,23},{8,24},{9,... | collective-permute-start | bytes 49160 | tf_op jit(solution)/shard_map/ppermute | solution.py:22
  21.8 9.0 %collective-permute-start = (f32[1,32,128]{2,1,0:T(8,128)S(1)}, f32[1,32,128]{2,1,0:T(8,128)S(1)}, u32[]{:S(2)}, u32[]{:S(2)}) collective-permute-start(f32[1,32,128]{2,1,0:T(8,128)S(1)} %get-tuple-element.128), channel_id=1, source_target_pairs={{16,0},{17,1},{18,2},{19,3},{20,4},{21,5},{22,6},{23,7},{24,8},{25... | collective-permute-start | bytes 49160 | tf_op jit(solution)/shard_map/ppermute | solution.py:23
  31.5 8.8 %collective-permute-start.4 = (f32[10,32,1]{2,1,0:T(8,128)S(1)}, f32[10,32,1]{2,1,0:T(8,128)S(1)}, u32[]{:S(2)}, u32[]{:S(2)}) collective-permute-start(f32[10,32,1]{2,1,0:T(8,128)S(1)} %get-tuple-element.125), channel_id=1, source_target_pairs={{0,4},{4,8},{8,12},{1,5},{5,9},{9,13},{2,6},{6,10},{10,14},{3,7},{... | collective-permute-start | bytes 3848 | tf_op jit(solution)/shard_map/ppermute | solution.py:22
  36.1 8.9 %collective-permute-start.5 = (f32[10,32,1]{2,1,0:T(8,128)S(1)}, f32[10,32,1]{2,1,0:T(8,128)S(1)}, u32[]{:S(2)}, u32[]{:S(2)}) collective-permute-start(f32[10,32,1]{2,1,0:T(8,128)S(1)} %get-tuple-element.126), channel_id=1, source_target_pairs={{4,0},{8,4},{12,8},{5,1},{9,5},{13,9},{6,2},{10,6},{14,10},{7,3},{... | collective-permute-start | bytes 3848 | tf_op jit(solution)/shard_map/ppermute | solution.py:23
  53.4 6.2 %collective-permute-start.12 = (f32[4,1,32,128]{3,2,1,0:T(8,128)S(1)}, f32[4,1,32,128]{3,2,1,0:T(8,128)S(1)}, u32[]{:S(2)}, u32[]{:S(2)}) collective-permute-start(f32[4,1,32,128]{3,2,1,0:T(8,128)S(1)} %get-tuple-element.81), channel_id=1, source_target_pairs={{16,0},{17,1},{18,2},{19,3},{20,4},{21,5},{22,6},{23,7},{24,8},{25... | collective-permute-start | bytes 196616 | tf_op jit(solution)/shard_map/ppermute | solution.py:23
  54.7 6.4 %collective-permute-start.13 = (f32[4,1,32,128]{3,2,1,0:T(8,128)S(1)}, f32[4,1,32,128]{3,2,1,0:T(8,128)S(1)}, u32[]{:S(2)}, u32[]{:S(2)}) collective-permute-start(f32[4,1,32,128]{3,2,1,0:T(8,128)S(1)} %get-tuple-element.80), channel_id=1, source_target_pairs={{0,16},{1,17},{2,18},{3,19},{4,20},{5,21},{6,22},{7,23},{8,24},{9,... | collective-permute-start | bytes 196616 | tf_op jit(solution)/shard_map/ppermute | solution.py:22
  81.2 6.2 %collective-permute-start.18 = (f32[4,1,32,128]{3,2,1,0:T(8,128)S(1)}, f32[4,1,32,128]{3,2,1,0:T(8,128)S(1)}, u32[]{:S(2)}, u32[]{:S(2)}) collective-permute-start(f32[4,1,32,128]{3,2,1,0:T(8,128)S(1)} %get-tuple-element.79), channel_id=1, source_target_pairs={{16,0},{17,1},{18,2},{19,3},{20,4},{21,5},{22,6},{23,7},{24,8},{25... | collective-permute-start | bytes 196616 | tf_op jit(solution)/shard_map/ppermute | solution.py:23
  82.5 6.4 %collective-permute-start.19 = (f32[4,1,32,128]{3,2,1,0:T(8,128)S(1)}, f32[4,1,32,128]{3,2,1,0:T(8,128)S(1)}, u32[]{:S(2)}, u32[]{:S(2)}) collective-permute-start(f32[4,1,32,128]{3,2,1,0:T(8,128)S(1)} %get-tuple-element.78), channel_id=1, source_target_pairs={{0,16},{1,17},{2,18},{3,19},{4,20},{5,21},{6,22},{7,23},{8,24},{9,... | collective-permute-start | bytes 196616 | tf_op jit(solution)/shard_map/ppermute | solution.py:22
  101.7 14.2 %collective-permute-start.22 = (f32[4,10,1,130]{3,0,2,1:T(4,128)S(1)}, f32[4,10,1,130]{3,0,2,1:T(4,128)S(1)}, u32[]{:S(2)}, u32[]{:S(2)}) collective-permute-start(f32[4,10,1,130]{3,0,2,1:T(4,128)S(1)} %copy.629), channel_id=1, source_target_pairs={{1,0},{2,1},{3,2},{5,4},{6,5},{7,6},{9,8},{10,9},{11,10},{13,12},{... | collective-permute-start | bytes 62408 | tf_op jit(solution)/shard_map/ppermute | solution.py:23
  103.0 13.0 %collective-permute-start.23 = (f32[4,10,1,130]{3,0,2,1:T(4,128)S(1)}, f32[4,10,1,130]{3,0,2,1:T(4,128)S(1)}, u32[]{:S(2)}, u32[]{:S(2)}) collective-permute-start(f32[4,10,1,130]{3,0,2,1:T(4,128)S(1)} %copy.631), channel_id=1, source_target_pairs={{0,1},{1,2},{2,3},{4,5},{5,6},{6,7},{8,9},{9,10},{10,11},{12,13},{... | collective-permute-start | bytes 62408 | tf_op jit(solution)/shard_map/ppermute | solution.py:22
  178.6 6.2 %collective-permute-start.25 = (f32[8,16,1]{2,1,0:T(8,128)S(1)}, f32[8,16,1]{2,1,0:T(8,128)S(1)}, u32[]{:S(2)}, u32[]{:S(2)}) collective-permute-start(f32[8,16,1]{2,1,0:T(8,128)S(1)} %get-tuple-element.143), channel_id=1, source_target_pairs={{4,0},{8,4},{12,8},{5,1},{9,5},{13,9},{6,2},{10,6},{14,10},{7,3},{... | collective-permute-start | bytes 1544 | tf_op jit(solution)/shard_map/ppermute | solution.py:23
  195.1 7.2 %collective-permute-start.28 = (f32[4,8,16,1]{3,2,1,0:T(8,128)S(1)}, f32[4,8,16,1]{3,2,1,0:T(8,128)S(1)}, u32[]{:S(2)}, u32[]{:S(2)}) collective-permute-start(f32[4,8,16,1]{3,2,1,0:T(8,128)S(1)} %get-tuple-element.122), channel_id=1, source_target_pairs={{0,4},{4,8},{8,12},{1,5},{5,9},{9,13},{2,6},{6,10},{10,14},{3,7},{... | collective-permute-start | bytes 6152 | tf_op jit(solution)/shard_map/ppermute | solution.py:22
  197.1 9.9 %collective-permute-start.29 = (f32[4,8,16,1]{3,2,1,0:T(8,128)S(1)}, f32[4,8,16,1]{3,2,1,0:T(8,128)S(1)}, u32[]{:S(2)}, u32[]{:S(2)}) collective-permute-start(f32[4,8,16,1]{3,2,1,0:T(8,128)S(1)} %get-tuple-element.121), channel_id=1, source_target_pairs={{4,0},{8,4},{12,8},{5,1},{9,5},{13,9},{6,2},{10,6},{14,10},{7,3},{... | collective-permute-start | bytes 6152 | tf_op jit(solution)/shard_map/ppermute | solution.py:23
  214.5 7.6 %collective-permute-start.32 = (f32[4,8,16,1]{3,2,1,0:T(8,128)S(1)}, f32[4,8,16,1]{3,2,1,0:T(8,128)S(1)}, u32[]{:S(2)}, u32[]{:S(2)}) collective-permute-start(f32[4,8,16,1]{3,2,1,0:T(8,128)S(1)} %get-tuple-element.120), channel_id=1, source_target_pairs={{0,4},{4,8},{8,12},{1,5},{5,9},{9,13},{2,6},{6,10},{10,14},{3,7},{... | collective-permute-start | bytes 6152 | tf_op jit(solution)/shard_map/ppermute | solution.py:22
  216.4 10.4 %collective-permute-start.33 = (f32[4,8,16,1]{3,2,1,0:T(8,128)S(1)}, f32[4,8,16,1]{3,2,1,0:T(8,128)S(1)}, u32[]{:S(2)}, u32[]{:S(2)}) collective-permute-start(f32[4,8,16,1]{3,2,1,0:T(8,128)S(1)} %get-tuple-element.119), channel_id=1, source_target_pairs={{4,0},{8,4},{12,8},{5,1},{9,5},{13,9},{6,2},{10,6},{14,10},{7,3},{... | collective-permute-start | bytes 6152 | tf_op jit(solution)/shard_map/ppermute | solution.py:23
  233.9 7.6 %collective-permute-start.36 = (f32[4,8,16,1]{3,2,1,0:T(8,128)S(1)}, f32[4,8,16,1]{3,2,1,0:T(8,128)S(1)}, u32[]{:S(2)}, u32[]{:S(2)}) collective-permute-start(f32[4,8,16,1]{3,2,1,0:T(8,128)S(1)} %get-tuple-element.118), channel_id=1, source_target_pairs={{0,4},{4,8},{8,12},{1,5},{5,9},{9,13},{2,6},{6,10},{10,14},{3,7},{... | collective-permute-start | bytes 6152 | tf_op jit(solution)/shard_map/ppermute | solution.py:22
  235.8 10.4 %collective-permute-start.37 = (f32[4,8,16,1]{3,2,1,0:T(8,128)S(1)}, f32[4,8,16,1]{3,2,1,0:T(8,128)S(1)}, u32[]{:S(2)}, u32[]{:S(2)}) collective-permute-start(f32[4,8,16,1]{3,2,1,0:T(8,128)S(1)} %get-tuple-element.117), channel_id=1, source_target_pairs={{4,0},{8,4},{12,8},{5,1},{9,5},{13,9},{6,2},{10,6},{14,10},{7,3},{... | collective-permute-start | bytes 6152 | tf_op jit(solution)/shard_map/ppermute | solution.py:23
  260.0 6.4 %collective-permute-start.41 = (f32[4,1,32,128]{3,2,1,0:T(8,128)S(1)}, f32[4,1,32,128]{3,2,1,0:T(8,128)S(1)}, u32[]{:S(2)}, u32[]{:S(2)}) collective-permute-start(f32[4,1,32,128]{3,2,1,0:T(8,128)S(1)} %get-tuple-element.76), channel_id=1, source_target_pairs={{0,16},{1,17},{2,18},{3,19},{4,20},{5,21},{6,22},{7,23},{8,24},{9,... | collective-permute-start | bytes 196616 | tf_op jit(solution)/shard_map/ppermute | solution.py:22
  283.6 6.2 %collective-permute-start.46 = (f32[4,1,32,128]{3,2,1,0:T(8,128)S(1)}, f32[4,1,32,128]{3,2,1,0:T(8,128)S(1)}, u32[]{:S(2)}, u32[]{:S(2)}) collective-permute-start(f32[4,1,32,128]{3,2,1,0:T(8,128)S(1)} %get-tuple-element.75), channel_id=1, source_target_pairs={{16,0},{17,1},{18,2},{19,3},{20,4},{21,5},{22,6},{23,7},{24,8},{25... | collective-permute-start | bytes 196616 | tf_op jit(solution)/shard_map/ppermute | solution.py:23
  284.9 6.6 %collective-permute-start.47 = (f32[4,1,32,128]{3,2,1,0:T(8,128)S(1)}, f32[4,1,32,128]{3,2,1,0:T(8,128)S(1)}, u32[]{:S(2)}, u32[]{:S(2)}) collective-permute-start(f32[4,1,32,128]{3,2,1,0:T(8,128)S(1)} %get-tuple-element.74), channel_id=1, source_target_pairs={{0,16},{1,17},{2,18},{3,19},{4,20},{5,21},{6,22},{7,23},{8,24},{9,... | collective-permute-start | bytes 196616 | tf_op jit(solution)/shard_map/ppermute | solution.py:22
  (81 other events, 993.3 us)
where the time goes:
time: 315 us; the launch traced here: 310 us
  starting transfers between devices  118 us (37%)
  waiting for transfers between devices  80.8 us (26%)
  local copies, waits for them, and re-layouts  64.7 us (21%)
  other arithmetic  37.7 us (12%)
  blocking collectives  6.29 us (2%)
    ppermute x26, starting transfers between devices, padded_2(): before = lax.ppermute(last, axis, up)  83.9 us
    ppermute x26, waiting for transfers between devices, padded_2(): after = lax.ppermute(first, axis, down)  53.4 us
    concatenate x3, local copies, waits for them, and re-layouts, local(): jnp.concatenate([momentum, continuity[None], viscosity[None]], axis=0)  46 us
    ppermute x26, starting transfers between devices, padded_2(): after = lax.ppermute(first, axis, down)  33.8 us
    ppermute x26, waiting for transfers between devices, padded_2(): before = lax.ppermute(last, axis, up)  27.4 us
    reduce_sum x1, other arithmetic, restrict(): return blocks.mean(axis=(2, 4, 6))  14.7 us
    concatenate x19, other arithmetic, padded_2(): array = jnp.concatenate([before, array, after], axis=dim)  6.91 us
  transfers between devices with their start and end apart: 52, of which 33 were waited for; matrix products, arithmetic and copies ran while one was open for 5% of the time, Pallas kernels for 0%

commit v1 on v0

v1 whole, which is shorter than its diff:
```python
import jax
import jax.numpy as jnp
from jax import lax
from jax.experimental import pallas as pl
from jax.experimental.pallas import tpu as pltpu
from jax.sharding import PartitionSpec as P

LANES = 128
SLOT = 8
F32 = jnp.float32
relax_weight = 0.6


def call(body, outs, args, scratch=(), cost=1):
    return pl.pallas_call(
        body,
        out_shape=[jax.ShapeDtypeStruct(shape, F32) for shape in outs],
        in_specs=[pl.BlockSpec(memory_space=pltpu.VMEM)] * len(args),
        out_specs=[pl.BlockSpec(memory_space=pltpu.VMEM)] * len(outs),
        scratch_shapes=[pltpu.VMEM(shape, F32) for shape in scratch],
        compiler_params=pltpu.CompilerParams(vmem_limit_bytes=40 * 2**20),
        cost_estimate=pl.CostEstimate(
            flops=cost * 10**6, bytes_accessed=cost * 10**6, transcendentals=0
        ),
    )(*args)


def swap(array, axis, which):
    count = lax.axis_size(axis)
    if axis == "gy" and which == 1:
        other = lax.axis_size("gz")
        pairs = []
        for i in range(count):
            j = i + 1 if i % 2 else i - 1
            for k in range(other):
                to = j * other + k if 0 <= j < count else i * other + (k ^ 1)
                pairs.append((i * other + k, to))
        return lax.ppermute(array, ("gy", "gz"), pairs)
    pairs = []
    for i in range(which, count, 2):
        j = (i + 1) % count
        pairs += [(i, j), (j, i)]
    return lax.ppermute(array, axis, pairs)


def place(axis):
    i = lax.axis_index(axis)
    last = lax.axis_size(axis) - 1
    return i, jnp.where(i > 0, 1, 0), jnp.where(i < last, 1, 0)


def iota(shape, dim):
    return lax.broadcasted_iota(jnp.int32, shape, dim)


def truth(flag, shape):
    return jnp.full(shape, flag, jnp.int32) > 0


def roll(x, shift, dim):
    if isinstance(shift, int):
        shift %= x.shape[dim]
        return x if shift == 0 else pltpu.roll(x, shift, dim)
    return pltpu.roll(x, lax.rem(shift + 2 * x.shape[dim], x.shape[dim]), dim)


def high_side(axis, message):
    return jnp.where(lax.axis_index(axis) % 2 == message, 1, 0)


def left_right(axis, a, b):
    odd = truth(lax.axis_index(axis) % 2, a.shape)
    return jnp.where(odd, a, b), jnp.where(odd, b, a)


def x_messages():
    return 1 if lax.axis_size("gx") == 2 else 2


def pair_edges(planes, fields, rows):
    lane = iota((rows, LANES), 1) // SLOT
    half = fields // 2
    out = []
    for j in range(half):
        total = jnp.zeros((rows, LANES), F32)
        for part in range(2):
            for q, x in enumerate(planes(j + part * half)):
                slot = q + part * (LANES // SLOT // 2)
                total = jnp.where(lane == slot, roll(x, slot * SLOT + 4, 1), total)
        out.append(total)
    return out


def merge_y(a, b):
    _, has_left, has_right = place("gy")
    left, right = left_right("gy", a, b)
    spot = iota(a.shape, 1) % SLOT
    kept = (spot < 4 * has_left) | (spot >= SLOT - 4 * has_right)
    return jnp.where(kept, jnp.where(spot < 4, left, right), 0.0)


def first_pack(v, p, e, f, x_main, y_main):
    nx, nz, _ = p.shape

    def plane(i, q):
        return v[i, q] if i < 3 else p[q] if i == 3 else e[q] if i == 4 else f[i - 5, q]

    for m in range(x_main.shape[0]):
        high = high_side("gx", m)
        n = 0
        for i in range(8):
            width = 3 if i < 5 else 2
            for j in range(width):
                x_main[m, n] = plane(i, high * (nx - width) + j)
                n += 1
    edges = pair_edges(lambda i: [plane(i, q) for q in range(nx)], 8, nz)
    for j in range(4):
        y_main[j] = edges[j]


def z_strip(low, high, toward_right, shift):
    row = iota((8, LANES), 0)
    right = truth(toward_right, (8, LANES))
    first = jnp.where(right, roll(high[0], 4, 0), low[0])
    second = jnp.where(right, high[1], roll(low[1], 4, 0))
    return jnp.where(row < 4, first, second)


def second_pack(v, p, e, f, y_a, y_b, halo, z_a, z_b):
    nx, nz, _ = p.shape

    def tile(i, q, top):
        at = pl.ds(nz - 8, 8) if top else pl.ds(0, 8)
        if i < 3:
            return v[i, q, at]
        return p[q, at] if i == 3 else e[q, at] if i == 4 else f[i - 5, q, at]

    merged = [merge_y(y_a[j], y_b[j]) for j in range(4)]
    for j in range(4):
        halo[j] = merged[j]
    for m, out in enumerate((z_a, z_b)):
        right = high_side("gz", m)
        for j in range(4):
            for q in range(nx):
                low = tile(j, q, False), tile(j + 4, q, False)
                high = tile(j, q, True), tile(j + 4, q, True)
                out[j * nx + q] = z_strip(low, high, right, 4)
        for j in range(2):
            low = merged[j][:8], merged[j + 2][:8]
            high = merged[j][nz - 8 :], merged[j + 2][nz - 8 :]
            out[4 * nx + j] = z_strip(low, high, right, 4)


def z_tiles(a, b):
    _, has_left, has_right = place("gz")
    left, right = left_right("gz", a, b)
    row = iota(a.shape, 0)
    kept = (row < 4 * has_right) | (row >= 8 - 4 * has_left)
    first = jnp.where(row < 4, right, roll(left, 4, 0))
    second = jnp.where(row < 4, roll(right, 4, 0), left)
    return jnp.where(kept, first, 0.0), jnp.where(kept, second, 0.0)


def third_pack(z_a, z_b, halo, z_halo, halo_full, x_rim):
    nx = z_halo.shape[1]
    nz = halo.shape[1]
    for j in range(4):
        for q in range(nx):
            z_halo[j, q], z_halo[j + 4, q] = z_tiles(z_a[j * nx + q], z_b[j * nx + q])
    for j in range(4):
        halo_full[j, pl.ds(0, nz)] = halo[j]
    for j in range(2):
        first, second = z_tiles(z_a[4 * nx + j], z_b[4 * nx + j])
        halo_full[j, pl.ds(nz, 8)] = first
        halo_full[j + 2, pl.ds(nz, 8)] = second
    pack_rim(x_rim, z_halo, lambda j: halo_full[j], 8, (2,) * 5 + (1,) * 3, 3, 32)


def pack_rim(x_rim, z_halo, halo_pair, fields, widths, planes, stride):
    nx = z_halo.shape[1]
    half = fields // 2
    per_column = LANES // stride
    for m in range(x_rim.shape[0]):
        high = high_side("gx", m)
        n = 0
        for i in range(fields):
            for j in range(widths[i]):
                x_rim[m, n] = z_halo[i, high * (nx - widths[i]) + j]
                n += 1
        pairs = [halo_pair(j) for j in range(half)]
        rows = pairs[0].shape[0]
        column = iota((rows, LANES), 1) // stride
        first = high * (nx - planes) * SLOT
        for c in range(-(-fields // per_column)):
            total = jnp.zeros((rows, LANES), F32)
            for t in range(min(per_column, fields - c * per_column)):
                i = c * per_column + t
                at = t * stride - first - (i // half) * (LANES // 2)
                total = jnp.where(column == t, roll(pairs[i % half], at + LANES, 1), total)
            for r in range(rows // 8):
                x_rim[m, n] = total[8 * r : 8 * r + 8]
                n += 1


def main_shifts(x, halo, p):
    lane = iota(x.shape, 1)
    beside = roll(halo, LANES - SLOT * p - 4, 1)
    rows = x.shape[0]
    return (
        roll(jnp.where(lane == 0, beside, x), LANES - 1, 1),
        roll(jnp.where(lane == LANES - 1, beside, x), 1, 1),
        roll(x, rows - 1, 0),
        roll(x, 1, 0),
    )


def halo_shifts(x, edge):
    spot = iota(x.shape, 1) % SLOT
    rows = x.shape[0]
    return (
        roll(x, LANES - SLOT, 1),
        roll(x, SLOT, 1),
        roll(jnp.where(spot == 4, edge, x), LANES - 1, 1),
        roll(jnp.where(spot == 3, edge, x), 1, 1),
        roll(x, rows - 1, 0),
        roll(x, 1, 0),
    )


def main_weights(e, halo_e, w, lo, hi):
    def face(p, carry):
        w[0][p] = e[p] + e[p + 1]
        return carry

    lax.fori_loop(lo - 1, hi, face, 0)

    def body(p, carry):
        x = e[p]
        total = w[0][p] + w[0][p - 1]
        for n, y in enumerate(main_shifts(x, halo_e[...], p)):
            total += x + y
            w[1 + n][p] = x + y
        w[5][p] = relax_weight / total
        return carry

    lax.fori_loop(lo, hi, body, 0)


def halo_weights(e, edge_e, w):
    x = e[...]
    total = jnp.zeros_like(x)
    for n, y in enumerate(halo_shifts(x, edge_e[...])):
        total += x + y
        w[n] = x + y
    w[6] = relax_weight / total


def terms(k, up, down, yp, ym, zp, zm):
    return (up - down, zp - zm, yp - ym)[k]


def main_operator(src, halo, w, force, p, fields=(0, 1, 2)):
    wxp, wxm, wyp, wym, wzp, wzm = w[0][p], w[0][p - 1], w[1][p], w[2][p], w[3][p], w[4][p]
    x = src[3, p]
    around = main_shifts(x, halo[3], p)
    up, down = src[3, p + 1], src[3, p - 1]
    olds, sums, spread = [], [], 0.0
    for k in range(3):
        u = src[k, p]
        yp, ym, zp, zm = main_shifts(u, halo[k], p)
        xp, xm = src[k, p + 1], src[k, p - 1]
        total = force[k, p] - terms(k, up, down, *around)
        total += wxp * xp + wxm * xm
        total += wyp * yp + wym * ym
        total += wzp * zp + wzm * zm
        spread += terms(k, xp, xm, yp, ym, zp, zm)
        olds.append(u)
        sums.append(total)
    olds.append(x)
    return olds, sums, spread


def halo_operator(halo, edge, w, force):
    x = halo[3]
    px = halo_shifts(x, edge[3])
    olds, sums, spread = [], [], 0.0
    for k in range(3):
        u = halo[k]
        around = halo_shifts(u, edge[k])
        total = force[k] - terms(k, *px)
        for n in range(6):
            total += w[n] * around[n]
        spread += terms(k, *around)
        olds.append(u)
        sums.append(total)
    olds.append(x)
    return olds, sums, spread


def relaxed(olds, sums, spread, factor, e):
    new = [0.4 * olds[k] + factor * sums[k] for k in range(3)]
    return new + [olds[3] - 0.25 * e * spread]


def add_edge(edge, k, p, x):
    slot = iota(x.shape, 1) // SLOT
    edge[k] = jnp.where(slot == p, roll(x, p * SLOT + 4, 1), edge[k])


def fill_edges(edge, src, fields, lo, hi):
    for k in range(fields):
        edge[k] = jnp.zeros(edge.shape[1:], F32)

    def body(p, carry):
        for k in range(fields):
            add_edge(edge, k, p, src[k, p])
        return carry

    lax.fori_loop(lo, hi, body, 0)


def fine_masks(rows, slots):
    nz = rows - 8
    _, zl, zr = place("gz")
    _, yl, yr = place("gy")
    _, xl, xr = place("gx")
    r = iota((8, LANES), 0)
    tile = (r < 4 * zr) | (r >= 8 - 4 * zl)
    r = iota((rows, LANES), 0)
    lane = iota((rows, LANES), 1)
    spot, slot = lane % SLOT, lane // SLOT
    column = (r < nz + 4 * zr) | (r >= rows - 4 * zl)
    column &= (spot < 4 * yl) | (spot >= SLOT - 4 * yr)
    column &= (slot >= 3 - 3 * xl) & (slot < slots - 3 + 3 * xr)
    return tile, column


def fine_sweep(src, halo, edge, dst, halo_dst, edge_dst, w, hw, e, halo_e, force, halo_f, lo, hi, masks):
    tile, column = masks
    nz = src.shape[2] - 8
    if edge_dst is not None:
        for k in range(4):
            edge_dst[k] = jnp.zeros(edge_dst.shape[1:], F32)

    def body(p, carry):
        new = relaxed(*main_operator(src, halo, w, force, p), w[5][p], e[p])
        for k in range(4):
            x = new[k]
            dst[k, p, pl.ds(0, nz)] = x[:nz]
            x8 = jnp.where(tile, x[nz:], 0.0)
            dst[k, p, pl.ds(nz, 8)] = x8
            if edge_dst is not None:
                add_edge(edge_dst, k, p, jnp.concatenate([x[:nz], x8], axis=0))
        return carry

    lax.fori_loop(lo, hi, body, 0)
    new = relaxed(*halo_operator(halo, edge, hw, halo_f), hw[6], halo_e[...])
    for k in range(4):
        halo_dst[k] = jnp.where(column, new[k], 0.0)


def spans(slots, width):
    _, xl, xr = place("gx")
    return 3 - width * xl, slots - 3 + width * xr


def own_slots(x, nx, part):
    lane = iota(x.shape, 1)
    x = roll(x, 3 * SLOT - part * (LANES // 2), 1)
    return jnp.where((lane >= 3 * SLOT) & (lane < (3 + nx) * SLOT), x, 0.0)


def x_side(m):
    right = high_side("gx", m)
    _, has_left, has_right = place("gx")
    return right, jnp.where(right > 0, has_right, has_left)


def rim_halo(x, t, stride, planes, right, valid, nx):
    base = right * (nx + 3) + (1 - right) * (3 - planes)
    lane = iota(x.shape, 1)
    x = roll(x, base * SLOT - t * stride + LANES, 1)
    kept = (lane >= base * SLOT) & (lane < (base + planes * valid) * SLOT)
    return jnp.where(kept, x, 0.0), kept


def viscosity_force(e_in, f_in, z_halo, halo_full, x_main, x_rim, e, halo_e, force, halo_f):
    nx, nz, _ = e_in.shape
    slots = nx + 6
    zero = jnp.zeros((nz + 8, LANES), F32)
    for p in list(range(3)) + list(range(nx + 3, slots)):
        e[p] = zero
        for k in range(3):
            force[k, p] = zero
    for q in range(nx):
        e[q + 3, pl.ds(0, nz)] = e_in[q]
        e[q + 3, pl.ds(nz, 8)] = z_halo[4, q]
        for k in range(3):
            force[k, q + 3, pl.ds(0, nz)] = 2.0 * f_in[k, q]
            force[k, q + 3, pl.ds(nz, 8)] = 2.0 * z_halo[5 + k, q]
    halo_e[...] = own_slots(halo_full[0], nx, 1)
    for k in range(3):
        halo_f[k] = 2.0 * own_slots(halo_full[k + 1], nx, 1)
    for m in range(x_main.shape[0]):
        right, valid = x_side(m)
        there = truth(valid, (nz, LANES))
        there8 = truth(valid, (8, LANES))
        for j in range(3):
            e[right * (nx + 3) + j, pl.ds(0, nz)] = jnp.where(there, x_main[m, 12 + j], 0.0)
        for j in range(2):
            at = right * (nx + 2) + 1 + j
            e[at, pl.ds(nz, 8)] = jnp.where(there8, x_rim[m, 8 + j], 0.0)
            for k in range(3):
                force[k, at, pl.ds(0, nz)] = jnp.where(there, 2.0 * x_main[m, 15 + 2 * k + j], 0.0)
        for k in range(3):
            at = right * (nx + 1) + 2
            force[k, at, pl.ds(nz, 8)] = jnp.where(there8, 2.0 * x_rim[m, 10 + k], 0.0)
        tiles = (nz + 8) // 8
        column = jnp.concatenate([x_rim[m, 13 + tiles + r] for r in range(tiles)], axis=0)
        x, kept = rim_halo(column, 0, 32, 3, right, valid, nx)
        halo_e[...] = jnp.where(kept, x, halo_e[...])
        for k in range(3):
            x, kept = rim_halo(column, 1 + k, 32, 3, right, valid, nx)
            halo_f[k] = jnp.where(kept, 2.0 * x, halo_f[k])


def first_fields(v, p_in, z_halo, halo_full, x_main, x_rim, u, other, halo):
    nx, nz, _ = p_in.shape
    slots = nx + 6
    zero = jnp.zeros((nz + 8, LANES), F32)
    for k in range(4):
        for p in list(range(3)) + list(range(nx + 3, slots)):
            u[k, p] = zero
            other[k, p] = zero
        for q in range(nx):
            u[k, q + 3, pl.ds(0, nz)] = v[k, q] if k < 3 else p_in[q]
            u[k, q + 3, pl.ds(nz, 8)] = z_halo[k, q]
        halo[k] = own_slots(halo_full[k], nx, 0)
    for m in range(x_main.shape[0]):
        right, valid = x_side(m)
        there = truth(valid, (nz, LANES))
        there8 = truth(valid, (8, LANES))
        tiles = (nz + 8) // 8
        column = jnp.concatenate([x_rim[m, 13 + r] for r in range(tiles)], axis=0)
        for k in range(4):
            for j in range(3):
                x = jnp.where(there, x_main[m, 3 * k + j], 0.0)
                u[k, right * (nx + 3) + j, pl.ds(0, nz)] = x
            for j in range(2):
                x = jnp.where(there8, x_rim[m, 2 * k + j], 0.0)
                u[k, right * (nx + 2) + 1 + j, pl.ds(nz, 8)] = x
            x, kept = rim_halo(column, k, 32, 3, right, valid, nx)
            halo[k] = jnp.where(kept, x, halo[k])


def pre_smooth(
    v, p_in, e_in, f_in, z_halo, halo_full, x_main, x_rim,
    fields, coarse, edges, x_fine,
    ua, ub, ha, hb, ca, cb, e, halo_e, edge_e, force, halo_f, w0, w1, w2, w3, w4, w5, hw, summed,
):
    nx, nz, _ = p_in.shape
    slots = nx + 6
    w = (w0, w1, w2, w3, w4, w5)
    viscosity_force(e_in, f_in, z_halo, halo_full, x_main, x_rim, e, halo_e, force, halo_f)
    first_fields(v, p_in, z_halo, halo_full, x_main, x_rim, ua, ub, ha)
    masks = fine_masks(nz + 8, slots)
    fill_edges(ca, ua, 4, 0, slots)
    edge_e[...] = jnp.zeros(edge_e.shape, F32)

    def body(p, carry):
        slot = iota(edge_e.shape, 1) // SLOT
        edge_e[...] = jnp.where(slot == p, roll(e[p], p * SLOT + 4, 1), edge_e[...])
        return carry

    lax.fori_loop(0, slots, body, 0)
    lo, hi = spans(slots, 2)
    main_weights(e, halo_e, w, lo, hi)
    halo_weights(halo_e, edge_e, hw)
    rest = (w, hw, e, halo_e, force, halo_f)
    fine_sweep(ua, ha, ca, ub, hb, cb, *rest, lo, hi, masks)
    lo, hi = spans(slots, 1)
    fine_sweep(ub, hb, cb, ua, ha, ca, *rest, lo, hi, masks)
    for k in range(4):
        for q in range(nx):
            fields[k, q] = ua[k, q + 3, pl.ds(0, nz)]
    for m in range(x_fine.shape[0]):
        high = high_side("gx", m)
        for k in range(4):
            for j in range(2):
                x_fine[m, 2 * k + j] = ua[k, 3 + high * (nx - 2) + j, pl.ds(0, nz)]
    lane = iota((nz, LANES), 1)
    for j in range(2):
        first = roll(ca[j][:nz], -3 * SLOT, 1)
        second = roll(ca[j + 2][:nz], LANES // 2 - 3 * SLOT, 1)
        edges[j] = jnp.where(lane < LANES // 2, first, second)

    def block(q, carry):
        totals = [0.0] * 5
        for j in range(2):
            p = 2 * q + 3 + j
            olds, sums, spread = main_operator(ua, ha, w, force, p)
            diagonal = w0[p] + w0[p - 1] + w1[p] + w2[p] + w3[p] + w4[p]
            for k in range(3):
                totals[k] += sums[k] - diagonal * olds[k]
            totals[3] += spread
            totals[4] += e[p]
        for k in range(5):
            summed[k, q] = totals[k][:nz]
        return carry

    lax.fori_loop(0, nx // 2, block, 0)
    scale = (0.5, 0.5, 0.5, -1.0 / 32.0, 0.125)
    cz = nz // 2
    left = []
    for k in range(5):
        for r in range(nx // 4):
            halves = []
            for s in range(2):
                q = 2 * r + s
                even = summed[k, q, pl.ds(0, cz, stride=2)]
                halves.append((even + summed[k, q, pl.ds(1, cz, stride=2)]) * scale[k])
            left.append(jnp.concatenate(halves, axis=1))
    left = jnp.concatenate(left, axis=0)
    pick = iota((2 * LANES, LANES), 0) // 2 == iota((2 * LANES, LANES), 1)
    out = jnp.dot(
        left, pick.astype(F32), precision=lax.Precision.HIGHEST, preferred_element_type=F32
    )
    for k in range(5):
        for r in range(nx // 4):
            at = (k * (nx // 4) + r) * cz
            coarse[k, r] = out[at : at + cz]


def fourth_pack(own, other, fields, whole, z_a, z_b):
    nx, nz = fields.shape[1:3]
    pairs = whole.shape[1]
    cz = whole.shape[2]
    gx = lax.axis_index("gx")
    for k in range(5):
        for r in range(pairs):
            if other is None:
                whole[k, r] = own[k, r]
            else:
                mine = truth(jnp.where(gx == r // (pairs // 2), 1, 0), (cz, LANES))
                n = r % (pairs // 2)
                whole[k, r] = jnp.where(mine, own[k, n], other[k, n])
    row = iota((8, LANES), 0) // 2
    for m, out in enumerate((z_a, z_b)):
        right = high_side("gz", m)
        start = pl.multiple_of(right * (cz - 8), 8)
        for k in range(5):
            for r in range(pairs):
                out[k * pairs + r] = whole[k, r, pl.ds(start, 8)]
        toward = truth(right, (8, LANES))
        for q in range(nx):
            total = jnp.zeros((8, LANES), F32)
            for k in range(4):
                low = roll(fields[k, q, pl.ds(0, 8)], 2 * k, 0)
                high = roll(fields[k, q, pl.ds(nz - 8, 8)], 2 * k - 6, 0)
                total = jnp.where(row == k, jnp.where(toward, high, low), total)
            out[5 * pairs + q] = total


def fifth_pack(whole, z_a, z_b, edges, full, z_halo, y_a, y_b):
    pairs, cz = whole.shape[1:3]
    nx = z_halo.shape[1]
    nz = edges.shape[1]
    _, has_left, has_right = place("gz")
    to_left = truth(has_left, (8, LANES))
    to_right = truth(has_right, (8, LANES))
    for k in range(5):
        for r in range(pairs):
            n = k * pairs + r
            left, right = left_right("gz", z_a[n], z_b[n])
            full[k, r, pl.ds(0, cz)] = whole[k, r]
            full[k, r, pl.ds(cz, 8)] = jnp.where(to_right, right, 0.0)
            full[k, r, pl.ds(cz + 8, 8)] = jnp.where(to_left, left, 0.0)
    row = iota((8, LANES), 0)
    for q in range(nx):
        left, right = left_right("gz", z_a[5 * pairs + q], z_b[5 * pairs + q])
        for k in range(4):
            x = jnp.where(row < 2 * has_right, roll(right, -2 * k, 0), 0.0)
            z_halo[k, q] = jnp.where(row >= 8 - 2 * has_left, roll(left, 6 - 2 * k, 0), x)
    rows = cz + 16
    tiles = rows // 8
    slot = iota((rows, LANES), 1) // SLOT
    per = LANES // SLOT
    count = 5 * pairs * 2
    columns = -(-count // per)
    behind = pair_edges(lambda i: [z_halo[i, q] for q in range(nx)], 4, 8)
    for m, out in enumerate((y_a, y_b)):
        high = high_side("gy", m) * (LANES // 2 - SLOT)
        for c in range(columns):
            total = jnp.zeros((rows, LANES), F32)
            for t in range(min(per, count - c * per)):
                n = c * per + t
                k, r, s = n // (2 * pairs), n // 2 % pairs, n % 2
                at = SLOT * t - s * (LANES // 2) - high
                total = jnp.where(slot == t, roll(full[k, r], at + LANES, 1), total)
            for i in range(tiles):
                out[c * tiles + i] = total[8 * i : 8 * i + 8]
        n = columns * tiles
        for j in range(2):
            for i in range(nz // 8):
                out[n] = edges[j, pl.ds(8 * i, 8)]
                n += 1
            out[n] = behind[j]
            n += 1


def sixth_pack(y_a, y_b, z_halo, halo_full, x_rim):
    tiles = halo_full.shape[1] // 8
    first = y_a.shape[0] - 2 * tiles
    for j in range(2):
        for i in range(tiles):
            n = first + j * tiles + i
            halo_full[j, pl.ds(8 * i, 8)] = merge_y(y_a[n], y_b[n])
    pack_rim(x_rim, z_halo, lambda j: halo_full[j], 4, (1,) * 4, 1, SLOT)


def coarse_solve(full, y_a, y_b, main, halo, ca, cb, force, e, w0, w1, w2, w3, w4, w5, grown):
    pairs, rows = full.shape[1:3]
    planes = 2 * pairs
    own = main.shape[1] - 2
    tiles = rows // 8
    per = LANES // SLOT
    lane = iota((rows, LANES), 1)
    row = iota((rows, LANES), 0)
    _, zl, zr = place("gz")
    _, yl, yr = place("gy")
    half = LANES // 2
    inside = (row < rows - 16 + 8 * zr) | (row >= rows - 8 * zl)
    inside &= (lane < half + SLOT * yr) | (lane >= LANES - SLOT * yl)
    zero = jnp.zeros((rows, LANES), F32)
    w = (w0, w1, w2, w3, w4, w5)
    for k in range(4):
        for p in (0, planes + 1):
            ca[k, p] = zero
            cb[k, p] = zero
    e[0] = zero
    e[planes + 1] = zero
    for n in range(10 * pairs):
        k, r, s = n // (2 * pairs), n // 2 % pairs, n % 2
        c, t = n // per, n % per
        a = jnp.concatenate([y_a[c * tiles + i] for i in range(tiles)], axis=0)
        b = jnp.concatenate([y_b[c * tiles + i] for i in range(tiles)], axis=0)
        left, right = left_right("gy", a, b)
        x = roll(full[k, r], -s * half, 1)
        x = jnp.where(lane < half, x, roll(right, half - SLOT * t, 1))
        x = jnp.where(lane < LANES - SLOT, x, roll(left, LANES - SLOT - SLOT * t, 1))
        x = jnp.where(inside, x, 0.0)
        if k < 4:
            force[k, 2 * r + s] = x
        else:
            e[2 * r + s + 1] = x

    def shifts(x):
        return (
            roll(x, LANES - 1, 1),
            roll(x, 1, 1),
            roll(x, rows - 1, 0),
            roll(x, 1, 0),
        )

    for p in range(planes + 1):
        w0[p] = e[p] + e[p + 1]

    def start(p, carry):
        x = e[p]
        total = w0[p] + w0[p - 1]
        for n, y in enumerate(shifts(x)):
            total += x + y
            w[1 + n][p] = x + y
        factor = jnp.where(inside, relax_weight / total, 0.0)
        w5[p] = factor
        for k in range(3):
            ca[k, p] = factor * force[k, p - 1]
        ca[3, p] = x * force[3, p - 1]
        return carry

    lax.fori_loop(1, planes + 1, start, 0)

    def sweep(src, dst):
        def body(p, carry):
            wxp, wxm = w0[p], w0[p - 1]
            wyp, wym, wzp, wzm = w1[p], w2[p], w3[p], w4[p]
            x = src[3, p]
            around = shifts(x)
            up, down = src[3, p + 1], src[3, p - 1]
            spread = 0.0
            for k in range(3):
                u = src[k, p]
                yp, ym, zp, zm = shifts(u)
                xp, xm = src[k, p + 1], src[k, p - 1]
                total = force[k, p - 1] - 2.0 * terms(k, up, down, *around)
                total += wxp * xp + wxm * xm
                total += wyp * yp + wym * ym
                total += wzp * zp + wzm * zm
                spread += terms(k, xp, xm, yp, ym, zp, zm)
                dst[k, p] = jnp.where(inside, 0.4 * u + w5[p] * total, 0.0)
            dst[3, p] = jnp.where(inside, x + e[p] * (force[3, p - 1] - 0.125 * spread), 0.0)
            return carry

        lax.fori_loop(1, planes + 1, body, 0)

    sweep(ca, cb)
    sweep(cb, ca)
    sweep(ca, cb)

    cz = rows - 16
    spread_lanes = (iota((LANES, LANES), 1) // 2 == iota((LANES, LANES), 0)).astype(F32)
    lane = iota((LANES, LANES), 1)
    cell = iota((LANES, LANES), 0)
    spot = lane % SLOT
    wanted = jnp.where(spot < 4, LANES - 2, half - 2) + spot // 2
    column = jnp.zeros((4 * rows, LANES), F32)
    first = lax.axis_index("gx") * own

    def grow(ref, index, x):
        ref[index + (pl.ds(0, cz, stride=2),)] = x[:cz]
        ref[index + (pl.ds(1, cz, stride=2),)] = x[:cz]
        edge = jnp.concatenate([x[cz : cz + 8], x[rows - 8 :]], axis=0)
        grown[pl.ds(0, 16, stride=2)] = edge
        grown[pl.ds(1, 16, stride=2)] = edge
        r = iota((8, LANES), 0)
        tail = jnp.where(r < 4, grown[pl.ds(0, 8)], grown[pl.ds(24, 8)])
        ref[index + (pl.ds(2 * cz, 8),)] = tail

    for i in range(own + 2):
        x = jnp.concatenate([cb[k, first + i] for k in range(4)], axis=0)
        wide = jnp.dot(
            x, spread_lanes, precision=lax.Precision.HIGHEST, preferred_element_type=F32
        )
        for k in range(4):
            grow(main, (k, i), wide[k * rows : (k + 1) * rows])
        here = (lane // SLOT + 1) // 2 - 1 == i
        chosen = (here & (cell == wanted)).astype(F32)
        column += jnp.dot(
            x, chosen, precision=lax.Precision.HIGHEST, preferred_element_type=F32
        )
    for k in range(4):
        grow(halo, (k,), column[k * rows : (k + 1) * rows])


def post_smooth(
    e_in, f_in, z_first, halo_first, x_main, x_first, fields, z_halo, halo_full, x_fine, x_rim,
    main, column, v_out, p_out,
    ua, ub, ha, hb, ca, cb, e, halo_e, edge_e, force, halo_f, w0, w1, w2, w3, w4, w5, hw,
):
    nx, nz, _ = e_in.shape
    slots = nx + 6
    w = (w0, w1, w2, w3, w4, w5)
    viscosity_force(e_in, f_in, z_first, halo_first, x_main, x_first, e, halo_e, force, halo_f)
    zero = jnp.zeros((nz + 8, LANES), F32)
    for k in range(4):
        for p in (1, 2, nx + 3, nx + 4):
            ua[k, p] = zero
            ub[k, p] = zero
        for q in range(nx):
            i = q // 2 + 1
            ua[k, q + 3, pl.ds(0, nz)] = fields[k, q] + main[k, i, pl.ds(0, nz)]
            ua[k, q + 3, pl.ds(nz, 8)] = z_halo[k, q] + main[k, i, pl.ds(nz, 8)]
        ha[k] = own_slots(halo_full[k % 2], nx, k // 2)
    for m in range(x_fine.shape[0]):
        right, valid = x_side(m)
        there = truth(valid, (nz, LANES))
        there8 = truth(valid, (8, LANES))
        tiles = (nz + 8) // 8
        side = jnp.concatenate([x_rim[m, 4 + r] for r in range(tiles)], axis=0)
        i = right * (nx // 2 + 1)
        for k in range(4):
            for j in range(2):
                at = 1 + right * (nx + 2) + j
                x = x_fine[m, 2 * k + j] + main[k, i, pl.ds(0, nz)]
                ua[k, at, pl.ds(0, nz)] = jnp.where(there, x, 0.0)
            x = x_rim[m, k] + main[k, i, pl.ds(nz, 8)]
            ua[k, 2 + right * (nx + 1), pl.ds(nz, 8)] = jnp.where(there8, x, 0.0)
            x, kept = rim_halo(side, k, SLOT, 1, right, valid, nx)
            ha[k] = jnp.where(kept, x, ha[k])
    masks = fine_masks(nz + 8, slots)
    for k in range(4):
        ha[k] = jnp.where(masks[1], ha[k] + column[k], 0.0)
    fill_edges(ca, ua, 4, 1, slots - 1)
    edge_e[...] = jnp.zeros(edge_e.shape, F32)

    def body(p, carry):
        slot = iota(edge_e.shape, 1) // SLOT
        edge_e[...] = jnp.where(slot == p, roll(e[p], p * SLOT + 4, 1), edge_e[...])
        return carry

    lax.fori_loop(1, slots - 1, body, 0)
    lo, hi = spans(slots, 1)
    main_weights(e, halo_e, w, lo, hi)
    halo_weights(halo_e, edge_e, hw)
    rest = (w, hw, e, halo_e, force, halo_f)
    fine_sweep(ua, ha, ca, ub, hb, cb, *rest, lo, hi, masks)

    def last(p, carry):
        new = relaxed(*main_operator(ub, hb, w, force, p), w5[p], e[p])
        for k in range(3):
            v_out[k, p - 3] = new[k][:nz]
        p_out[p - 3] = new[3][:nz]
        return carry

    lax.fori_loop(3, nx + 3, last, 0)


def local(velocity, pressure, viscosity, body_force):
    nx, nz, ny = pressure.shape
    if ny != LANES or nx * SLOT * 2 != LANES or nz % 16:
        raise ValueError("unsupported block")
    sides = x_messages()
    rows, slots = nz + 8, nx + 6
    inputs = [velocity, pressure, viscosity, body_force]
    block = (nz, LANES)

    x_main, y_main = call(first_pack, [(sides, 21) + block, (4,) + block], inputs)
    x_main = swap_x(x_main)
    y_a, y_b = swap(y_main, "gy", 0), swap(y_main, "gy", 1)
    z_shape = (4 * nx + 2, 8, LANES)
    halo, z_a, z_b = call(
        second_pack, [(4,) + block, z_shape, z_shape], inputs + [y_a, y_b]
    )
    z_a, z_b = swap(z_a, "gz", 0), swap(z_b, "gz", 1)
    tiles = rows // 8
    z_first, halo_first, x_first = call(
        third_pack,
        [(8, nx, 8, LANES), (4, rows, LANES), (sides, 13 + 2 * tiles, 8, LANES)],
        [z_a, z_b, halo],
    )
    x_first = swap_x(x_first)

    state = [(4, slots, rows, LANES)] * 2 + [(4, rows, LANES)] * 4
    state += [(slots, rows, LANES), (rows, LANES), (rows, LANES)]
    state += [(3, slots, rows, LANES), (3, rows, LANES)]
    state += [(slots, rows, LANES)] * 6 + [(7, rows, LANES)]
    fields, own, edges, x_fine = call(
        pre_smooth,
        [(4, nx) + block, (5, nx // 4, nz // 2, LANES), (2,) + block, (sides, 8) + block],
        inputs + [z_first, halo_first, x_main, x_first],
        state + [(5, nx // 2, nz, LANES)],
        cost=8,
    )
    if lax.axis_size("gx") == 2:
        parts = [own, swap(own, "gx", 0)]
        gather = fourth_pack
    else:
        parts = [lax.all_gather(own, "gx", axis=1, tiled=True)]

        def gather(a, *refs):
            fourth_pack(a, None, *refs)

    x_fine = swap_x(x_fine)
    pairs = lax.axis_size("gx") * (nx // 4)
    z_shape = (5 * pairs + nx, 8, LANES)
    whole, z_a, z_b = call(
        gather, [(5, pairs, nz // 2, LANES), z_shape, z_shape], parts + [fields]
    )
    z_a, z_b = swap(z_a, "gz", 0), swap(z_b, "gz", 1)
    deep = nz // 2 + 16
    y_shape = (-(-10 * pairs * SLOT // LANES) * (deep // 8) + 2 * tiles, 8, LANES)
    full, z_halo, y_a, y_b = call(
        fifth_pack,
        [(5, pairs, deep, LANES), (4, nx, 8, LANES), y_shape, y_shape],
        [whole, z_a, z_b, edges],
    )
    y_a, y_b = swap(y_a, "gy", 0), swap(y_b, "gy", 1)
    halo_full, x_rim = call(
        sixth_pack,
        [(2, rows, LANES), (sides, 4 + tiles, 8, LANES)],
        [y_a, y_b, z_halo],
    )
    x_rim = swap_x(x_rim)
    planes = 2 * pairs
    deep_plane = (deep, LANES)
    main, column = call(
        coarse_solve,
        [(4, nx // 2 + 2, rows, LANES), (4, rows, LANES)],
        [full, y_a, y_b],
        [(4, planes + 2) + deep_plane] * 2
        + [(4, planes) + deep_plane]
        + [(planes + 2,) + deep_plane] * 7
        + [(32, LANES)],
        cost=4,
    )
    v_out, p_out = call(
        post_smooth,
        [(3, nx) + block, (nx,) + block],
        [viscosity, body_force, z_first, halo_first, x_main, x_first]
        + [fields, z_halo, halo_full, x_fine, x_rim, main, column],
        state,
        cost=8,
    )
    return v_out, p_out


def swap_x(array):
    if array.shape[0] == 1:
        return swap(array, "gx", 0)
    parts = [swap(array[m], "gx", m) for m in range(2)]
    return jnp.stack(parts)


def solution(mesh):
    return jax.shard_map(
        local,
        mesh=mesh,
        in_specs=(
            P(None, "gx", "gz", "gy"),
            P("gx", "gz", "gy"),
            P("gx", "gz", "gy"),
            P(None, "gx", "gz", "gy"),
        ),
        out_specs=(P(None, "gx", "gz", "gy"), P("gx", "gz", "gy")),
        check_vma=False,
    )
```

time: 315 us -> 65.3 us (0.21); the launches traced: 310 us -> 65.1 us
  starting transfers between devices: 118 us -> 14.3 us
  local copies, waits for them, and re-layouts: 64.7 us -> 3.81 us
  waiting for transfers between devices: 80.8 us -> 20.4 us
  other arithmetic: 37.7 us -> 0 us
  Pallas kernels: 0 us -> 25.9 us
  blocking collectives: 6.29 us -> 0 us
    ppermute x52 -> x13, starting transfers between devices: 118 us -> 14.3 us  [the longest x11 13.9 us: swap(): return lax.ppermute(array, axis, pairs)]
    ppermute x52 -> x13, waiting for transfers between devices: 80.8 us -> 20.4 us  [the longest x11 20.4 us: swap(): return lax.ppermute(array, axis, pairs)]
    concatenate x4 -> x0, local copies, waits for them, and re-layouts: 46 us -> none  [the longest x3 46 us: local(): jnp.concatenate([momentum, continuity[None], viscosity[None]], axis=0)]
    pallas_call x0 -> x9, Pallas kernels: none -> 25.9 us  [call(): pl.pallas_call(body, out_shape=[jax.ShapeDtypeStruct(shape, F32) for shap...]
    reduce_sum x1 -> x0, other arithmetic: 14.7 us -> none  [restrict(): return blocks.mean(axis=(2, 4, 6))]
    add x10 -> x0, other arithmetic: 8.76 us -> none  [the longest x7 5.56 us: relax_sweep(): new_velocity = velocity + relax_weight * momentum / diagonal]
    concatenate x27 -> x0, other arithmetic: 8.22 us -> none  [the longest x19 6.91 us: padded_2(): array = jnp.concatenate([before, array, after], axis=dim)]
    all_gather x1 -> x0, blocking collectives: 6.29 us -> none  [local(): coarse = lax.all_gather(packed, 'gx', axis=1, tiled=True)]
  transfers between devices with their start and end apart: 52 -> 13, of which waited for: 33 -> 6; matrix products, arithmetic and copies ran while one was open for 5% -> 0% of each run, Pallas kernels for 0% -> 8%
where the time goes in v1:
time: 65.3 us; the launch traced here: 65.1 us
  Pallas kernels  25.9 us (40%)
  waiting for transfers between devices  20.4 us (31%)
  starting transfers between devices  14.3 us (22%)
  local copies, waits for them, and re-layouts  3.81 us (6%)
  between operations  0.74 us (1%)
    pallas_call x9, Pallas kernels, call(): pl.pallas_call(body, out_shape=[jax.ShapeDtypeStruct(shape, F32) for shap...  25.9 us
    ppermute x11, waiting for transfers between devices, swap(): return lax.ppermute(array, axis, pairs)  20.4 us
    ppermute x11, starting transfers between devices, swap(): return lax.ppermute(array, axis, pairs)  13.9 us
    unnamed x16, local copies, waits for them, and re-layouts  3.81 us
  transfers between devices with their start and end apart: 13, of which 6 were waited for; matrix products, arithmetic and copies ran while one was open for 0% of the time, Pallas kernels for 8%

profile of v1, /device:TPU:0, one launch (start us, length us, event | category | flops | bytes accessed | tf_op | source)
XLA Modules:
  0.0 65.1 jit_solution(16771848949648036128)
XLA Ops:
  0.6 1.0 %copy-done = f32[3,8,32,128]{3,2,1,0:T(8,128)S(1)} copy-done((f32[3,8,32,128]{3,2,1,0:T(8,128)S(1)}, f32[3,8,32,128]{3,2,1,0:T(8,128)}, u32[]{:S(2)}) %copy-start) | copy-done | bytes 393240
  1.6 1.0 %copy-done.2 = f32[3,8,32,128]{3,2,1,0:T(8,128)S(1)} copy-done((f32[3,8,32,128]{3,2,1,0:T(8,128)S(1)}, f32[3,8,32,128]{3,2,1,0:T(8,128)}, u32[]{:S(2)}) %copy-start.2) | copy-done | bytes 393240
  2.6 0.9 %copy-done.4 = f32[8,32,128]{2,1,0:T(8,128)S(1)} copy-done((f32[8,32,128]{2,1,0:T(8,128)S(1)}, f32[8,32,128]{2,1,0:T(8,128)}, u32[]{:S(2)}) %copy-start.4) | copy-done | bytes 131096
  3.5 0.9 %copy-done.6 = f32[8,32,128]{2,1,0:T(8,128)S(1)} copy-done((f32[8,32,128]{2,1,0:T(8,128)S(1)}, f32[8,32,128]{2,1,0:T(8,128)}, u32[]{:S(2)}) %copy-start.6) | copy-done | bytes 131096
  4.8 3.0 %collective-permute-start.4 = (f32[1,21,32,128]{3,2,1,0:T(8,128)S(1)}, f32[1,21,32,128]{3,2,1,0:T(8,128)S(1)}, u32[]{:S(2)}, u32[]{:S(2)}) collective-permute-start(f32[1,21,32,128]{3,2,1,0:T(8,128)S(1)} %get-tuple-element.31), channel_id=1, source_target_pairs={{0,16},{16,0},{1,17},{17,1},{2,18},{18,2},{3,19},{19,3},{4,20},{20... | collective-permute-start | bytes 1032200 | tf_op jit(solution)/shard_map/ppermute | solution.py:43
  7.8 3.1 %collective-permute-start = (f32[4,32,128]{2,1,0:T(8,128)S(1)}, f32[4,32,128]{2,1,0:T(8,128)S(1)}, u32[]{:S(2)}, u32[]{:S(2)}) collective-permute-start(f32[4,32,128]{2,1,0:T(8,128)S(1)} %get-tuple-element.25), channel_id=1, source_target_pairs={{0,4},{4,0},{8,12},{12,8},{1,5},{5,1},{9,13},{13,9},{2,6},{6,2},{1... | collective-permute-start | bytes 196616 | tf_op jit(solution)/shard_map/ppermute | solution.py:43
  11.0 2.2 %collective-permute-done.y_a = f32[4,32,128]{2,1,0:T(8,128)S(1)} collective-permute-done((f32[4,32,128]{2,1,0:T(8,128)S(1)}, f32[4,32,128]{2,1,0:T(8,128)S(1)}, u32[]{:S(2)}, u32[]{:S(2)}) %collective-permute-start) | collective-permute-done | bytes 65568 | tf_op jit(solution)/shard_map/ppermute | solution.py:43
  13.4 1.6 %collective-permute-start.3 = (f32[34,8,128]{2,1,0:T(8,128)S(1)}, f32[34,8,128]{2,1,0:T(8,128)S(1)}, u32[]{:S(2)}, u32[]{:S(2)}) collective-permute-start(f32[34,8,128]{2,1,0:T(8,128)S(1)} %get-tuple-element.27), channel_id=1, source_target_pairs={{1,2},{2,1},{3,0},{0,3},{5,6},{6,5},{7,4},{4,7},{9,10},{10,9},{11,... | collective-permute-start | bytes 417800 | tf_op jit(solution)/shard_map/ppermute | solution.py:43
  15.0 3.9 %collective-permute-done.3.z_b = f32[34,8,128]{2,1,0:T(8,128)S(1)} collective-permute-done((f32[34,8,128]{2,1,0:T(8,128)S(1)}, f32[34,8,128]{2,1,0:T(8,128)S(1)}, u32[]{:S(2)}, u32[]{:S(2)}) %collective-permute-start.3) | collective-permute-done | bytes 139296 | tf_op jit(solution)/shard_map/ppermute | solution.py:43
  19.0 0.6 collective-permute-start.5
  19.6 4.5 %collective-permute-done.5.x_rim.x_first = f32[1,23,8,128]{3,2,1,0:T(8,128)S(1)} collective-permute-done((f32[1,23,8,128]{3,2,1,0:T(8,128)S(1)}, f32[1,23,8,128]{3,2,1,0:T(8,128)S(1)}, u32[]{:S(2)}, u32[]{:S(2)}) %collective-permute-start.5) | collective-permute-done | bytes 94240 | tf_op jit(solution)/shard_map/ppermute | solution.py:43
  24.1 11.2 %shard_map.62 = (f32[4,8,32,128]{3,2,1,0:T(8,128)S(1)}, f32[5,2,16,128]{3,2,1,0:T(8,128)S(1)}, f32[2,32,128]{2,1,0:T(8,128)S(1)}, f32[1,8,32,128]{3,2,1,0:T(8,128)S(1)}) custom-call(f32[3,8,32,128]{3,2,1,0:T(8,128)S(1)} %copy-done.3, f32[8,32,128]{2,1,0:T(8,128)S(1)} %copy-done.7, f32[8,32,128]{2,1,0:T(8,128)S(1)} %copy-done.5, ...), custom_call_target="tpu_custom_call" | custom-call | flops 8000000 | bytes 8000000 | tf_op jit(solution)/shard_map/pallas_call | solution.py:15
  35.3 0.6 collective-permute-start.6
  35.9 3.9 %collective-permute-done.6.other = f32[5,2,16,128]{3,2,1,0:T(8,128)S(1)} collective-permute-done((f32[5,2,16,128]{3,2,1,0:T(8,128)S(1)}, f32[5,2,16,128]{3,2,1,0:T(8,128)S(1)}, u32[]{:S(2)}, u32[]{:S(2)}) %collective-permute-start.6) | collective-permute-done | bytes 81952 | tf_op jit(solution)/shard_map/ppermute | solution.py:43
  40.0 1.6 %collective-permute-start.8 = (f32[28,8,128]{2,1,0:T(8,128)S(1)}, f32[28,8,128]{2,1,0:T(8,128)S(1)}, u32[]{:S(2)}, u32[]{:S(2)}) collective-permute-start(f32[28,8,128]{2,1,0:T(8,128)S(1)} %get-tuple-element.37), channel_id=1, source_target_pairs={{1,2},{2,1},{3,0},{0,3},{5,6},{6,5},{7,4},{4,7},{9,10},{10,9},{11,... | collective-permute-start | bytes 344072 | tf_op jit(solution)/shard_map/ppermute | solution.py:43
  41.6 0.5 collective-permute-start.11
  42.1 2.8 %collective-permute-done.8.z_b = f32[28,8,128]{2,1,0:T(8,128)S(1)} collective-permute-done((f32[28,8,128]{2,1,0:T(8,128)S(1)}, f32[28,8,128]{2,1,0:T(8,128)S(1)}, u32[]{:S(2)}, u32[]{:S(2)}) %collective-permute-start.8) | collective-permute-done | bytes 114720 | tf_op jit(solution)/shard_map/ppermute | solution.py:43
  44.9 0.4 shard_map.64
  45.4 2.1 %collective-permute-start.9 = (f32[22,8,128]{2,1,0:T(8,128)S(1)}, f32[22,8,128]{2,1,0:T(8,128)S(1)}, u32[]{:S(2)}, u32[]{:S(2)}) collective-permute-start(f32[22,8,128]{2,1,0:T(8,128)S(1)} %get-tuple-element.40), channel_id=1, source_target_pairs={{0,4},{4,0},{8,12},{12,8},{1,5},{5,1},{9,13},{13,9},{2,6},{6,2},{1... | collective-permute-start | bytes 270344 | tf_op jit(solution)/shard_map/ppermute | solution.py:43
  47.5 0.4 collective-permute-start.10
  47.9 3.1 %collective-permute-done.9.y_a = f32[22,8,128]{2,1,0:T(8,128)S(1)} collective-permute-done((f32[22,8,128]{2,1,0:T(8,128)S(1)}, f32[22,8,128]{2,1,0:T(8,128)S(1)}, u32[]{:S(2)}, u32[]{:S(2)}) %collective-permute-start.9) | collective-permute-done | bytes 90144 | tf_op jit(solution)/shard_map/ppermute | solution.py:43
  51.0 0.6 collective-permute-start.12
  51.6 4.6 %shard_map.66 = (f32[4,6,40,128]{3,2,1,0:T(8,128)S(1)}, f32[4,40,128]{2,1,0:T(8,128)S(1)}) custom-call(f32[5,4,32,128]{3,2,1,0:T(8,128)S(1)} %get-tuple-element.45.full, f32[22,8,128]{2,1,0:T(8,128)S(1)} %collective-permute-done.9.y_a, f32[22,8,128]{2,1,0:T(8,128)S(1)} %collective-permute-done.10.y_b), custom_call_target="tpu_custom_call" | custom-call | flops 4000000 | bytes 4000000 | tf_op jit(solution)/shard_map/pallas_call | solution.py:15
  56.3 8.8 %shard_map.67 = (f32[3,8,32,128]{3,2,1,0:T(8,128)}, f32[8,32,128]{2,1,0:T(8,128)}) custom-call(f32[8,32,128]{2,1,0:T(8,128)S(1)} %copy-done.5, f32[3,8,32,128]{3,2,1,0:T(8,128)S(1)} %copy-done.1, f32[8,8,8,128]{3,2,1,0:T(8,128)S(1)} %get-tuple-element.29.z_halo.z_first, f32[4,40,128]{2,1,0:T(8,128)S(1)} %get-tuple-element.30.halo_full.halo_first, ...), custom_call_target="tpu_custom_call" | custom-call | flops 8000000 | bytes 8000000 | tf_op jit(solution)/shard_map/pallas_call | solution.py:15
  (27 shorter events, 0.9 us)
Async XLA Ops:
  0.6 1.0 %copy-start = (f32[3,8,32,128]{3,2,1,0:T(8,128)S(1)}, f32[3,8,32,128]{3,2,1,0:T(8,128)}, u32[]{:S(2)}) copy-start(f32[3,8,32,128]{3,2,1,0:T(8,128)} %f_in.3) | copy-start | bytes 1179652
  1.6 1.0 %copy-start.2 = (f32[3,8,32,128]{3,2,1,0:T(8,128)S(1)}, f32[3,8,32,128]{3,2,1,0:T(8,128)}, u32[]{:S(2)}) copy-start(f32[3,8,32,128]{3,2,1,0:T(8,128)} %v.5) | copy-start | bytes 1179652
  2.6 0.9 %copy-start.4 = (f32[8,32,128]{2,1,0:T(8,128)S(1)}, f32[8,32,128]{2,1,0:T(8,128)}, u32[]{:S(2)}) copy-start(f32[8,32,128]{2,1,0:T(8,128)} %e_in.3) | copy-start | bytes 393220
  3.5 0.9 %copy-start.6 = (f32[8,32,128]{2,1,0:T(8,128)S(1)}, f32[8,32,128]{2,1,0:T(8,128)}, u32[]{:S(2)}) copy-start(f32[8,32,128]{2,1,0:T(8,128)} %p_in.1) | copy-start | bytes 393220
  4.8 19.3 %collective-permute-start.4 = (f32[1,21,32,128]{3,2,1,0:T(8,128)S(1)}, f32[1,21,32,128]{3,2,1,0:T(8,128)S(1)}, u32[]{:S(2)}, u32[]{:S(2)}) collective-permute-start(f32[1,21,32,128]{3,2,1,0:T(8,128)S(1)} %get-tuple-element.31), channel_id=1, source_target_pairs={{0,16},{16,0},{1,17},{17,1},{2,18},{18,2},{3,19},{19,3},{4,20},{20... | collective-permute-start | bytes 1032200 | tf_op jit(solution)/shard_map/ppermute | solution.py:43
  7.8 3.2 %collective-permute-start.1 = (f32[4,32,128]{2,1,0:T(8,128)S(1)}, f32[4,32,128]{2,1,0:T(8,128)S(1)}, u32[]{:S(2)}, u32[]{:S(2)}) collective-permute-start(f32[4,32,128]{2,1,0:T(8,128)S(1)} %get-tuple-element.25), channel_id=1, source_target_pairs={{0,1},{1,0},{2,3},{3,2},{4,8},{5,9},{6,10},{7,11},{8,4},{9,5},{10,... | collective-permute-start | bytes 196616 | tf_op jit(solution)/shard_map/ppermute | solution.py:38
  7.8 5.4 %collective-permute-start = (f32[4,32,128]{2,1,0:T(8,128)S(1)}, f32[4,32,128]{2,1,0:T(8,128)S(1)}, u32[]{:S(2)}, u32[]{:S(2)}) collective-permute-start(f32[4,32,128]{2,1,0:T(8,128)S(1)} %get-tuple-element.25), channel_id=1, source_target_pairs={{0,4},{4,0},{8,12},{12,8},{1,5},{5,1},{9,13},{13,9},{2,6},{6,2},{1... | collective-permute-start | bytes 196616 | tf_op jit(solution)/shard_map/ppermute | solution.py:43
  13.2 10.9 %copy-start.1 = (f32[3,8,32,128]{3,2,1,0:T(8,128)S(1)}, f32[3,8,32,128]{3,2,1,0:T(8,128)}, u32[]{:S(2)}) copy-start(f32[3,8,32,128]{3,2,1,0:T(8,128)} %f_in.3) | copy-start | bytes 1179652
  13.2 10.9 %copy-start.3 = (f32[3,8,32,128]{3,2,1,0:T(8,128)S(1)}, f32[3,8,32,128]{3,2,1,0:T(8,128)}, u32[]{:S(2)}) copy-start(f32[3,8,32,128]{3,2,1,0:T(8,128)} %v.5) | copy-start | bytes 1179652
  13.3 1.7 %collective-permute-start.2 = (f32[34,8,128]{2,1,0:T(8,128)S(1)}, f32[34,8,128]{2,1,0:T(8,128)S(1)}, u32[]{:S(2)}, u32[]{:S(2)}) collective-permute-start(f32[34,8,128]{2,1,0:T(8,128)S(1)} %get-tuple-element.26), channel_id=1, source_target_pairs={{0,1},{1,0},{2,3},{3,2},{4,5},{5,4},{6,7},{7,6},{8,9},{9,8},{10,11... | collective-permute-start | bytes 417800 | tf_op jit(solution)/shard_map/ppermute | solution.py:43
  13.4 5.5 %collective-permute-start.3 = (f32[34,8,128]{2,1,0:T(8,128)S(1)}, f32[34,8,128]{2,1,0:T(8,128)S(1)}, u32[]{:S(2)}, u32[]{:S(2)}) collective-permute-start(f32[34,8,128]{2,1,0:T(8,128)S(1)} %get-tuple-element.27), channel_id=1, source_target_pairs={{1,2},{2,1},{3,0},{0,3},{5,6},{6,5},{7,4},{4,7},{9,10},{10,9},{11,... | collective-permute-start | bytes 417800 | tf_op jit(solution)/shard_map/ppermute | solution.py:43
  18.8 5.2 %copy-start.5 = (f32[8,32,128]{2,1,0:T(8,128)S(1)}, f32[8,32,128]{2,1,0:T(8,128)}, u32[]{:S(2)}) copy-start(f32[8,32,128]{2,1,0:T(8,128)} %e_in.3) | copy-start | bytes 393220
  18.8 5.2 %copy-start.7 = (f32[8,32,128]{2,1,0:T(8,128)S(1)}, f32[8,32,128]{2,1,0:T(8,128)}, u32[]{:S(2)}) copy-start(f32[8,32,128]{2,1,0:T(8,128)} %p_in.1) | copy-start | bytes 393220
  19.0 5.1 %collective-permute-start.5 = (f32[1,23,8,128]{3,2,1,0:T(8,128)S(1)}, f32[1,23,8,128]{3,2,1,0:T(8,128)S(1)}, u32[]{:S(2)}, u32[]{:S(2)}) collective-permute-start(f32[1,23,8,128]{3,2,1,0:T(8,128)S(1)} %get-tuple-element.32), channel_id=1, source_target_pairs={{0,16},{16,0},{1,17},{17,1},{2,18},{18,2},{3,19},{19,3},{4,20},{20... | collective-permute-start | bytes 282632 | tf_op jit(solution)/shard_map/ppermute | solution.py:43
  35.3 4.5 %collective-permute-start.6 = (f32[5,2,16,128]{3,2,1,0:T(8,128)S(1)}, f32[5,2,16,128]{3,2,1,0:T(8,128)S(1)}, u32[]{:S(2)}, u32[]{:S(2)}) collective-permute-start(f32[5,2,16,128]{3,2,1,0:T(8,128)S(1)} %get-tuple-element.34.own), channel_id=1, source_target_pairs={{0,16},{16,0},{1,17},{17,1},{2,18},{18,2},{3,19},{19,3},{4,20},{20... | collective-permute-start | bytes 245768 | tf_op jit(solution)/shard_map/ppermute | solution.py:43
  39.9 2.2 %collective-permute-start.7 = (f32[28,8,128]{2,1,0:T(8,128)S(1)}, f32[28,8,128]{2,1,0:T(8,128)S(1)}, u32[]{:S(2)}, u32[]{:S(2)}) collective-permute-start(f32[28,8,128]{2,1,0:T(8,128)S(1)} %get-tuple-element.36), channel_id=1, source_target_pairs={{0,1},{1,0},{2,3},{3,2},{4,5},{5,4},{6,7},{7,6},{8,9},{9,8},{10,11... | collective-permute-start | bytes 344072 | tf_op jit(solution)/shard_map/ppermute | solution.py:43
  40.0 4.9 %collective-permute-start.8 = (f32[28,8,128]{2,1,0:T(8,128)S(1)}, f32[28,8,128]{2,1,0:T(8,128)S(1)}, u32[]{:S(2)}, u32[]{:S(2)}) collective-permute-start(f32[28,8,128]{2,1,0:T(8,128)S(1)} %get-tuple-element.37), channel_id=1, source_target_pairs={{1,2},{2,1},{3,0},{0,3},{5,6},{6,5},{7,4},{4,7},{9,10},{10,9},{11,... | collective-permute-start | bytes 344072 | tf_op jit(solution)/shard_map/ppermute | solution.py:43
  41.6 14.7 %collective-permute-start.11 = (f32[1,8,32,128]{3,2,1,0:T(8,128)S(1)}, f32[1,8,32,128]{3,2,1,0:T(8,128)S(1)}, u32[]{:S(2)}, u32[]{:S(2)}) collective-permute-start(f32[1,8,32,128]{3,2,1,0:T(8,128)S(1)} %get-tuple-element.43), channel_id=1, source_target_pairs={{0,16},{16,0},{1,17},{17,1},{2,18},{18,2},{3,19},{19,3},{4,20},{20... | collective-permute-start | bytes 393224 | tf_op jit(solution)/shard_map/ppermute | solution.py:43
  45.4 5.6 %collective-permute-start.9 = (f32[22,8,128]{2,1,0:T(8,128)S(1)}, f32[22,8,128]{2,1,0:T(8,128)S(1)}, u32[]{:S(2)}, u32[]{:S(2)}) collective-permute-start(f32[22,8,128]{2,1,0:T(8,128)S(1)} %get-tuple-element.40), channel_id=1, source_target_pairs={{0,4},{4,0},{8,12},{12,8},{1,5},{5,1},{9,13},{13,9},{2,6},{6,2},{1... | collective-permute-start | bytes 270344 | tf_op jit(solution)/shard_map/ppermute | solution.py:43
  47.5 3.5 %collective-permute-start.10 = (f32[22,8,128]{2,1,0:T(8,128)S(1)}, f32[22,8,128]{2,1,0:T(8,128)S(1)}, u32[]{:S(2)}, u32[]{:S(2)}) collective-permute-start(f32[22,8,128]{2,1,0:T(8,128)S(1)} %get-tuple-element.41), channel_id=1, source_target_pairs={{0,1},{1,0},{2,3},{3,2},{4,8},{5,9},{6,10},{7,11},{8,4},{9,5},{10,... | collective-permute-start | bytes 270344 | tf_op jit(solution)/shard_map/ppermute | solution.py:38
  51.0 5.2 %collective-permute-start.12 = (f32[1,9,8,128]{3,2,1,0:T(8,128)S(1)}, f32[1,9,8,128]{3,2,1,0:T(8,128)S(1)}, u32[]{:S(2)}, u32[]{:S(2)}) collective-permute-start(f32[1,9,8,128]{3,2,1,0:T(8,128)S(1)} %get-tuple-element.44), channel_id=1, source_target_pairs={{0,16},{16,0},{1,17},{17,1},{2,18},{18,2},{3,19},{19,3},{4,20},{20... | collective-permute-start | bytes 110600 | tf_op jit(solution)/shard_map/ppermute | solution.py:43

commit v2 on v1

--- a/solution.py
+++ b/solution.py
@@ -9,16 +9,20 @@
 SLOT = 8
 F32 = jnp.float32
 relax_weight = 0.6
-
-
-def call(body, outs, args, scratch=(), cost=1):
+HELD = 429 * 2**17
+
+
+def call(body, outs, args, scratch=(), cost=1, outside=0, copies=0):
     return pl.pallas_call(
         body,
         out_shape=[jax.ShapeDtypeStruct(shape, F32) for shape in outs],
-        in_specs=[pl.BlockSpec(memory_space=pltpu.VMEM)] * len(args),
-        out_specs=[pl.BlockSpec(memory_space=pltpu.VMEM)] * len(outs),
-        scratch_shapes=[pltpu.VMEM(shape, F32) for shape in scratch],
-        compiler_params=pltpu.CompilerParams(vmem_limit_bytes=40 * 2**20),
+        in_specs=[pl.BlockSpec(memory_space=pltpu.HBM)] * outside
+        + [pl.BlockSpec(memory_space=pltpu.VMEM)] * (len(args) - outside),
+        out_specs=[pl.BlockSpec(memory_space=pltpu.HBM)] * (outside > 0)
+        + [pl.BlockSpec(memory_space=pltpu.VMEM)] * (len(outs) - (outside > 0)),
+        scratch_shapes=[pltpu.VMEM(shape, F32) for shape in scratch]
+        + [pltpu.SemaphoreType.DMA((copies,))] * (copies > 0),
+        compiler_params=pltpu.CompilerParams(vmem_limit_bytes=HELD if outside else 40 * 2**20),
         cost_estimate=pl.CostEstimate(
             flops=cost * 10**6, bytes_accessed=cost * 10**6, transcendentals=0
         ),
@@ -27,14 +31,18 @@
 
 def swap(array, axis, which):
     count = lax.axis_size(axis)
-    if axis == "gy" and which == 1:
-        other = lax.axis_size("gz")
+    if axis != "gx" and which == 1:
+        ys, zs = lax.axis_size("gy"), lax.axis_size("gz")
         pairs = []
-        for i in range(count):
-            j = i + 1 if i % 2 else i - 1
-            for k in range(other):
-                to = j * other + k if 0 <= j < count else i * other + (k ^ 1)
-                pairs.append((i * other + k, to))
+        for y in range(ys):
+            for z in range(zs):
+                i = y if axis == "gy" else z
+                j = i + 1 if i % 2 else i - 1
+                if axis == "gy":
+                    to = (j, z) if 0 <= j < count else (y, z ^ 1)
+                else:
+                    to = (y, j) if 0 <= j < count else (y ^ 1, z)
+                pairs.append((y * zs + z, to[0] * zs + to[1]))
         return lax.ppermute(array, ("gy", "gz"), pairs)
     pairs = []
     for i in range(which, count, 2):
@@ -96,29 +104,76 @@
     left, right = left_right("gy", a, b)
     spot = iota(a.shape, 1) % SLOT
     kept = (spot < 4 * has_left) | (spot >= SLOT - 4 * has_right)
-    return jnp.where(kept, jnp.where(spot < 4, left, right), 0.0)
-
-
-def first_pack(v, p, e, f, x_main, y_main):
+    first = jnp.where(spot < 4, left, roll(right, 4, 1))
+    second = jnp.where(spot < 4, roll(left, -4, 1), right)
+    return jnp.where(kept, first, 0.0), jnp.where(kept, second, 0.0)
+
+
+def first_pack(v_in, p_in, e_in, f_in, x_main, y_a, y_b, z_a, z_b, v, p, e, f, arrived):
     nx, nz, _ = p.shape
-
-    def plane(i, q):
-        return v[i, q] if i < 3 else p[q] if i == 3 else e[q] if i == 4 else f[i - 5, q]
-
+    loads = [
+        pltpu.make_async_copy(a, b, arrived.at[i])
+        for i, (a, b) in enumerate(((v_in, v), (p_in, p), (e_in, e), (f_in, f)))
+    ]
+    for load in loads:
+        load.start()
+    sends = []
     for m in range(x_main.shape[0]):
         high = high_side("gx", m)
         n = 0
         for i in range(8):
             width = 3 if i < 5 else 2
-            for j in range(width):
-                x_main[m, n] = plane(i, high * (nx - width) + j)
-                n += 1
+            at = pl.ds(high * (nx - width), width)
+            if i < 3:
+                planes = v.at[i, at]
+            elif i < 5:
+                planes = (p, e)[i - 3].at[at]
+            else:
+                planes = f.at[i - 5, at]
+            sends.append(
+                pltpu.make_async_copy(
+                    planes, x_main.at[m, pl.ds(n, width)], arrived.at[4 + 8 * m + i]
+                )
+            )
+            n += width
+    for load in loads:
+        load.wait()
+    for send in sends:
+        send.start()
+
+    def plane(i, q):
+        return v[i, q] if i < 3 else p[q] if i == 3 else e[q] if i == 4 else f[i - 5, q]
+
     edges = pair_edges(lambda i: [plane(i, q) for q in range(nx)], 8, nz)
-    for j in range(4):
-        y_main[j] = edges[j]
-
-
-def z_strip(low, high, toward_right, shift):
+    for m, out in enumerate((y_a, y_b)):
+        for j in range(2):
+            out[j] = y_strip(edges[j], edges[j + 2], high_side("gy", m))
+
+    def tile(i, q, top):
+        at = pl.ds(nz - 8, 8) if top else pl.ds(0, 8)
+        if i < 3:
+            return v[i, q, at]
+        return p[q, at] if i == 3 else e[q, at] if i == 4 else f[i - 5, q, at]
+
+    for m, out in enumerate((z_a, z_b)):
+        for j in range(4):
+            for q in range(nx):
+                low = tile(j, q, False), tile(j + 4, q, False)
+                high = tile(j, q, True), tile(j + 4, q, True)
+                out[j * nx + q] = z_strip(low, high, high_side("gz", m))
+    for send in sends:
+        send.wait()
+
+
+def y_strip(first, second, toward_right):
+    right = truth(toward_right, first.shape)
+    spot = iota(first.shape, 1) % SLOT
+    first = jnp.where(right, first, roll(first, -4, 1))
+    second = jnp.where(right, roll(second, 4, 1), second)
+    return jnp.where(spot < 4, first, second)
+
+
+def z_strip(low, high, toward_right):
     row = iota((8, LANES), 0)
     right = truth(toward_right, (8, LANES))
     first = jnp.where(right, roll(high[0], 4, 0), low[0])
@@ -126,29 +181,20 @@
     return jnp.where(row < 4, first, second)
 
 
-def second_pack(v, p, e, f, y_a, y_b, halo, z_a, z_b):
-    nx, nz, _ = p.shape
-
-    def tile(i, q, top):
-        at = pl.ds(nz - 8, 8) if top else pl.ds(0, 8)
-        if i < 3:
-            return v[i, q, at]
-        return p[q, at] if i == 3 else e[q, at] if i == 4 else f[i - 5, q, at]
-
-    merged = [merge_y(y_a[j], y_b[j]) for j in range(4)]
+def second_pack(z_first_a, z_first_b, y_a, y_b, halo, z_a, z_b):
+    nz = y_a.shape[1]
+    count = z_first_a.shape[0]
+    both = [merge_y(y_a[j], y_b[j]) for j in range(2)]
+    merged = [both[j % 2][j // 2] for j in range(4)]
     for j in range(4):
         halo[j] = merged[j]
-    for m, out in enumerate((z_a, z_b)):
-        right = high_side("gz", m)
-        for j in range(4):
-            for q in range(nx):
-                low = tile(j, q, False), tile(j + 4, q, False)
-                high = tile(j, q, True), tile(j + 4, q, True)
-                out[j * nx + q] = z_strip(low, high, right, 4)
+    for m, (first, out) in enumerate(((z_first_a, z_a), (z_first_b, z_b))):
+        for n in range(count):
+            out[n] = first[n]
         for j in range(2):
             low = merged[j][:8], merged[j + 2][:8]
             high = merged[j][nz - 8 :], merged[j + 2][nz - 8 :]
-            out[4 * nx + j] = z_strip(low, high, right, 4)
+            out[count + j] = z_strip(low, high, high_side("gz", m))
 
 
 def z_tiles(a, b):
@@ -204,7 +250,7 @@
 
 def main_shifts(x, halo, p):
     lane = iota(x.shape, 1)
-    beside = roll(halo, LANES - SLOT * p - 4, 1)
+    beside = halo
     rows = x.shape[0]
     return (
         roll(jnp.where(lane == 0, beside, x), LANES - 1, 1),
@@ -227,23 +273,20 @@
     )
 
 
-def main_weights(e, halo_e, w, lo, hi):
-    def face(p, carry):
+def main_weights(e, halo_e, w, width):
+    slots = e.shape[0]
+    for p in range(2 - width, slots - 3 + width):
         w[0][p] = e[p] + e[p + 1]
-        return carry
-
-    lax.fori_loop(lo - 1, hi, face, 0)
-
-    def body(p, carry):
+
+    def body(p):
         x = e[p]
         total = w[0][p] + w[0][p - 1]
-        for n, y in enumerate(main_shifts(x, halo_e[...], p)):
+        for n, y in enumerate(main_shifts(x, roll(halo_e[...], LANES - SLOT * p - 4, 1), p)):
             total += x + y
             w[1 + n][p] = x + y
         w[5][p] = relax_weight / total
-        return carry
-
-    lax.fori_loop(lo, hi, body, 0)
+
+    over_planes(slots, width, body)
 
 
 def halo_weights(e, edge_e, w):
@@ -259,7 +302,24 @@
     return (up - down, zp - zm, yp - ym)[k]
 
 
+def spread_halo(halo, beside, slots, width):
+    def body(p):
+        for k in range(4):
+            beside[k, p] = roll(halo[k], LANES - SLOT * p - 4, 1)
+
+    over_planes(slots, width, body)
+
+
+class Beside:
+    def __init__(self, ref, p):
+        self.ref, self.p = ref, p
+
+    def __getitem__(self, k):
+        return self.ref[k, self.p]
+
+
 def main_operator(src, halo, w, force, p, fields=(0, 1, 2)):
+    halo = Beside(halo, p)
     wxp, wxm, wyp, wym, wzp, wzm = w[0][p], w[0][p - 1], w[1][p], w[2][p], w[3][p], w[4][p]
     x = src[3, p]
     around = main_shifts(x, halo[3], p)
@@ -302,21 +362,18 @@
     return new + [olds[3] - 0.25 * e * spread]
 
 
-def add_edge(edge, k, p, x):
-    slot = iota(x.shape, 1) // SLOT
-    edge[k] = jnp.where(slot == p, roll(x, p * SLOT + 4, 1), edge[k])
+def edges_of(plane, lo, hi):
+    first = plane(lo)
+    slot = iota(first.shape, 1) // SLOT
+    total = jnp.zeros(first.shape, F32)
+    for p in range(lo, hi):
+        total = jnp.where(slot == p, roll(plane(p), p * SLOT + 4, 1), total)
+    return total
 
 
 def fill_edges(edge, src, fields, lo, hi):
     for k in range(fields):
-        edge[k] = jnp.zeros(edge.shape[1:], F32)
-
-    def body(p, carry):
-        for k in range(fields):
-            add_edge(edge, k, p, src[k, p])
-        return carry
-
-    lax.fori_loop(lo, hi, body, 0)
+        edge[k] = edges_of(lambda p: src[k, p], lo, hi)
 
 
 def fine_masks(rows, slots):
@@ -335,33 +392,35 @@
     return tile, column
 
 
-def fine_sweep(src, halo, edge, dst, halo_dst, edge_dst, w, hw, e, halo_e, force, halo_f, lo, hi, masks):
+def fine_sweep(src, halo, edge, dst, halo_dst, edge_dst, w, hw, e, halo_e, force, halo_f, width, masks, beside):
     tile, column = masks
     nz = src.shape[2] - 8
-    if edge_dst is not None:
-        for k in range(4):
-            edge_dst[k] = jnp.zeros(edge_dst.shape[1:], F32)
-
-    def body(p, carry):
-        new = relaxed(*main_operator(src, halo, w, force, p), w[5][p], e[p])
+
+    def body(p):
+        new = relaxed(*main_operator(src, beside, w, force, p), w[5][p], e[p])
         for k in range(4):
             x = new[k]
             dst[k, p, pl.ds(0, nz)] = x[:nz]
-            x8 = jnp.where(tile, x[nz:], 0.0)
-            dst[k, p, pl.ds(nz, 8)] = x8
-            if edge_dst is not None:
-                add_edge(edge_dst, k, p, jnp.concatenate([x[:nz], x8], axis=0))
-        return carry
-
-    lax.fori_loop(lo, hi, body, 0)
+            dst[k, p, pl.ds(nz, 8)] = jnp.where(tile, x[nz:], 0.0)
+
+    spread_halo(halo, beside, src.shape[1], width)
+    over_planes(src.shape[1], width, body)
     new = relaxed(*halo_operator(halo, edge, hw, halo_f), hw[6], halo_e[...])
     for k in range(4):
         halo_dst[k] = jnp.where(column, new[k], 0.0)
-
-
-def spans(slots, width):
+    if edge_dst is not None:
+        fill_edges(edge_dst, dst, 4, 3 - width, dst.shape[1] - 3 + width)
+
+
+def over_planes(slots, width, body):
     _, xl, xr = place("gx")
-    return 3 - width * xl, slots - 3 + width * xr
+    for p in range(3 - width, slots - 3 + width):
+        if p < 3:
+            pl.when(xl > 0)(lambda p=p: body(p))
+        elif p >= slots - 3:
+            pl.when(xr > 0)(lambda p=p: body(p))
+        else:
+            body(p)
 
 
 def own_slots(x, nx, part):
@@ -456,7 +515,7 @@
 def pre_smooth(
     v, p_in, e_in, f_in, z_halo, halo_full, x_main, x_rim,
     fields, coarse, edges, x_fine,
-    ua, ub, ha, hb, ca, cb, e, halo_e, edge_e, force, halo_f, w0, w1, w2, w3, w4, w5, hw, summed,
+    ua, ub, ha, hb, ca, cb, e, halo_e, edge_e, force, halo_f, w0, w1, w2, w3, w4, w5, hw, beside, summed,
 ):
     nx, nz, _ = p_in.shape
     slots = nx + 6
@@ -465,21 +524,12 @@
     first_fields(v, p_in, z_halo, halo_full, x_main, x_rim, ua, ub, ha)
     masks = fine_masks(nz + 8, slots)
     fill_edges(ca, ua, 4, 0, slots)
-    edge_e[...] = jnp.zeros(edge_e.shape, F32)
-
-    def body(p, carry):
-        slot = iota(edge_e.shape, 1) // SLOT
-        edge_e[...] = jnp.where(slot == p, roll(e[p], p * SLOT + 4, 1), edge_e[...])
-        return carry
-
-    lax.fori_loop(0, slots, body, 0)
-    lo, hi = spans(slots, 2)
-    main_weights(e, halo_e, w, lo, hi)
+    edge_e[...] = edges_of(lambda p: e[p], 0, slots)
+    main_weights(e, halo_e, w, 2)
     halo_weights(halo_e, edge_e, hw)
     rest = (w, hw, e, halo_e, force, halo_f)
-    fine_sweep(ua, ha, ca, ub, hb, cb, *rest, lo, hi, masks)
-    lo, hi = spans(slots, 1)
-    fine_sweep(ub, hb, cb, ua, ha, ca, *rest, lo, hi, masks)
+    fine_sweep(ua, ha, ca, ub, hb, cb, *rest, 2, masks, beside)
+    fine_sweep(ub, hb, cb, ua, ha, ca, *rest, 1, masks, beside)
     for k in range(4):
         for q in range(nx):
             fields[k, q] = ua[k, q + 3, pl.ds(0, nz)]
@@ -494,11 +544,12 @@
         second = roll(ca[j + 2][:nz], LANES // 2 - 3 * SLOT, 1)
         edges[j] = jnp.where(lane < LANES // 2, first, second)
 
-    def block(q, carry):
+    spread_halo(ha, beside, slots, 0)
+    for q in range(nx // 2):
         totals = [0.0] * 5
         for j in range(2):
             p = 2 * q + 3 + j
-            olds, sums, spread = main_operator(ua, ha, w, force, p)
+            olds, sums, spread = main_operator(ua, beside, w, force, p)
             diagonal = w0[p] + w0[p - 1] + w1[p] + w2[p] + w3[p] + w4[p]
             for k in range(3):
                 totals[k] += sums[k] - diagonal * olds[k]
@@ -506,9 +557,6 @@
             totals[4] += e[p]
         for k in range(5):
             summed[k, q] = totals[k][:nz]
-        return carry
-
-    lax.fori_loop(0, nx // 2, block, 0)
     scale = (0.5, 0.5, 0.5, -1.0 / 32.0, 0.125)
     cz = nz // 2
     left = []
@@ -600,21 +648,19 @@
             for i in range(tiles):
                 out[c * tiles + i] = total[8 * i : 8 * i + 8]
         n = columns * tiles
-        for j in range(2):
-            for i in range(nz // 8):
-                out[n] = edges[j, pl.ds(8 * i, 8)]
-                n += 1
-            out[n] = behind[j]
+        toward = high_side("gy", m)
+        for i in range(nz // 8):
+            out[n] = y_strip(edges[0, pl.ds(8 * i, 8)], edges[1, pl.ds(8 * i, 8)], toward)
             n += 1
+        out[n] = y_strip(behind[0], behind[1], toward)
 
 
 def sixth_pack(y_a, y_b, z_halo, halo_full, x_rim):
     tiles = halo_full.shape[1] // 8
-    first = y_a.shape[0] - 2 * tiles
-    for j in range(2):
-        for i in range(tiles):
-            n = first + j * tiles + i
-            halo_full[j, pl.ds(8 * i, 8)] = merge_y(y_a[n], y_b[n])
+    first = y_a.shape[0] - tiles
+    for i in range(tiles):
+        for j, x in enumerate(merge_y(y_a[first + i], y_b[first + i])):
+            halo_full[j, pl.ds(8 * i, 8)] = x
     pack_rim(x_rim, z_halo, lambda j: halo_full[j], 4, (1,) * 4, 1, SLOT)
 
 
@@ -745,7 +791,7 @@
 def post_smooth(
     e_in, f_in, z_first, halo_first, x_main, x_first, fields, z_halo, halo_full, x_fine, x_rim,
     main, column, v_out, p_out,
-    ua, ub, ha, hb, ca, cb, e, halo_e, edge_e, force, halo_f, w0, w1, w2, w3, w4, w5, hw,
+    ua, ub, ha, hb, ca, cb, e, halo_e, edge_e, force, halo_f, w0, w1, w2, w3, w4, w5, hw, beside,
 ):
     nx, nz, _ = e_in.shape
     slots = nx + 6
@@ -781,28 +827,21 @@
     for k in range(4):
         ha[k] = jnp.where(masks[1], ha[k] + column[k], 0.0)
     fill_edges(ca, ua, 4, 1, slots - 1)
-    edge_e[...] = jnp.zeros(edge_e.shape, F32)
-
-    def body(p, carry):
-        slot = iota(edge_e.shape, 1) // SLOT
-        edge_e[...] = jnp.where(slot == p, roll(e[p], p * SLOT + 4, 1), edge_e[...])
-        return carry
-
-    lax.fori_loop(1, slots - 1, body, 0)
-    lo, hi = spans(slots, 1)
-    main_weights(e, halo_e, w, lo, hi)
+    edge_e[...] = edges_of(lambda p: e[p], 1, slots - 1)
+    main_weights(e, halo_e, w, 1)
     halo_weights(halo_e, edge_e, hw)
     rest = (w, hw, e, halo_e, force, halo_f)
-    fine_sweep(ua, ha, ca, ub, hb, cb, *rest, lo, hi, masks)
-
-    def last(p, carry):
-        new = relaxed(*main_operator(ub, hb, w, force, p), w5[p], e[p])
+    fine_sweep(ua, ha, ca, ub, hb, None, *rest, 1, masks, beside)
+
+    spread_halo(hb, beside, slots, 0)
+
+    def last(p):
+        new = relaxed(*main_operator(ub, beside, w, force, p), w5[p], e[p])
         for k in range(3):
             v_out[k, p - 3] = new[k][:nz]
         p_out[p - 3] = new[3][:nz]
-        return carry
-
-    lax.fori_loop(3, nx + 3, last, 0)
+
+    over_planes(slots, 0, last)
 
 
 def local(velocity, pressure, viscosity, body_force):
@@ -814,12 +853,20 @@
     inputs = [velocity, pressure, viscosity, body_force]
     block = (nz, LANES)
 
-    x_main, y_main = call(first_pack, [(sides, 21) + block, (4,) + block], inputs)
+    z_shape = (4 * nx, 8, LANES)
+    x_main, y_a, y_b, z_a, z_b = call(
+        first_pack,
+        [(sides, 21) + block, (2,) + block, (2,) + block, z_shape, z_shape],
+        inputs,
+        [a.shape for a in inputs],
+        outside=4,
+        copies=4 + 8 * sides,
+    )
     x_main = swap_x(x_main)
-    y_a, y_b = swap(y_main, "gy", 0), swap(y_main, "gy", 1)
+    y_a, y_b = swap(y_a, "gy", 0), swap(y_b, "gy", 1)
     z_shape = (4 * nx + 2, 8, LANES)
     halo, z_a, z_b = call(
-        second_pack, [(4,) + block, z_shape, z_shape], inputs + [y_a, y_b]
+        second_pack, [(4,) + block, z_shape, z_shape], [z_a, z_b, y_a, y_b]
     )
     z_a, z_b = swap(z_a, "gz", 0), swap(z_b, "gz", 1)
     tiles = rows // 8
@@ -833,7 +880,7 @@
     state = [(4, slots, rows, LANES)] * 2 + [(4, rows, LANES)] * 4
     state += [(slots, rows, LANES), (rows, LANES), (rows, LANES)]
     state += [(3, slots, rows, LANES), (3, rows, LANES)]
-    state += [(slots, rows, LANES)] * 6 + [(7, rows, LANES)]
+    state += [(slots, rows, LANES)] * 6 + [(7, rows, LANES), (4, slots, rows, LANES)]
     fields, own, edges, x_fine = call(
         pre_smooth,
         [(4, nx) + block, (5, nx // 4, nz // 2, LANES), (2,) + block, (sides, 8) + block],
@@ -858,7 +905,7 @@
     )
     z_a, z_b = swap(z_a, "gz", 0), swap(z_b, "gz", 1)
     deep = nz // 2 + 16
-    y_shape = (-(-10 * pairs * SLOT // LANES) * (deep // 8) + 2 * tiles, 8, LANES)
+    y_shape = (-(-10 * pairs * SLOT // LANES) * (deep // 8) + tiles, 8, LANES)
     full, z_halo, y_a, y_b = call(
         fifth_pack,
         [(5, pairs, deep, LANES), (4, nx, 8, LANES), y_shape, y_shape],
@@ -886,7 +933,7 @@
     v_out, p_out = call(
         post_smooth,
         [(3, nx) + block, (nx,) + block],
-        [viscosity, body_force, z_first, halo_first, x_main, x_first]
+        inputs[2:] + [z_first, halo_first, x_main, x_first]
         + [fields, z_halo, halo_full, x_fine, x_rim, main, column],
         state,
         cost=8,

time: 65.3 us -> 49.5 us (0.76)
  Pallas kernels: 25.9 us -> 16.2 us
  local copies, waits for them, and re-layouts: 3.81 us -> 0.02 us
  waiting for transfers between devices: 20.4 us -> 17.9 us
    pallas_call x9, Pallas kernels: 25.9 us -> 16.2 us  [call(): pl.pallas_call(body, out_shape=[jax.ShapeDtypeStruct(shape, F32) for shap...]
    ppermute x11 -> x9, waiting for transfers between devices: 20.4 us -> 12.7 us  [swap(): return lax.ppermute(array, axis, pairs)]
    ppermute x2 -> x4, waiting for transfers between devices: 0.01 us -> 5.18 us  [swap(): return lax.ppermute(array, ('gy', 'gz'), pairs)]
    ppermute x2 -> x4, starting transfers between devices: 0.41 us -> 5.01 us  [swap(): return lax.ppermute(array, ('gy', 'gz'), pairs)]
    ppermute x11 -> x9, starting transfers between devices: 13.9 us -> 9.41 us  [swap(): return lax.ppermute(array, axis, pairs)]
    unnamed x16 -> x8, local copies, waits for them, and re-layouts: 3.81 us -> 0.02 us
  transfers between devices with their start and end apart: 13 -> 13, of which waited for: 6 -> 6; matrix products, arithmetic and copies ran while one was open for 0% -> 0% of each run, Pallas kernels for 8% -> 11%
where the time goes in v2:
time: 49.5 us; the launch traced here: 49.3 us
  waiting for transfers between devices  17.9 us (36%)
  Pallas kernels  16.2 us (33%)
  starting transfers between devices  14.4 us (29%)
  between operations  0.76 us (2%)
    pallas_call x9, Pallas kernels, call(): pl.pallas_call(body, out_shape=[jax.ShapeDtypeStruct(shape, F32) for shap...  16.2 us
    ppermute x9, waiting for transfers between devices, swap(): return lax.ppermute(array, axis, pairs)  12.7 us
    ppermute x9, starting transfers between devices, swap(): return lax.ppermute(array, axis, pairs)  9.41 us
    ppermute x4, waiting for transfers between devices, swap(): return lax.ppermute(array, ('gy', 'gz'), pairs)  5.18 us
    ppermute x4, starting transfers between devices, swap(): return lax.ppermute(array, ('gy', 'gz'), pairs)  5.01 us
  transfers between devices with their start and end apart: 13, of which 6 were waited for; matrix products, arithmetic and copies ran while one was open for 0% of the time, Pallas kernels for 11%

profile of v2, /device:TPU:0, one launch (start us, length us, event | category | flops | bytes accessed | tf_op | source)
XLA Modules:
  0.0 49.3 jit_solution(8059521465807344052)
XLA Ops:
  0.6 2.4 %shard_map.59 = (f32[1,21,32,128]{3,2,1,0:T(8,128)}, f32[2,32,128]{2,1,0:T(8,128)S(1)}, f32[2,32,128]{2,1,0:T(8,128)S(1)}, f32[32,8,128]{2,1,0:T(8,128)S(1)}, f32[32,8,128]{2,1,0:T(8,128)S(1)}) custom-call(f32[3,8,32,128]{3,2,1,0:T(8,128)} %v.1, f32[8,32,128]{2,1,0:T(8,128)} %p_in.3, f32[8,32,128]{2,1,0:T(8,128)} %e_in.5, f32[3,8,32,128]{3,2,1,0:T(8,128)} %f_in.5), custom_call_target="tpu_custom_call" | custom-call | flops 1000000 | bytes 1000000 | tf_op jit(solution)/shard_map/pallas_call | solution.py:16
  3.0 3.0 %collective-permute-start.4 = (f32[1,21,32,128]{3,2,1,0:T(8,128)}, f32[1,21,32,128]{3,2,1,0:T(8,128)S(1)}, u32[]{:S(2)}, u32[]{:S(2)}) collective-permute-start(f32[1,21,32,128]{3,2,1,0:T(8,128)} %get-tuple-element.37), channel_id=1, source_target_pairs={{0,16},{16,0},{1,17},{17,1},{2,18},{18,2},{3,19},{19,3},{4,20},{20... | collective-permute-start | bytes 1032200 | tf_op jit(solution)/shard_map/ppermute | solution.py:51
  6.1 1.6 %collective-permute-start = (f32[2,32,128]{2,1,0:T(8,128)S(1)}, f32[2,32,128]{2,1,0:T(8,128)S(1)}, u32[]{:S(2)}, u32[]{:S(2)}) collective-permute-start(f32[2,32,128]{2,1,0:T(8,128)S(1)} %get-tuple-element.30), channel_id=1, source_target_pairs={{0,4},{4,0},{8,12},{12,8},{1,5},{5,1},{9,13},{13,9},{2,6},{6,2},{1... | collective-permute-start | bytes 98312 | tf_op jit(solution)/shard_map/ppermute | solution.py:51
  7.6 2.3 %collective-permute-done.y_a = f32[2,32,128]{2,1,0:T(8,128)S(1)} collective-permute-done((f32[2,32,128]{2,1,0:T(8,128)S(1)}, f32[2,32,128]{2,1,0:T(8,128)S(1)}, u32[]{:S(2)}, u32[]{:S(2)}) %collective-permute-start) | collective-permute-done | bytes 32800 | tf_op jit(solution)/shard_map/ppermute | solution.py:51
  10.0 0.1 shard_map.60
  10.2 2.8 %collective-permute-start.3 = (f32[34,8,128]{2,1,0:T(8,128)S(1)}, f32[34,8,128]{2,1,0:T(8,128)S(1)}, u32[]{:S(2)}, u32[]{:S(2)}) collective-permute-start(f32[34,8,128]{2,1,0:T(8,128)S(1)} %get-tuple-element.33), channel_id=1, source_target_pairs={{0,4},{1,2},{2,1},{3,7},{4,0},{5,6},{6,5},{7,3},{8,12},{9,10},{10,... | collective-permute-start | bytes 417800 | tf_op jit(solution)/shard_map/ppermute | solution.py:46
  12.9 3.0 %collective-permute-done.3.z_b = f32[34,8,128]{2,1,0:T(8,128)S(1)} collective-permute-done((f32[34,8,128]{2,1,0:T(8,128)S(1)}, f32[34,8,128]{2,1,0:T(8,128)S(1)}, u32[]{:S(2)}, u32[]{:S(2)}) %collective-permute-start.3) | collective-permute-done | bytes 139296 | tf_op jit(solution)/shard_map/ppermute | solution.py:46
  16.0 0.2 shard_map.61
  16.1 0.6 %collective-permute-start.5 = (f32[1,23,8,128]{3,2,1,0:T(8,128)S(1)}, f32[1,23,8,128]{3,2,1,0:T(8,128)S(1)}, u32[]{:S(2)}, u32[]{:S(2)}) collective-permute-start(f32[1,23,8,128]{3,2,1,0:T(8,128)S(1)} %get-tuple-element.38), channel_id=1, source_target_pairs={{0,16},{16,0},{1,17},{17,1},{2,18},{18,2},{3,19},{19,3},{4,20},{20... | collective-permute-start | bytes 282632 | tf_op jit(solution)/shard_map/ppermute | solution.py:51
  16.7 4.1 %collective-permute-done.5.x_rim.x_first = f32[1,23,8,128]{3,2,1,0:T(8,128)S(1)} collective-permute-done((f32[1,23,8,128]{3,2,1,0:T(8,128)S(1)}, f32[1,23,8,128]{3,2,1,0:T(8,128)S(1)}, u32[]{:S(2)}, u32[]{:S(2)}) %collective-permute-start.5) | collective-permute-done | bytes 94240 | tf_op jit(solution)/shard_map/ppermute | solution.py:51
  20.8 4.8 %shard_map.62 = (f32[4,8,32,128]{3,2,1,0:T(8,128)S(1)}, f32[5,2,16,128]{3,2,1,0:T(8,128)S(1)}, f32[2,32,128]{2,1,0:T(8,128)S(1)}, f32[1,8,32,128]{3,2,1,0:T(8,128)S(1)}) custom-call(f32[3,8,32,128]{3,2,1,0:T(8,128)S(1)} %copy-done.1, f32[8,32,128]{2,1,0:T(8,128)S(1)} %copy-done.3, f32[8,32,128]{2,1,0:T(8,128)S(1)} %copy-done.2, ...), custom_call_target="tpu_custom_call" | custom-call | flops 8000000 | bytes 8000000 | tf_op jit(solution)/shard_map/pallas_call | solution.py:16
  25.6 0.7 %collective-permute-start.6 = (f32[5,2,16,128]{3,2,1,0:T(8,128)S(1)}, f32[5,2,16,128]{3,2,1,0:T(8,128)S(1)}, u32[]{:S(2)}, u32[]{:S(2)}) collective-permute-start(f32[5,2,16,128]{3,2,1,0:T(8,128)S(1)} %get-tuple-element.40.own), channel_id=1, source_target_pairs={{0,16},{16,0},{1,17},{17,1},{2,18},{18,2},{3,19},{19,3},{4,20},{20... | collective-permute-start | bytes 245768 | tf_op jit(solution)/shard_map/ppermute | solution.py:51
  26.2 3.8 %collective-permute-done.6.other = f32[5,2,16,128]{3,2,1,0:T(8,128)S(1)} collective-permute-done((f32[5,2,16,128]{3,2,1,0:T(8,128)S(1)}, f32[5,2,16,128]{3,2,1,0:T(8,128)S(1)}, u32[]{:S(2)}, u32[]{:S(2)}) %collective-permute-start.6) | collective-permute-done | bytes 81952 | tf_op jit(solution)/shard_map/ppermute | solution.py:51
  30.1 0.1 collective-permute-start.7
  30.2 2.2 %collective-permute-start.8 = (f32[28,8,128]{2,1,0:T(8,128)S(1)}, f32[28,8,128]{2,1,0:T(8,128)S(1)}, u32[]{:S(2)}, u32[]{:S(2)}) collective-permute-start(f32[28,8,128]{2,1,0:T(8,128)S(1)} %get-tuple-element.43), channel_id=1, source_target_pairs={{0,4},{1,2},{2,1},{3,7},{4,0},{5,6},{6,5},{7,3},{8,12},{9,10},{10,... | collective-permute-start | bytes 344072 | tf_op jit(solution)/shard_map/ppermute | solution.py:46
  32.5 0.6 %collective-permute-start.11 = (f32[1,8,32,128]{3,2,1,0:T(8,128)S(1)}, f32[1,8,32,128]{3,2,1,0:T(8,128)S(1)}, u32[]{:S(2)}, u32[]{:S(2)}) collective-permute-start(f32[1,8,32,128]{3,2,1,0:T(8,128)S(1)} %get-tuple-element.49), channel_id=1, source_target_pairs={{0,16},{16,0},{1,17},{17,1},{2,18},{18,2},{3,19},{19,3},{4,20},{20... | collective-permute-start | bytes 393224 | tf_op jit(solution)/shard_map/ppermute | solution.py:51
  33.1 2.1 %collective-permute-done.8.z_b = f32[28,8,128]{2,1,0:T(8,128)S(1)} collective-permute-done((f32[28,8,128]{2,1,0:T(8,128)S(1)}, f32[28,8,128]{2,1,0:T(8,128)S(1)}, u32[]{:S(2)}, u32[]{:S(2)}) %collective-permute-start.8) | collective-permute-done | bytes 114720 | tf_op jit(solution)/shard_map/ppermute | solution.py:46
  35.2 0.5 shard_map.64
  35.7 2.1 %collective-permute-start.9 = (f32[17,8,128]{2,1,0:T(8,128)S(1)}, f32[17,8,128]{2,1,0:T(8,128)S(1)}, u32[]{:S(2)}, u32[]{:S(2)}) collective-permute-start(f32[17,8,128]{2,1,0:T(8,128)S(1)} %get-tuple-element.46), channel_id=1, source_target_pairs={{0,4},{4,0},{8,12},{12,8},{1,5},{5,1},{9,13},{13,9},{2,6},{6,2},{1... | collective-permute-start | bytes 208904 | tf_op jit(solution)/shard_map/ppermute | solution.py:51
  37.8 2.5 %collective-permute-done.9.y_a = f32[17,8,128]{2,1,0:T(8,128)S(1)} collective-permute-done((f32[17,8,128]{2,1,0:T(8,128)S(1)}, f32[17,8,128]{2,1,0:T(8,128)S(1)}, u32[]{:S(2)}, u32[]{:S(2)}) %collective-permute-start.9) | collective-permute-done | bytes 69664 | tf_op jit(solution)/shard_map/ppermute | solution.py:51
  40.3 0.2 shard_map.65
  40.5 0.7 %collective-permute-start.12 = (f32[1,9,8,128]{3,2,1,0:T(8,128)S(1)}, f32[1,9,8,128]{3,2,1,0:T(8,128)S(1)}, u32[]{:S(2)}, u32[]{:S(2)}) collective-permute-start(f32[1,9,8,128]{3,2,1,0:T(8,128)S(1)} %get-tuple-element.50), channel_id=1, source_target_pairs={{0,16},{16,0},{1,17},{17,1},{2,18},{18,2},{3,19},{19,3},{4,20},{20... | collective-permute-start | bytes 110600 | tf_op jit(solution)/shard_map/ppermute | solution.py:51
  41.1 4.6 %shard_map.66 = (f32[4,6,40,128]{3,2,1,0:T(8,128)S(1)}, f32[4,40,128]{2,1,0:T(8,128)S(1)}) custom-call(f32[5,4,32,128]{3,2,1,0:T(8,128)S(1)} %get-tuple-element.51.full, f32[17,8,128]{2,1,0:T(8,128)S(1)} %collective-permute-done.9.y_a, f32[17,8,128]{2,1,0:T(8,128)S(1)} %collective-permute-done.10.y_b), custom_call_target="tpu_custom_call" | custom-call | flops 4000000 | bytes 4000000 | tf_op jit(solution)/shard_map/pallas_call | solution.py:16
  45.8 3.5 %shard_map.67 = (f32[3,8,32,128]{3,2,1,0:T(8,128)}, f32[8,32,128]{2,1,0:T(8,128)}) custom-call(f32[8,32,128]{2,1,0:T(8,128)S(1)} %copy-done.2, f32[3,8,32,128]{3,2,1,0:T(8,128)S(1)} %copy-done, f32[8,8,8,128]{3,2,1,0:T(8,128)S(1)} %get-tuple-element.35.z_halo.z_first, f32[4,40,128]{2,1,0:T(8,128)S(1)} %get-tuple-element.36.halo_full.halo_first, ...), custom_call_target="tpu_custom_call" | custom-call | flops 8000000 | bytes 8000000 | tf_op jit(solution)/shard_map/pallas_call | solution.py:16
  (19 shorter events, 0.2 us)
Async XLA Ops:
  0.6 20.1 %copy-start.1 = (f32[3,8,32,128]{3,2,1,0:T(8,128)S(1)}, f32[3,8,32,128]{3,2,1,0:T(8,128)}, u32[]{:S(2)}) copy-start(f32[3,8,32,128]{3,2,1,0:T(8,128)} %v.1) | copy-start | bytes 1179652
  3.0 17.8 %copy-start = (f32[3,8,32,128]{3,2,1,0:T(8,128)S(1)}, f32[3,8,32,128]{3,2,1,0:T(8,128)}, u32[]{:S(2)}) copy-start(f32[3,8,32,128]{3,2,1,0:T(8,128)} %f_in.5) | copy-start | bytes 1179652
  3.0 17.7 %collective-permute-start.4 = (f32[1,21,32,128]{3,2,1,0:T(8,128)}, f32[1,21,32,128]{3,2,1,0:T(8,128)S(1)}, u32[]{:S(2)}, u32[]{:S(2)}) collective-permute-start(f32[1,21,32,128]{3,2,1,0:T(8,128)} %get-tuple-element.37), channel_id=1, source_target_pairs={{0,16},{16,0},{1,17},{17,1},{2,18},{18,2},{3,19},{19,3},{4,20},{20... | collective-permute-start | bytes 1032200 | tf_op jit(solution)/shard_map/ppermute | solution.py:51
  6.1 3.9 %collective-permute-start = (f32[2,32,128]{2,1,0:T(8,128)S(1)}, f32[2,32,128]{2,1,0:T(8,128)S(1)}, u32[]{:S(2)}, u32[]{:S(2)}) collective-permute-start(f32[2,32,128]{2,1,0:T(8,128)S(1)} %get-tuple-element.30), channel_id=1, source_target_pairs={{0,4},{4,0},{8,12},{12,8},{1,5},{5,1},{9,13},{13,9},{2,6},{6,2},{1... | collective-permute-start | bytes 98312 | tf_op jit(solution)/shard_map/ppermute | solution.py:51
  7.6 2.3 %collective-permute-start.1 = (f32[2,32,128]{2,1,0:T(8,128)S(1)}, f32[2,32,128]{2,1,0:T(8,128)S(1)}, u32[]{:S(2)}, u32[]{:S(2)}) collective-permute-start(f32[2,32,128]{2,1,0:T(8,128)S(1)} %get-tuple-element.31), channel_id=1, source_target_pairs={{0,1},{1,0},{2,3},{3,2},{4,8},{5,9},{6,10},{7,11},{8,4},{9,5},{10,... | collective-permute-start | bytes 98312 | tf_op jit(solution)/shard_map/ppermute | solution.py:46
  10.1 2.8 %collective-permute-start.2 = (f32[34,8,128]{2,1,0:T(8,128)S(1)}, f32[34,8,128]{2,1,0:T(8,128)S(1)}, u32[]{:S(2)}, u32[]{:S(2)}) collective-permute-start(f32[34,8,128]{2,1,0:T(8,128)S(1)} %get-tuple-element.32), channel_id=1, source_target_pairs={{0,1},{1,0},{2,3},{3,2},{4,5},{5,4},{6,7},{7,6},{8,9},{9,8},{10,11... | collective-permute-start | bytes 417800 | tf_op jit(solution)/shard_map/ppermute | solution.py:51
  10.2 5.8 %collective-permute-start.3 = (f32[34,8,128]{2,1,0:T(8,128)S(1)}, f32[34,8,128]{2,1,0:T(8,128)S(1)}, u32[]{:S(2)}, u32[]{:S(2)}) collective-permute-start(f32[34,8,128]{2,1,0:T(8,128)S(1)} %get-tuple-element.33), channel_id=1, source_target_pairs={{0,4},{1,2},{2,1},{3,7},{4,0},{5,6},{6,5},{7,3},{8,12},{9,10},{10,... | collective-permute-start | bytes 417800 | tf_op jit(solution)/shard_map/ppermute | solution.py:46
  16.0 4.8 %copy-start.2 = (f32[8,32,128]{2,1,0:T(8,128)S(1)}, f32[8,32,128]{2,1,0:T(8,128)}, u32[]{:S(2)}) copy-start(f32[8,32,128]{2,1,0:T(8,128)} %e_in.5) | copy-start | bytes 393220
  16.0 4.8 %copy-start.3 = (f32[8,32,128]{2,1,0:T(8,128)S(1)}, f32[8,32,128]{2,1,0:T(8,128)}, u32[]{:S(2)}) copy-start(f32[8,32,128]{2,1,0:T(8,128)} %p_in.3) | copy-start | bytes 393220
  16.1 4.6 %collective-permute-start.5 = (f32[1,23,8,128]{3,2,1,0:T(8,128)S(1)}, f32[1,23,8,128]{3,2,1,0:T(8,128)S(1)}, u32[]{:S(2)}, u32[]{:S(2)}) collective-permute-start(f32[1,23,8,128]{3,2,1,0:T(8,128)S(1)} %get-tuple-element.38), channel_id=1, source_target_pairs={{0,16},{16,0},{1,17},{17,1},{2,18},{18,2},{3,19},{19,3},{4,20},{20... | collective-permute-start | bytes 282632 | tf_op jit(solution)/shard_map/ppermute | solution.py:51
  25.6 4.5 %collective-permute-start.6 = (f32[5,2,16,128]{3,2,1,0:T(8,128)S(1)}, f32[5,2,16,128]{3,2,1,0:T(8,128)S(1)}, u32[]{:S(2)}, u32[]{:S(2)}) collective-permute-start(f32[5,2,16,128]{3,2,1,0:T(8,128)S(1)} %get-tuple-element.40.own), channel_id=1, source_target_pairs={{0,16},{16,0},{1,17},{17,1},{2,18},{18,2},{3,19},{19,3},{4,20},{20... | collective-permute-start | bytes 245768 | tf_op jit(solution)/shard_map/ppermute | solution.py:51
  30.1 2.9 %collective-permute-start.7 = (f32[28,8,128]{2,1,0:T(8,128)S(1)}, f32[28,8,128]{2,1,0:T(8,128)S(1)}, u32[]{:S(2)}, u32[]{:S(2)}) collective-permute-start(f32[28,8,128]{2,1,0:T(8,128)S(1)} %get-tuple-element.42), channel_id=1, source_target_pairs={{0,1},{1,0},{2,3},{3,2},{4,5},{5,4},{6,7},{7,6},{8,9},{9,8},{10,11... | collective-permute-start | bytes 344072 | tf_op jit(solution)/shard_map/ppermute | solution.py:51
  30.2 5.0 %collective-permute-start.8 = (f32[28,8,128]{2,1,0:T(8,128)S(1)}, f32[28,8,128]{2,1,0:T(8,128)S(1)}, u32[]{:S(2)}, u32[]{:S(2)}) collective-permute-start(f32[28,8,128]{2,1,0:T(8,128)S(1)} %get-tuple-element.43), channel_id=1, source_target_pairs={{0,4},{1,2},{2,1},{3,7},{4,0},{5,6},{6,5},{7,3},{8,12},{9,10},{10,... | collective-permute-start | bytes 344072 | tf_op jit(solution)/shard_map/ppermute | solution.py:46
  32.5 13.3 %collective-permute-start.11 = (f32[1,8,32,128]{3,2,1,0:T(8,128)S(1)}, f32[1,8,32,128]{3,2,1,0:T(8,128)S(1)}, u32[]{:S(2)}, u32[]{:S(2)}) collective-permute-start(f32[1,8,32,128]{3,2,1,0:T(8,128)S(1)} %get-tuple-element.49), channel_id=1, source_target_pairs={{0,16},{16,0},{1,17},{17,1},{2,18},{18,2},{3,19},{19,3},{4,20},{20... | collective-permute-start | bytes 393224 | tf_op jit(solution)/shard_map/ppermute | solution.py:51
  35.7 4.6 %collective-permute-start.9 = (f32[17,8,128]{2,1,0:T(8,128)S(1)}, f32[17,8,128]{2,1,0:T(8,128)S(1)}, u32[]{:S(2)}, u32[]{:S(2)}) collective-permute-start(f32[17,8,128]{2,1,0:T(8,128)S(1)} %get-tuple-element.46), channel_id=1, source_target_pairs={{0,4},{4,0},{8,12},{12,8},{1,5},{5,1},{9,13},{13,9},{2,6},{6,2},{1... | collective-permute-start | bytes 208904 | tf_op jit(solution)/shard_map/ppermute | solution.py:51
  37.8 2.5 %collective-permute-start.10 = (f32[17,8,128]{2,1,0:T(8,128)S(1)}, f32[17,8,128]{2,1,0:T(8,128)S(1)}, u32[]{:S(2)}, u32[]{:S(2)}) collective-permute-start(f32[17,8,128]{2,1,0:T(8,128)S(1)} %get-tuple-element.47), channel_id=1, source_target_pairs={{0,1},{1,0},{2,3},{3,2},{4,8},{5,9},{6,10},{7,11},{8,4},{9,5},{10,... | collective-permute-start | bytes 208904 | tf_op jit(solution)/shard_map/ppermute | solution.py:46
  40.5 5.3 %collective-permute-start.12 = (f32[1,9,8,128]{3,2,1,0:T(8,128)S(1)}, f32[1,9,8,128]{3,2,1,0:T(8,128)S(1)}, u32[]{:S(2)}, u32[]{:S(2)}) collective-permute-start(f32[1,9,8,128]{3,2,1,0:T(8,128)S(1)} %get-tuple-element.50), channel_id=1, source_target_pairs={{0,16},{16,0},{1,17},{17,1},{2,18},{18,2},{3,19},{19,3},{4,20},{20... | collective-permute-start | bytes 110600 | tf_op jit(solution)/shard_map/ppermute | solution.py:51

commit v3 on v2

--- a/solution.py
+++ b/solution.py
@@ -10,6 +10,11 @@
 F32 = jnp.float32
 relax_weight = 0.6
 HELD = 429 * 2**17
+Z_PLACES = (
+    ((0, 0, 3), (1, 3, 3), (5, 6, 2)),
+    ((2, 0, 3), (3, 3, 3), (6, 6, 2)),
+    ((4, 0, 3), (7, 3, 2)),
+)
 
 
 def call(body, outs, args, scratch=(), cost=1, outside=0, copies=0):
@@ -155,108 +160,130 @@
             return v[i, q, at]
         return p[q, at] if i == 3 else e[q, at] if i == 4 else f[i - 5, q, at]
 
-    for m, out in enumerate((z_a, z_b)):
-        for j in range(4):
-            for q in range(nx):
-                low = tile(j, q, False), tile(j + 4, q, False)
-                high = tile(j, q, True), tile(j + 4, q, True)
-                out[j * nx + q] = z_strip(low, high, high_side("gz", m))
+    for q in range(nx):
+        for n, fields in enumerate(Z_PLACES):
+            for m, out in enumerate((z_a, z_b)):
+                out[3 * q + n] = z_strip(
+                    [(tile(i, q, False), tile(i, q, True), at, rows) for i, at, rows in fields],
+                    high_side("gz", m),
+                )
     for send in sends:
         send.wait()
 
 
+def strip(first, second, toward_right, width):
+    right = truth(toward_right, first.shape)
+    spot = iota(first.shape, 1) % (2 * width)
+    first = jnp.where(right, first, roll(first, -width, 1))
+    second = jnp.where(right, roll(second, width, 1), second)
+    return jnp.where(spot < width, first, second)
+
+
 def y_strip(first, second, toward_right):
-    right = truth(toward_right, first.shape)
-    spot = iota(first.shape, 1) % SLOT
-    first = jnp.where(right, first, roll(first, -4, 1))
-    second = jnp.where(right, roll(second, 4, 1), second)
-    return jnp.where(spot < 4, first, second)
-
-
-def z_strip(low, high, toward_right):
+    return strip(first, second, toward_right, SLOT // 2)
+
+
+def z_strip(parts, toward_right):
+    right = truth(toward_right, (8, LANES))
+    return rows_of(
+        [
+            (jnp.where(right, roll(high, at + rows, 0), roll(low, at, 0)), 0, at, rows)
+            for low, high, at, rows in parts
+        ]
+    )
+
+
+def z_tail(halo, first, out, message):
+    nz = halo.shape[1]
     row = iota((8, LANES), 0)
-    right = truth(toward_right, (8, LANES))
-    first = jnp.where(right, roll(high[0], 4, 0), low[0])
-    second = jnp.where(right, high[1], roll(low[1], 4, 0))
-    return jnp.where(row < 4, first, second)
-
-
-def second_pack(z_first_a, z_first_b, y_a, y_b, halo, z_a, z_b):
-    nz = y_a.shape[1]
-    count = z_first_a.shape[0]
-    both = [merge_y(y_a[j], y_b[j]) for j in range(2)]
-    merged = [both[j % 2][j // 2] for j in range(4)]
+    for n in range(first.shape[0]):
+        out[n] = first[n]
     for j in range(4):
-        halo[j] = merged[j]
-    for m, (first, out) in enumerate(((z_first_a, z_a), (z_first_b, z_b))):
-        for n in range(count):
-            out[n] = first[n]
-        for j in range(2):
-            low = merged[j][:8], merged[j + 2][:8]
-            high = merged[j][nz - 8 :], merged[j + 2][nz - 8 :]
-            out[count + j] = z_strip(low, high, high_side("gz", m))
-
-
-def z_tiles(a, b):
+        tiles = halo[j, pl.ds(0, 8)], halo[j, pl.ds(nz - 8, 8)]
+        x = z_strip([tiles + (5, 3)], high_side("gz", message))
+        out[3 * j + 2] = jnp.where(row < 5, first[3 * j + 2], x)
+
+
+def second_pack(z_first, y_a, y_b, halo, z_b):
+    for j in range(2):
+        halo[j], halo[j + 2] = merge_y(y_a[j], y_b[j])
+    z_tail(halo, z_first, z_b, 1)
+
+
+def second_pack_near(z_first, halo, z_a):
+    z_tail(halo, z_first, z_a, 0)
+
+
+def z_tile(a, b, at, rows):
     _, has_left, has_right = place("gz")
     left, right = left_right("gz", a, b)
     row = iota(a.shape, 0)
-    kept = (row < 4 * has_right) | (row >= 8 - 4 * has_left)
-    first = jnp.where(row < 4, right, roll(left, 4, 0))
-    second = jnp.where(row < 4, roll(right, 4, 0), left)
-    return jnp.where(kept, first, 0.0), jnp.where(kept, second, 0.0)
+    x = jnp.where(row < rows * has_right, roll(right, -at, 0), 0.0)
+    return jnp.where(row >= 8 - rows * has_left, roll(left, 8 - at - rows, 0), x)
 
 
 def third_pack(z_a, z_b, halo, z_halo, halo_full, x_rim):
     nx = z_halo.shape[1]
     nz = halo.shape[1]
-    for j in range(4):
-        for q in range(nx):
-            z_halo[j, q], z_halo[j + 4, q] = z_tiles(z_a[j * nx + q], z_b[j * nx + q])
+    for q in range(nx):
+        for n, fields in enumerate(Z_PLACES):
+            for i, at, rows in fields:
+                z_halo[i, q] = z_tile(z_a[3 * q + n], z_b[3 * q + n], at, rows)
     for j in range(4):
         halo_full[j, pl.ds(0, nz)] = halo[j]
-    for j in range(2):
-        first, second = z_tiles(z_a[4 * nx + j], z_b[4 * nx + j])
-        halo_full[j, pl.ds(nz, 8)] = first
-        halo_full[j + 2, pl.ds(nz, 8)] = second
-    pack_rim(x_rim, z_halo, lambda j: halo_full[j], 8, (2,) * 5 + (1,) * 3, 3, 32)
-
-
-def pack_rim(x_rim, z_halo, halo_pair, fields, widths, planes, stride):
-    nx = z_halo.shape[1]
+        halo_full[j, pl.ds(nz, 8)] = z_tile(z_a[3 * j + 2], z_b[3 * j + 2], 5, 3)
+
+    def tiles(plane):
+        out = [
+            rows_of([(z_halo[i, plane(1)], 0, 6, 4), (z_halo[i, plane(2)], 3, 2, 2)])
+            for i in range(5)
+        ]
+        force = zip((0, 3, 5), (7, 2, 4))
+        out.append(
+            rows_of([(z_halo[5 + k, plane(1)], at, row, 2) for k, (at, row) in enumerate(force)])
+        )
+        return out
+
+    pack_rim(x_rim, tiles, lambda j: halo_full[j], 8, 2, nx)
+
+
+def rows_of(parts):
+    row = iota((8, LANES), 0)
+    total = jnp.zeros((8, LANES), F32)
+    for x, shift, first, count in parts:
+        total = jnp.where((row - first) % 8 < count, roll(x, shift, 0), total)
+    return total
+
+
+def pack_rim(x_rim, tiles, halo_pair, fields, planes, nx):
     half = fields // 2
-    per_column = LANES // stride
+    stride = LANES // 8 if fields == 8 else SLOT
     for m in range(x_rim.shape[0]):
         high = high_side("gx", m)
-        n = 0
-        for i in range(fields):
-            for j in range(widths[i]):
-                x_rim[m, n] = z_halo[i, high * (nx - widths[i]) + j]
-                n += 1
+        done = tiles(lambda d, high=high: high * (nx - 2 * d + 1) + d - 1)
+        for n, x in enumerate(done):
+            x_rim[m, n] = x
         pairs = [halo_pair(j) for j in range(half)]
         rows = pairs[0].shape[0]
         column = iota((rows, LANES), 1) // stride
         first = high * (nx - planes) * SLOT
-        for c in range(-(-fields // per_column)):
-            total = jnp.zeros((rows, LANES), F32)
-            for t in range(min(per_column, fields - c * per_column)):
-                i = c * per_column + t
-                at = t * stride - first - (i // half) * (LANES // 2)
-                total = jnp.where(column == t, roll(pairs[i % half], at + LANES, 1), total)
-            for r in range(rows // 8):
-                x_rim[m, n] = total[8 * r : 8 * r + 8]
-                n += 1
-
-
-def main_shifts(x, halo, p):
-    lane = iota(x.shape, 1)
-    beside = halo
+        total = jnp.zeros((rows, LANES), F32)
+        for i in range(fields):
+            at = i * stride - first - (i // half) * (LANES // 2)
+            total = jnp.where(column == i, roll(pairs[i % half], at + LANES, 1), total)
+        for r in range(rows // 8):
+            x_rim[m, len(done) + r] = total[8 * r : 8 * r + 8]
+
+
+def main_shifts(x, beside, kept):
     rows = x.shape[0]
+    y, beside = x[:kept], beside[:kept]
+    lane = iota(y.shape, 1)
     return (
-        roll(jnp.where(lane == 0, beside, x), LANES - 1, 1),
-        roll(jnp.where(lane == LANES - 1, beside, x), 1, 1),
-        roll(x, rows - 1, 0),
-        roll(x, 1, 0),
+        roll(jnp.where(lane == 0, beside, y), LANES - 1, 1),
+        roll(jnp.where(lane == LANES - 1, beside, y), 1, 1),
+        roll(x, rows - 1, 0)[:kept],
+        roll(x, 1, 0)[:kept],
     )
 
 
@@ -281,7 +308,7 @@
     def body(p):
         x = e[p]
         total = w[0][p] + w[0][p - 1]
-        for n, y in enumerate(main_shifts(x, roll(halo_e[...], LANES - SLOT * p - 4, 1), p)):
+        for n, y in enumerate(main_shifts(x, roll(halo_e[...], LANES - SLOT * p - 4, 1), x.shape[0])):
             total += x + y
             w[1 + n][p] = x + y
         w[5][p] = relax_weight / total
@@ -303,40 +330,36 @@
 
 
 def spread_halo(halo, beside, slots, width):
+    kept = beside.shape[2] - (0 if width else 8)
+
     def body(p):
         for k in range(4):
-            beside[k, p] = roll(halo[k], LANES - SLOT * p - 4, 1)
+            beside[k, p, pl.ds(0, kept)] = roll(halo[k][:kept], LANES - SLOT * p - 4, 1)
 
     over_planes(slots, width, body)
 
 
-class Beside:
-    def __init__(self, ref, p):
-        self.ref, self.p = ref, p
-
-    def __getitem__(self, k):
-        return self.ref[k, self.p]
-
-
-def main_operator(src, halo, w, force, p, fields=(0, 1, 2)):
-    halo = Beside(halo, p)
-    wxp, wxm, wyp, wym, wzp, wzm = w[0][p], w[0][p - 1], w[1][p], w[2][p], w[3][p], w[4][p]
-    x = src[3, p]
-    around = main_shifts(x, halo[3], p)
-    up, down = src[3, p + 1], src[3, p - 1]
+def main_operator(src, beside, w, force, p, kept):
+    def at(ref, *index):
+        return ref[index + (pl.ds(0, kept),)]
+
+    wxp, wxm, wyp, wym, wzp, wzm = (
+        at(ref, q) for ref, q in zip((w[0],) + w[:5], (p, p - 1, p, p, p, p))
+    )
+    around = main_shifts(src[3, p], at(beside, 3, p), kept)
+    up, down = at(src, 3, p + 1), at(src, 3, p - 1)
     olds, sums, spread = [], [], 0.0
     for k in range(3):
-        u = src[k, p]
-        yp, ym, zp, zm = main_shifts(u, halo[k], p)
-        xp, xm = src[k, p + 1], src[k, p - 1]
-        total = force[k, p] - terms(k, up, down, *around)
+        yp, ym, zp, zm = main_shifts(src[k, p], at(beside, k, p), kept)
+        xp, xm = at(src, k, p + 1), at(src, k, p - 1)
+        total = at(force, k, p) - terms(k, up, down, *around)
         total += wxp * xp + wxm * xm
         total += wyp * yp + wym * ym
         total += wzp * zp + wzm * zm
         spread += terms(k, xp, xm, yp, ym, zp, zm)
-        olds.append(u)
+        olds.append(at(src, k, p))
         sums.append(total)
-    olds.append(x)
+    olds.append(at(src, 3, p))
     return olds, sums, spread
 
 
@@ -397,7 +420,7 @@
     nz = src.shape[2] - 8
 
     def body(p):
-        new = relaxed(*main_operator(src, beside, w, force, p), w[5][p], e[p])
+        new = relaxed(*main_operator(src, beside, w, force, p, nz + 8), w[5][p], e[p])
         for k in range(4):
             x = new[k]
             dst[k, p, pl.ds(0, nz)] = x[:nz]
@@ -468,18 +491,21 @@
             e[right * (nx + 3) + j, pl.ds(0, nz)] = jnp.where(there, x_main[m, 12 + j], 0.0)
         for j in range(2):
             at = right * (nx + 2) + 1 + j
-            e[at, pl.ds(nz, 8)] = jnp.where(there8, x_rim[m, 8 + j], 0.0)
             for k in range(3):
                 force[k, at, pl.ds(0, nz)] = jnp.where(there, 2.0 * x_main[m, 15 + 2 * k + j], 0.0)
-        for k in range(3):
-            at = right * (nx + 1) + 2
-            force[k, at, pl.ds(nz, 8)] = jnp.where(there8, 2.0 * x_rim[m, 10 + k], 0.0)
+        near = right * (nx + 1) + 2
+        x = jnp.where(there8, x_rim[m, 4], 0.0)
+        e[near, pl.ds(nz, 8)] = x
+        e[near + 2 * right - 1, pl.ds(nz, 8)] = roll(x, -3, 0)
+        x = jnp.where(there8, 2.0 * x_rim[m, 5], 0.0)
+        for k, at in enumerate((0, 3, 5)):
+            force[k, near, pl.ds(nz, 8)] = roll(x, -at, 0)
         tiles = (nz + 8) // 8
-        column = jnp.concatenate([x_rim[m, 13 + tiles + r] for r in range(tiles)], axis=0)
-        x, kept = rim_halo(column, 0, 32, 3, right, valid, nx)
+        column = jnp.concatenate([x_rim[m, 6 + r] for r in range(tiles)], axis=0)
+        x, kept = rim_halo(column, 4, LANES // 8, 2, right, valid, nx)
         halo_e[...] = jnp.where(kept, x, halo_e[...])
         for k in range(3):
-            x, kept = rim_halo(column, 1 + k, 32, 3, right, valid, nx)
+            x, kept = rim_halo(column, 5 + k, LANES // 8, 2, right, valid, nx)
             halo_f[k] = jnp.where(kept, 2.0 * x, halo_f[k])
 
 
@@ -500,22 +526,23 @@
         there = truth(valid, (nz, LANES))
         there8 = truth(valid, (8, LANES))
         tiles = (nz + 8) // 8
-        column = jnp.concatenate([x_rim[m, 13 + r] for r in range(tiles)], axis=0)
+        column = jnp.concatenate([x_rim[m, 6 + r] for r in range(tiles)], axis=0)
+        near = right * (nx + 1) + 2
         for k in range(4):
             for j in range(3):
                 x = jnp.where(there, x_main[m, 3 * k + j], 0.0)
                 u[k, right * (nx + 3) + j, pl.ds(0, nz)] = x
-            for j in range(2):
-                x = jnp.where(there8, x_rim[m, 2 * k + j], 0.0)
-                u[k, right * (nx + 2) + 1 + j, pl.ds(nz, 8)] = x
-            x, kept = rim_halo(column, k, 32, 3, right, valid, nx)
+            x = jnp.where(there8, x_rim[m, k], 0.0)
+            u[k, near, pl.ds(nz, 8)] = x
+            u[k, near + 2 * right - 1, pl.ds(nz, 8)] = roll(x, -3, 0)
+            x, kept = rim_halo(column, k, LANES // 8, 2, right, valid, nx)
             halo[k] = jnp.where(kept, x, halo[k])
 
 
 def pre_smooth(
     v, p_in, e_in, f_in, z_halo, halo_full, x_main, x_rim,
-    fields, coarse, edges, x_fine,
-    ua, ub, ha, hb, ca, cb, e, halo_e, edge_e, force, halo_f, w0, w1, w2, w3, w4, w5, hw, beside, summed,
+    fields, coarse, edges, x_fine, e, halo_e, force, halo_f, w0, w1, w2, w3, w4, w5, hw,
+    ua, ub, ha, hb, ca, cb, edge_e, beside, summed,
 ):
     nx, nz, _ = p_in.shape
     slots = nx + 6
@@ -549,14 +576,14 @@
         totals = [0.0] * 5
         for j in range(2):
             p = 2 * q + 3 + j
-            olds, sums, spread = main_operator(ua, beside, w, force, p)
-            diagonal = w0[p] + w0[p - 1] + w1[p] + w2[p] + w3[p] + w4[p]
+            olds, sums, spread = main_operator(ua, beside, w, force, p, nz)
+            diagonal = (w0[p] + w0[p - 1] + w1[p] + w2[p] + w3[p] + w4[p])[:nz]
             for k in range(3):
                 totals[k] += sums[k] - diagonal * olds[k]
             totals[3] += spread
-            totals[4] += e[p]
+            totals[4] += e[p, pl.ds(0, nz)]
         for k in range(5):
-            summed[k, q] = totals[k][:nz]
+            summed[k, q] = totals[k]
     scale = (0.5, 0.5, 0.5, -1.0 / 32.0, 0.125)
     cz = nz // 2
     left = []
@@ -596,9 +623,15 @@
     for m, out in enumerate((z_a, z_b)):
         right = high_side("gz", m)
         start = pl.multiple_of(right * (cz - 8), 8)
-        for k in range(5):
-            for r in range(pairs):
-                out[k * pairs + r] = whole[k, r, pl.ds(start, 8)]
+        for r in range(pairs):
+            for k in range(2):
+                parts = [
+                    (whole[k + 2 * h, r, pl.ds(0, 8)], whole[k + 2 * h, r, pl.ds(cz - 8, 8)])
+                    + (4 * h, 4)
+                    for h in range(2)
+                ]
+                out[k * pairs + r] = z_strip(parts, right)
+            out[2 * pairs + r] = whole[4, r, pl.ds(start, 8)]
         toward = truth(right, (8, LANES))
         for q in range(nx):
             total = jnp.zeros((8, LANES), F32)
@@ -606,53 +639,76 @@
                 low = roll(fields[k, q, pl.ds(0, 8)], 2 * k, 0)
                 high = roll(fields[k, q, pl.ds(nz - 8, 8)], 2 * k - 6, 0)
                 total = jnp.where(row == k, jnp.where(toward, high, low), total)
-            out[5 * pairs + q] = total
-
-
-def fifth_pack(whole, z_a, z_b, edges, full, z_halo, y_a, y_b):
+            out[3 * pairs + q] = total
+
+
+def fold_rows(x):
+    own = x.shape[0] - 16
+    row = iota((8, LANES), 0)
+    halo = jnp.where(row < 4, x[own : own + 8], x[own + 8 :])
+    return jnp.concatenate([x[:own], halo], axis=0)
+
+
+def deep_edges(pairs):
+    per = LANES // 16
+    columns = []
+    for n, x in enumerate(pairs):
+        for g in range(2):
+            t = (2 * n + g) % per
+            x_t = roll(x, 16 * t + 8 - 64 * g, 1)
+            if t == 0:
+                columns.append(x_t)
+            else:
+                slot = iota(x.shape, 1) // 16
+                columns[-1] = jnp.where(slot == t, x_t, columns[-1])
+    return columns
+
+
+def fifth_pack(whole, z_a, z_b, edges, full, full_e, z_halo, y_a, y_b):
     pairs, cz = whole.shape[1:3]
     nx = z_halo.shape[1]
     nz = edges.shape[1]
     _, has_left, has_right = place("gz")
     to_left = truth(has_left, (8, LANES))
     to_right = truth(has_right, (8, LANES))
+    deep = []
     for k in range(5):
         for r in range(pairs):
-            n = k * pairs + r
-            left, right = left_right("gz", z_a[n], z_b[n])
-            full[k, r, pl.ds(0, cz)] = whole[k, r]
-            full[k, r, pl.ds(cz, 8)] = jnp.where(to_right, right, 0.0)
-            full[k, r, pl.ds(cz + 8, 8)] = jnp.where(to_left, left, 0.0)
+            if k < 4:
+                n = k % 2 * pairs + r
+                tile = z_tile(z_a[n], z_b[n], k // 2 * 4, 4)
+                x = jnp.concatenate([whole[k, r], tile], axis=0)
+                full[k, r] = x
+            else:
+                left, right = left_right("gz", z_a[2 * pairs + r], z_b[2 * pairs + r])
+                right = jnp.where(to_right, right, 0.0)
+                left = jnp.where(to_left, left, 0.0)
+                x = jnp.concatenate([whole[k, r], right, left], axis=0)
+                full_e[r] = x
+            deep.append(x)
     row = iota((8, LANES), 0)
     for q in range(nx):
-        left, right = left_right("gz", z_a[5 * pairs + q], z_b[5 * pairs + q])
+        left, right = left_right("gz", z_a[3 * pairs + q], z_b[3 * pairs + q])
         for k in range(4):
             x = jnp.where(row < 2 * has_right, roll(right, -2 * k, 0), 0.0)
             z_halo[k, q] = jnp.where(row >= 8 - 2 * has_left, roll(left, 6 - 2 * k, 0), x)
-    rows = cz + 16
-    tiles = rows // 8
-    slot = iota((rows, LANES), 1) // SLOT
-    per = LANES // SLOT
-    count = 5 * pairs * 2
-    columns = -(-count // per)
+    columns = deep_edges(deep[: 4 * pairs])
+    half = len(columns) // 2
+    columns_e = deep_edges(deep[4 * pairs :])
     behind = pair_edges(lambda i: [z_halo[i, q] for q in range(nx)], 4, 8)
     for m, out in enumerate((y_a, y_b)):
-        high = high_side("gy", m) * (LANES // 2 - SLOT)
-        for c in range(columns):
-            total = jnp.zeros((rows, LANES), F32)
-            for t in range(min(per, count - c * per)):
-                n = c * per + t
-                k, r, s = n // (2 * pairs), n // 2 % pairs, n % 2
-                at = SLOT * t - s * (LANES // 2) - high
-                total = jnp.where(slot == t, roll(full[k, r], at + LANES, 1), total)
-            for i in range(tiles):
-                out[c * tiles + i] = total[8 * i : 8 * i + 8]
-        n = columns * tiles
         toward = high_side("gy", m)
+        parts = [
+            strip(columns[j], columns[j + half], toward, 8) for j in range(half)
+        ] + columns_e
         for i in range(nz // 8):
-            out[n] = y_strip(edges[0, pl.ds(8 * i, 8)], edges[1, pl.ds(8 * i, 8)], toward)
-            n += 1
-        out[n] = y_strip(behind[0], behind[1], toward)
+            parts.append(y_strip(edges[0, pl.ds(8 * i, 8)], edges[1, pl.ds(8 * i, 8)], toward))
+        parts.append(y_strip(behind[0], behind[1], toward))
+        n = 0
+        for x in parts:
+            for i in range(x.shape[0] // 8):
+                out[n] = x[8 * i : 8 * i + 8]
+                n += 1
 
 
 def sixth_pack(y_a, y_b, z_halo, halo_full, x_rim):
@@ -661,22 +717,31 @@
     for i in range(tiles):
         for j, x in enumerate(merge_y(y_a[first + i], y_b[first + i])):
             halo_full[j, pl.ds(8 * i, 8)] = x
-    pack_rim(x_rim, z_halo, lambda j: halo_full[j], 4, (1,) * 4, 1, SLOT)
-
-
-def coarse_solve(full, y_a, y_b, main, halo, ca, cb, force, e, w0, w1, w2, w3, w4, w5, grown):
+    nx = z_halo.shape[1]
+
+    def rim(plane):
+        return [rows_of([(z_halo[k, plane(1)], 2 * k, 2 * k - 1, 2) for k in range(4)])]
+
+    pack_rim(x_rim, rim, lambda j: halo_full[j], 4, 1, nx)
+
+
+def coarse_solve(full, full_e, y_a, y_b, main, halo, ca, cb, force, e, w0, w1, w2, w3, w4, w5, deep_e, grown):
     pairs, rows = full.shape[1:3]
+    deep = full_e.shape[1]
     planes = 2 * pairs
     own = main.shape[1] - 2
-    tiles = rows // 8
-    per = LANES // SLOT
-    lane = iota((rows, LANES), 1)
-    row = iota((rows, LANES), 0)
+    cz = rows - 8
+    half = LANES // 2
     _, zl, zr = place("gz")
     _, yl, yr = place("gy")
-    half = LANES // 2
-    inside = (row < rows - 16 + 8 * zr) | (row >= rows - 8 * zl)
-    inside &= (lane < half + SLOT * yr) | (lane >= LANES - SLOT * yl)
+    gx = lax.axis_index("gx")
+
+    def inside(rows, width):
+        lane = iota((rows, LANES), 1)
+        row = iota((rows, LANES), 0)
+        kept = (row < cz + width * zr) | (row >= rows - width * zl)
+        return kept & ((lane < half + SLOT * yr) | (lane >= LANES - SLOT * yl))
+
     zero = jnp.zeros((rows, LANES), F32)
     w = (w0, w1, w2, w3, w4, w5)
     for k in range(4):
@@ -685,49 +750,89 @@
             cb[k, p] = zero
     e[0] = zero
     e[planes + 1] = zero
-    for n in range(10 * pairs):
-        k, r, s = n // (2 * pairs), n // 2 % pairs, n % 2
-        c, t = n // per, n % per
-        a = jnp.concatenate([y_a[c * tiles + i] for i in range(tiles)], axis=0)
-        b = jnp.concatenate([y_b[c * tiles + i] for i in range(tiles)], axis=0)
-        left, right = left_right("gy", a, b)
-        x = roll(full[k, r], -s * half, 1)
-        x = jnp.where(lane < half, x, roll(right, half - SLOT * t, 1))
-        x = jnp.where(lane < LANES - SLOT, x, roll(left, LANES - SLOT - SLOT * t, 1))
-        x = jnp.where(inside, x, 0.0)
-        if k < 4:
-            force[k, 2 * r + s] = x
-        else:
-            e[2 * r + s + 1] = x
+    deep_e[0] = jnp.zeros((deep, LANES), F32)
+    deep_e[planes + 1] = jnp.zeros((deep, LANES), F32)
+
+    tiles, deep_tiles = rows // 8, deep // 8
+    count = pairs // 2
+    columns = []
+
+    def taken(ref, n, tiles):
+        return jnp.concatenate([ref[n + i] for i in range(tiles)], axis=0)
+
+    seconds = []
+    for j in range(count):
+        left, right = left_right("gy", taken(y_a, j * tiles, tiles), taken(y_b, j * tiles, tiles))
+        spot = iota(left.shape, 1) % 16
+        columns.append(jnp.where(spot < 8, left, roll(right, 8, 1)))
+        seconds.append(jnp.where(spot < 8, roll(left, -8, 1), right))
+    columns += seconds
+    columns_e = []
+    for j in range(-(-pairs // 4)):
+        n = count * tiles + j * deep_tiles
+        left, right = left_right("gy", taken(y_a, n, deep_tiles), taken(y_b, n, deep_tiles))
+        spot = iota(left.shape, 1) % 16
+        columns_e.append(jnp.where(spot < 8, left, right))
+
+    def whole_plane(pair, columns, n, s):
+        lane = iota(pair.shape, 1)
+        last, first = 2 * n + 1 - s, 2 * n + s
+        low = roll(columns[first // 8], half - 16 * (first % 8) - 8, 1)
+        high = roll(columns[last // 8], LANES - 8 - 16 * (last % 8), 1)
+        x = jnp.where(lane < half, roll(pair, -s * half, 1), low)
+        return jnp.where(lane < LANES - 8, x, high)
+
+    near, far = inside(rows, 4), inside(deep, 8)
+    for r in range(pairs):
+        for s in range(2):
+            p = 2 * r + s
+            x = jnp.where(far, whole_plane(full_e[r], columns_e, r, s), 0.0)
+            deep_e[p + 1] = x
+            e[p + 1] = fold_rows(x)
+            for k in range(4):
+                x = whole_plane(full[k, r], columns, k * pairs + r, s)
+                force[k, p] = jnp.where(near, x, 0.0)
 
     def shifts(x):
         return (
             roll(x, LANES - 1, 1),
             roll(x, 1, 1),
-            roll(x, rows - 1, 0),
+            roll(x, x.shape[0] - 1, 0),
             roll(x, 1, 0),
         )
 
-    for p in range(planes + 1):
-        w0[p] = e[p] + e[p + 1]
-
-    def start(p, carry):
-        x = e[p]
-        total = w0[p] + w0[p - 1]
+    def two_by_two(width, body):
+        lo = jnp.maximum(gx * own - width, 0)
+        hi = jnp.minimum(gx * own + own + width, planes)
+        steps = (hi - lo + 1) // 2
+        lo = jnp.minimum(lo, planes - 2 * steps)
+
+        def step(i, carry):
+            body(lo + 2 * i + 1)
+            body(lo + 2 * i + 2)
+            return carry
+
+        lax.fori_loop(0, steps, step, 0)
+
+    def start(p):
+        x = deep_e[p]
+        up, down = x + deep_e[p + 1], x + deep_e[p - 1]
+        w0[p] = fold_rows(up)
+        total = up + down
         for n, y in enumerate(shifts(x)):
             total += x + y
-            w[1 + n][p] = x + y
-        factor = jnp.where(inside, relax_weight / total, 0.0)
+            w[1 + n][p] = fold_rows(x + y)
+        factor = jnp.where(near, fold_rows(relax_weight / total), 0.0)
         w5[p] = factor
         for k in range(3):
             ca[k, p] = factor * force[k, p - 1]
-        ca[3, p] = x * force[3, p - 1]
-        return carry
-
-    lax.fori_loop(1, planes + 1, start, 0)
-
-    def sweep(src, dst):
-        def body(p, carry):
+        ca[3, p] = e[p] * force[3, p - 1]
+
+    w0[0] = e[0] + e[1]
+    two_by_two(planes, start)
+
+    def sweep(src, dst, width):
+        def body(p):
             wxp, wxm = w0[p], w0[p - 1]
             wyp, wym, wzp, wzm = w1[p], w2[p], w3[p], w4[p]
             x = src[3, p]
@@ -743,60 +848,52 @@
                 total += wyp * yp + wym * ym
                 total += wzp * zp + wzm * zm
                 spread += terms(k, xp, xm, yp, ym, zp, zm)
-                dst[k, p] = jnp.where(inside, 0.4 * u + w5[p] * total, 0.0)
-            dst[3, p] = jnp.where(inside, x + e[p] * (force[3, p - 1] - 0.125 * spread), 0.0)
-            return carry
-
-        lax.fori_loop(1, planes + 1, body, 0)
-
-    sweep(ca, cb)
-    sweep(cb, ca)
-    sweep(ca, cb)
-
-    cz = rows - 16
-    spread_lanes = (iota((LANES, LANES), 1) // 2 == iota((LANES, LANES), 0)).astype(F32)
-    lane = iota((LANES, LANES), 1)
-    cell = iota((LANES, LANES), 0)
+                dst[k, p] = jnp.where(near, 0.4 * u + w5[p] * total, 0.0)
+            dst[3, p] = jnp.where(near, x + e[p] * (force[3, p - 1] - 0.125 * spread), 0.0)
+
+        two_by_two(width, body)
+
+    sweep(ca, cb, 3)
+    sweep(cb, ca, 2)
+    sweep(ca, cb, 1)
+
+    lane = iota((LANES, 2 * LANES), 1)
+    cell = iota((LANES, 2 * LANES), 0)
     spot = lane % SLOT
     wanted = jnp.where(spot < 4, LANES - 2, half - 2) + spot // 2
+    slot = (lane - LANES) // SLOT
     column = jnp.zeros((4 * rows, LANES), F32)
-    first = lax.axis_index("gx") * own
+    first = gx * own
 
     def grow(ref, index, x):
         ref[index + (pl.ds(0, cz, stride=2),)] = x[:cz]
         ref[index + (pl.ds(1, cz, stride=2),)] = x[:cz]
-        edge = jnp.concatenate([x[cz : cz + 8], x[rows - 8 :]], axis=0)
-        grown[pl.ds(0, 16, stride=2)] = edge
-        grown[pl.ds(1, 16, stride=2)] = edge
+        grown[pl.ds(0, 8, stride=2)] = x[cz:]
+        grown[pl.ds(1, 8, stride=2)] = x[cz:]
         r = iota((8, LANES), 0)
-        tail = jnp.where(r < 4, grown[pl.ds(0, 8)], grown[pl.ds(24, 8)])
+        tail = jnp.where(r < 4, grown[pl.ds(0, 8)], grown[pl.ds(8, 8)])
         ref[index + (pl.ds(2 * cz, 8),)] = tail
 
     for i in range(own + 2):
         x = jnp.concatenate([cb[k, first + i] for k in range(4)], axis=0)
-        wide = jnp.dot(
-            x, spread_lanes, precision=lax.Precision.HIGHEST, preferred_element_type=F32
-        )
+        here = (lane >= LANES) & ((slot + 1) // 2 - 1 == i) & (cell == wanted)
+        chosen = (here | ((lane < LANES) & (lane // 2 == cell))).astype(F32)
+        wide = jnp.dot(x, chosen, precision=lax.Precision.HIGHEST, preferred_element_type=F32)
         for k in range(4):
-            grow(main, (k, i), wide[k * rows : (k + 1) * rows])
-        here = (lane // SLOT + 1) // 2 - 1 == i
-        chosen = (here & (cell == wanted)).astype(F32)
-        column += jnp.dot(
-            x, chosen, precision=lax.Precision.HIGHEST, preferred_element_type=F32
-        )
+            grow(main, (k, i), wide[k * rows : (k + 1) * rows, :LANES])
+        column += wide[:, LANES:]
     for k in range(4):
         grow(halo, (k,), column[k * rows : (k + 1) * rows])
 
 
 def post_smooth(
-    e_in, f_in, z_first, halo_first, x_main, x_first, fields, z_halo, halo_full, x_fine, x_rim,
-    main, column, v_out, p_out,
-    ua, ub, ha, hb, ca, cb, e, halo_e, edge_e, force, halo_f, w0, w1, w2, w3, w4, w5, hw, beside,
+    e, halo_e, force, halo_f, w0, w1, w2, w3, w4, w5, hw,
+    fields, z_halo, halo_full, x_fine, x_rim, main, column, v_out, p_out,
+    ua, ub, ha, hb, ca, cb, beside,
 ):
-    nx, nz, _ = e_in.shape
+    nx, nz, _ = p_out.shape
     slots = nx + 6
     w = (w0, w1, w2, w3, w4, w5)
-    viscosity_force(e_in, f_in, z_first, halo_first, x_main, x_first, e, halo_e, force, halo_f)
     zero = jnp.zeros((nz + 8, LANES), F32)
     for k in range(4):
         for p in (1, 2, nx + 3, nx + 4):
@@ -812,14 +909,14 @@
         there = truth(valid, (nz, LANES))
         there8 = truth(valid, (8, LANES))
         tiles = (nz + 8) // 8
-        side = jnp.concatenate([x_rim[m, 4 + r] for r in range(tiles)], axis=0)
+        side = jnp.concatenate([x_rim[m, 1 + r] for r in range(tiles)], axis=0)
         i = right * (nx // 2 + 1)
         for k in range(4):
             for j in range(2):
                 at = 1 + right * (nx + 2) + j
                 x = x_fine[m, 2 * k + j] + main[k, i, pl.ds(0, nz)]
                 ua[k, at, pl.ds(0, nz)] = jnp.where(there, x, 0.0)
-            x = x_rim[m, k] + main[k, i, pl.ds(nz, 8)]
+            x = roll(x_rim[m, 0], -2 * k, 0) + main[k, i, pl.ds(nz, 8)]
             ua[k, 2 + right * (nx + 1), pl.ds(nz, 8)] = jnp.where(there8, x, 0.0)
             x, kept = rim_halo(side, k, SLOT, 1, right, valid, nx)
             ha[k] = jnp.where(kept, x, ha[k])
@@ -827,19 +924,17 @@
     for k in range(4):
         ha[k] = jnp.where(masks[1], ha[k] + column[k], 0.0)
     fill_edges(ca, ua, 4, 1, slots - 1)
-    edge_e[...] = edges_of(lambda p: e[p], 1, slots - 1)
-    main_weights(e, halo_e, w, 1)
-    halo_weights(halo_e, edge_e, hw)
     rest = (w, hw, e, halo_e, force, halo_f)
     fine_sweep(ua, ha, ca, ub, hb, None, *rest, 1, masks, beside)
 
     spread_halo(hb, beside, slots, 0)
 
     def last(p):
-        new = relaxed(*main_operator(ub, beside, w, force, p), w5[p], e[p])
+        new = main_operator(ub, beside, w, force, p, nz)
+        new = relaxed(*new, w5[p, pl.ds(0, nz)], e[p, pl.ds(0, nz)])
         for k in range(3):
-            v_out[k, p - 3] = new[k][:nz]
-        p_out[p - 3] = new[3][:nz]
+            v_out[k, p - 3] = new[k]
+        p_out[p - 3] = new[3]
 
     over_planes(slots, 0, last)
 
@@ -853,7 +948,7 @@
     inputs = [velocity, pressure, viscosity, body_force]
     block = (nz, LANES)
 
-    z_shape = (4 * nx, 8, LANES)
+    z_shape = (3 * nx, 8, LANES)
     x_main, y_a, y_b, z_a, z_b = call(
         first_pack,
         [(sides, 21) + block, (2,) + block, (2,) + block, z_shape, z_shape],
@@ -864,28 +959,27 @@
     )
     x_main = swap_x(x_main)
     y_a, y_b = swap(y_a, "gy", 0), swap(y_b, "gy", 1)
-    z_shape = (4 * nx + 2, 8, LANES)
-    halo, z_a, z_b = call(
-        second_pack, [(4,) + block, z_shape, z_shape], [z_a, z_b, y_a, y_b]
-    )
+    halo, z_b = call(second_pack, [(4,) + block, z_shape], [z_b, y_a, y_b])
+    (z_a,) = call(second_pack_near, [z_shape], [z_a, halo])
     z_a, z_b = swap(z_a, "gz", 0), swap(z_b, "gz", 1)
     tiles = rows // 8
     z_first, halo_first, x_first = call(
         third_pack,
-        [(8, nx, 8, LANES), (4, rows, LANES), (sides, 13 + 2 * tiles, 8, LANES)],
+        [(8, nx, 8, LANES), (4, rows, LANES), (sides, 6 + tiles, 8, LANES)],
         [z_a, z_b, halo],
     )
     x_first = swap_x(x_first)
 
     state = [(4, slots, rows, LANES)] * 2 + [(4, rows, LANES)] * 4
-    state += [(slots, rows, LANES), (rows, LANES), (rows, LANES)]
-    state += [(3, slots, rows, LANES), (3, rows, LANES)]
-    state += [(slots, rows, LANES)] * 6 + [(7, rows, LANES), (4, slots, rows, LANES)]
-    fields, own, edges, x_fine = call(
+    spread = (4, slots, rows, LANES)
+    operator = [(slots, rows, LANES), (rows, LANES), (3, slots, rows, LANES), (3, rows, LANES)]
+    operator += [(slots, rows, LANES)] * 6 + [(7, rows, LANES)]
+    fields, own, edges, x_fine, *operator = call(
         pre_smooth,
-        [(4, nx) + block, (5, nx // 4, nz // 2, LANES), (2,) + block, (sides, 8) + block],
+        [(4, nx) + block, (5, nx // 4, nz // 2, LANES), (2,) + block, (sides, 8) + block]
+        + operator,
         inputs + [z_first, halo_first, x_main, x_first],
-        state + [(5, nx // 2, nz, LANES)],
+        state + [(rows, LANES), spread, (5, nx // 2, nz, LANES)],
         cost=8,
     )
     if lax.axis_size("gx") == 2:
@@ -899,43 +993,43 @@
 
     x_fine = swap_x(x_fine)
     pairs = lax.axis_size("gx") * (nx // 4)
-    z_shape = (5 * pairs + nx, 8, LANES)
+    z_shape = (3 * pairs + nx, 8, LANES)
     whole, z_a, z_b = call(
         gather, [(5, pairs, nz // 2, LANES), z_shape, z_shape], parts + [fields]
     )
     z_a, z_b = swap(z_a, "gz", 0), swap(z_b, "gz", 1)
     deep = nz // 2 + 16
-    y_shape = (-(-10 * pairs * SLOT // LANES) * (deep // 8) + tiles, 8, LANES)
-    full, z_halo, y_a, y_b = call(
+    shallow = deep - 8
+    y_shape = (pairs // 2 * (shallow // 8) + -(-pairs // 4) * (deep // 8) + tiles, 8, LANES)
+    full, full_e, z_halo, y_a, y_b = call(
         fifth_pack,
-        [(5, pairs, deep, LANES), (4, nx, 8, LANES), y_shape, y_shape],
+        [(4, pairs, shallow, LANES), (pairs, deep, LANES), (4, nx, 8, LANES), y_shape, y_shape],
         [whole, z_a, z_b, edges],
     )
     y_a, y_b = swap(y_a, "gy", 0), swap(y_b, "gy", 1)
     halo_full, x_rim = call(
         sixth_pack,
-        [(2, rows, LANES), (sides, 4 + tiles, 8, LANES)],
+        [(2, rows, LANES), (sides, 1 + tiles, 8, LANES)],
         [y_a, y_b, z_halo],
     )
     x_rim = swap_x(x_rim)
     planes = 2 * pairs
-    deep_plane = (deep, LANES)
+    plane = (shallow, LANES)
     main, column = call(
         coarse_solve,
         [(4, nx // 2 + 2, rows, LANES), (4, rows, LANES)],
-        [full, y_a, y_b],
-        [(4, planes + 2) + deep_plane] * 2
-        + [(4, planes) + deep_plane]
-        + [(planes + 2,) + deep_plane] * 7
-        + [(32, LANES)],
+        [full, full_e, y_a, y_b],
+        [(4, planes + 2) + plane] * 2
+        + [(4, planes) + plane]
+        + [(planes + 2,) + plane] * 7
+        + [(planes + 2, deep, LANES), (16, LANES)],
         cost=4,
     )
     v_out, p_out = call(
         post_smooth,
         [(3, nx) + block, (nx,) + block],
-        inputs[2:] + [z_first, halo_first, x_main, x_first]
-        + [fields, z_halo, halo_full, x_fine, x_rim, main, column],
-        state,
+        operator + [fields, z_halo, halo_full, x_fine, x_rim, main, column],
+        state + [spread],
         cost=8,
     )
     return v_out, p_out

time: 49.5 us -> 45.8 us (0.925)
  Pallas kernels: 16.2 us -> 13.8 us
  waiting for transfers between devices: 17.9 us -> 16.9 us
    pallas_call x9 -> x10, Pallas kernels: 16.2 us -> 13.8 us  [call(): pl.pallas_call(body, out_shape=[jax.ShapeDtypeStruct(shape, F32) for shap...]
    ppermute x4, waiting for transfers between devices: 5.18 us -> 4.4 us  [swap(): return lax.ppermute(array, ('gy', 'gz'), pairs)]
  transfers between devices with their start and end apart: 13 -> 13, of which waited for: 6 -> 7; matrix products, arithmetic and copies ran while one was open for 0% -> 0% of each run, Pallas kernels for 11% -> 8%
where the time goes in v3:
time: 45.8 us; the launch traced here: 45.7 us
  waiting for transfers between devices  16.9 us (37%)
  starting transfers between devices  14.2 us (31%)
  Pallas kernels  13.8 us (30%)
  between operations  0.76 us (2%)
    pallas_call x10, Pallas kernels, call(): pl.pallas_call(body, out_shape=[jax.ShapeDtypeStruct(shape, F32) for shap...  13.8 us
    ppermute x9, waiting for transfers between devices, swap(): return lax.ppermute(array, axis, pairs)  12.5 us
    ppermute x9, starting transfers between devices, swap(): return lax.ppermute(array, axis, pairs)  9.37 us
    ppermute x4, starting transfers between devices, swap(): return lax.ppermute(array, ('gy', 'gz'), pairs)  4.85 us
    ppermute x4, waiting for transfers between devices, swap(): return lax.ppermute(array, ('gy', 'gz'), pairs)  4.4 us
  transfers between devices with their start and end apart: 13, of which 7 were waited for; matrix products, arithmetic and copies ran while one was open for 0% of the time, Pallas kernels for 8%

profile of v3, /device:TPU:0, one launch (start us, length us, event | category | flops | bytes accessed | tf_op | source)
XLA Modules:
  0.0 45.7 jit_solution(11490976939157778990)
XLA Ops:
  0.6 2.3 %shard_map.59 = (f32[1,21,32,128]{3,2,1,0:T(8,128)}, f32[2,32,128]{2,1,0:T(8,128)S(1)}, f32[2,32,128]{2,1,0:T(8,128)S(1)}, f32[24,8,128]{2,1,0:T(8,128)S(1)}, f32[24,8,128]{2,1,0:T(8,128)S(1)}) custom-call(f32[3,8,32,128]{3,2,1,0:T(8,128)} %v.1, f32[8,32,128]{2,1,0:T(8,128)} %p_in.3, f32[8,32,128]{2,1,0:T(8,128)} %e_in.3, f32[3,8,32,128]{3,2,1,0:T(8,128)} %f_in.3), custom_call_target="tpu_custom_call" | custom-call | flops 1000000 | bytes 1000000 | tf_op jit(solution)/shard_map/pallas_call | solution.py:21
  3.0 3.0 %collective-permute-start.4 = (f32[1,21,32,128]{3,2,1,0:T(8,128)}, f32[1,21,32,128]{3,2,1,0:T(8,128)S(1)}, u32[]{:S(2)}, u32[]{:S(2)}) collective-permute-start(f32[1,21,32,128]{3,2,1,0:T(8,128)} %get-tuple-element.47), channel_id=1, source_target_pairs={{0,16},{16,0},{1,17},{17,1},{2,18},{18,2},{3,19},{19,3},{4,20},{20... | collective-permute-start | bytes 1032200 | tf_op jit(solution)/shard_map/ppermute | solution.py:56
  6.0 1.6 %collective-permute-start = (f32[2,32,128]{2,1,0:T(8,128)S(1)}, f32[2,32,128]{2,1,0:T(8,128)S(1)}, u32[]{:S(2)}, u32[]{:S(2)}) collective-permute-start(f32[2,32,128]{2,1,0:T(8,128)S(1)} %get-tuple-element.41), channel_id=1, source_target_pairs={{0,4},{4,0},{8,12},{12,8},{1,5},{5,1},{9,13},{13,9},{2,6},{6,2},{1... | collective-permute-start | bytes 98312 | tf_op jit(solution)/shard_map/ppermute | solution.py:56
  7.6 2.3 %collective-permute-done.y_a = f32[2,32,128]{2,1,0:T(8,128)S(1)} collective-permute-done((f32[2,32,128]{2,1,0:T(8,128)S(1)}, f32[2,32,128]{2,1,0:T(8,128)S(1)}, u32[]{:S(2)}, u32[]{:S(2)}) %collective-permute-start) | collective-permute-done | bytes 32800 | tf_op jit(solution)/shard_map/ppermute | solution.py:56
  10.0 0.1 shard_map.60
  10.2 2.8 %collective-permute-start.3 = (f32[24,8,128]{2,1,0:T(8,128)S(1)}, f32[24,8,128]{2,1,0:T(8,128)S(1)}, u32[]{:S(2)}, u32[]{:S(2)}) collective-permute-start(f32[24,8,128]{2,1,0:T(8,128)S(1)} %get-tuple-element.44), channel_id=1, source_target_pairs={{0,4},{1,2},{2,1},{3,7},{4,0},{5,6},{6,5},{7,3},{8,12},{9,10},{10,... | collective-permute-start | bytes 294920 | tf_op jit(solution)/shard_map/ppermute | solution.py:51
  13.0 2.6 %collective-permute-done.3.z_b = f32[24,8,128]{2,1,0:T(8,128)S(1)} collective-permute-done((f32[24,8,128]{2,1,0:T(8,128)S(1)}, f32[24,8,128]{2,1,0:T(8,128)S(1)}, u32[]{:S(2)}, u32[]{:S(2)}) %collective-permute-start.3) | collective-permute-done | bytes 98336 | tf_op jit(solution)/shard_map/ppermute | solution.py:51
  15.6 0.1 shard_map.62
  15.7 0.6 %collective-permute-start.5 = (f32[1,11,8,128]{3,2,1,0:T(8,128)S(1)}, f32[1,11,8,128]{3,2,1,0:T(8,128)S(1)}, u32[]{:S(2)}, u32[]{:S(2)}) collective-permute-start(f32[1,11,8,128]{3,2,1,0:T(8,128)S(1)} %get-tuple-element.48), channel_id=1, source_target_pairs={{0,16},{16,0},{1,17},{17,1},{2,18},{18,2},{3,19},{19,3},{4,20},{20... | collective-permute-start | bytes 135176 | tf_op jit(solution)/shard_map/ppermute | solution.py:56
  16.3 3.5 %collective-permute-done.5.x_rim = f32[1,11,8,128]{3,2,1,0:T(8,128)S(1)} collective-permute-done((f32[1,11,8,128]{3,2,1,0:T(8,128)S(1)}, f32[1,11,8,128]{3,2,1,0:T(8,128)S(1)}, u32[]{:S(2)}, u32[]{:S(2)}) %collective-permute-start.5) | collective-permute-done | bytes 45088 | tf_op jit(solution)/shard_map/ppermute | solution.py:56
  19.8 5.0 %shard_map.63 = (f32[4,8,32,128]{3,2,1,0:T(8,128)S(1)}, f32[5,2,16,128]{3,2,1,0:T(8,128)S(1)}, f32[2,32,128]{2,1,0:T(8,128)S(1)}, f32[1,8,32,128]{3,2,1,0:T(8,12...) custom-call(f32[3,8,32,128]{3,2,1,0:T(8,128)S(1)} %copy-done, ...), custom_call_target="tpu_custom_call" | custom-call | flops 8000000 | bytes 8000000 | tf_op jit(solution)/shard_map/pallas_call | solution.py:21
  24.8 0.7 %collective-permute-start.6 = (f32[5,2,16,128]{3,2,1,0:T(8,128)S(1)}, f32[5,2,16,128]{3,2,1,0:T(8,128)S(1)}, u32[]{:S(2)}, u32[]{:S(2)}) collective-permute-start(f32[5,2,16,128]{3,2,1,0:T(8,128)S(1)} %get-tuple-element.61.own), channel_id=1, source_target_pairs={{0,16},{16,0},{1,17},{17,1},{2,18},{18,2},{3,19},{19,3},{4,20},{20... | collective-permute-start | bytes 245768 | tf_op jit(solution)/shard_map/ppermute | solution.py:56
  25.5 3.8 %collective-permute-done.6.other = f32[5,2,16,128]{3,2,1,0:T(8,128)S(1)} collective-permute-done((f32[5,2,16,128]{3,2,1,0:T(8,128)S(1)}, f32[5,2,16,128]{3,2,1,0:T(8,128)S(1)}, u32[]{:S(2)}, u32[]{:S(2)}) %collective-permute-start.6) | collective-permute-done | bytes 81952 | tf_op jit(solution)/shard_map/ppermute | solution.py:56
  29.5 2.1 %collective-permute-start.8 = (f32[20,8,128]{2,1,0:T(8,128)S(1)}, f32[20,8,128]{2,1,0:T(8,128)S(1)}, u32[]{:S(2)}, u32[]{:S(2)}) collective-permute-start(f32[20,8,128]{2,1,0:T(8,128)S(1)} %get-tuple-element.64), channel_id=1, source_target_pairs={{0,4},{1,2},{2,1},{3,7},{4,0},{5,6},{6,5},{7,3},{8,12},{9,10},{10,... | collective-permute-start | bytes 245768 | tf_op jit(solution)/shard_map/ppermute | solution.py:51
  31.5 0.6 %collective-permute-start.11 = (f32[1,8,32,128]{3,2,1,0:T(8,128)S(1)}, f32[1,8,32,128]{3,2,1,0:T(8,128)S(1)}, u32[]{:S(2)}, u32[]{:S(2)}) collective-permute-start(f32[1,8,32,128]{3,2,1,0:T(8,128)S(1)} %get-tuple-element.70), channel_id=1, source_target_pairs={{0,16},{16,0},{1,17},{17,1},{2,18},{18,2},{3,19},{19,3},{4,20},{20... | collective-permute-start | bytes 393224 | tf_op jit(solution)/shard_map/ppermute | solution.py:56
  32.2 1.8 %collective-permute-done.8.z_b = f32[20,8,128]{2,1,0:T(8,128)S(1)} collective-permute-done((f32[20,8,128]{2,1,0:T(8,128)S(1)}, f32[20,8,128]{2,1,0:T(8,128)S(1)}, u32[]{:S(2)}, u32[]{:S(2)}) %collective-permute-start.8) | collective-permute-done | bytes 81952 | tf_op jit(solution)/shard_map/ppermute | solution.py:51
  34.0 0.3 shard_map.65
  34.3 2.1 %collective-permute-start.9 = (f32[15,8,128]{2,1,0:T(8,128)S(1)}, f32[15,8,128]{2,1,0:T(8,128)S(1)}, u32[]{:S(2)}, u32[]{:S(2)}) collective-permute-start(f32[15,8,128]{2,1,0:T(8,128)S(1)} %get-tuple-element.67), channel_id=1, source_target_pairs={{0,4},{4,0},{8,12},{12,8},{1,5},{5,1},{9,13},{13,9},{2,6},{6,2},{1... | collective-permute-start | bytes 184328 | tf_op jit(solution)/shard_map/ppermute | solution.py:56
  36.4 2.3 %collective-permute-done.9.y_a = f32[15,8,128]{2,1,0:T(8,128)S(1)} collective-permute-done((f32[15,8,128]{2,1,0:T(8,128)S(1)}, f32[15,8,128]{2,1,0:T(8,128)S(1)}, u32[]{:S(2)}, u32[]{:S(2)}) %collective-permute-start.9) | collective-permute-done | bytes 61472 | tf_op jit(solution)/shard_map/ppermute | solution.py:56
  38.7 0.2 shard_map.66
  38.9 0.7 %collective-permute-start.12 = (f32[1,6,8,128]{3,2,1,0:T(8,128)S(1)}, f32[1,6,8,128]{3,2,1,0:T(8,128)S(1)}, u32[]{:S(2)}, u32[]{:S(2)}) collective-permute-start(f32[1,6,8,128]{3,2,1,0:T(8,128)S(1)} %get-tuple-element.71), channel_id=1, source_target_pairs={{0,16},{16,0},{1,17},{17,1},{2,18},{18,2},{3,19},{19,3},{4,20},{20... | collective-permute-start | bytes 73736 | tf_op jit(solution)/shard_map/ppermute | solution.py:56
  39.5 2.8 %shard_map.67 = (f32[4,6,40,128]{3,2,1,0:T(8,128)S(1)}, f32[4,40,128]{2,1,0:T(8,128)S(1)}) custom-call(f32[4,4,24,128]{3,2,1,0:T(8,128)S(1)} %get-tuple-element.72.full, f32[4,32,128]{2,1,0:T(8,128)S(1)} %get-tuple-element.73.full_e, f32[15,8,128]{2,1,0:T(8,128)S(1)} %collective-permute-done.9.y_a, f32[15,8,128]{2,1,0:T(8,128)S(1)} %collective-permute-done.10.y_b), custom_call_target="tpu_custom_call" | custom-call | flops 4000000 | bytes 4000000 | tf_op jit(solution)/shard_map/pallas_call | solution.py:21
  42.3 0.4 collective-permute-done.12.x_rim
  42.7 2.9 %shard_map.68 = (f32[3,8,32,128]{3,2,1,0:T(8,128)}, f32[8,32,128]{2,1,0:T(8,128)}) custom-call(f32[14,40,128]{2,1,0:T(8,128)S(1)} %get-tuple-element.49.e, f32[40,128]{1,0:T(8,128)S(1)} %get-tuple-element.50.halo_e, f32[3,14,40,128]{3,2,1,0:T(8,128)S(1)} %get-tuple-element.51.force, f32[3,40,128]{2,1,0:T(8,128)S(1)} %get-tuple-element.52.halo_f, ...), custom_call_target="tpu_custom_call" | custom-call | flops 8000000 | bytes 8000000 | tf_op jit(solution)/shard_map/pallas_call | solution.py:21
  (20 shorter events, 0.3 us)
Async XLA Ops:
  0.6 19.2 %copy-start.1 = (f32[3,8,32,128]{3,2,1,0:T(8,128)S(1)}, f32[3,8,32,128]{3,2,1,0:T(8,128)}, u32[]{:S(2)}) copy-start(f32[3,8,32,128]{3,2,1,0:T(8,128)} %f_in.3) | copy-start | bytes 1179652
  3.0 16.8 %copy-start = (f32[3,8,32,128]{3,2,1,0:T(8,128)S(1)}, f32[3,8,32,128]{3,2,1,0:T(8,128)}, u32[]{:S(2)}) copy-start(f32[3,8,32,128]{3,2,1,0:T(8,128)} %v.1) | copy-start | bytes 1179652
  3.0 16.8 %collective-permute-start.4 = (f32[1,21,32,128]{3,2,1,0:T(8,128)}, f32[1,21,32,128]{3,2,1,0:T(8,128)S(1)}, u32[]{:S(2)}, u32[]{:S(2)}) collective-permute-start(f32[1,21,32,128]{3,2,1,0:T(8,128)} %get-tuple-element.47), channel_id=1, source_target_pairs={{0,16},{16,0},{1,17},{17,1},{2,18},{18,2},{3,19},{19,3},{4,20},{20... | collective-permute-start | bytes 1032200 | tf_op jit(solution)/shard_map/ppermute | solution.py:56
  6.0 3.9 %collective-permute-start = (f32[2,32,128]{2,1,0:T(8,128)S(1)}, f32[2,32,128]{2,1,0:T(8,128)S(1)}, u32[]{:S(2)}, u32[]{:S(2)}) collective-permute-start(f32[2,32,128]{2,1,0:T(8,128)S(1)} %get-tuple-element.41), channel_id=1, source_target_pairs={{0,4},{4,0},{8,12},{12,8},{1,5},{5,1},{9,13},{13,9},{2,6},{6,2},{1... | collective-permute-start | bytes 98312 | tf_op jit(solution)/shard_map/ppermute | solution.py:56
  7.6 2.3 %collective-permute-start.1 = (f32[2,32,128]{2,1,0:T(8,128)S(1)}, f32[2,32,128]{2,1,0:T(8,128)S(1)}, u32[]{:S(2)}, u32[]{:S(2)}) collective-permute-start(f32[2,32,128]{2,1,0:T(8,128)S(1)} %get-tuple-element.42), channel_id=1, source_target_pairs={{0,1},{1,0},{2,3},{3,2},{4,8},{5,9},{6,10},{7,11},{8,4},{9,5},{10,... | collective-permute-start | bytes 98312 | tf_op jit(solution)/shard_map/ppermute | solution.py:51
  10.1 2.9 %collective-permute-start.2 = (f32[24,8,128]{2,1,0:T(8,128)S(1)}, f32[24,8,128]{2,1,0:T(8,128)S(1)}, u32[]{:S(2)}, u32[]{:S(2)}) collective-permute-start(f32[24,8,128]{2,1,0:T(8,128)S(1)} %shard_map.61), channel_id=1, source_target_pairs={{0,1},{1,0},{2,3},{3,2},{4,5},{5,4},{6,7},{7,6},{8,9},{9,8},{10,11... | collective-permute-start | bytes 294920 | tf_op jit(solution)/shard_map/ppermute | solution.py:56
  10.2 9.7 %copy-start.2 = (f32[8,32,128]{2,1,0:T(8,128)S(1)}, f32[8,32,128]{2,1,0:T(8,128)}, u32[]{:S(2)}) copy-start(f32[8,32,128]{2,1,0:T(8,128)} %p_in.3) | copy-start | bytes 393220
  10.2 9.7 %copy-start.3 = (f32[8,32,128]{2,1,0:T(8,128)S(1)}, f32[8,32,128]{2,1,0:T(8,128)}, u32[]{:S(2)}) copy-start(f32[8,32,128]{2,1,0:T(8,128)} %e_in.3) | copy-start | bytes 393220
  10.2 5.4 %collective-permute-start.3 = (f32[24,8,128]{2,1,0:T(8,128)S(1)}, f32[24,8,128]{2,1,0:T(8,128)S(1)}, u32[]{:S(2)}, u32[]{:S(2)}) collective-permute-start(f32[24,8,128]{2,1,0:T(8,128)S(1)} %get-tuple-element.44), channel_id=1, source_target_pairs={{0,4},{1,2},{2,1},{3,7},{4,0},{5,6},{6,5},{7,3},{8,12},{9,10},{10,... | collective-permute-start | bytes 294920 | tf_op jit(solution)/shard_map/ppermute | solution.py:51
  15.7 4.1 %collective-permute-start.5 = (f32[1,11,8,128]{3,2,1,0:T(8,128)S(1)}, f32[1,11,8,128]{3,2,1,0:T(8,128)S(1)}, u32[]{:S(2)}, u32[]{:S(2)}) collective-permute-start(f32[1,11,8,128]{3,2,1,0:T(8,128)S(1)} %get-tuple-element.48), channel_id=1, source_target_pairs={{0,16},{16,0},{1,17},{17,1},{2,18},{18,2},{3,19},{19,3},{4,20},{20... | collective-permute-start | bytes 135176 | tf_op jit(solution)/shard_map/ppermute | solution.py:56
  24.8 4.5 %collective-permute-start.6 = (f32[5,2,16,128]{3,2,1,0:T(8,128)S(1)}, f32[5,2,16,128]{3,2,1,0:T(8,128)S(1)}, u32[]{:S(2)}, u32[]{:S(2)}) collective-permute-start(f32[5,2,16,128]{3,2,1,0:T(8,128)S(1)} %get-tuple-element.61.own), channel_id=1, source_target_pairs={{0,16},{16,0},{1,17},{17,1},{2,18},{18,2},{3,19},{19,3},{4,20},{20... | collective-permute-start | bytes 245768 | tf_op jit(solution)/shard_map/ppermute | solution.py:56
  29.4 2.8 %collective-permute-start.7 = (f32[20,8,128]{2,1,0:T(8,128)S(1)}, f32[20,8,128]{2,1,0:T(8,128)S(1)}, u32[]{:S(2)}, u32[]{:S(2)}) collective-permute-start(f32[20,8,128]{2,1,0:T(8,128)S(1)} %get-tuple-element.63), channel_id=1, source_target_pairs={{0,1},{1,0},{2,3},{3,2},{4,5},{5,4},{6,7},{7,6},{8,9},{9,8},{10,11... | collective-permute-start | bytes 245768 | tf_op jit(solution)/shard_map/ppermute | solution.py:56
  29.5 4.5 %collective-permute-start.8 = (f32[20,8,128]{2,1,0:T(8,128)S(1)}, f32[20,8,128]{2,1,0:T(8,128)S(1)}, u32[]{:S(2)}, u32[]{:S(2)}) collective-permute-start(f32[20,8,128]{2,1,0:T(8,128)S(1)} %get-tuple-element.64), channel_id=1, source_target_pairs={{0,4},{1,2},{2,1},{3,7},{4,0},{5,6},{6,5},{7,3},{8,12},{9,10},{10,... | collective-permute-start | bytes 245768 | tf_op jit(solution)/shard_map/ppermute | solution.py:51
  31.5 10.8 %collective-permute-start.11 = (f32[1,8,32,128]{3,2,1,0:T(8,128)S(1)}, f32[1,8,32,128]{3,2,1,0:T(8,128)S(1)}, u32[]{:S(2)}, u32[]{:S(2)}) collective-permute-start(f32[1,8,32,128]{3,2,1,0:T(8,128)S(1)} %get-tuple-element.70), channel_id=1, source_target_pairs={{0,16},{16,0},{1,17},{17,1},{2,18},{18,2},{3,19},{19,3},{4,20},{20... | collective-permute-start | bytes 393224 | tf_op jit(solution)/shard_map/ppermute | solution.py:56
  34.3 4.4 %collective-permute-start.9 = (f32[15,8,128]{2,1,0:T(8,128)S(1)}, f32[15,8,128]{2,1,0:T(8,128)S(1)}, u32[]{:S(2)}, u32[]{:S(2)}) collective-permute-start(f32[15,8,128]{2,1,0:T(8,128)S(1)} %get-tuple-element.67), channel_id=1, source_target_pairs={{0,4},{4,0},{8,12},{12,8},{1,5},{5,1},{9,13},{13,9},{2,6},{6,2},{1... | collective-permute-start | bytes 184328 | tf_op jit(solution)/shard_map/ppermute | solution.py:56
  36.4 2.3 %collective-permute-start.10 = (f32[15,8,128]{2,1,0:T(8,128)S(1)}, f32[15,8,128]{2,1,0:T(8,128)S(1)}, u32[]{:S(2)}, u32[]{:S(2)}) collective-permute-start(f32[15,8,128]{2,1,0:T(8,128)S(1)} %get-tuple-element.68), channel_id=1, source_target_pairs={{0,1},{1,0},{2,3},{3,2},{4,8},{5,9},{6,10},{7,11},{8,4},{9,5},{10,... | collective-permute-start | bytes 184328 | tf_op jit(solution)/shard_map/ppermute | solution.py:51
  38.9 3.9 %collective-permute-start.12 = (f32[1,6,8,128]{3,2,1,0:T(8,128)S(1)}, f32[1,6,8,128]{3,2,1,0:T(8,128)S(1)}, u32[]{:S(2)}, u32[]{:S(2)}) collective-permute-start(f32[1,6,8,128]{3,2,1,0:T(8,128)S(1)} %get-tuple-element.71), channel_id=1, source_target_pairs={{0,16},{16,0},{1,17},{17,1},{2,18},{18,2},{3,19},{19,3},{4,20},{20... | collective-permute-start | bytes 73736 | tf_op jit(solution)/shard_map/ppermute | solution.py:56

commit v4 on v3

--- a/solution.py
+++ b/solution.py
@@ -9,7 +9,7 @@
 SLOT = 8
 F32 = jnp.float32
 relax_weight = 0.6
-HELD = 429 * 2**17
+HELD = 846 * 2**16
 Z_PLACES = (
     ((0, 0, 3), (1, 3, 3), (5, 6, 2)),
     ((2, 0, 3), (3, 3, 3), (6, 6, 2)),
@@ -17,16 +17,16 @@
 )
 
 
-def call(body, outs, args, scratch=(), cost=1, outside=0, copies=0):
+def call(body, outs, args, scratch=(), cost=1, outside=0, copies=0, aliases=None):
     return pl.pallas_call(
         body,
         out_shape=[jax.ShapeDtypeStruct(shape, F32) for shape in outs],
         in_specs=[pl.BlockSpec(memory_space=pltpu.HBM)] * outside
         + [pl.BlockSpec(memory_space=pltpu.VMEM)] * (len(args) - outside),
-        out_specs=[pl.BlockSpec(memory_space=pltpu.HBM)] * (outside > 0)
-        + [pl.BlockSpec(memory_space=pltpu.VMEM)] * (len(outs) - (outside > 0)),
+        out_specs=[pl.BlockSpec(memory_space=pltpu.VMEM)] * len(outs),
         scratch_shapes=[pltpu.VMEM(shape, F32) for shape in scratch]
         + [pltpu.SemaphoreType.DMA((copies,))] * (copies > 0),
+        input_output_aliases=aliases or {},
         compiler_params=pltpu.CompilerParams(vmem_limit_bytes=HELD if outside else 40 * 2**20),
         cost_estimate=pl.CostEstimate(
             flops=cost * 10**6, bytes_accessed=cost * 10**6, transcendentals=0
@@ -114,61 +114,61 @@
     return jnp.where(kept, first, 0.0), jnp.where(kept, second, 0.0)
 
 
-def first_pack(v_in, p_in, e_in, f_in, x_main, y_a, y_b, z_a, z_b, v, p, e, f, arrived):
-    nx, nz, _ = p.shape
-    loads = [
-        pltpu.make_async_copy(a, b, arrived.at[i])
-        for i, (a, b) in enumerate(((v_in, v), (p_in, p), (e_in, e), (f_in, f)))
-    ]
+class Staged:
+    def __init__(self, refs):
+        self.refs = refs
+        self.half, self.nz = refs[0].shape[:2]
+        self.nx = 2 * self.half
+
+    def __getitem__(self, index):
+        i, q = index[:2]
+        return self.refs[2 * i + q // self.half][(q % self.half,) + index[2:]]
+
+
+def first_pack(v_in, p_in, e_in, f_in, *refs):
+    staged = Staged(refs[:16])
+    y_a, y_b, arrived = refs[16:]
+    nx, nz = staged.nx, staged.nz
+    loads = []
+    for n in range(16):
+        i, planes = n // 2, pl.ds(n % 2 * staged.half, staged.half)
+        if i < 3:
+            part = v_in.at[i, planes]
+        elif i < 5:
+            part = (p_in, e_in)[i - 3].at[planes]
+        else:
+            part = f_in.at[i - 5, planes]
+        loads.append(pltpu.make_async_copy(part, refs[n], arrived.at[n]))
     for load in loads:
         load.start()
-    sends = []
+    for load in loads:
+        load.wait()
+    edges = pair_edges(lambda i: [staged[i, q] for q in range(nx)], 8, nz)
+    for m, out in enumerate((y_a, y_b)):
+        for j in range(2):
+            out[j] = y_strip(edges[j], edges[j + 2], high_side("gy", m))
+
+
+def side_pack(*refs):
+    staged = Staged(refs[:16])
+    x_main, z_a, z_b = refs[16:]
+    nx, nz = staged.nx, staged.nz
     for m in range(x_main.shape[0]):
-        high = high_side("gx", m)
+        top = truth(high_side("gx", m), (nz, LANES))
         n = 0
         for i in range(8):
             width = 3 if i < 5 else 2
-            at = pl.ds(high * (nx - width), width)
-            if i < 3:
-                planes = v.at[i, at]
-            elif i < 5:
-                planes = (p, e)[i - 3].at[at]
-            else:
-                planes = f.at[i - 5, at]
-            sends.append(
-                pltpu.make_async_copy(
-                    planes, x_main.at[m, pl.ds(n, width)], arrived.at[4 + 8 * m + i]
-                )
-            )
-            n += width
-    for load in loads:
-        load.wait()
-    for send in sends:
-        send.start()
-
-    def plane(i, q):
-        return v[i, q] if i < 3 else p[q] if i == 3 else e[q] if i == 4 else f[i - 5, q]
-
-    edges = pair_edges(lambda i: [plane(i, q) for q in range(nx)], 8, nz)
-    for m, out in enumerate((y_a, y_b)):
-        for j in range(2):
-            out[j] = y_strip(edges[j], edges[j + 2], high_side("gy", m))
-
-    def tile(i, q, top):
-        at = pl.ds(nz - 8, 8) if top else pl.ds(0, 8)
-        if i < 3:
-            return v[i, q, at]
-        return p[q, at] if i == 3 else e[q, at] if i == 4 else f[i - 5, q, at]
-
+            for j in range(width):
+                x_main[m, n] = jnp.where(top, staged[i, nx - width + j], staged[i, j])
+                n += 1
+    low, high = pl.ds(0, 8), pl.ds(nz - 8, 8)
     for q in range(nx):
         for n, fields in enumerate(Z_PLACES):
             for m, out in enumerate((z_a, z_b)):
                 out[3 * q + n] = z_strip(
-                    [(tile(i, q, False), tile(i, q, True), at, rows) for i, at, rows in fields],
+                    [(staged[i, q, low], staged[i, q, high], at, rows) for i, at, rows in fields],
                     high_side("gz", m),
                 )
-    for send in sends:
-        send.wait()
 
 
 def strip(first, second, toward_right, width):
@@ -300,9 +300,9 @@
     )
 
 
-def main_weights(e, halo_e, w, width):
+def main_weights(e, halo_e, w, width, chosen, faces):
     slots = e.shape[0]
-    for p in range(2 - width, slots - 3 + width):
+    for p in faces:
         w[0][p] = e[p] + e[p + 1]
 
     def body(p):
@@ -313,7 +313,7 @@
             w[1 + n][p] = x + y
         w[5][p] = relax_weight / total
 
-    over_planes(slots, width, body)
+    over_planes(slots, width, body, chosen)
 
 
 def halo_weights(e, edge_e, w):
@@ -329,14 +329,14 @@
     return (up - down, zp - zm, yp - ym)[k]
 
 
-def spread_halo(halo, beside, slots, width):
-    kept = beside.shape[2] - (0 if width else 8)
+def spread_halo(halo, beside, slots, width, chosen=None, full=True):
+    kept = beside.shape[2] - (0 if full else 8)
 
     def body(p):
         for k in range(4):
             beside[k, p, pl.ds(0, kept)] = roll(halo[k][:kept], LANES - SLOT * p - 4, 1)
 
-    over_planes(slots, width, body)
+    over_planes(slots, width, body, chosen)
 
 
 def main_operator(src, beside, w, force, p, kept):
@@ -385,18 +385,18 @@
     return new + [olds[3] - 0.25 * e * spread]
 
 
-def edges_of(plane, lo, hi):
-    first = plane(lo)
-    slot = iota(first.shape, 1) // SLOT
-    total = jnp.zeros(first.shape, F32)
-    for p in range(lo, hi):
+def edges_of(plane, slots, total=None):
+    shape = plane(slots[0]).shape
+    slot = iota(shape, 1) // SLOT
+    total = jnp.zeros(shape, F32) if total is None else total
+    for p in slots:
         total = jnp.where(slot == p, roll(plane(p), p * SLOT + 4, 1), total)
     return total
 
 
-def fill_edges(edge, src, fields, lo, hi):
-    for k in range(fields):
-        edge[k] = edges_of(lambda p: src[k, p], lo, hi)
+def fill_edges(edge, src, slots, fresh=True):
+    for k in range(4):
+        edge[k] = edges_of(lambda p: src[k, p], slots, None if fresh else edge[k])
 
 
 def fine_masks(rows, slots):
@@ -415,9 +415,9 @@
     return tile, column
 
 
-def fine_sweep(src, halo, edge, dst, halo_dst, edge_dst, w, hw, e, halo_e, force, halo_f, width, masks, beside):
-    tile, column = masks
+def main_sweep(src, halo, dst, w, e, force, width, tile, beside, chosen=None):
     nz = src.shape[2] - 8
+    slots = src.shape[1]
 
     def body(p):
         new = relaxed(*main_operator(src, beside, w, force, p, nz + 8), w[5][p], e[p])
@@ -426,24 +426,30 @@
             dst[k, p, pl.ds(0, nz)] = x[:nz]
             dst[k, p, pl.ds(nz, 8)] = jnp.where(tile, x[nz:], 0.0)
 
-    spread_halo(halo, beside, src.shape[1], width)
-    over_planes(src.shape[1], width, body)
+    spread_halo(halo, beside, slots, width, chosen)
+    over_planes(slots, width, body, chosen)
+
+
+def halo_sweep(halo, edge, halo_dst, hw, halo_e, halo_f, column):
     new = relaxed(*halo_operator(halo, edge, hw, halo_f), hw[6], halo_e[...])
     for k in range(4):
         halo_dst[k] = jnp.where(column, new[k], 0.0)
-    if edge_dst is not None:
-        fill_edges(edge_dst, dst, 4, 3 - width, dst.shape[1] - 3 + width)
-
-
-def over_planes(slots, width, body):
+
+
+def over_planes(slots, width, body, chosen=None):
     _, xl, xr = place("gx")
     for p in range(3 - width, slots - 3 + width):
+        wanted = True if chosen is None else chosen(p)
+        if wanted is False:
+            continue
         if p < 3:
-            pl.when(xl > 0)(lambda p=p: body(p))
+            wanted = xl > 0
         elif p >= slots - 3:
-            pl.when(xr > 0)(lambda p=p: body(p))
+            wanted = xr > 0
+        if wanted is True:
+            body(p)
         else:
-            body(p)
+            pl.when(wanted)(lambda p=p: body(p))
 
 
 def own_slots(x, nx, part):
@@ -466,8 +472,8 @@
     return jnp.where(kept, x, 0.0), kept
 
 
-def viscosity_force(e_in, f_in, z_halo, halo_full, x_main, x_rim, e, halo_e, force, halo_f):
-    nx, nz, _ = e_in.shape
+def viscosity_force(staged, z_halo, halo_full, x_main, e, halo_e, force, halo_f):
+    nx, nz = staged.nx, staged.nz
     slots = nx + 6
     zero = jnp.zeros((nz + 8, LANES), F32)
     for p in list(range(3)) + list(range(nx + 3, slots)):
@@ -475,10 +481,10 @@
         for k in range(3):
             force[k, p] = zero
     for q in range(nx):
-        e[q + 3, pl.ds(0, nz)] = e_in[q]
+        e[q + 3, pl.ds(0, nz)] = staged[4, q]
         e[q + 3, pl.ds(nz, 8)] = z_halo[4, q]
         for k in range(3):
-            force[k, q + 3, pl.ds(0, nz)] = 2.0 * f_in[k, q]
+            force[k, q + 3, pl.ds(0, nz)] = 2.0 * staged[5 + k, q]
             force[k, q + 3, pl.ds(nz, 8)] = 2.0 * z_halo[5 + k, q]
     halo_e[...] = own_slots(halo_full[0], nx, 1)
     for k in range(3):
@@ -486,31 +492,16 @@
     for m in range(x_main.shape[0]):
         right, valid = x_side(m)
         there = truth(valid, (nz, LANES))
-        there8 = truth(valid, (8, LANES))
         for j in range(3):
             e[right * (nx + 3) + j, pl.ds(0, nz)] = jnp.where(there, x_main[m, 12 + j], 0.0)
         for j in range(2):
             at = right * (nx + 2) + 1 + j
             for k in range(3):
                 force[k, at, pl.ds(0, nz)] = jnp.where(there, 2.0 * x_main[m, 15 + 2 * k + j], 0.0)
-        near = right * (nx + 1) + 2
-        x = jnp.where(there8, x_rim[m, 4], 0.0)
-        e[near, pl.ds(nz, 8)] = x
-        e[near + 2 * right - 1, pl.ds(nz, 8)] = roll(x, -3, 0)
-        x = jnp.where(there8, 2.0 * x_rim[m, 5], 0.0)
-        for k, at in enumerate((0, 3, 5)):
-            force[k, near, pl.ds(nz, 8)] = roll(x, -at, 0)
-        tiles = (nz + 8) // 8
-        column = jnp.concatenate([x_rim[m, 6 + r] for r in range(tiles)], axis=0)
-        x, kept = rim_halo(column, 4, LANES // 8, 2, right, valid, nx)
-        halo_e[...] = jnp.where(kept, x, halo_e[...])
-        for k in range(3):
-            x, kept = rim_halo(column, 5 + k, LANES // 8, 2, right, valid, nx)
-            halo_f[k] = jnp.where(kept, 2.0 * x, halo_f[k])
-
-
-def first_fields(v, p_in, z_halo, halo_full, x_main, x_rim, u, other, halo):
-    nx, nz, _ = p_in.shape
+
+
+def first_fields(staged, z_halo, halo_full, x_main, u, other, halo):
+    nx, nz = staged.nx, staged.nz
     slots = nx + 6
     zero = jnp.zeros((nz + 8, LANES), F32)
     for k in range(4):
@@ -518,72 +509,149 @@
             u[k, p] = zero
             other[k, p] = zero
         for q in range(nx):
-            u[k, q + 3, pl.ds(0, nz)] = v[k, q] if k < 3 else p_in[q]
+            u[k, q + 3, pl.ds(0, nz)] = staged[k, q]
             u[k, q + 3, pl.ds(nz, 8)] = z_halo[k, q]
         halo[k] = own_slots(halo_full[k], nx, 0)
     for m in range(x_main.shape[0]):
         right, valid = x_side(m)
         there = truth(valid, (nz, LANES))
-        there8 = truth(valid, (8, LANES))
-        tiles = (nz + 8) // 8
-        column = jnp.concatenate([x_rim[m, 6 + r] for r in range(tiles)], axis=0)
-        near = right * (nx + 1) + 2
         for k in range(4):
             for j in range(3):
                 x = jnp.where(there, x_main[m, 3 * k + j], 0.0)
                 u[k, right * (nx + 3) + j, pl.ds(0, nz)] = x
-            x = jnp.where(there8, x_rim[m, k], 0.0)
-            u[k, near, pl.ds(nz, 8)] = x
-            u[k, near + 2 * right - 1, pl.ds(nz, 8)] = roll(x, -3, 0)
+
+
+def add_rims(x_rim, nx, u, halo, e, halo_e, force, halo_f, edge, edge_e):
+    nz = e.shape[1] - 8
+    tiles = (nz + 8) // 8
+    tail = pl.ds(nz, 8)
+    slot = iota((8, LANES), 1) // SLOT
+    for m in range(x_rim.shape[0]):
+        right, valid = x_side(m)
+        there = truth(valid, (8, LANES))
+        column = jnp.concatenate([x_rim[m, 6 + r] for r in range(tiles)], axis=0)
+        near = right * (nx + 1) + 2
+        far = near + 2 * right - 1
+        for k in range(5):
+            x = jnp.where(there, x_rim[m, k], 0.0)
+            for p, y in ((near, x), (far, roll(x, -3, 0))):
+                moved = roll(y, p * SLOT + 4, 1)
+                if k < 4:
+                    u[k, p, tail] = y
+                    edge[k, tail] = jnp.where(slot == p, moved, edge[k, tail])
+                else:
+                    e[p, tail] = y
+                    edge_e[tail] = jnp.where(slot == p, moved, edge_e[tail])
             x, kept = rim_halo(column, k, LANES // 8, 2, right, valid, nx)
-            halo[k] = jnp.where(kept, x, halo[k])
-
-
-def pre_smooth(
-    v, p_in, e_in, f_in, z_halo, halo_full, x_main, x_rim,
-    fields, coarse, edges, x_fine, e, halo_e, force, halo_f, w0, w1, w2, w3, w4, w5, hw,
-    ua, ub, ha, hb, ca, cb, edge_e, beside, summed,
-):
-    nx, nz, _ = p_in.shape
-    slots = nx + 6
-    w = (w0, w1, w2, w3, w4, w5)
-    viscosity_force(e_in, f_in, z_halo, halo_full, x_main, x_rim, e, halo_e, force, halo_f)
-    first_fields(v, p_in, z_halo, halo_full, x_main, x_rim, ua, ub, ha)
-    masks = fine_masks(nz + 8, slots)
-    fill_edges(ca, ua, 4, 0, slots)
-    edge_e[...] = edges_of(lambda p: e[p], 0, slots)
-    main_weights(e, halo_e, w, 2)
-    halo_weights(halo_e, edge_e, hw)
-    rest = (w, hw, e, halo_e, force, halo_f)
-    fine_sweep(ua, ha, ca, ub, hb, cb, *rest, 2, masks, beside)
-    fine_sweep(ub, hb, cb, ua, ha, ca, *rest, 1, masks, beside)
-    for k in range(4):
-        for q in range(nx):
-            fields[k, q] = ua[k, q + 3, pl.ds(0, nz)]
-    for m in range(x_fine.shape[0]):
-        high = high_side("gx", m)
-        for k in range(4):
-            for j in range(2):
-                x_fine[m, 2 * k + j] = ua[k, 3 + high * (nx - 2) + j, pl.ds(0, nz)]
-    lane = iota((nz, LANES), 1)
-    for j in range(2):
-        first = roll(ca[j][:nz], -3 * SLOT, 1)
-        second = roll(ca[j + 2][:nz], LANES // 2 - 3 * SLOT, 1)
-        edges[j] = jnp.where(lane < LANES // 2, first, second)
-
-    spread_halo(ha, beside, slots, 0)
-    for q in range(nx // 2):
+            if k < 4:
+                halo[k] = jnp.where(kept, x, halo[k])
+            else:
+                halo_e[...] = jnp.where(kept, x, halo_e[...])
+        x = jnp.where(there, 2.0 * x_rim[m, 5], 0.0)
+        for k, at in enumerate((0, 3, 5)):
+            force[k, near, tail] = roll(x, -at, 0)
+            x_k, kept = rim_halo(column, 5 + k, LANES // 8, 2, right, valid, nx)
+            halo_f[k] = jnp.where(kept, 2.0 * x_k, halo_f[k])
+
+
+def early(nx, sweep):
+    _, xl, xr = place("gx")
+
+    def chosen(p):
+        if 3 + sweep <= p < nx + 3 - sweep:
+            return True
+        if 3 <= p < nx + 3:
+            return xl == 0 if p < 3 + sweep else xr == 0
+        return False
+
+    return chosen
+
+
+def early_block(nx):
+    _, xl, xr = place("gx")
+    return lambda q: xl == 0 if 2 * q + 5 <= nx else xr == 0 if 2 * q + 2 >= 5 else False
+
+
+def late(chosen):
+    def rest(p):
+        flag = chosen(p)
+        return not flag if isinstance(flag, bool) else jnp.logical_not(flag)
+
+    return rest
+
+
+def residuals(u, halo, beside, w, force, e, summed, chosen):
+    _, blocks, nz, _ = summed.shape
+    slots = u.shape[1]
+    spread_halo(halo, beside, slots, 0, lambda p: chosen((p - 3) // 2), False)
+
+    def body(q):
         totals = [0.0] * 5
         for j in range(2):
             p = 2 * q + 3 + j
-            olds, sums, spread = main_operator(ua, beside, w, force, p, nz)
-            diagonal = (w0[p] + w0[p - 1] + w1[p] + w2[p] + w3[p] + w4[p])[:nz]
+            olds, sums, spread = main_operator(u, beside, w, force, p, nz)
+            diagonal = (w[0][p] + w[0][p - 1] + w[1][p] + w[2][p] + w[3][p] + w[4][p])[:nz]
             for k in range(3):
                 totals[k] += sums[k] - diagonal * olds[k]
             totals[3] += spread
             totals[4] += e[p, pl.ds(0, nz)]
         for k in range(5):
             summed[k, q] = totals[k]
+
+    for q in range(blocks):
+        wanted = chosen(q)
+        if wanted is True:
+            body(q)
+        elif wanted is not False:
+            pl.when(wanted)(lambda q=q: body(q))
+
+
+def pre_start(*refs):
+    pre_start_on(Staged(refs[:16]), *refs[16:])
+
+
+def pre_start_on(
+    staged, z_halo, halo_full, x_main,
+    e, halo_e, force, halo_f, w0, w1, w2, w3, w4, w5, ua, ub, ha, ca, cb, edge_e, summed,
+    hw, hb, hc, beside,
+):
+    nx, nz = staged.nx, staged.nz
+    slots = nx + 6
+    w = (w0, w1, w2, w3, w4, w5)
+    viscosity_force(staged, z_halo, halo_full, x_main, e, halo_e, force, halo_f)
+    first_fields(staged, z_halo, halo_full, x_main, ua, ub, ha)
+    tile, column = fine_masks(nz + 8, slots)
+    fill_edges(ca, ua, range(slots))
+    edge_e[...] = edges_of(lambda p: e[p], range(slots))
+    main_weights(e, halo_e, w, 0, early(nx, 1), range(2, nx + 3))
+    main_sweep(ua, ha, ub, w, e, force, 0, tile, beside, early(nx, 1))
+    halo_weights(halo_e, edge_e, hw)
+    halo_sweep(ha, ca, hb, hw, halo_e, halo_f, column)
+    fill_edges(cb, ub, range(3, nx + 3))
+    main_sweep(ub, hb, ua, w, e, force, 0, tile, beside, early(nx, 2))
+    halo_sweep(hb, cb, hc, hw, halo_e, halo_f, column)
+    residuals(ua, hc, beside, w, force, e, summed, early_block(nx))
+
+
+def pre_smooth(
+    x_rim, _e, _halo_e, _force, _halo_f, _w0, _w1, _w2, _w3, _w4, _w5, _ua, _ub, _ha, _ca, _cb,
+    _edge_e, _summed, e, halo_e, force, halo_f, w0, w1, w2, w3, w4, w5, ua, ub, ha, ca, cb, edge_e,
+    summed, hw, coarse, hb, beside,
+):
+    slots = e.shape[0]
+    nx, nz = slots - 6, e.shape[1] - 8
+    w = (w0, w1, w2, w3, w4, w5)
+    add_rims(x_rim, nx, ua, ha, e, halo_e, force, halo_f, ca, edge_e)
+    tile, column = fine_masks(nz + 8, slots)
+    faces = [p for p in range(slots - 1) if not 3 <= p < nx + 2]
+    main_weights(e, halo_e, w, 2, late(early(nx, 1)), faces)
+    halo_weights(halo_e, edge_e, hw)
+    main_sweep(ua, ha, ub, w, e, force, 2, tile, beside, late(early(nx, 1)))
+    halo_sweep(ha, ca, hb, hw, halo_e, halo_f, column)
+    fill_edges(cb, ub, [p for p in range(1, slots - 1) if not 4 <= p < nx + 2], False)
+    main_sweep(ub, hb, ua, w, e, force, 1, tile, beside, late(early(nx, 2)))
+    halo_sweep(hb, cb, ha, hw, halo_e, halo_f, column)
+    residuals(ua, ha, beside, w, force, e, summed, late(early_block(nx)))
     scale = (0.5, 0.5, 0.5, -1.0 / 32.0, 0.125)
     cz = nz // 2
     left = []
@@ -606,8 +674,23 @@
             coarse[k, r] = out[at : at + cz]
 
 
+def smooth_pack(fields, edges, x_fine):
+    nx, nz = fields.shape[1] - 6, fields.shape[2] - 8
+    for m in range(x_fine.shape[0]):
+        high = high_side("gx", m)
+        for k in range(4):
+            for j in range(2):
+                x_fine[m, 2 * k + j] = fields[k, 3 + high * (nx - 2) + j, pl.ds(0, nz)]
+
+    def planes(k):
+        return [fields[k, q + 3, pl.ds(0, nz)] for q in range(nx)]
+
+    for j, x in enumerate(pair_edges(planes, 4, nz)):
+        edges[j] = x
+
+
 def fourth_pack(own, other, fields, whole, z_a, z_b):
-    nx, nz = fields.shape[1:3]
+    nx, nz = fields.shape[1] - 6, fields.shape[2] - 8
     pairs = whole.shape[1]
     cz = whole.shape[2]
     gx = lax.axis_index("gx")
@@ -636,8 +719,8 @@
         for q in range(nx):
             total = jnp.zeros((8, LANES), F32)
             for k in range(4):
-                low = roll(fields[k, q, pl.ds(0, 8)], 2 * k, 0)
-                high = roll(fields[k, q, pl.ds(nz - 8, 8)], 2 * k - 6, 0)
+                low = roll(fields[k, q + 3, pl.ds(0, 8)], 2 * k, 0)
+                high = roll(fields[k, q + 3, pl.ds(nz - 8, 8)], 2 * k - 6, 0)
                 total = jnp.where(row == k, jnp.where(toward, high, low), total)
             out[3 * pairs + q] = total
 
@@ -889,7 +972,7 @@
 def post_smooth(
     e, halo_e, force, halo_f, w0, w1, w2, w3, w4, w5, hw,
     fields, z_halo, halo_full, x_fine, x_rim, main, column, v_out, p_out,
-    ua, ub, ha, hb, ca, cb, beside,
+    ua, ub, ha, hb, ca, beside,
 ):
     nx, nz, _ = p_out.shape
     slots = nx + 6
@@ -901,7 +984,7 @@
             ub[k, p] = zero
         for q in range(nx):
             i = q // 2 + 1
-            ua[k, q + 3, pl.ds(0, nz)] = fields[k, q] + main[k, i, pl.ds(0, nz)]
+            ua[k, q + 3, pl.ds(0, nz)] = fields[k, q + 3, pl.ds(0, nz)] + main[k, i, pl.ds(0, nz)]
             ua[k, q + 3, pl.ds(nz, 8)] = z_halo[k, q] + main[k, i, pl.ds(nz, 8)]
         ha[k] = own_slots(halo_full[k % 2], nx, k // 2)
     for m in range(x_fine.shape[0]):
@@ -923,11 +1006,11 @@
     masks = fine_masks(nz + 8, slots)
     for k in range(4):
         ha[k] = jnp.where(masks[1], ha[k] + column[k], 0.0)
-    fill_edges(ca, ua, 4, 1, slots - 1)
-    rest = (w, hw, e, halo_e, force, halo_f)
-    fine_sweep(ua, ha, ca, ub, hb, None, *rest, 1, masks, beside)
-
-    spread_halo(hb, beside, slots, 0)
+    fill_edges(ca, ua, range(1, slots - 1))
+    main_sweep(ua, ha, ub, w, e, force, 1, masks[0], beside)
+    halo_sweep(ha, ca, hb, hw, halo_e, halo_f, masks[1])
+
+    spread_halo(hb, beside, slots, 0, full=False)
 
     def last(p):
         new = main_operator(ub, beside, w, force, p, nz)
@@ -949,16 +1032,13 @@
     block = (nz, LANES)
 
     z_shape = (3 * nx, 8, LANES)
-    x_main, y_a, y_b, z_a, z_b = call(
-        first_pack,
-        [(sides, 21) + block, (2,) + block, (2,) + block, z_shape, z_shape],
-        inputs,
-        [a.shape for a in inputs],
-        outside=4,
-        copies=4 + 8 * sides,
-    )
+    half = (nx // 2,) + block
+    *staged, y_a, y_b = call(
+        first_pack, [half] * 16 + [(2,) + block] * 2, inputs, outside=4, copies=16
+    )
+    x_main, z_a, z_b = call(side_pack, [(sides, 21) + block, z_shape, z_shape], staged)
+    y_a, y_b = swap(y_a, "gy", 0), swap(y_b, "gy", 1)
     x_main = swap_x(x_main)
-    y_a, y_b = swap(y_a, "gy", 0), swap(y_b, "gy", 1)
     halo, z_b = call(second_pack, [(4,) + block, z_shape], [z_b, y_a, y_b])
     (z_a,) = call(second_pack_near, [z_shape], [z_a, halo])
     z_a, z_b = swap(z_a, "gz", 0), swap(z_b, "gz", 1)
@@ -970,18 +1050,27 @@
     )
     x_first = swap_x(x_first)
 
-    state = [(4, slots, rows, LANES)] * 2 + [(4, rows, LANES)] * 4
-    spread = (4, slots, rows, LANES)
-    operator = [(slots, rows, LANES), (rows, LANES), (3, slots, rows, LANES), (3, rows, LANES)]
-    operator += [(slots, rows, LANES)] * 6 + [(7, rows, LANES)]
-    fields, own, edges, x_fine, *operator = call(
+    spread, column = (4, slots, rows, LANES), (4, rows, LANES)
+    started = [(slots, rows, LANES), (rows, LANES), (3, slots, rows, LANES), (3, rows, LANES)]
+    started += [(slots, rows, LANES)] * 6 + [spread, spread] + [column] * 3 + [(rows, LANES)]
+    started += [(5, nx // 2, nz, LANES)]
+    state = call(
+        pre_start,
+        started,
+        [*staged, z_first, halo_first, x_main],
+        [(7, rows, LANES), column, column, spread],
+        cost=4,
+    )
+    *operator, fields, _, _, _, _, _, _, factors, own = call(
         pre_smooth,
-        [(4, nx) + block, (5, nx // 4, nz // 2, LANES), (2,) + block, (sides, 8) + block]
-        + operator,
-        inputs + [z_first, halo_first, x_main, x_first],
-        state + [(rows, LANES), spread, (5, nx // 2, nz, LANES)],
+        started + [(7, rows, LANES), (5, nx // 4, nz // 2, LANES)],
+        [x_first, *state],
+        [column, spread],
         cost=8,
-    )
+        aliases={i + 1: i for i in range(len(started))},
+    )
+    operator.append(factors)
+    edges, x_fine = call(smooth_pack, [(2,) + block, (sides, 8) + block], [fields])
     if lax.axis_size("gx") == 2:
         parts = [own, swap(own, "gx", 0)]
         gather = fourth_pack
@@ -1015,7 +1104,7 @@
     x_rim = swap_x(x_rim)
     planes = 2 * pairs
     plane = (shallow, LANES)
-    main, column = call(
+    grown, beside = call(
         coarse_solve,
         [(4, nx // 2 + 2, rows, LANES), (4, rows, LANES)],
         [full, full_e, y_a, y_b],
@@ -1028,8 +1117,8 @@
     v_out, p_out = call(
         post_smooth,
         [(3, nx) + block, (nx,) + block],
-        operator + [fields, z_halo, halo_full, x_fine, x_rim, main, column],
-        state + [spread],
+        operator + [fields, z_halo, halo_full, x_fine, x_rim, grown, beside],
+        [spread] * 2 + [column] * 3 + [spread],
         cost=8,
     )
     return v_out, p_out

time: 45.8 us -> 43.6 us (0.952)
  waiting for transfers between devices: 16.9 us -> 11.1 us
  starting transfers between devices: 14.2 us -> 16.5 us
  Pallas kernels: 13.8 us -> 15 us
    ppermute x9, waiting for transfers between devices: 12.5 us -> 7.75 us  [swap(): return lax.ppermute(array, axis, pairs)]
    ppermute x9, starting transfers between devices: 9.37 us -> 11.7 us  [swap(): return lax.ppermute(array, axis, pairs)]
    pallas_call x10 -> x13, Pallas kernels: 13.8 us -> 15 us  [call(): pl.pallas_call(body, out_shape=[jax.ShapeDtypeStruct(shape, F32) for shap...]
    ppermute x4, waiting for transfers between devices: 4.4 us -> 3.39 us  [swap(): return lax.ppermute(array, ('gy', 'gz'), pairs)]
  transfers between devices with their start and end apart: 13 -> 13, of which waited for: 7 -> 5; matrix products, arithmetic and copies ran while one was open for 0% -> 0% of each run, Pallas kernels for 8% -> 17%
where the time goes in v4:
time: 43.6 us; the launch traced here: 43.5 us
  starting transfers between devices  16.5 us (38%)
  Pallas kernels  15 us (34%)
  waiting for transfers between devices  11.1 us (25%)
  between operations  0.75 us (2%)
    pallas_call x13, Pallas kernels, call(): pl.pallas_call(body, out_shape=[jax.ShapeDtypeStruct(shape, F32) for shap...  15 us
    ppermute x9, starting transfers between devices, swap(): return lax.ppermute(array, axis, pairs)  11.7 us
    ppermute x9, waiting for transfers between devices, swap(): return lax.ppermute(array, axis, pairs)  7.75 us
    ppermute x4, starting transfers between devices, swap(): return lax.ppermute(array, ('gy', 'gz'), pairs)  4.86 us
    ppermute x4, waiting for transfers between devices, swap(): return lax.ppermute(array, ('gy', 'gz'), pairs)  3.39 us
  transfers between devices with their start and end apart: 13, of which 5 were waited for; matrix products, arithmetic and copies ran while one was open for 0% of the time, Pallas kernels for 17%

profile of v4, /device:TPU:0, one launch (start us, length us, event | category | flops | bytes accessed | tf_op | source)
XLA Modules:
  0.0 43.5 jit_solution(10492989105063537760)
XLA Ops:
  0.6 1.8 %shard_map.59 = (f32[4,32,128]{2,1,0:T(8,128)S(1)}, f32[4,32,128]{2,1,0:T(8,128)S(1)}, f32[4,32,128]{2,1,0:T(8,128)S(1)}, f32[4,32,128]{2,1,0:T(8,128)S(1)}, f32...) custom-call(f32[3,8,32,128]{3,2,1,0:T(8,128)} %v_in.1, ...), custom_call_target="tpu_custom_call" | custom-call | flops 1000000 | bytes 1000000 | tf_op jit(solution)/shard_map/pallas_call | solution.py:21
  2.4 0.1 shard_map.60
  2.5 3.0 %collective-permute-start.5 = (f32[1,21,32,128]{3,2,1,0:T(8,128)S(1)}, f32[1,21,32,128]{3,2,1,0:T(8,128)S(1)}, u32[]{:S(2)}, u32[]{:S(2)}) collective-permute-start(f32[1,21,32,128]{3,2,1,0:T(8,128)S(1)} %get-tuple-element.97), channel_id=1, source_target_pairs={{0,16},{16,0},{1,17},{17,1},{2,18},{18,2},{3,19},{19,3},{4,20},{20... | collective-permute-start | bytes 1032200 | tf_op jit(solution)/shard_map/ppermute | solution.py:56
  5.6 1.6 %collective-permute-start = (f32[2,32,128]{2,1,0:T(8,128)S(1)}, f32[2,32,128]{2,1,0:T(8,128)S(1)}, u32[]{:S(2)}, u32[]{:S(2)}) collective-permute-start(f32[2,32,128]{2,1,0:T(8,128)S(1)} %get-tuple-element.90), channel_id=1, source_target_pairs={{0,4},{4,0},{8,12},{12,8},{1,5},{5,1},{9,13},{13,9},{2,6},{6,2},{1... | collective-permute-start | bytes 98312 | tf_op jit(solution)/shard_map/ppermute | solution.py:56
  7.1 2.3 %collective-permute-done.y_a = f32[2,32,128]{2,1,0:T(8,128)S(1)} collective-permute-done((f32[2,32,128]{2,1,0:T(8,128)S(1)}, f32[2,32,128]{2,1,0:T(8,128)S(1)}, u32[]{:S(2)}, u32[]{:S(2)}) %collective-permute-start) | collective-permute-done | bytes 32800 | tf_op jit(solution)/shard_map/ppermute | solution.py:56
  9.7 2.8 %collective-permute-start.3 = (f32[24,8,128]{2,1,0:T(8,128)S(1)}, f32[24,8,128]{2,1,0:T(8,128)S(1)}, u32[]{:S(2)}, u32[]{:S(2)}) collective-permute-start(f32[24,8,128]{2,1,0:T(8,128)S(1)} %get-tuple-element.93), channel_id=1, source_target_pairs={{0,4},{1,2},{2,1},{3,7},{4,0},{5,6},{6,5},{7,3},{8,12},{9,10},{10,... | collective-permute-start | bytes 294920 | tf_op jit(solution)/shard_map/ppermute | solution.py:51
  12.5 2.6 %collective-permute-done.3.z_b = f32[24,8,128]{2,1,0:T(8,128)S(1)} collective-permute-done((f32[24,8,128]{2,1,0:T(8,128)S(1)}, f32[24,8,128]{2,1,0:T(8,128)S(1)}, u32[]{:S(2)}, u32[]{:S(2)}) %collective-permute-start.3) | collective-permute-done | bytes 98336 | tf_op jit(solution)/shard_map/ppermute | solution.py:51
  15.1 0.1 shard_map.63
  15.2 0.6 %collective-permute-start.4 = (f32[1,11,8,128]{3,2,1,0:T(8,128)S(1)}, f32[1,11,8,128]{3,2,1,0:T(8,128)S(1)}, u32[]{:S(2)}, u32[]{:S(2)}) collective-permute-start(f32[1,11,8,128]{3,2,1,0:T(8,128)S(1)} %get-tuple-element.94), channel_id=1, source_target_pairs={{0,16},{16,0},{1,17},{17,1},{2,18},{18,2},{3,19},{19,3},{4,20},{20... | collective-permute-start | bytes 135176 | tf_op jit(solution)/shard_map/ppermute | solution.py:56
  15.8 3.6 %shard_map.64 = (f32[14,40,128]{2,1,0:T(8,128)S(1)}, f32[40,128]{1,0:T(8,128)S(1)}, f32[3,14,40,128]{3,2,1,0:T(8,128)S(1)}, f32[3,40,128]{2,1,0:T(8,128)S(1)}, f...) custom-call(f32[4,32,128]{2,1,0:T(8,128)S(1)} %get-tuple-element.72., ...), custom_call_target="tpu_custom_call" | custom-call | flops 4000000 | bytes 4000000 | tf_op jit(solution)/shard_map/pallas_call | solution.py:21
  19.4 2.8 %shard_map.65 = (f32[14,40,128]{2,1,0:T(8,128)S(1)}, f32[40,128]{1,0:T(8,128)S(1)}, f32[3,14,40,128]{3,2,1,0:T(8,128)S(1)}, f32[3,40,128]{2,1,0:T(8,128)S(1)}, f...) custom-call(f32[1,11,8,128]{3,2,1,0:T(8,128)S(1)} %collective-permut, ...), custom_call_target="tpu_custom_call", output_to_operand_aliasing={{0}: (1, {}), {1}: (2, {}), {2}: (3, {}), {3}: (4, {}), {4}... | custom-call | flops 8000000 | bytes 8000000 | tf_op jit(solution)/shard_map/pallas_call | solution.py:21
  22.2 1.4 %collective-permute-start.6 = (f32[5,2,16,128]{3,2,1,0:T(8,128)S(1)}, f32[5,2,16,128]{3,2,1,0:T(8,128)S(1)}, u32[]{:S(2)}, u32[]{:S(2)}) collective-permute-start(f32[5,2,16,128]{3,2,1,0:T(8,128)S(1)} %get-tuple-element.127.own), channel_id=1, source_target_pairs={{0,16},{16,0},{1,17},{17,1},{2,18},{18,2},{3,19},{19,3},{4,20},{20... | collective-permute-start | bytes 245768 | tf_op jit(solution)/shard_map/ppermute | solution.py:56
  23.6 3.1 %collective-permute-done.6.other = f32[5,2,16,128]{3,2,1,0:T(8,128)S(1)} collective-permute-done((f32[5,2,16,128]{3,2,1,0:T(8,128)S(1)}, f32[5,2,16,128]{3,2,1,0:T(8,128)S(1)}, u32[]{:S(2)}, u32[]{:S(2)}) %collective-permute-start.6) | collective-permute-done | bytes 81952 | tf_op jit(solution)/shard_map/ppermute | solution.py:56
  26.9 2.1 %collective-permute-start.8 = (f32[20,8,128]{2,1,0:T(8,128)S(1)}, f32[20,8,128]{2,1,0:T(8,128)S(1)}, u32[]{:S(2)}, u32[]{:S(2)}) collective-permute-start(f32[20,8,128]{2,1,0:T(8,128)S(1)} %get-tuple-element.130), channel_id=1, source_target_pairs={{0,4},{1,2},{2,1},{3,7},{4,0},{5,6},{6,5},{7,3},{8,12},{9,10},{10,... | collective-permute-start | bytes 245768 | tf_op jit(solution)/shard_map/ppermute | solution.py:51
  29.0 0.2 shard_map.67
  29.2 1.4 %collective-permute-start.11 = (f32[1,8,32,128]{3,2,1,0:T(8,128)S(1)}, f32[1,8,32,128]{3,2,1,0:T(8,128)S(1)}, u32[]{:S(2)}, u32[]{:S(2)}) collective-permute-start(f32[1,8,32,128]{3,2,1,0:T(8,128)S(1)} %get-tuple-element.136), channel_id=1, source_target_pairs={{0,16},{16,0},{1,17},{17,1},{2,18},{18,2},{3,19},{19,3},{4,20},{20... | collective-permute-start | bytes 393224 | tf_op jit(solution)/shard_map/ppermute | solution.py:56
  30.6 0.8 %collective-permute-done.8.z_b = f32[20,8,128]{2,1,0:T(8,128)S(1)} collective-permute-done((f32[20,8,128]{2,1,0:T(8,128)S(1)}, f32[20,8,128]{2,1,0:T(8,128)S(1)}, u32[]{:S(2)}, u32[]{:S(2)}) %collective-permute-start.8) | collective-permute-done | bytes 81952 | tf_op jit(solution)/shard_map/ppermute | solution.py:51
  31.4 0.3 shard_map.68
  31.7 2.1 %collective-permute-start.9 = (f32[15,8,128]{2,1,0:T(8,128)S(1)}, f32[15,8,128]{2,1,0:T(8,128)S(1)}, u32[]{:S(2)}, u32[]{:S(2)}) collective-permute-start(f32[15,8,128]{2,1,0:T(8,128)S(1)} %get-tuple-element.133), channel_id=1, source_target_pairs={{0,4},{4,0},{8,12},{12,8},{1,5},{5,1},{9,13},{13,9},{2,6},{6,2},{1... | collective-permute-start | bytes 184328 | tf_op jit(solution)/shard_map/ppermute | solution.py:56
  33.8 2.3 %collective-permute-done.9.y_a = f32[15,8,128]{2,1,0:T(8,128)S(1)} collective-permute-done((f32[15,8,128]{2,1,0:T(8,128)S(1)}, f32[15,8,128]{2,1,0:T(8,128)S(1)}, u32[]{:S(2)}, u32[]{:S(2)}) %collective-permute-start.9) | collective-permute-done | bytes 61472 | tf_op jit(solution)/shard_map/ppermute | solution.py:56
  36.1 0.2 shard_map.69
  36.3 1.4 %collective-permute-start.12 = (f32[1,6,8,128]{3,2,1,0:T(8,128)S(1)}, f32[1,6,8,128]{3,2,1,0:T(8,128)S(1)}, u32[]{:S(2)}, u32[]{:S(2)}) collective-permute-start(f32[1,6,8,128]{3,2,1,0:T(8,128)S(1)} %get-tuple-element.137), channel_id=1, source_target_pairs={{0,16},{16,0},{1,17},{17,1},{2,18},{18,2},{3,19},{19,3},{4,20},{20... | collective-permute-start | bytes 73736 | tf_op jit(solution)/shard_map/ppermute | solution.py:56
  37.7 2.8 %shard_map.70 = (f32[4,6,40,128]{3,2,1,0:T(8,128)S(1)}, f32[4,40,128]{2,1,0:T(8,128)S(1)}) custom-call(f32[4,4,24,128]{3,2,1,0:T(8,128)S(1)} %get-tuple-element.138.full, f32[4,32,128]{2,1,0:T(8,128)S(1)} %get-tuple-element.139.full_e, f32[15,8,128]{2,1,0:T(8,128)S(1)} %collective-permute-done.9.y_a, f32[15,8,128]{2,1,0:T(8,128)S(1)} %collective-permute-done.10.y_b), custom_call_target="tpu_custom_call" | custom-call | flops 4000000 | bytes 4000000 | tf_op jit(solution)/shard_map/pallas_call | solution.py:21
  40.5 3.0 %shard_map.71 = (f32[3,8,32,128]{3,2,1,0:T(8,128)}, f32[8,32,128]{2,1,0:T(8,128)}) custom-call(f32[14,40,128]{2,1,0:T(8,128)S(1)} %get-tuple-element.115.e, f32[40,128]{1,0:T(8,128)S(1)} %get-tuple-element.116.halo_e, f32[3,14,40,128]{3,2,1,0:T(8,128)S(1)} %get-tuple-element.117.force, f32[3,40,128]{2,1,0:T(8,128)S(1)} %get-tuple-element.118.halo_f, ...), custom_call_target="tpu_custom_call" | custom-call | flops 8000000 | bytes 8000000 | tf_op jit(solution)/shard_map/pallas_call | solution.py:21
  (15 shorter events, 0.4 us)
Async XLA Ops:
  2.5 13.2 %collective-permute-start.5 = (f32[1,21,32,128]{3,2,1,0:T(8,128)S(1)}, f32[1,21,32,128]{3,2,1,0:T(8,128)S(1)}, u32[]{:S(2)}, u32[]{:S(2)}) collective-permute-start(f32[1,21,32,128]{3,2,1,0:T(8,128)S(1)} %get-tuple-element.97), channel_id=1, source_target_pairs={{0,16},{16,0},{1,17},{17,1},{2,18},{18,2},{3,19},{19,3},{4,20},{20... | collective-permute-start | bytes 1032200 | tf_op jit(solution)/shard_map/ppermute | solution.py:56
  5.6 3.9 %collective-permute-start = (f32[2,32,128]{2,1,0:T(8,128)S(1)}, f32[2,32,128]{2,1,0:T(8,128)S(1)}, u32[]{:S(2)}, u32[]{:S(2)}) collective-permute-start(f32[2,32,128]{2,1,0:T(8,128)S(1)} %get-tuple-element.90), channel_id=1, source_target_pairs={{0,4},{4,0},{8,12},{12,8},{1,5},{5,1},{9,13},{13,9},{2,6},{6,2},{1... | collective-permute-start | bytes 98312 | tf_op jit(solution)/shard_map/ppermute | solution.py:56
  7.1 2.3 %collective-permute-start.1 = (f32[2,32,128]{2,1,0:T(8,128)S(1)}, f32[2,32,128]{2,1,0:T(8,128)S(1)}, u32[]{:S(2)}, u32[]{:S(2)}) collective-permute-start(f32[2,32,128]{2,1,0:T(8,128)S(1)} %get-tuple-element.91), channel_id=1, source_target_pairs={{0,1},{1,0},{2,3},{3,2},{4,8},{5,9},{6,10},{7,11},{8,4},{9,5},{10,... | collective-permute-start | bytes 98312 | tf_op jit(solution)/shard_map/ppermute | solution.py:51
  9.6 2.8 %collective-permute-start.2 = (f32[24,8,128]{2,1,0:T(8,128)S(1)}, f32[24,8,128]{2,1,0:T(8,128)S(1)}, u32[]{:S(2)}, u32[]{:S(2)}) collective-permute-start(f32[24,8,128]{2,1,0:T(8,128)S(1)} %shard_map.62), channel_id=1, source_target_pairs={{0,1},{1,0},{2,3},{3,2},{4,5},{5,4},{6,7},{7,6},{8,9},{9,8},{10,11... | collective-permute-start | bytes 294920 | tf_op jit(solution)/shard_map/ppermute | solution.py:56
  9.7 5.4 %collective-permute-start.3 = (f32[24,8,128]{2,1,0:T(8,128)S(1)}, f32[24,8,128]{2,1,0:T(8,128)S(1)}, u32[]{:S(2)}, u32[]{:S(2)}) collective-permute-start(f32[24,8,128]{2,1,0:T(8,128)S(1)} %get-tuple-element.93), channel_id=1, source_target_pairs={{0,4},{1,2},{2,1},{3,7},{4,0},{5,6},{6,5},{7,3},{8,12},{9,10},{10,... | collective-permute-start | bytes 294920 | tf_op jit(solution)/shard_map/ppermute | solution.py:51
  15.2 4.2 %collective-permute-start.4 = (f32[1,11,8,128]{3,2,1,0:T(8,128)S(1)}, f32[1,11,8,128]{3,2,1,0:T(8,128)S(1)}, u32[]{:S(2)}, u32[]{:S(2)}) collective-permute-start(f32[1,11,8,128]{3,2,1,0:T(8,128)S(1)} %get-tuple-element.94), channel_id=1, source_target_pairs={{0,16},{16,0},{1,17},{17,1},{2,18},{18,2},{3,19},{19,3},{4,20},{20... | collective-permute-start | bytes 135176 | tf_op jit(solution)/shard_map/ppermute | solution.py:56
  22.2 4.5 %collective-permute-start.6 = (f32[5,2,16,128]{3,2,1,0:T(8,128)S(1)}, f32[5,2,16,128]{3,2,1,0:T(8,128)S(1)}, u32[]{:S(2)}, u32[]{:S(2)}) collective-permute-start(f32[5,2,16,128]{3,2,1,0:T(8,128)S(1)} %get-tuple-element.127.own), channel_id=1, source_target_pairs={{0,16},{16,0},{1,17},{17,1},{2,18},{18,2},{3,19},{19,3},{4,20},{20... | collective-permute-start | bytes 245768 | tf_op jit(solution)/shard_map/ppermute | solution.py:56
  26.8 3.8 %collective-permute-start.7 = (f32[20,8,128]{2,1,0:T(8,128)S(1)}, f32[20,8,128]{2,1,0:T(8,128)S(1)}, u32[]{:S(2)}, u32[]{:S(2)}) collective-permute-start(f32[20,8,128]{2,1,0:T(8,128)S(1)} %get-tuple-element.129), channel_id=1, source_target_pairs={{0,1},{1,0},{2,3},{3,2},{4,5},{5,4},{6,7},{7,6},{8,9},{9,8},{10,11... | collective-permute-start | bytes 245768 | tf_op jit(solution)/shard_map/ppermute | solution.py:56
  26.9 4.5 %collective-permute-start.8 = (f32[20,8,128]{2,1,0:T(8,128)S(1)}, f32[20,8,128]{2,1,0:T(8,128)S(1)}, u32[]{:S(2)}, u32[]{:S(2)}) collective-permute-start(f32[20,8,128]{2,1,0:T(8,128)S(1)} %get-tuple-element.130), channel_id=1, source_target_pairs={{0,4},{1,2},{2,1},{3,7},{4,0},{5,6},{6,5},{7,3},{8,12},{9,10},{10,... | collective-permute-start | bytes 245768 | tf_op jit(solution)/shard_map/ppermute | solution.py:51
  29.2 11.3 %collective-permute-start.11 = (f32[1,8,32,128]{3,2,1,0:T(8,128)S(1)}, f32[1,8,32,128]{3,2,1,0:T(8,128)S(1)}, u32[]{:S(2)}, u32[]{:S(2)}) collective-permute-start(f32[1,8,32,128]{3,2,1,0:T(8,128)S(1)} %get-tuple-element.136), channel_id=1, source_target_pairs={{0,16},{16,0},{1,17},{17,1},{2,18},{18,2},{3,19},{19,3},{4,20},{20... | collective-permute-start | bytes 393224 | tf_op jit(solution)/shard_map/ppermute | solution.py:56
  31.7 4.4 %collective-permute-start.9 = (f32[15,8,128]{2,1,0:T(8,128)S(1)}, f32[15,8,128]{2,1,0:T(8,128)S(1)}, u32[]{:S(2)}, u32[]{:S(2)}) collective-permute-start(f32[15,8,128]{2,1,0:T(8,128)S(1)} %get-tuple-element.133), channel_id=1, source_target_pairs={{0,4},{4,0},{8,12},{12,8},{1,5},{5,1},{9,13},{13,9},{2,6},{6,2},{1... | collective-permute-start | bytes 184328 | tf_op jit(solution)/shard_map/ppermute | solution.py:56
  33.8 2.3 %collective-permute-start.10 = (f32[15,8,128]{2,1,0:T(8,128)S(1)}, f32[15,8,128]{2,1,0:T(8,128)S(1)}, u32[]{:S(2)}, u32[]{:S(2)}) collective-permute-start(f32[15,8,128]{2,1,0:T(8,128)S(1)} %get-tuple-element.134), channel_id=1, source_target_pairs={{0,1},{1,0},{2,3},{3,2},{4,8},{5,9},{6,10},{7,11},{8,4},{9,5},{10,... | collective-permute-start | bytes 184328 | tf_op jit(solution)/shard_map/ppermute | solution.py:51
  36.3 4.2 %collective-permute-start.12 = (f32[1,6,8,128]{3,2,1,0:T(8,128)S(1)}, f32[1,6,8,128]{3,2,1,0:T(8,128)S(1)}, u32[]{:S(2)}, u32[]{:S(2)}) collective-permute-start(f32[1,6,8,128]{3,2,1,0:T(8,128)S(1)} %get-tuple-element.137), channel_id=1, source_target_pairs={{0,16},{16,0},{1,17},{17,1},{2,18},{18,2},{3,19},{19,3},{4,20},{20... | collective-permute-start | bytes 73736 | tf_op jit(solution)/shard_map/ppermute | solution.py:56

commit v5 on v4

--- a/solution.py
+++ b/solution.py
@@ -56,7 +56,28 @@
     return lax.ppermute(array, axis, pairs)
 
 
+FIXED = []
+
+
+def by_sides(body):
+    def kernel(*refs):
+        count = lax.axis_size("gx")
+        _, xl, xr = place("gx")
+        for sides in [(0, 1), (1, 0), (1, 1)][: 2 if count == 2 else 3]:
+
+            def branch(sides=sides):
+                FIXED.append(sides)
+                body(*refs)
+                FIXED.pop()
+
+            pl.when((xl == sides[0]) & (xr == sides[1]))(branch)
+
+    return kernel
+
+
 def place(axis):
+    if axis == "gx" and FIXED:
+        return (None,) + FIXED[-1]
     i = lax.axis_index(axis)
     last = lax.axis_size(axis) - 1
     return i, jnp.where(i > 0, 1, 0), jnp.where(i < last, 1, 0)
@@ -440,16 +461,8 @@
     _, xl, xr = place("gx")
     for p in range(3 - width, slots - 3 + width):
         wanted = True if chosen is None else chosen(p)
-        if wanted is False:
-            continue
-        if p < 3:
-            wanted = xl > 0
-        elif p >= slots - 3:
-            wanted = xr > 0
-        if wanted is True:
+        if wanted and (p >= 3 or xl) and (p < slots - 3 or xr):
             body(p)
-        else:
-            pl.when(wanted)(lambda p=p: body(p))
 
 
 def own_slots(x, nx, part):
@@ -459,8 +472,10 @@
 
 
 def x_side(m):
+    _, has_left, has_right = place("gx")
+    if lax.axis_size("gx") == 2:
+        return has_right, 1
     right = high_side("gx", m)
-    _, has_left, has_right = place("gx")
     return right, jnp.where(right > 0, has_right, has_left)
 
 
@@ -573,11 +588,13 @@
 
 
 def late(chosen):
-    def rest(p):
-        flag = chosen(p)
-        return not flag if isinstance(flag, bool) else jnp.logical_not(flag)
-
-    return rest
+    return lambda p: not chosen(p)
+
+
+def inside_slots(slots, width, chosen=None):
+    _, xl, xr = place("gx")
+    inside = range(3 - width * xl, slots - 3 + width * xr)
+    return [p for p in inside if chosen is None or chosen(p)]
 
 
 def residuals(u, halo, beside, w, force, e, summed, chosen):
@@ -599,11 +616,8 @@
             summed[k, q] = totals[k]
 
     for q in range(blocks):
-        wanted = chosen(q)
-        if wanted is True:
+        if chosen(q):
             body(q)
-        elif wanted is not False:
-            pl.when(wanted)(lambda q=q: body(q))
 
 
 def pre_start(*refs):
@@ -621,13 +635,13 @@
     viscosity_force(staged, z_halo, halo_full, x_main, e, halo_e, force, halo_f)
     first_fields(staged, z_halo, halo_full, x_main, ua, ub, ha)
     tile, column = fine_masks(nz + 8, slots)
-    fill_edges(ca, ua, range(slots))
-    edge_e[...] = edges_of(lambda p: e[p], range(slots))
+    fill_edges(ca, ua, inside_slots(slots, 3))
+    edge_e[...] = edges_of(lambda p: e[p], inside_slots(slots, 3))
     main_weights(e, halo_e, w, 0, early(nx, 1), range(2, nx + 3))
     main_sweep(ua, ha, ub, w, e, force, 0, tile, beside, early(nx, 1))
     halo_weights(halo_e, edge_e, hw)
     halo_sweep(ha, ca, hb, hw, halo_e, halo_f, column)
-    fill_edges(cb, ub, range(3, nx + 3))
+    fill_edges(cb, ub, inside_slots(slots, 0, early(nx, 1)))
     main_sweep(ub, hb, ua, w, e, force, 0, tile, beside, early(nx, 2))
     halo_sweep(hb, cb, hc, hw, halo_e, halo_f, column)
     residuals(ua, hc, beside, w, force, e, summed, early_block(nx))
@@ -648,7 +662,7 @@
     halo_weights(halo_e, edge_e, hw)
     main_sweep(ua, ha, ub, w, e, force, 2, tile, beside, late(early(nx, 1)))
     halo_sweep(ha, ca, hb, hw, halo_e, halo_f, column)
-    fill_edges(cb, ub, [p for p in range(1, slots - 1) if not 4 <= p < nx + 2], False)
+    fill_edges(cb, ub, inside_slots(slots, 2, late(early(nx, 1))), False)
     main_sweep(ub, hb, ua, w, e, force, 1, tile, beside, late(early(nx, 2)))
     halo_sweep(hb, cb, ha, hw, halo_e, halo_f, column)
     residuals(ua, ha, beside, w, force, e, summed, late(early_block(nx)))
@@ -817,7 +831,8 @@
     half = LANES // 2
     _, zl, zr = place("gz")
     _, yl, yr = place("gy")
-    gx = lax.axis_index("gx")
+    two = lax.axis_size("gx") == 2
+    gx = FIXED[-1][0] if two else lax.axis_index("gx")
 
     def inside(rows, width):
         lane = iota((rows, LANES), 1)
@@ -885,6 +900,10 @@
         )
 
     def two_by_two(width, body):
+        if two:
+            for p in range(max(gx * own - width, 0), min(gx * own + own + width, planes)):
+                body(p + 1)
+            return
         lo = jnp.maximum(gx * own - width, 0)
         hi = jnp.minimum(gx * own + own + width, planes)
         steps = (hi - lo + 1) // 2
@@ -1006,7 +1025,7 @@
     masks = fine_masks(nz + 8, slots)
     for k in range(4):
         ha[k] = jnp.where(masks[1], ha[k] + column[k], 0.0)
-    fill_edges(ca, ua, range(1, slots - 1))
+    fill_edges(ca, ua, inside_slots(slots, 2))
     main_sweep(ua, ha, ub, w, e, force, 1, masks[0], beside)
     halo_sweep(ha, ca, hb, hw, halo_e, halo_f, masks[1])
 
@@ -1055,14 +1074,14 @@
     started += [(slots, rows, LANES)] * 6 + [spread, spread] + [column] * 3 + [(rows, LANES)]
     started += [(5, nx // 2, nz, LANES)]
     state = call(
-        pre_start,
+        by_sides(pre_start),
         started,
         [*staged, z_first, halo_first, x_main],
         [(7, rows, LANES), column, column, spread],
         cost=4,
     )
     *operator, fields, _, _, _, _, _, _, factors, own = call(
-        pre_smooth,
+        by_sides(pre_smooth),
         started + [(7, rows, LANES), (5, nx // 4, nz // 2, LANES)],
         [x_first, *state],
         [column, spread],
@@ -1105,7 +1124,7 @@
     planes = 2 * pairs
     plane = (shallow, LANES)
     grown, beside = call(
-        coarse_solve,
+        by_sides(coarse_solve),
         [(4, nx // 2 + 2, rows, LANES), (4, rows, LANES)],
         [full, full_e, y_a, y_b],
         [(4, planes + 2) + plane] * 2
@@ -1115,7 +1134,7 @@
         cost=4,
     )
     v_out, p_out = call(
-        post_smooth,
+        by_sides(post_smooth),
         [(3, nx) + block, (nx,) + block],
         operator + [fields, z_halo, halo_full, x_fine, x_rim, grown, beside],
         [spread] * 2 + [column] * 3 + [spread],

time: 43.6 us -> 41.7 us (0.956)
  Pallas kernels: 15 us -> 11.7 us
  waiting for transfers between devices: 11.1 us -> 13.9 us
  starting transfers between devices: 16.5 us -> 15.2 us
    pallas_call x13, Pallas kernels: 15 us -> 11.7 us  [call(): pl.pallas_call(body, out_shape=[jax.ShapeDtypeStruct(shape, F32) for shap...]
    ppermute x9, waiting for transfers between devices: 7.75 us -> 10.1 us  [swap(): return lax.ppermute(array, axis, pairs)]
    ppermute x9, starting transfers between devices: 11.7 us -> 10.4 us  [swap(): return lax.ppermute(array, axis, pairs)]
    ppermute x4, waiting for transfers between devices: 3.39 us -> 3.84 us  [swap(): return lax.ppermute(array, ('gy', 'gz'), pairs)]
  transfers between devices with their start and end apart: 13 -> 13, of which waited for: 5 -> 7; matrix products, arithmetic and copies ran while one was open for 0% -> 0% of each run, Pallas kernels for 17% -> 13%
where the time goes in v5:
time: 41.7 us; the launch traced here: 41.6 us
  starting transfers between devices  15.2 us (36%)
  waiting for transfers between devices  13.9 us (33%)
  Pallas kernels  11.7 us (28%)
  between operations  0.75 us (2%)
    pallas_call x13, Pallas kernels, call(): pl.pallas_call(body, out_shape=[jax.ShapeDtypeStruct(shape, F32) for shap...  11.7 us
    ppermute x9, starting transfers between devices, swap(): return lax.ppermute(array, axis, pairs)  10.4 us
    ppermute x9, waiting for transfers between devices, swap(): return lax.ppermute(array, axis, pairs)  10.1 us
    ppermute x4, starting transfers between devices, swap(): return lax.ppermute(array, ('gy', 'gz'), pairs)  4.86 us
    ppermute x4, waiting for transfers between devices, swap(): return lax.ppermute(array, ('gy', 'gz'), pairs)  3.84 us
  transfers between devices with their start and end apart: 13, of which 7 were waited for; matrix products, arithmetic and copies ran while one was open for 0% of the time, Pallas kernels for 13%

profile of v5, /device:TPU:0, one launch (start us, length us, event | category | flops | bytes accessed | tf_op | source)
XLA Modules:
  0.0 41.6 jit_solution(5830764667193450893)
XLA Ops:
  0.6 1.8 %shard_map.59 = (f32[4,32,128]{2,1,0:T(8,128)S(1)}, f32[4,32,128]{2,1,0:T(8,128)S(1)}, f32[4,32,128]{2,1,0:T(8,128)S(1)}, f32[4,32,128]{2,1,0:T(8,128)S(1)}, f32...) custom-call(f32[3,8,32,128]{3,2,1,0:T(8,128)} %v_in.1, ...), custom_call_target="tpu_custom_call" | custom-call | flops 1000000 | bytes 1000000 | tf_op jit(solution)/shard_map/pallas_call | solution.py:21
  2.5 3.0 %collective-permute-start.5 = (f32[1,21,32,128]{3,2,1,0:T(8,128)S(1)}, f32[1,21,32,128]{3,2,1,0:T(8,128)S(1)}, u32[]{:S(2)}, u32[]{:S(2)}) collective-permute-start(f32[1,21,32,128]{3,2,1,0:T(8,128)S(1)} %get-tuple-element.97), channel_id=1, source_target_pairs={{0,16},{16,0},{1,17},{17,1},{2,18},{18,2},{3,19},{19,3},{4,20},{20... | collective-permute-start | bytes 1032200 | tf_op jit(solution)/shard_map/ppermute | solution.py:56
  5.6 1.6 %collective-permute-start = (f32[2,32,128]{2,1,0:T(8,128)S(1)}, f32[2,32,128]{2,1,0:T(8,128)S(1)}, u32[]{:S(2)}, u32[]{:S(2)}) collective-permute-start(f32[2,32,128]{2,1,0:T(8,128)S(1)} %get-tuple-element.90), channel_id=1, source_target_pairs={{0,4},{4,0},{8,12},{12,8},{1,5},{5,1},{9,13},{13,9},{2,6},{6,2},{1... | collective-permute-start | bytes 98312 | tf_op jit(solution)/shard_map/ppermute | solution.py:56
  7.1 2.3 %collective-permute-done.y_a = f32[2,32,128]{2,1,0:T(8,128)S(1)} collective-permute-done((f32[2,32,128]{2,1,0:T(8,128)S(1)}, f32[2,32,128]{2,1,0:T(8,128)S(1)}, u32[]{:S(2)}, u32[]{:S(2)}) %collective-permute-start) | collective-permute-done | bytes 32800 | tf_op jit(solution)/shard_map/ppermute | solution.py:56
  9.7 2.8 %collective-permute-start.3 = (f32[24,8,128]{2,1,0:T(8,128)S(1)}, f32[24,8,128]{2,1,0:T(8,128)S(1)}, u32[]{:S(2)}, u32[]{:S(2)}) collective-permute-start(f32[24,8,128]{2,1,0:T(8,128)S(1)} %get-tuple-element.93), channel_id=1, source_target_pairs={{0,4},{1,2},{2,1},{3,7},{4,0},{5,6},{6,5},{7,3},{8,12},{9,10},{10,... | collective-permute-start | bytes 294920 | tf_op jit(solution)/shard_map/ppermute | solution.py:51
  12.5 2.6 %collective-permute-done.3.z_b = f32[24,8,128]{2,1,0:T(8,128)S(1)} collective-permute-done((f32[24,8,128]{2,1,0:T(8,128)S(1)}, f32[24,8,128]{2,1,0:T(8,128)S(1)}, u32[]{:S(2)}, u32[]{:S(2)}) %collective-permute-start.3) | collective-permute-done | bytes 98336 | tf_op jit(solution)/shard_map/ppermute | solution.py:51
  15.2 0.6 %collective-permute-start.4 = (f32[1,11,8,128]{3,2,1,0:T(8,128)S(1)}, f32[1,11,8,128]{3,2,1,0:T(8,128)S(1)}, u32[]{:S(2)}, u32[]{:S(2)}) collective-permute-start(f32[1,11,8,128]{3,2,1,0:T(8,128)S(1)} %get-tuple-element.94), channel_id=1, source_target_pairs={{0,16},{16,0},{1,17},{17,1},{2,18},{18,2},{3,19},{19,3},{4,20},{20... | collective-permute-start | bytes 135176 | tf_op jit(solution)/shard_map/ppermute | solution.py:56
  15.8 2.8 %shard_map.64 = (f32[14,40,128]{2,1,0:T(8,128)S(1)}, f32[40,128]{1,0:T(8,128)S(1)}, f32[3,14,40,128]{3,2,1,0:T(8,128)S(1)}, f32[3,40,128]{2,1,0:T(8,128)S(1)}, f...) custom-call(f32[4,32,128]{2,1,0:T(8,128)S(1)} %get-tuple-element.72., ...), custom_call_target="tpu_custom_call" | custom-call | flops 4000000 | bytes 4000000 | tf_op jit(solution)/shard_map/pallas_call | solution.py:21
  18.6 0.7 %collective-permute-done.4.refs_0_ = f32[1,11,8,128]{3,2,1,0:T(8,128)S(1)} collective-permute-done((f32[1,11,8,128]{3,2,1,0:T(8,128)S(1)}, f32[1,11,8,128]{3,2,1,0:T(8,128)S(1)}, u32[]{:S(2)}, u32[]{:S(2)}) %collective-permute-start.4) | collective-permute-done | bytes 45088 | tf_op jit(solution)/shard_map/ppermute | solution.py:56
  19.3 1.6 %shard_map.65 = (f32[14,40,128]{2,1,0:T(8,128)S(1)}, f32[40,128]{1,0:T(8,128)S(1)}, f32[3,14,40,128]{3,2,1,0:T(8,128)S(1)}, f32[3,40,128]{2,1,0:T(8,128)S(1)}, f...) custom-call(f32[1,11,8,128]{3,2,1,0:T(8,128)S(1)} %collective-permut, ...), custom_call_target="tpu_custom_call", output_to_operand_aliasing={{0}: (1, {}), {1}: (2, {}), {2}: (3, {}), {3}: (4, {}), {4}... | custom-call | flops 8000000 | bytes 8000000 | tf_op jit(solution)/shard_map/pallas_call | solution.py:21
  21.0 1.0 %collective-permute-start.6 = (f32[5,2,16,128]{3,2,1,0:T(8,128)S(1)}, f32[5,2,16,128]{3,2,1,0:T(8,128)S(1)}, u32[]{:S(2)}, u32[]{:S(2)}) collective-permute-start(f32[5,2,16,128]{3,2,1,0:T(8,128)S(1)} %get-tuple-element.127.own), channel_id=1, source_target_pairs={{0,16},{16,0},{1,17},{17,1},{2,18},{18,2},{3,19},{19,3},{4,20},{20... | collective-permute-start | bytes 245768 | tf_op jit(solution)/shard_map/ppermute | solution.py:56
  21.9 3.5 %collective-permute-done.6.other = f32[5,2,16,128]{3,2,1,0:T(8,128)S(1)} collective-permute-done((f32[5,2,16,128]{3,2,1,0:T(8,128)S(1)}, f32[5,2,16,128]{3,2,1,0:T(8,128)S(1)}, u32[]{:S(2)}, u32[]{:S(2)}) %collective-permute-start.6) | collective-permute-done | bytes 81952 | tf_op jit(solution)/shard_map/ppermute | solution.py:56
  25.6 2.1 %collective-permute-start.8 = (f32[20,8,128]{2,1,0:T(8,128)S(1)}, f32[20,8,128]{2,1,0:T(8,128)S(1)}, u32[]{:S(2)}, u32[]{:S(2)}) collective-permute-start(f32[20,8,128]{2,1,0:T(8,128)S(1)} %get-tuple-element.130), channel_id=1, source_target_pairs={{0,4},{1,2},{2,1},{3,7},{4,0},{5,6},{6,5},{7,3},{8,12},{9,10},{10,... | collective-permute-start | bytes 245768 | tf_op jit(solution)/shard_map/ppermute | solution.py:51
  27.7 0.2 shard_map.67
  27.9 1.0 %collective-permute-start.11 = (f32[1,8,32,128]{3,2,1,0:T(8,128)S(1)}, f32[1,8,32,128]{3,2,1,0:T(8,128)S(1)}, u32[]{:S(2)}, u32[]{:S(2)}) collective-permute-start(f32[1,8,32,128]{3,2,1,0:T(8,128)S(1)} %get-tuple-element.136), channel_id=1, source_target_pairs={{0,16},{16,0},{1,17},{17,1},{2,18},{18,2},{3,19},{19,3},{4,20},{20... | collective-permute-start | bytes 393224 | tf_op jit(solution)/shard_map/ppermute | solution.py:56
  28.9 1.2 %collective-permute-done.8.z_b = f32[20,8,128]{2,1,0:T(8,128)S(1)} collective-permute-done((f32[20,8,128]{2,1,0:T(8,128)S(1)}, f32[20,8,128]{2,1,0:T(8,128)S(1)}, u32[]{:S(2)}, u32[]{:S(2)}) %collective-permute-start.8) | collective-permute-done | bytes 81952 | tf_op jit(solution)/shard_map/ppermute | solution.py:51
  30.1 0.3 shard_map.68
  30.4 2.1 %collective-permute-start.9 = (f32[15,8,128]{2,1,0:T(8,128)S(1)}, f32[15,8,128]{2,1,0:T(8,128)S(1)}, u32[]{:S(2)}, u32[]{:S(2)}) collective-permute-start(f32[15,8,128]{2,1,0:T(8,128)S(1)} %get-tuple-element.133), channel_id=1, source_target_pairs={{0,4},{4,0},{8,12},{12,8},{1,5},{5,1},{9,13},{13,9},{2,6},{6,2},{1... | collective-permute-start | bytes 184328 | tf_op jit(solution)/shard_map/ppermute | solution.py:56
  32.5 2.3 %collective-permute-done.9.y_a.refs_2_ = f32[15,8,128]{2,1,0:T(8,128)S(1)} collective-permute-done((f32[15,8,128]{2,1,0:T(8,128)S(1)}, f32[15,8,128]{2,1,0:T(8,128)S(1)}, u32[]{:S(2)}, u32[]{:S(2)}) %collective-permute-start.9) | collective-permute-done | bytes 61472 | tf_op jit(solution)/shard_map/ppermute | solution.py:56
  34.9 0.2 shard_map.69
  35.0 1.0 %collective-permute-start.12 = (f32[1,6,8,128]{3,2,1,0:T(8,128)S(1)}, f32[1,6,8,128]{3,2,1,0:T(8,128)S(1)}, u32[]{:S(2)}, u32[]{:S(2)}) collective-permute-start(f32[1,6,8,128]{3,2,1,0:T(8,128)S(1)} %get-tuple-element.137), channel_id=1, source_target_pairs={{0,16},{16,0},{1,17},{17,1},{2,18},{18,2},{3,19},{19,3},{4,20},{20... | collective-permute-start | bytes 73736 | tf_op jit(solution)/shard_map/ppermute | solution.py:56
  36.0 1.7 %shard_map.70 = (f32[4,6,40,128]{3,2,1,0:T(8,128)S(1)}, f32[4,40,128]{2,1,0:T(8,128)S(1)}) custom-call(f32[4,4,24,128]{3,2,1,0:T(8,128)S(1)} %get-tuple-element.138.refs_0_, f32[4,32,128]{2,1,0:T(8,128)S(1)} %get-tuple-element.139.refs_1_, f32[15,8,128]{2,1,0:T(8,128)S(1)} %collective-permute-done.9.y_a.refs_2_, ...), custom_call_target="tpu_custom_call" | custom-call | flops 4000000 | bytes 4000000 | tf_op jit(solution)/shard_map/pallas_call | solution.py:21
  37.7 1.2 %collective-permute-done.12.refs_15_ = f32[1,6,8,128]{3,2,1,0:T(8,128)S(1)} collective-permute-done((f32[1,6,8,128]{3,2,1,0:T(8,128)S(1)}, f32[1,6,8,128]{3,2,1,0:T(8,128)S(1)}, u32[]{:S(2)}, u32[]{:S(2)}) %collective-permute-start.12) | collective-permute-done | bytes 24608 | tf_op jit(solution)/shard_map/ppermute | solution.py:56
  38.9 2.7 %shard_map.71 = (f32[3,8,32,128]{3,2,1,0:T(8,128)}, f32[8,32,128]{2,1,0:T(8,128)}) custom-call(f32[14,40,128]{2,1,0:T(8,128)S(1)} %get-tuple-element.115.refs_0_, f32[40,128]{1,0:T(8,128)S(1)} %get-tuple-element.116.refs_1_, f32[3,14,40,128]{3,2,1,0:T(8,128)S(1)} %get-tuple-element.117.refs_2_, f32[3,40,128]{2,1,0:T(8,128)S(1)} %get-tuple-element.118.refs_3_, ...), custom_call_target="tpu_custom_call" | custom-call | flops 8000000 | bytes 8000000 | tf_op jit(solution)/shard_map/pallas_call | solution.py:21
  (15 shorter events, 0.6 us)
Async XLA Ops:
  2.5 13.2 %collective-permute-start.5 = (f32[1,21,32,128]{3,2,1,0:T(8,128)S(1)}, f32[1,21,32,128]{3,2,1,0:T(8,128)S(1)}, u32[]{:S(2)}, u32[]{:S(2)}) collective-permute-start(f32[1,21,32,128]{3,2,1,0:T(8,128)S(1)} %get-tuple-element.97), channel_id=1, source_target_pairs={{0,16},{16,0},{1,17},{17,1},{2,18},{18,2},{3,19},{19,3},{4,20},{20... | collective-permute-start | bytes 1032200 | tf_op jit(solution)/shard_map/ppermute | solution.py:56
  5.6 3.9 %collective-permute-start = (f32[2,32,128]{2,1,0:T(8,128)S(1)}, f32[2,32,128]{2,1,0:T(8,128)S(1)}, u32[]{:S(2)}, u32[]{:S(2)}) collective-permute-start(f32[2,32,128]{2,1,0:T(8,128)S(1)} %get-tuple-element.90), channel_id=1, source_target_pairs={{0,4},{4,0},{8,12},{12,8},{1,5},{5,1},{9,13},{13,9},{2,6},{6,2},{1... | collective-permute-start | bytes 98312 | tf_op jit(solution)/shard_map/ppermute | solution.py:56
  7.1 2.3 %collective-permute-start.1 = (f32[2,32,128]{2,1,0:T(8,128)S(1)}, f32[2,32,128]{2,1,0:T(8,128)S(1)}, u32[]{:S(2)}, u32[]{:S(2)}) collective-permute-start(f32[2,32,128]{2,1,0:T(8,128)S(1)} %get-tuple-element.91), channel_id=1, source_target_pairs={{0,1},{1,0},{2,3},{3,2},{4,8},{5,9},{6,10},{7,11},{8,4},{9,5},{10,... | collective-permute-start | bytes 98312 | tf_op jit(solution)/shard_map/ppermute | solution.py:51
  9.6 2.8 %collective-permute-start.2 = (f32[24,8,128]{2,1,0:T(8,128)S(1)}, f32[24,8,128]{2,1,0:T(8,128)S(1)}, u32[]{:S(2)}, u32[]{:S(2)}) collective-permute-start(f32[24,8,128]{2,1,0:T(8,128)S(1)} %shard_map.62), channel_id=1, source_target_pairs={{0,1},{1,0},{2,3},{3,2},{4,5},{5,4},{6,7},{7,6},{8,9},{9,8},{10,11... | collective-permute-start | bytes 294920 | tf_op jit(solution)/shard_map/ppermute | solution.py:56
  9.7 5.4 %collective-permute-start.3 = (f32[24,8,128]{2,1,0:T(8,128)S(1)}, f32[24,8,128]{2,1,0:T(8,128)S(1)}, u32[]{:S(2)}, u32[]{:S(2)}) collective-permute-start(f32[24,8,128]{2,1,0:T(8,128)S(1)} %get-tuple-element.93), channel_id=1, source_target_pairs={{0,4},{1,2},{2,1},{3,7},{4,0},{5,6},{6,5},{7,3},{8,12},{9,10},{10,... | collective-permute-start | bytes 294920 | tf_op jit(solution)/shard_map/ppermute | solution.py:51
  15.2 4.1 %collective-permute-start.4 = (f32[1,11,8,128]{3,2,1,0:T(8,128)S(1)}, f32[1,11,8,128]{3,2,1,0:T(8,128)S(1)}, u32[]{:S(2)}, u32[]{:S(2)}) collective-permute-start(f32[1,11,8,128]{3,2,1,0:T(8,128)S(1)} %get-tuple-element.94), channel_id=1, source_target_pairs={{0,16},{16,0},{1,17},{17,1},{2,18},{18,2},{3,19},{19,3},{4,20},{20... | collective-permute-start | bytes 135176 | tf_op jit(solution)/shard_map/ppermute | solution.py:56
  21.0 4.5 %collective-permute-start.6 = (f32[5,2,16,128]{3,2,1,0:T(8,128)S(1)}, f32[5,2,16,128]{3,2,1,0:T(8,128)S(1)}, u32[]{:S(2)}, u32[]{:S(2)}) collective-permute-start(f32[5,2,16,128]{3,2,1,0:T(8,128)S(1)} %get-tuple-element.127.own), channel_id=1, source_target_pairs={{0,16},{16,0},{1,17},{17,1},{2,18},{18,2},{3,19},{19,3},{4,20},{20... | collective-permute-start | bytes 245768 | tf_op jit(solution)/shard_map/ppermute | solution.py:56
  25.5 3.3 %collective-permute-start.7 = (f32[20,8,128]{2,1,0:T(8,128)S(1)}, f32[20,8,128]{2,1,0:T(8,128)S(1)}, u32[]{:S(2)}, u32[]{:S(2)}) collective-permute-start(f32[20,8,128]{2,1,0:T(8,128)S(1)} %get-tuple-element.129), channel_id=1, source_target_pairs={{0,1},{1,0},{2,3},{3,2},{4,5},{5,4},{6,7},{7,6},{8,9},{9,8},{10,11... | collective-permute-start | bytes 245768 | tf_op jit(solution)/shard_map/ppermute | solution.py:56
  25.6 4.5 %collective-permute-start.8 = (f32[20,8,128]{2,1,0:T(8,128)S(1)}, f32[20,8,128]{2,1,0:T(8,128)S(1)}, u32[]{:S(2)}, u32[]{:S(2)}) collective-permute-start(f32[20,8,128]{2,1,0:T(8,128)S(1)} %get-tuple-element.130), channel_id=1, source_target_pairs={{0,4},{1,2},{2,1},{3,7},{4,0},{5,6},{6,5},{7,3},{8,12},{9,10},{10,... | collective-permute-start | bytes 245768 | tf_op jit(solution)/shard_map/ppermute | solution.py:51
  27.9 9.8 %collective-permute-start.11 = (f32[1,8,32,128]{3,2,1,0:T(8,128)S(1)}, f32[1,8,32,128]{3,2,1,0:T(8,128)S(1)}, u32[]{:S(2)}, u32[]{:S(2)}) collective-permute-start(f32[1,8,32,128]{3,2,1,0:T(8,128)S(1)} %get-tuple-element.136), channel_id=1, source_target_pairs={{0,16},{16,0},{1,17},{17,1},{2,18},{18,2},{3,19},{19,3},{4,20},{20... | collective-permute-start | bytes 393224 | tf_op jit(solution)/shard_map/ppermute | solution.py:56
  30.4 4.4 %collective-permute-start.9 = (f32[15,8,128]{2,1,0:T(8,128)S(1)}, f32[15,8,128]{2,1,0:T(8,128)S(1)}, u32[]{:S(2)}, u32[]{:S(2)}) collective-permute-start(f32[15,8,128]{2,1,0:T(8,128)S(1)} %get-tuple-element.133), channel_id=1, source_target_pairs={{0,4},{4,0},{8,12},{12,8},{1,5},{5,1},{9,13},{13,9},{2,6},{6,2},{1... | collective-permute-start | bytes 184328 | tf_op jit(solution)/shard_map/ppermute | solution.py:56
  32.5 2.3 %collective-permute-start.10 = (f32[15,8,128]{2,1,0:T(8,128)S(1)}, f32[15,8,128]{2,1,0:T(8,128)S(1)}, u32[]{:S(2)}, u32[]{:S(2)}) collective-permute-start(f32[15,8,128]{2,1,0:T(8,128)S(1)} %get-tuple-element.134), channel_id=1, source_target_pairs={{0,1},{1,0},{2,3},{3,2},{4,8},{5,9},{6,10},{7,11},{8,4},{9,5},{10,... | collective-permute-start | bytes 184328 | tf_op jit(solution)/shard_map/ppermute | solution.py:51
  35.0 3.9 %collective-permute-start.12 = (f32[1,6,8,128]{3,2,1,0:T(8,128)S(1)}, f32[1,6,8,128]{3,2,1,0:T(8,128)S(1)}, u32[]{:S(2)}, u32[]{:S(2)}) collective-permute-start(f32[1,6,8,128]{3,2,1,0:T(8,128)S(1)} %get-tuple-element.137), channel_id=1, source_target_pairs={{0,16},{16,0},{1,17},{17,1},{2,18},{18,2},{3,19},{19,3},{4,20},{20... | collective-permute-start | bytes 73736 | tf_op jit(solution)/shard_map/ppermute | solution.py:56

commit v6 on v5

--- a/solution.py
+++ b/solution.py
@@ -746,19 +746,26 @@
     return jnp.concatenate([x[:own], halo], axis=0)
 
 
-def deep_edges(pairs):
-    per = LANES // 16
+def deep_edges(pairs, width):
+    per = LANES // (2 * width)
     columns = []
     for n, x in enumerate(pairs):
         for g in range(2):
             t = (2 * n + g) % per
-            x_t = roll(x, 16 * t + 8 - 64 * g, 1)
+            x_t = roll(x, 2 * width * t + width - 64 * g, 1)
             if t == 0:
                 columns.append(x_t)
             else:
-                slot = iota(x.shape, 1) // 16
+                slot = iota(x.shape, 1) // (2 * width)
                 columns[-1] = jnp.where(slot == t, x_t, columns[-1])
     return columns
+
+
+def unfold(left, right, width):
+    spot = iota(left.shape, 1) % (2 * width)
+    first = jnp.where(spot < width, left, roll(right, width, 1))
+    second = jnp.where(spot < width, roll(left, -width, 1), right)
+    return first, second
 
 
 def fifth_pack(whole, z_a, z_b, edges, full, full_e, z_halo, y_a, y_b):
@@ -789,15 +796,16 @@
         for k in range(4):
             x = jnp.where(row < 2 * has_right, roll(right, -2 * k, 0), 0.0)
             z_halo[k, q] = jnp.where(row >= 8 - 2 * has_left, roll(left, 6 - 2 * k, 0), x)
-    columns = deep_edges(deep[: 4 * pairs])
+    columns = deep_edges(deep[: 4 * pairs], 4)
     half = len(columns) // 2
-    columns_e = deep_edges(deep[4 * pairs :])
+    columns_e = deep_edges(deep[4 * pairs :], 8)
+    upper = (cz + 16) // 2
     behind = pair_edges(lambda i: [z_halo[i, q] for q in range(nx)], 4, 8)
     for m, out in enumerate((y_a, y_b)):
         toward = high_side("gy", m)
         parts = [
-            strip(columns[j], columns[j + half], toward, 8) for j in range(half)
-        ] + columns_e
+            strip(columns[j], columns[j + half], toward, 4) for j in range(half)
+        ] + [strip(x[:upper], x[upper:], toward, 8) for x in columns_e]
         for i in range(nz // 8):
             parts.append(y_strip(edges[0, pl.ds(8 * i, 8)], edges[1, pl.ds(8 * i, 8)], toward))
         parts.append(y_strip(behind[0], behind[1], toward))
@@ -838,7 +846,7 @@
         lane = iota((rows, LANES), 1)
         row = iota((rows, LANES), 0)
         kept = (row < cz + width * zr) | (row >= rows - width * zl)
-        return kept & ((lane < half + SLOT * yr) | (lane >= LANES - SLOT * yl))
+        return kept & ((lane < half + width * yr) | (lane >= LANES - width * yl))
 
     zero = jnp.zeros((rows, LANES), F32)
     w = (w0, w1, w2, w3, w4, w5)
@@ -851,44 +859,39 @@
     deep_e[0] = jnp.zeros((deep, LANES), F32)
     deep_e[planes + 1] = jnp.zeros((deep, LANES), F32)
 
-    tiles, deep_tiles = rows // 8, deep // 8
-    count = pairs // 2
+    tiles, deep_tiles = rows // 8, deep // 16
+    count = pairs // 4
     columns = []
 
-    def taken(ref, n, tiles):
-        return jnp.concatenate([ref[n + i] for i in range(tiles)], axis=0)
-
-    seconds = []
-    for j in range(count):
-        left, right = left_right("gy", taken(y_a, j * tiles, tiles), taken(y_b, j * tiles, tiles))
-        spot = iota(left.shape, 1) % 16
-        columns.append(jnp.where(spot < 8, left, roll(right, 8, 1)))
-        seconds.append(jnp.where(spot < 8, roll(left, -8, 1), right))
-    columns += seconds
+    def taken(n, tiles):
+        a, b = (jnp.concatenate([ref[n + i] for i in range(tiles)], axis=0) for ref in (y_a, y_b))
+        return left_right("gy", a, b)
+
+    unfolded = [unfold(*taken(j * tiles, tiles), 4) for j in range(count)]
+    columns = [x for x, _ in unfolded] + [x for _, x in unfolded]
     columns_e = []
     for j in range(-(-pairs // 4)):
-        n = count * tiles + j * deep_tiles
-        left, right = left_right("gy", taken(y_a, n, deep_tiles), taken(y_b, n, deep_tiles))
-        spot = iota(left.shape, 1) % 16
-        columns_e.append(jnp.where(spot < 8, left, right))
-
-    def whole_plane(pair, columns, n, s):
+        x = unfold(*taken(count * tiles + j * deep_tiles, deep_tiles), 8)
+        columns_e.append(jnp.concatenate(x, axis=0))
+
+    def whole_plane(pair, columns, n, s, width):
         lane = iota(pair.shape, 1)
+        per = LANES // (2 * width)
         last, first = 2 * n + 1 - s, 2 * n + s
-        low = roll(columns[first // 8], half - 16 * (first % 8) - 8, 1)
-        high = roll(columns[last // 8], LANES - 8 - 16 * (last % 8), 1)
+        low = roll(columns[first // per], half - 2 * width * (first % per) - width, 1)
+        high = roll(columns[last // per], LANES - width - 2 * width * (last % per), 1)
         x = jnp.where(lane < half, roll(pair, -s * half, 1), low)
-        return jnp.where(lane < LANES - 8, x, high)
+        return jnp.where(lane < LANES - width, x, high)
 
     near, far = inside(rows, 4), inside(deep, 8)
     for r in range(pairs):
         for s in range(2):
             p = 2 * r + s
-            x = jnp.where(far, whole_plane(full_e[r], columns_e, r, s), 0.0)
+            x = jnp.where(far, whole_plane(full_e[r], columns_e, r, s, 8), 0.0)
             deep_e[p + 1] = x
             e[p + 1] = fold_rows(x)
             for k in range(4):
-                x = whole_plane(full[k, r], columns, k * pairs + r, s)
+                x = whole_plane(full[k, r], columns, k * pairs + r, s, 4)
                 force[k, p] = jnp.where(near, x, 0.0)
 
     def shifts(x):
@@ -988,15 +991,16 @@
         grow(halo, (k,), column[k * rows : (k + 1) * rows])
 
 
-def post_smooth(
+def post_start(
     e, halo_e, force, halo_f, w0, w1, w2, w3, w4, w5, hw,
-    fields, z_halo, halo_full, x_fine, x_rim, main, column, v_out, p_out,
-    ua, ub, ha, hb, ca, beside,
+    fields, z_halo, halo_full, x_fine, main, column, ua, ub, ha, ca, part,
+    hb, beside,
 ):
-    nx, nz, _ = p_out.shape
+    _, nx, nz, _ = part.shape
     slots = nx + 6
     w = (w0, w1, w2, w3, w4, w5)
     zero = jnp.zeros((nz + 8, LANES), F32)
+    tile, inside = fine_masks(nz + 8, slots)
     for k in range(4):
         for p in (1, 2, nx + 3, nx + 4):
             ua[k, p] = zero
@@ -1005,40 +1009,80 @@
             i = q // 2 + 1
             ua[k, q + 3, pl.ds(0, nz)] = fields[k, q + 3, pl.ds(0, nz)] + main[k, i, pl.ds(0, nz)]
             ua[k, q + 3, pl.ds(nz, 8)] = z_halo[k, q] + main[k, i, pl.ds(nz, 8)]
-        ha[k] = own_slots(halo_full[k % 2], nx, k // 2)
+        x = own_slots(halo_full[k % 2], nx, k // 2) + column[k]
+        ha[k] = jnp.where(inside, x, 0.0)
     for m in range(x_fine.shape[0]):
         right, valid = x_side(m)
         there = truth(valid, (nz, LANES))
         there8 = truth(valid, (8, LANES))
-        tiles = (nz + 8) // 8
-        side = jnp.concatenate([x_rim[m, 1 + r] for r in range(tiles)], axis=0)
         i = right * (nx // 2 + 1)
         for k in range(4):
             for j in range(2):
                 at = 1 + right * (nx + 2) + j
                 x = x_fine[m, 2 * k + j] + main[k, i, pl.ds(0, nz)]
                 ua[k, at, pl.ds(0, nz)] = jnp.where(there, x, 0.0)
-            x = roll(x_rim[m, 0], -2 * k, 0) + main[k, i, pl.ds(nz, 8)]
-            ua[k, 2 + right * (nx + 1), pl.ds(nz, 8)] = jnp.where(there8, x, 0.0)
-            x, kept = rim_halo(side, k, SLOT, 1, right, valid, nx)
-            ha[k] = jnp.where(kept, x, ha[k])
-    masks = fine_masks(nz + 8, slots)
-    for k in range(4):
-        ha[k] = jnp.where(masks[1], ha[k] + column[k], 0.0)
+            x = jnp.where(there8, main[k, i, pl.ds(nz, 8)], 0.0)
+            ua[k, 2 + right * (nx + 1), pl.ds(nz, 8)] = x
     fill_edges(ca, ua, inside_slots(slots, 2))
-    main_sweep(ua, ha, ub, w, e, force, 1, masks[0], beside)
-    halo_sweep(ha, ca, hb, hw, halo_e, halo_f, masks[1])
-
-    spread_halo(hb, beside, slots, 0, full=False)
-
-    def last(p):
-        new = main_operator(ub, beside, w, force, p, nz)
-        new = relaxed(*new, w5[p, pl.ds(0, nz)], e[p, pl.ds(0, nz)])
-        for k in range(3):
-            v_out[k, p - 3] = new[k]
-        p_out[p - 3] = new[3]
-
-    over_planes(slots, 0, last)
+    main_sweep(ua, ha, ub, w, e, force, 0, tile, beside, early(nx, 1))
+    halo_sweep(ha, ca, hb, hw, halo_e, halo_f, inside)
+
+    def store(p, k, x):
+        part[k, p - 3] = x
+
+    last_sweep(ub, hb, beside, w, e, force, early(nx, 2), store)
+
+
+def last_sweep(src, halo, beside, w, e, force, chosen, store):
+    slots, nz = src.shape[1], src.shape[2] - 8
+    spread_halo(halo, beside, slots, 0, chosen, False)
+
+    def body(p):
+        new = main_operator(src, beside, w, force, p, nz)
+        new = relaxed(*new, w[5][p, pl.ds(0, nz)], e[p, pl.ds(0, nz)])
+        for k in range(4):
+            store(p, k, new[k])
+
+    over_planes(slots, 0, body, chosen)
+
+
+def post_smooth(
+    x_rim, part, e, halo_e, force, halo_f, w0, w1, w2, w3, w4, w5, hw,
+    _ua, _ub, _ha, _ca, v_out, p_out, ua, ub, ha, ca,
+    hb, beside,
+):
+    nx, nz, _ = p_out.shape
+    slots = nx + 6
+    w = (w0, w1, w2, w3, w4, w5)
+    tile, inside = fine_masks(nz + 8, slots)
+    tail = pl.ds(nz, 8)
+    slot = iota((8, LANES), 1) // SLOT
+    for m in range(x_rim.shape[0]):
+        right, valid = x_side(m)
+        there = truth(valid, (8, LANES))
+        tiles = (nz + 8) // 8
+        side = jnp.concatenate([x_rim[m, 1 + r] for r in range(tiles)], axis=0)
+        near = 2 + right * (nx + 1)
+        for k in range(4):
+            x = ua[k, near, tail] + jnp.where(there, roll(x_rim[m, 0], -2 * k, 0), 0.0)
+            ua[k, near, tail] = x
+            ca[k, tail] = jnp.where(slot == near, roll(x, near * SLOT + 4, 1), ca[k, tail])
+            x, _ = rim_halo(side, k, SLOT, 1, right, valid, nx)
+            ha[k] = ha[k] + x
+    main_sweep(ua, ha, ub, w, e, force, 1, tile, beside, late(early(nx, 1)))
+    halo_sweep(ha, ca, hb, hw, halo_e, halo_f, inside)
+
+    def store(p, k, x):
+        if k < 3:
+            v_out[k, p - 3] = x
+        else:
+            p_out[p - 3] = x
+
+    last_sweep(ub, hb, beside, w, e, force, late(early(nx, 2)), store)
+    for q in range(nx):
+        if early(nx, 2)(q + 3):
+            for k in range(4):
+                store(q + 3, k, part[k, q])
 
 
 def local(velocity, pressure, viscosity, body_force):
@@ -1108,7 +1152,7 @@
     z_a, z_b = swap(z_a, "gz", 0), swap(z_b, "gz", 1)
     deep = nz // 2 + 16
     shallow = deep - 8
-    y_shape = (pairs // 2 * (shallow // 8) + -(-pairs // 4) * (deep // 8) + tiles, 8, LANES)
+    y_shape = (pairs // 4 * (shallow // 8) + -(-pairs // 4) * (deep // 16) + tiles, 8, LANES)
     full, full_e, z_halo, y_a, y_b = call(
         fifth_pack,
         [(4, pairs, shallow, LANES), (pairs, deep, LANES), (4, nx, 8, LANES), y_shape, y_shape],
@@ -1133,12 +1177,21 @@
         + [(planes + 2, deep, LANES), (16, LANES)],
         cost=4,
     )
-    v_out, p_out = call(
+    *state, part = call(
+        by_sides(post_start),
+        [spread, spread, column, column, (4, nx) + block],
+        operator + [fields, z_halo, halo_full, x_fine, grown, beside],
+        [column, spread],
+        cost=4,
+    )
+    first = 2 + len(operator)
+    v_out, p_out, *_ = call(
         by_sides(post_smooth),
-        [(3, nx) + block, (nx,) + block],
-        operator + [fields, z_halo, halo_full, x_fine, x_rim, grown, beside],
-        [spread] * 2 + [column] * 3 + [spread],
+        [(3, nx) + block, (nx,) + block, spread, spread, column, column],
+        [x_rim, part] + operator + state,
+        [column, spread],
         cost=8,
+        aliases={first + i: 2 + i for i in range(4)},
     )
     return v_out, p_out
 

time: 41.7 us -> 40.7 us (0.976)
  waiting for transfers between devices: 13.9 us -> 12.5 us
  Pallas kernels: 11.7 us -> 12.2 us
    ppermute x9, waiting for transfers between devices: 10.1 us -> 8.59 us  [swap(): return lax.ppermute(array, axis, pairs)]
    pallas_call x13 -> x14, Pallas kernels: 11.7 us -> 12.2 us  [call(): pl.pallas_call(body, out_shape=[jax.ShapeDtypeStruct(shape, F32) for shap...]
  transfers between devices with their start and end apart: 13 -> 13, of which waited for: 7 -> 6; matrix products, arithmetic and copies ran while one was open for 0% -> 0% of each run, Pallas kernels for 13% -> 17%
where the time goes in v6:
time: 40.7 us; the launch traced here: 40.6 us
  starting transfers between devices  15.1 us (37%)
  waiting for transfers between devices  12.5 us (31%)
  Pallas kernels  12.2 us (30%)
  between operations  0.76 us (2%)
    pallas_call x14, Pallas kernels, call(): pl.pallas_call(body, out_shape=[jax.ShapeDtypeStruct(shape, F32) for shap...  12.2 us
    ppermute x9, starting transfers between devices, swap(): return lax.ppermute(array, axis, pairs)  10.3 us
    ppermute x9, waiting for transfers between devices, swap(): return lax.ppermute(array, axis, pairs)  8.59 us
    ppermute x4, starting transfers between devices, swap(): return lax.ppermute(array, ('gy', 'gz'), pairs)  4.86 us
    ppermute x4, waiting for transfers between devices, swap(): return lax.ppermute(array, ('gy', 'gz'), pairs)  3.86 us
  transfers between devices with their start and end apart: 13, of which 6 were waited for; matrix products, arithmetic and copies ran while one was open for 0% of the time, Pallas kernels for 17%

profile of v6, /device:TPU:0, one launch (start us, length us, event | category | flops | bytes accessed | tf_op | source)
XLA Modules:
  0.0 40.6 jit_solution(3095679647880057430)
XLA Ops:
  0.6 1.8 %shard_map.59 = (f32[4,32,128]{2,1,0:T(8,128)S(1)}, f32[4,32,128]{2,1,0:T(8,128)S(1)}, f32[4,32,128]{2,1,0:T(8,128)S(1)}, f32[4,32,128]{2,1,0:T(8,128)S(1)}, f32...) custom-call(f32[3,8,32,128]{3,2,1,0:T(8,128)} %v_in.1, ...), custom_call_target="tpu_custom_call" | custom-call | flops 1000000 | bytes 1000000 | tf_op jit(solution)/shard_map/pallas_call | solution.py:21
  2.5 3.0 %collective-permute-start.5 = (f32[1,21,32,128]{3,2,1,0:T(8,128)S(1)}, f32[1,21,32,128]{3,2,1,0:T(8,128)S(1)}, u32[]{:S(2)}, u32[]{:S(2)}) collective-permute-start(f32[1,21,32,128]{3,2,1,0:T(8,128)S(1)} %get-tuple-element.104), channel_id=1, source_target_pairs={{0,16},{16,0},{1,17},{17,1},{2,18},{18,2},{3,19},{19,3},{4,20},{20... | collective-permute-start | bytes 1032200 | tf_op jit(solution)/shard_map/ppermute | solution.py:56
  5.6 1.6 %collective-permute-start = (f32[2,32,128]{2,1,0:T(8,128)S(1)}, f32[2,32,128]{2,1,0:T(8,128)S(1)}, u32[]{:S(2)}, u32[]{:S(2)}) collective-permute-start(f32[2,32,128]{2,1,0:T(8,128)S(1)} %get-tuple-element.97), channel_id=1, source_target_pairs={{0,4},{4,0},{8,12},{12,8},{1,5},{5,1},{9,13},{13,9},{2,6},{6,2},{1... | collective-permute-start | bytes 98312 | tf_op jit(solution)/shard_map/ppermute | solution.py:56
  7.1 2.3 %collective-permute-done.y_a = f32[2,32,128]{2,1,0:T(8,128)S(1)} collective-permute-done((f32[2,32,128]{2,1,0:T(8,128)S(1)}, f32[2,32,128]{2,1,0:T(8,128)S(1)}, u32[]{:S(2)}, u32[]{:S(2)}) %collective-permute-start) | collective-permute-done | bytes 32800 | tf_op jit(solution)/shard_map/ppermute | solution.py:56
  9.7 2.8 %collective-permute-start.3 = (f32[24,8,128]{2,1,0:T(8,128)S(1)}, f32[24,8,128]{2,1,0:T(8,128)S(1)}, u32[]{:S(2)}, u32[]{:S(2)}) collective-permute-start(f32[24,8,128]{2,1,0:T(8,128)S(1)} %get-tuple-element.100), channel_id=1, source_target_pairs={{0,4},{1,2},{2,1},{3,7},{4,0},{5,6},{6,5},{7,3},{8,12},{9,10},{10,... | collective-permute-start | bytes 294920 | tf_op jit(solution)/shard_map/ppermute | solution.py:51
  12.5 2.6 %collective-permute-done.3.z_b = f32[24,8,128]{2,1,0:T(8,128)S(1)} collective-permute-done((f32[24,8,128]{2,1,0:T(8,128)S(1)}, f32[24,8,128]{2,1,0:T(8,128)S(1)}, u32[]{:S(2)}, u32[]{:S(2)}) %collective-permute-start.3) | collective-permute-done | bytes 98336 | tf_op jit(solution)/shard_map/ppermute | solution.py:51
  15.2 0.6 %collective-permute-start.4 = (f32[1,11,8,128]{3,2,1,0:T(8,128)S(1)}, f32[1,11,8,128]{3,2,1,0:T(8,128)S(1)}, u32[]{:S(2)}, u32[]{:S(2)}) collective-permute-start(f32[1,11,8,128]{3,2,1,0:T(8,128)S(1)} %get-tuple-element.101), channel_id=1, source_target_pairs={{0,16},{16,0},{1,17},{17,1},{2,18},{18,2},{3,19},{19,3},{4,20},{20... | collective-permute-start | bytes 135176 | tf_op jit(solution)/shard_map/ppermute | solution.py:56
  15.8 2.8 %shard_map.64 = (f32[14,40,128]{2,1,0:T(8,128)S(1)}, f32[40,128]{1,0:T(8,128)S(1)}, f32[3,14,40,128]{3,2,1,0:T(8,128)S(1)}, f32[3,40,128]{2,1,0:T(8,128)S(1)}, f...) custom-call(f32[4,32,128]{2,1,0:T(8,128)S(1)} %get-tuple-element.79., ...), custom_call_target="tpu_custom_call" | custom-call | flops 4000000 | bytes 4000000 | tf_op jit(solution)/shard_map/pallas_call | solution.py:21
  18.6 0.7 %collective-permute-done.4.refs_0_ = f32[1,11,8,128]{3,2,1,0:T(8,128)S(1)} collective-permute-done((f32[1,11,8,128]{3,2,1,0:T(8,128)S(1)}, f32[1,11,8,128]{3,2,1,0:T(8,128)S(1)}, u32[]{:S(2)}, u32[]{:S(2)}) %collective-permute-start.4) | collective-permute-done | bytes 45088 | tf_op jit(solution)/shard_map/ppermute | solution.py:56
  19.3 1.6 %shard_map.65 = (f32[14,40,128]{2,1,0:T(8,128)S(1)}, f32[40,128]{1,0:T(8,128)S(1)}, f32[3,14,40,128]{3,2,1,0:T(8,128)S(1)}, f32[3,40,128]{2,1,0:T(8,128)S(1)}, f...) custom-call(f32[1,11,8,128]{3,2,1,0:T(8,128)S(1)} %collective-permut, ...), custom_call_target="tpu_custom_call", output_to_operand_aliasing={{0}: (1, {}), {1}: (2, {}), {2}: (3, {}), {3}: (4, {}), {4}... | custom-call | flops 8000000 | bytes 8000000 | tf_op jit(solution)/shard_map/pallas_call | solution.py:21
  21.0 1.0 %collective-permute-start.6 = (f32[5,2,16,128]{3,2,1,0:T(8,128)S(1)}, f32[5,2,16,128]{3,2,1,0:T(8,128)S(1)}, u32[]{:S(2)}, u32[]{:S(2)}) collective-permute-start(f32[5,2,16,128]{3,2,1,0:T(8,128)S(1)} %get-tuple-element.122.own), channel_id=1, source_target_pairs={{0,16},{16,0},{1,17},{17,1},{2,18},{18,2},{3,19},{19,3},{4,20},{20... | collective-permute-start | bytes 245768 | tf_op jit(solution)/shard_map/ppermute | solution.py:56
  21.9 3.6 %collective-permute-done.6.other = f32[5,2,16,128]{3,2,1,0:T(8,128)S(1)} collective-permute-done((f32[5,2,16,128]{3,2,1,0:T(8,128)S(1)}, f32[5,2,16,128]{3,2,1,0:T(8,128)S(1)}, u32[]{:S(2)}, u32[]{:S(2)}) %collective-permute-start.6) | collective-permute-done | bytes 81952 | tf_op jit(solution)/shard_map/ppermute | solution.py:56
  25.6 2.1 %collective-permute-start.8 = (f32[20,8,128]{2,1,0:T(8,128)S(1)}, f32[20,8,128]{2,1,0:T(8,128)S(1)}, u32[]{:S(2)}, u32[]{:S(2)}) collective-permute-start(f32[20,8,128]{2,1,0:T(8,128)S(1)} %get-tuple-element.126), channel_id=1, source_target_pairs={{0,4},{1,2},{2,1},{3,7},{4,0},{5,6},{6,5},{7,3},{8,12},{9,10},{10,... | collective-permute-start | bytes 245768 | tf_op jit(solution)/shard_map/ppermute | solution.py:51
  27.7 0.2 shard_map.67
  27.9 1.0 %collective-permute-start.12 = (f32[1,8,32,128]{3,2,1,0:T(8,128)S(1)}, f32[1,8,32,128]{3,2,1,0:T(8,128)S(1)}, u32[]{:S(2)}, u32[]{:S(2)}) collective-permute-start(f32[1,8,32,128]{3,2,1,0:T(8,128)S(1)} %get-tuple-element.144), channel_id=1, source_target_pairs={{0,16},{16,0},{1,17},{17,1},{2,18},{18,2},{3,19},{19,3},{4,20},{20... | collective-permute-start | bytes 393224 | tf_op jit(solution)/shard_map/ppermute | solution.py:56
  28.9 1.3 %collective-permute-done.8.z_b = f32[20,8,128]{2,1,0:T(8,128)S(1)} collective-permute-done((f32[20,8,128]{2,1,0:T(8,128)S(1)}, f32[20,8,128]{2,1,0:T(8,128)S(1)}, u32[]{:S(2)}, u32[]{:S(2)}) %collective-permute-start.8) | collective-permute-done | bytes 81952 | tf_op jit(solution)/shard_map/ppermute | solution.py:51
  30.1 0.3 shard_map.68
  30.5 2.1 %collective-permute-start.9 = (f32[10,8,128]{2,1,0:T(8,128)S(1)}, f32[10,8,128]{2,1,0:T(8,128)S(1)}, u32[]{:S(2)}, u32[]{:S(2)}) collective-permute-start(f32[10,8,128]{2,1,0:T(8,128)S(1)} %get-tuple-element.128), channel_id=1, source_target_pairs={{0,4},{4,0},{8,12},{12,8},{1,5},{5,1},{9,13},{13,9},{2,6},{6,2},{1... | collective-permute-start | bytes 122888 | tf_op jit(solution)/shard_map/ppermute | solution.py:56
  32.5 2.0 %collective-permute-done.9.y_a.refs_2_ = f32[10,8,128]{2,1,0:T(8,128)S(1)} collective-permute-done((f32[10,8,128]{2,1,0:T(8,128)S(1)}, f32[10,8,128]{2,1,0:T(8,128)S(1)}, u32[]{:S(2)}, u32[]{:S(2)}) %collective-permute-start.9) | collective-permute-done | bytes 40992 | tf_op jit(solution)/shard_map/ppermute | solution.py:56
  34.5 0.2 shard_map.69
  34.7 1.0 %collective-permute-start.11 = (f32[1,6,8,128]{3,2,1,0:T(8,128)S(1)}, f32[1,6,8,128]{3,2,1,0:T(8,128)S(1)}, u32[]{:S(2)}, u32[]{:S(2)}) collective-permute-start(f32[1,6,8,128]{3,2,1,0:T(8,128)S(1)} %get-tuple-element.131), channel_id=1, source_target_pairs={{0,16},{16,0},{1,17},{17,1},{2,18},{18,2},{3,19},{19,3},{4,20},{20... | collective-permute-start | bytes 73736 | tf_op jit(solution)/shard_map/ppermute | solution.py:56
  35.6 1.7 %shard_map.70 = (f32[4,6,40,128]{3,2,1,0:T(8,128)S(1)}, f32[4,40,128]{2,1,0:T(8,128)S(1)}) custom-call(f32[4,4,24,128]{3,2,1,0:T(8,128)S(1)} %get-tuple-element.145.refs_0_, f32[4,32,128]{2,1,0:T(8,128)S(1)} %get-tuple-element.146.refs_1_, f32[10,8,128]{2,1,0:T(8,128)S(1)} %collective-permute-done.9.y_a.refs_2_, ...), custom_call_target="tpu_custom_call" | custom-call | flops 4000000 | bytes 4000000 | tf_op jit(solution)/shard_map/pallas_call | solution.py:21
  37.4 1.6 %shard_map.71 = (f32[4,14,40,128]{3,2,1,0:T(8,128)S(1)}, f32[4,14,40,128]{3,2,1,0:T(8,128)S(1)}, f32[4,40,128]{2,1,0:T(8,128)S(1)}, f32[4,40,128]{2,1,0:T(8,128)S(1)}, f32[4,8,32,128]{3,2,1,0:T(8,128)S(1)}) custom-call(f32[14,40,128]{2,1,0:T(8,128)S(1)} %get-tuple-element.132.refs_0_.refs_2_, f32[40,128]{1,0:T(8,128)S(1)} %get-tuple-element.133.refs_1_.refs_3_, ...), custom_call_target="tpu_custom_call" | custom-call | flops 4000000 | bytes 4000000 | tf_op jit(solution)/shard_map/pallas_call | solution.py:21
  39.1 1.5 %shard_map.72 = (f32[3,8,32,128]{3,2,1,0:T(8,128)}, f32[8,32,128]{2,1,0:T(8,128)}, f32[4,14,40,128]{3,2,1,0:T(8,128)S(1)}, f32[4,14,40,128]{3,2,1,0:T(8,128)S(1)...) custom-call(f32[1,6,8,128]{3,2,1,0:T(8,128)S(1)} %collective-permute, ...), custom_call_target="tpu_custom_call", output_to_operand_aliasing={{2}: (13, {}), {3}: (14, {}), {4}: (15, {}), {5}: (16, {})} | custom-call | flops 8000000 | bytes 8000000 | tf_op jit(solution)/shard_map/pallas_call | solution.py:21
  (16 shorter events, 0.6 us)
Async XLA Ops:
  2.5 13.2 %collective-permute-start.5 = (f32[1,21,32,128]{3,2,1,0:T(8,128)S(1)}, f32[1,21,32,128]{3,2,1,0:T(8,128)S(1)}, u32[]{:S(2)}, u32[]{:S(2)}) collective-permute-start(f32[1,21,32,128]{3,2,1,0:T(8,128)S(1)} %get-tuple-element.104), channel_id=1, source_target_pairs={{0,16},{16,0},{1,17},{17,1},{2,18},{18,2},{3,19},{19,3},{4,20},{20... | collective-permute-start | bytes 1032200 | tf_op jit(solution)/shard_map/ppermute | solution.py:56
  5.6 3.9 %collective-permute-start = (f32[2,32,128]{2,1,0:T(8,128)S(1)}, f32[2,32,128]{2,1,0:T(8,128)S(1)}, u32[]{:S(2)}, u32[]{:S(2)}) collective-permute-start(f32[2,32,128]{2,1,0:T(8,128)S(1)} %get-tuple-element.97), channel_id=1, source_target_pairs={{0,4},{4,0},{8,12},{12,8},{1,5},{5,1},{9,13},{13,9},{2,6},{6,2},{1... | collective-permute-start | bytes 98312 | tf_op jit(solution)/shard_map/ppermute | solution.py:56
  7.1 2.3 %collective-permute-start.1 = (f32[2,32,128]{2,1,0:T(8,128)S(1)}, f32[2,32,128]{2,1,0:T(8,128)S(1)}, u32[]{:S(2)}, u32[]{:S(2)}) collective-permute-start(f32[2,32,128]{2,1,0:T(8,128)S(1)} %get-tuple-element.98), channel_id=1, source_target_pairs={{0,1},{1,0},{2,3},{3,2},{4,8},{5,9},{6,10},{7,11},{8,4},{9,5},{10,... | collective-permute-start | bytes 98312 | tf_op jit(solution)/shard_map/ppermute | solution.py:51
  9.6 2.8 %collective-permute-start.2 = (f32[24,8,128]{2,1,0:T(8,128)S(1)}, f32[24,8,128]{2,1,0:T(8,128)S(1)}, u32[]{:S(2)}, u32[]{:S(2)}) collective-permute-start(f32[24,8,128]{2,1,0:T(8,128)S(1)} %shard_map.62), channel_id=1, source_target_pairs={{0,1},{1,0},{2,3},{3,2},{4,5},{5,4},{6,7},{7,6},{8,9},{9,8},{10,11... | collective-permute-start | bytes 294920 | tf_op jit(solution)/shard_map/ppermute | solution.py:56
  9.7 5.4 %collective-permute-start.3 = (f32[24,8,128]{2,1,0:T(8,128)S(1)}, f32[24,8,128]{2,1,0:T(8,128)S(1)}, u32[]{:S(2)}, u32[]{:S(2)}) collective-permute-start(f32[24,8,128]{2,1,0:T(8,128)S(1)} %get-tuple-element.100), channel_id=1, source_target_pairs={{0,4},{1,2},{2,1},{3,7},{4,0},{5,6},{6,5},{7,3},{8,12},{9,10},{10,... | collective-permute-start | bytes 294920 | tf_op jit(solution)/shard_map/ppermute | solution.py:51
  15.2 4.1 %collective-permute-start.4 = (f32[1,11,8,128]{3,2,1,0:T(8,128)S(1)}, f32[1,11,8,128]{3,2,1,0:T(8,128)S(1)}, u32[]{:S(2)}, u32[]{:S(2)}) collective-permute-start(f32[1,11,8,128]{3,2,1,0:T(8,128)S(1)} %get-tuple-element.101), channel_id=1, source_target_pairs={{0,16},{16,0},{1,17},{17,1},{2,18},{18,2},{3,19},{19,3},{4,20},{20... | collective-permute-start | bytes 135176 | tf_op jit(solution)/shard_map/ppermute | solution.py:56
  21.0 4.5 %collective-permute-start.6 = (f32[5,2,16,128]{3,2,1,0:T(8,128)S(1)}, f32[5,2,16,128]{3,2,1,0:T(8,128)S(1)}, u32[]{:S(2)}, u32[]{:S(2)}) collective-permute-start(f32[5,2,16,128]{3,2,1,0:T(8,128)S(1)} %get-tuple-element.122.own), channel_id=1, source_target_pairs={{0,16},{16,0},{1,17},{17,1},{2,18},{18,2},{3,19},{19,3},{4,20},{20... | collective-permute-start | bytes 245768 | tf_op jit(solution)/shard_map/ppermute | solution.py:56
  25.5 3.3 %collective-permute-start.7 = (f32[20,8,128]{2,1,0:T(8,128)S(1)}, f32[20,8,128]{2,1,0:T(8,128)S(1)}, u32[]{:S(2)}, u32[]{:S(2)}) collective-permute-start(f32[20,8,128]{2,1,0:T(8,128)S(1)} %get-tuple-element.125), channel_id=1, source_target_pairs={{0,1},{1,0},{2,3},{3,2},{4,5},{5,4},{6,7},{7,6},{8,9},{9,8},{10,11... | collective-permute-start | bytes 245768 | tf_op jit(solution)/shard_map/ppermute | solution.py:56
  25.6 4.5 %collective-permute-start.8 = (f32[20,8,128]{2,1,0:T(8,128)S(1)}, f32[20,8,128]{2,1,0:T(8,128)S(1)}, u32[]{:S(2)}, u32[]{:S(2)}) collective-permute-start(f32[20,8,128]{2,1,0:T(8,128)S(1)} %get-tuple-element.126), channel_id=1, source_target_pairs={{0,4},{1,2},{2,1},{3,7},{4,0},{5,6},{6,5},{7,3},{8,12},{9,10},{10,... | collective-permute-start | bytes 245768 | tf_op jit(solution)/shard_map/ppermute | solution.py:51
  27.9 9.5 %collective-permute-start.12 = (f32[1,8,32,128]{3,2,1,0:T(8,128)S(1)}, f32[1,8,32,128]{3,2,1,0:T(8,128)S(1)}, u32[]{:S(2)}, u32[]{:S(2)}) collective-permute-start(f32[1,8,32,128]{3,2,1,0:T(8,128)S(1)} %get-tuple-element.144), channel_id=1, source_target_pairs={{0,16},{16,0},{1,17},{17,1},{2,18},{18,2},{3,19},{19,3},{4,20},{20... | collective-permute-start | bytes 393224 | tf_op jit(solution)/shard_map/ppermute | solution.py:56
  30.5 4.1 %collective-permute-start.9 = (f32[10,8,128]{2,1,0:T(8,128)S(1)}, f32[10,8,128]{2,1,0:T(8,128)S(1)}, u32[]{:S(2)}, u32[]{:S(2)}) collective-permute-start(f32[10,8,128]{2,1,0:T(8,128)S(1)} %get-tuple-element.128), channel_id=1, source_target_pairs={{0,4},{4,0},{8,12},{12,8},{1,5},{5,1},{9,13},{13,9},{2,6},{6,2},{1... | collective-permute-start | bytes 122888 | tf_op jit(solution)/shard_map/ppermute | solution.py:56
  32.5 2.0 %collective-permute-start.10 = (f32[10,8,128]{2,1,0:T(8,128)S(1)}, f32[10,8,128]{2,1,0:T(8,128)S(1)}, u32[]{:S(2)}, u32[]{:S(2)}) collective-permute-start(f32[10,8,128]{2,1,0:T(8,128)S(1)} %get-tuple-element.129), channel_id=1, source_target_pairs={{0,1},{1,0},{2,3},{3,2},{4,8},{5,9},{6,10},{7,11},{8,4},{9,5},{10,... | collective-permute-start | bytes 122888 | tf_op jit(solution)/shard_map/ppermute | solution.py:51
  34.7 4.4 %collective-permute-start.11 = (f32[1,6,8,128]{3,2,1,0:T(8,128)S(1)}, f32[1,6,8,128]{3,2,1,0:T(8,128)S(1)}, u32[]{:S(2)}, u32[]{:S(2)}) collective-permute-start(f32[1,6,8,128]{3,2,1,0:T(8,128)S(1)} %get-tuple-element.131), channel_id=1, source_target_pairs={{0,16},{16,0},{1,17},{17,1},{2,18},{18,2},{3,19},{19,3},{4,20},{20... | collective-permute-start | bytes 73736 | tf_op jit(solution)/shard_map/ppermute | solution.py:56

commit v7 on v5

--- a/solution.py
+++ b/solution.py
@@ -650,7 +650,7 @@
 def pre_smooth(
     x_rim, _e, _halo_e, _force, _halo_f, _w0, _w1, _w2, _w3, _w4, _w5, _ua, _ub, _ha, _ca, _cb,
     _edge_e, _summed, e, halo_e, force, halo_f, w0, w1, w2, w3, w4, w5, ua, ub, ha, ca, cb, edge_e,
-    summed, hw, coarse, hb, beside,
+    summed, hw, message, hb, beside,
 ):
     slots = e.shape[0]
     nx, nz = slots - 6, e.shape[1] - 8
@@ -685,7 +685,26 @@
     for k in range(5):
         for r in range(nx // 4):
             at = (k * (nx // 4) + r) * cz
-            coarse[k, r] = out[at : at + cz]
+            for i in range(cz // 8):
+                message[at // 8 + i] = out[at + 8 * i : at + 8 * i + 8]
+    sides = x_messages()
+    lane = iota((nz, LANES), 1)
+    _, _, xr = place("gx")
+    for m in range(sides):
+        high = xr if sides == 1 else high_side("gx", m)
+        p = 3 + high * (nx - 1)
+        parts, total = [], jnp.zeros((nz, LANES), F32)
+        for k in range(4):
+            x = ua[k, p, pl.ds(0, nz)]
+            parts += [(x[:8], 2 * k, 2 * k, 1), (x[nz - 8 :], 2 * k + 2, 2 * k + 1, 1)]
+            total = jnp.where(lane // 2 == k, roll(x, 2 * k + 1, 1), total)
+        n = message.shape[0] - 2 * (sides - m)
+        message[n] = rows_of(parts)
+        column = total[:8]
+        for t in range(1, nz // 8):
+            x = roll(total[8 * t : 8 * t + 8], 8 * t, 1)
+            column = jnp.where(lane[:8] // 8 == t, x, column)
+        message[n + 1] = column
 
 
 def smooth_pack(fields, edges, x_fine):
@@ -703,19 +722,23 @@
         edges[j] = x
 
 
+def frame(ref, m, part):
+    return ref[ref.shape[0] - 2 * (x_messages() - m) + part]
+
+
 def fourth_pack(own, other, fields, whole, z_a, z_b):
     nx, nz = fields.shape[1] - 6, fields.shape[2] - 8
-    pairs = whole.shape[1]
-    cz = whole.shape[2]
+    pairs, cz = whole.shape[1:3]
     gx = lax.axis_index("gx")
     for k in range(5):
         for r in range(pairs):
-            if other is None:
+            if own.ndim == 4:
                 whole[k, r] = own[k, r]
-            else:
-                mine = truth(jnp.where(gx == r // (pairs // 2), 1, 0), (cz, LANES))
-                n = r % (pairs // 2)
-                whole[k, r] = jnp.where(mine, own[k, n], other[k, n])
+                continue
+            mine = truth(jnp.where(gx == r // (pairs // 2), 1, 0), (8, LANES))
+            for i in range(cz // 8):
+                n = (k * (pairs // 2) + r % (pairs // 2)) * (cz // 8) + i
+                whole[k, r, pl.ds(8 * i, 8)] = jnp.where(mine, own[n], other[n])
     row = iota((8, LANES), 0) // 2
     for m, out in enumerate((z_a, z_b)):
         right = high_side("gz", m)
@@ -737,6 +760,8 @@
                 high = roll(fields[k, q + 3, pl.ds(nz - 8, 8)], 2 * k - 6, 0)
                 total = jnp.where(row == k, jnp.where(toward, high, low), total)
             out[3 * pairs + q] = total
+        for m_x in range(x_messages()):
+            out[3 * pairs + nx + m_x] = frame(other, m_x, 0)
 
 
 def fold_rows(x):
@@ -746,22 +771,29 @@
     return jnp.concatenate([x[:own], halo], axis=0)
 
 
-def deep_edges(pairs):
-    per = LANES // 16
+def deep_edges(pairs, width):
+    per = LANES // (2 * width)
     columns = []
     for n, x in enumerate(pairs):
         for g in range(2):
             t = (2 * n + g) % per
-            x_t = roll(x, 16 * t + 8 - 64 * g, 1)
+            x_t = roll(x, 2 * width * t + width - 64 * g, 1)
             if t == 0:
                 columns.append(x_t)
             else:
-                slot = iota(x.shape, 1) // 16
+                slot = iota(x.shape, 1) // (2 * width)
                 columns[-1] = jnp.where(slot == t, x_t, columns[-1])
     return columns
 
 
-def fifth_pack(whole, z_a, z_b, edges, full, full_e, z_halo, y_a, y_b):
+def unfold(left, right, width):
+    spot = iota(left.shape, 1) % (2 * width)
+    first = jnp.where(spot < width, left, roll(right, width, 1))
+    second = jnp.where(spot < width, roll(left, -width, 1), right)
+    return first, second
+
+
+def fifth_pack(whole, z_a, z_b, edges, frames, full, full_e, z_halo, z_rim, y_a, y_b):
     pairs, cz = whole.shape[1:3]
     nx = z_halo.shape[1]
     nz = edges.shape[1]
@@ -789,18 +821,25 @@
         for k in range(4):
             x = jnp.where(row < 2 * has_right, roll(right, -2 * k, 0), 0.0)
             z_halo[k, q] = jnp.where(row >= 8 - 2 * has_left, roll(left, 6 - 2 * k, 0), x)
-    columns = deep_edges(deep[: 4 * pairs])
+    for m in range(z_rim.shape[0]):
+        n = 3 * pairs + nx + m
+        left, right = left_right("gz", z_a[n], z_b[n])
+        x = jnp.where(to_right & (row % 2 == 0), right, 0.0)
+        z_rim[m] = jnp.where(to_left & (row % 2 == 1), left, x)
+    columns = deep_edges(deep[: 4 * pairs], 4)
     half = len(columns) // 2
-    columns_e = deep_edges(deep[4 * pairs :])
+    columns_e = deep_edges(deep[4 * pairs :], 8)
+    upper = (cz + 16) // 2
     behind = pair_edges(lambda i: [z_halo[i, q] for q in range(nx)], 4, 8)
     for m, out in enumerate((y_a, y_b)):
         toward = high_side("gy", m)
         parts = [
-            strip(columns[j], columns[j + half], toward, 8) for j in range(half)
-        ] + columns_e
+            strip(columns[j], columns[j + half], toward, 4) for j in range(half)
+        ] + [strip(x[:upper], x[upper:], toward, 8) for x in columns_e]
         for i in range(nz // 8):
             parts.append(y_strip(edges[0, pl.ds(8 * i, 8)], edges[1, pl.ds(8 * i, 8)], toward))
         parts.append(y_strip(behind[0], behind[1], toward))
+        parts += [frame(frames, m_x, 1) for m_x in range(z_rim.shape[0])]
         n = 0
         for x in parts:
             for i in range(x.shape[0] // 8):
@@ -808,18 +847,18 @@
                 n += 1
 
 
-def sixth_pack(y_a, y_b, z_halo, halo_full, x_rim):
-    tiles = halo_full.shape[1] // 8
-    first = y_a.shape[0] - tiles
+def sixth_pack(y_a, y_b, halo_full, y_rim):
+    tiles, sides = halo_full.shape[1] // 8, y_rim.shape[0]
+    first = y_a.shape[0] - tiles - sides
     for i in range(tiles):
         for j, x in enumerate(merge_y(y_a[first + i], y_b[first + i])):
             halo_full[j, pl.ds(8 * i, 8)] = x
-    nx = z_halo.shape[1]
-
-    def rim(plane):
-        return [rows_of([(z_halo[k, plane(1)], 2 * k, 2 * k - 1, 2) for k in range(4)])]
-
-    pack_rim(x_rim, rim, lambda j: halo_full[j], 4, 1, nx)
+    _, has_left, has_right = place("gy")
+    odd = iota((8, LANES), 1) % 2
+    for m in range(sides):
+        left, right = left_right("gy", y_a[first + tiles + m], y_b[first + tiles + m])
+        kept = (odd < has_left) & (odd == 0) | (odd > 1 - has_right)
+        y_rim[m] = jnp.where(kept, jnp.where(odd == 0, left, right), 0.0)
 
 
 def coarse_solve(full, full_e, y_a, y_b, main, halo, ca, cb, force, e, w0, w1, w2, w3, w4, w5, deep_e, grown):
@@ -838,7 +877,7 @@
         lane = iota((rows, LANES), 1)
         row = iota((rows, LANES), 0)
         kept = (row < cz + width * zr) | (row >= rows - width * zl)
-        return kept & ((lane < half + SLOT * yr) | (lane >= LANES - SLOT * yl))
+        return kept & ((lane < half + width * yr) | (lane >= LANES - width * yl))
 
     zero = jnp.zeros((rows, LANES), F32)
     w = (w0, w1, w2, w3, w4, w5)
@@ -851,44 +890,39 @@
     deep_e[0] = jnp.zeros((deep, LANES), F32)
     deep_e[planes + 1] = jnp.zeros((deep, LANES), F32)
 
-    tiles, deep_tiles = rows // 8, deep // 8
-    count = pairs // 2
+    tiles, deep_tiles = rows // 8, deep // 16
+    count = pairs // 4
     columns = []
 
-    def taken(ref, n, tiles):
-        return jnp.concatenate([ref[n + i] for i in range(tiles)], axis=0)
-
-    seconds = []
-    for j in range(count):
-        left, right = left_right("gy", taken(y_a, j * tiles, tiles), taken(y_b, j * tiles, tiles))
-        spot = iota(left.shape, 1) % 16
-        columns.append(jnp.where(spot < 8, left, roll(right, 8, 1)))
-        seconds.append(jnp.where(spot < 8, roll(left, -8, 1), right))
-    columns += seconds
+    def taken(n, tiles):
+        a, b = (jnp.concatenate([ref[n + i] for i in range(tiles)], axis=0) for ref in (y_a, y_b))
+        return left_right("gy", a, b)
+
+    unfolded = [unfold(*taken(j * tiles, tiles), 4) for j in range(count)]
+    columns = [x for x, _ in unfolded] + [x for _, x in unfolded]
     columns_e = []
     for j in range(-(-pairs // 4)):
-        n = count * tiles + j * deep_tiles
-        left, right = left_right("gy", taken(y_a, n, deep_tiles), taken(y_b, n, deep_tiles))
-        spot = iota(left.shape, 1) % 16
-        columns_e.append(jnp.where(spot < 8, left, right))
-
-    def whole_plane(pair, columns, n, s):
+        x = unfold(*taken(count * tiles + j * deep_tiles, deep_tiles), 8)
+        columns_e.append(jnp.concatenate(x, axis=0))
+
+    def whole_plane(pair, columns, n, s, width):
         lane = iota(pair.shape, 1)
+        per = LANES // (2 * width)
         last, first = 2 * n + 1 - s, 2 * n + s
-        low = roll(columns[first // 8], half - 16 * (first % 8) - 8, 1)
-        high = roll(columns[last // 8], LANES - 8 - 16 * (last % 8), 1)
+        low = roll(columns[first // per], half - 2 * width * (first % per) - width, 1)
+        high = roll(columns[last // per], LANES - width - 2 * width * (last % per), 1)
         x = jnp.where(lane < half, roll(pair, -s * half, 1), low)
-        return jnp.where(lane < LANES - 8, x, high)
+        return jnp.where(lane < LANES - width, x, high)
 
     near, far = inside(rows, 4), inside(deep, 8)
     for r in range(pairs):
         for s in range(2):
             p = 2 * r + s
-            x = jnp.where(far, whole_plane(full_e[r], columns_e, r, s), 0.0)
+            x = jnp.where(far, whole_plane(full_e[r], columns_e, r, s, 8), 0.0)
             deep_e[p + 1] = x
             e[p + 1] = fold_rows(x)
             for k in range(4):
-                x = whole_plane(full[k, r], columns, k * pairs + r, s)
+                x = whole_plane(full[k, r], columns, k * pairs + r, s, 4)
                 force[k, p] = jnp.where(near, x, 0.0)
 
     def shifts(x):
@@ -988,9 +1022,22 @@
         grow(halo, (k,), column[k * rows : (k + 1) * rows])
 
 
+def last_sweep(src, halo, beside, w, e, force, chosen, store):
+    slots, nz = src.shape[1], src.shape[2] - 8
+    spread_halo(halo, beside, slots, 0, chosen, False)
+
+    def body(p):
+        new = main_operator(src, beside, w, force, p, nz)
+        new = relaxed(*new, w[5][p, pl.ds(0, nz)], e[p, pl.ds(0, nz)])
+        for k in range(4):
+            store(p, k, new[k])
+
+    over_planes(slots, 0, body, chosen)
+
+
 def post_smooth(
     e, halo_e, force, halo_f, w0, w1, w2, w3, w4, w5, hw,
-    fields, z_halo, halo_full, x_fine, x_rim, main, column, v_out, p_out,
+    fields, z_halo, halo_full, x_fine, z_rim, y_rim, main, column, v_out, p_out,
     ua, ub, ha, hb, ca, beside,
 ):
     nx, nz, _ = p_out.shape
@@ -1010,18 +1057,23 @@
         right, valid = x_side(m)
         there = truth(valid, (nz, LANES))
         there8 = truth(valid, (8, LANES))
-        tiles = (nz + 8) // 8
-        side = jnp.concatenate([x_rim[m, 1 + r] for r in range(tiles)], axis=0)
+        near = 2 + right * (nx + 1)
+        row = iota((8, LANES), 0)
+        lane = iota((nz, LANES), 1)
+        kept = (lane == near * SLOT + 3) | (lane == near * SLOT + 4)
         i = right * (nx // 2 + 1)
         for k in range(4):
             for j in range(2):
                 at = 1 + right * (nx + 2) + j
                 x = x_fine[m, 2 * k + j] + main[k, i, pl.ds(0, nz)]
                 ua[k, at, pl.ds(0, nz)] = jnp.where(there, x, 0.0)
-            x = roll(x_rim[m, 0], -2 * k, 0) + main[k, i, pl.ds(nz, 8)]
-            ua[k, 2 + right * (nx + 1), pl.ds(nz, 8)] = jnp.where(there8, x, 0.0)
-            x, kept = rim_halo(side, k, SLOT, 1, right, valid, nx)
-            ha[k] = jnp.where(kept, x, ha[k])
+            x = jnp.where(row == 0, roll(z_rim[m], -2 * k, 0), 0.0)
+            x = jnp.where(row == 7, roll(z_rim[m], 6 - 2 * k, 0), x) + main[k, i, pl.ds(nz, 8)]
+            ua[k, near, pl.ds(nz, 8)] = jnp.where(there8, x, 0.0)
+            at = near * SLOT + 3 + LANES
+            x = [roll(y_rim[m], at - SLOT * t - 2 * k, 1) for t in range(nz // 8)]
+            x = jnp.where(kept, jnp.concatenate(x, axis=0), ha[k, pl.ds(0, nz)])
+            ha[k, pl.ds(0, nz)] = jnp.where(there, x, ha[k, pl.ds(0, nz)])
     masks = fine_masks(nz + 8, slots)
     for k in range(4):
         ha[k] = jnp.where(masks[1], ha[k] + column[k], 0.0)
@@ -1029,16 +1081,13 @@
     main_sweep(ua, ha, ub, w, e, force, 1, masks[0], beside)
     halo_sweep(ha, ca, hb, hw, halo_e, halo_f, masks[1])
 
-    spread_halo(hb, beside, slots, 0, full=False)
-
-    def last(p):
-        new = main_operator(ub, beside, w, force, p, nz)
-        new = relaxed(*new, w5[p, pl.ds(0, nz)], e[p, pl.ds(0, nz)])
-        for k in range(3):
-            v_out[k, p - 3] = new[k]
-        p_out[p - 3] = new[3]
-
-    over_planes(slots, 0, last)
+    def store(p, k, x):
+        if k < 3:
+            v_out[k, p - 3] = x
+        else:
+            p_out[p - 3] = x
+
+    last_sweep(ub, hb, beside, w, e, force, None, store)
 
 
 def local(velocity, pressure, viscosity, body_force):
@@ -1073,6 +1122,7 @@
     started = [(slots, rows, LANES), (rows, LANES), (3, slots, rows, LANES), (3, rows, LANES)]
     started += [(slots, rows, LANES)] * 6 + [spread, spread] + [column] * 3 + [(rows, LANES)]
     started += [(5, nx // 2, nz, LANES)]
+    tiles_c = 5 * (nx // 4) * (nz // 16)
     state = call(
         by_sides(pre_start),
         started,
@@ -1082,7 +1132,7 @@
     )
     *operator, fields, _, _, _, _, _, _, factors, own = call(
         by_sides(pre_smooth),
-        started + [(7, rows, LANES), (5, nx // 4, nz // 2, LANES)],
+        started + [(7, rows, LANES), (tiles_c + 2 * sides, 8, LANES)],
         [x_first, *state],
         [column, spread],
         cost=8,
@@ -1091,36 +1141,32 @@
     operator.append(factors)
     edges, x_fine = call(smooth_pack, [(2,) + block, (sides, 8) + block], [fields])
     if lax.axis_size("gx") == 2:
-        parts = [own, swap(own, "gx", 0)]
-        gather = fourth_pack
+        frames = swap(own, "gx", 0)
     else:
-        parts = [lax.all_gather(own, "gx", axis=1, tiled=True)]
-
-        def gather(a, *refs):
-            fourth_pack(a, None, *refs)
-
+        frames = swap_x(own[tiles_c:].reshape(sides, 2, 8, LANES)).reshape(2 * sides, 8, LANES)
+        own = own[:tiles_c].reshape(5, nx // 4, nz // 2, LANES)
+        own = lax.all_gather(own, "gx", axis=1, tiled=True)
     x_fine = swap_x(x_fine)
     pairs = lax.axis_size("gx") * (nx // 4)
-    z_shape = (3 * pairs + nx, 8, LANES)
+    z_shape = (3 * pairs + nx + sides, 8, LANES)
     whole, z_a, z_b = call(
-        gather, [(5, pairs, nz // 2, LANES), z_shape, z_shape], parts + [fields]
+        fourth_pack,
+        [(5, pairs, nz // 2, LANES), z_shape, z_shape],
+        [own, frames, fields],
     )
     z_a, z_b = swap(z_a, "gz", 0), swap(z_b, "gz", 1)
     deep = nz // 2 + 16
     shallow = deep - 8
-    y_shape = (pairs // 2 * (shallow // 8) + -(-pairs // 4) * (deep // 8) + tiles, 8, LANES)
-    full, full_e, z_halo, y_a, y_b = call(
+    y_shape = (pairs // 4 * (shallow // 8) + -(-pairs // 4) * (deep // 16) + tiles, 8, LANES)
+    y_shape = (y_shape[0] + sides, 8, LANES)
+    rim = (sides, 8, LANES)
+    full, full_e, z_halo, z_rim, y_a, y_b = call(
         fifth_pack,
-        [(4, pairs, shallow, LANES), (pairs, deep, LANES), (4, nx, 8, LANES), y_shape, y_shape],
-        [whole, z_a, z_b, edges],
+        [(4, pairs, shallow, LANES), (pairs, deep, LANES), (4, nx, 8, LANES), rim, y_shape, y_shape],
+        [whole, z_a, z_b, edges, frames],
     )
     y_a, y_b = swap(y_a, "gy", 0), swap(y_b, "gy", 1)
-    halo_full, x_rim = call(
-        sixth_pack,
-        [(2, rows, LANES), (sides, 1 + tiles, 8, LANES)],
-        [y_a, y_b, z_halo],
-    )
-    x_rim = swap_x(x_rim)
+    halo_full, y_rim = call(sixth_pack, [(2, rows, LANES), rim], [y_a, y_b])
     planes = 2 * pairs
     plane = (shallow, LANES)
     grown, beside = call(
@@ -1136,7 +1182,7 @@
     v_out, p_out = call(
         by_sides(post_smooth),
         [(3, nx) + block, (nx,) + block],
-        operator + [fields, z_halo, halo_full, x_fine, x_rim, grown, beside],
+        operator + [fields, z_halo, halo_full, x_fine, z_rim, y_rim, grown, beside],
         [spread] * 2 + [column] * 3 + [spread],
         cost=8,
     )

time: 41.7 us -> 39.4 us (0.945)
  waiting for transfers between devices: 13.9 us -> 12.6 us
  starting transfers between devices: 15.2 us -> 14.2 us
    ppermute x9 -> x8, waiting for transfers between devices: 10.1 us -> 8.69 us  [swap(): return lax.ppermute(array, axis, pairs)]
    ppermute x9 -> x8, starting transfers between devices: 10.4 us -> 9.33 us  [swap(): return lax.ppermute(array, axis, pairs)]
  transfers between devices with their start and end apart: 13 -> 12, of which waited for: 7 -> 6; matrix products, arithmetic and copies ran while one was open for 0% -> 0% of each run, Pallas kernels for 13% -> 14%
where the time goes in v7:
time: 39.4 us; the launch traced here: 39.3 us
  starting transfers between devices  14.2 us (36%)
  waiting for transfers between devices  12.6 us (32%)
  Pallas kernels  11.7 us (30%)
  between operations  0.75 us (2%)
    pallas_call x13, Pallas kernels, call(): pl.pallas_call(body, out_shape=[jax.ShapeDtypeStruct(shape, F32) for shap...  11.7 us
    ppermute x8, starting transfers between devices, swap(): return lax.ppermute(array, axis, pairs)  9.33 us
    ppermute x8, waiting for transfers between devices, swap(): return lax.ppermute(array, axis, pairs)  8.69 us
    ppermute x4, starting transfers between devices, swap(): return lax.ppermute(array, ('gy', 'gz'), pairs)  4.86 us
    ppermute x4, waiting for transfers between devices, swap(): return lax.ppermute(array, ('gy', 'gz'), pairs)  3.9 us
  transfers between devices with their start and end apart: 12, of which 6 were waited for; matrix products, arithmetic and copies ran while one was open for 0% of the time, Pallas kernels for 14%

profile of v7, /device:TPU:0, one launch (start us, length us, event | category | flops | bytes accessed | tf_op | source)
XLA Modules:
  0.0 39.3 jit_solution(13901893492763801597)
XLA Ops:
  0.6 1.8 %shard_map.59 = (f32[4,32,128]{2,1,0:T(8,128)S(1)}, f32[4,32,128]{2,1,0:T(8,128)S(1)}, f32[4,32,128]{2,1,0:T(8,128)S(1)}, f32[4,32,128]{2,1,0:T(8,128)S(1)}, f32...) custom-call(f32[3,8,32,128]{3,2,1,0:T(8,128)} %v_in.1, ...), custom_call_target="tpu_custom_call" | custom-call | flops 1000000 | bytes 1000000 | tf_op jit(solution)/shard_map/pallas_call | solution.py:21
  2.4 0.1 shard_map.60
  2.5 3.0 %collective-permute-start.5 = (f32[1,21,32,128]{3,2,1,0:T(8,128)S(1)}, f32[1,21,32,128]{3,2,1,0:T(8,128)S(1)}, u32[]{:S(2)}, u32[]{:S(2)}) collective-permute-start(f32[1,21,32,128]{3,2,1,0:T(8,128)S(1)} %get-tuple-element.98), channel_id=1, source_target_pairs={{0,16},{16,0},{1,17},{17,1},{2,18},{18,2},{3,19},{19,3},{4,20},{20... | collective-permute-start | bytes 1032200 | tf_op jit(solution)/shard_map/ppermute | solution.py:56
  5.6 1.6 %collective-permute-start = (f32[2,32,128]{2,1,0:T(8,128)S(1)}, f32[2,32,128]{2,1,0:T(8,128)S(1)}, u32[]{:S(2)}, u32[]{:S(2)}) collective-permute-start(f32[2,32,128]{2,1,0:T(8,128)S(1)} %get-tuple-element.91), channel_id=1, source_target_pairs={{0,4},{4,0},{8,12},{12,8},{1,5},{5,1},{9,13},{13,9},{2,6},{6,2},{1... | collective-permute-start | bytes 98312 | tf_op jit(solution)/shard_map/ppermute | solution.py:56
  7.1 2.3 %collective-permute-done.y_a = f32[2,32,128]{2,1,0:T(8,128)S(1)} collective-permute-done((f32[2,32,128]{2,1,0:T(8,128)S(1)}, f32[2,32,128]{2,1,0:T(8,128)S(1)}, u32[]{:S(2)}, u32[]{:S(2)}) %collective-permute-start) | collective-permute-done | bytes 32800 | tf_op jit(solution)/shard_map/ppermute | solution.py:56
  9.5 0.1 shard_map.61
  9.7 2.8 %collective-permute-start.3 = (f32[24,8,128]{2,1,0:T(8,128)S(1)}, f32[24,8,128]{2,1,0:T(8,128)S(1)}, u32[]{:S(2)}, u32[]{:S(2)}) collective-permute-start(f32[24,8,128]{2,1,0:T(8,128)S(1)} %get-tuple-element.94), channel_id=1, source_target_pairs={{0,4},{1,2},{2,1},{3,7},{4,0},{5,6},{6,5},{7,3},{8,12},{9,10},{10,... | collective-permute-start | bytes 294920 | tf_op jit(solution)/shard_map/ppermute | solution.py:51
  12.5 2.6 %collective-permute-done.3.z_b = f32[24,8,128]{2,1,0:T(8,128)S(1)} collective-permute-done((f32[24,8,128]{2,1,0:T(8,128)S(1)}, f32[24,8,128]{2,1,0:T(8,128)S(1)}, u32[]{:S(2)}, u32[]{:S(2)}) %collective-permute-start.3) | collective-permute-done | bytes 98336 | tf_op jit(solution)/shard_map/ppermute | solution.py:51
  15.1 0.1 shard_map.63
  15.2 0.6 %collective-permute-start.4 = (f32[1,11,8,128]{3,2,1,0:T(8,128)S(1)}, f32[1,11,8,128]{3,2,1,0:T(8,128)S(1)}, u32[]{:S(2)}, u32[]{:S(2)}) collective-permute-start(f32[1,11,8,128]{3,2,1,0:T(8,128)S(1)} %get-tuple-element.95), channel_id=1, source_target_pairs={{0,16},{16,0},{1,17},{17,1},{2,18},{18,2},{3,19},{19,3},{4,20},{20... | collective-permute-start | bytes 135176 | tf_op jit(solution)/shard_map/ppermute | solution.py:56
  15.8 2.8 %shard_map.64 = (f32[14,40,128]{2,1,0:T(8,128)S(1)}, f32[40,128]{1,0:T(8,128)S(1)}, f32[3,14,40,128]{3,2,1,0:T(8,128)S(1)}, f32[3,40,128]{2,1,0:T(8,128)S(1)}, f...) custom-call(f32[4,32,128]{2,1,0:T(8,128)S(1)} %get-tuple-element.73., ...), custom_call_target="tpu_custom_call" | custom-call | flops 4000000 | bytes 4000000 | tf_op jit(solution)/shard_map/pallas_call | solution.py:21
  18.6 0.7 %collective-permute-done.4.refs_0_ = f32[1,11,8,128]{3,2,1,0:T(8,128)S(1)} collective-permute-done((f32[1,11,8,128]{3,2,1,0:T(8,128)S(1)}, f32[1,11,8,128]{3,2,1,0:T(8,128)S(1)}, u32[]{:S(2)}, u32[]{:S(2)}) %collective-permute-start.4) | collective-permute-done | bytes 45088 | tf_op jit(solution)/shard_map/ppermute | solution.py:56
  19.3 1.7 %shard_map.65 = (f32[14,40,128]{2,1,0:T(8,128)S(1)}, f32[40,128]{1,0:T(8,128)S(1)}, f32[3,14,40,128]{3,2,1,0:T(8,128)S(1)}, f32[3,40,128]{2,1,0:T(8,128)S(1)}, f...) custom-call(f32[1,11,8,128]{3,2,1,0:T(8,128)S(1)} %collective-permut, ...), custom_call_target="tpu_custom_call", output_to_operand_aliasing={{0}: (1, {}), {1}: (2, {}), {2}: (3, {}), {3}: (4, {}), {4}... | custom-call | flops 8000000 | bytes 8000000 | tf_op jit(solution)/shard_map/pallas_call | solution.py:21
  21.0 1.0 %collective-permute-start.6 = (f32[22,8,128]{2,1,0:T(8,128)S(1)}, f32[22,8,128]{2,1,0:T(8,128)S(1)}, u32[]{:S(2)}, u32[]{:S(2)}) collective-permute-start(f32[22,8,128]{2,1,0:T(8,128)S(1)} %get-tuple-element.128.own), channel_id=1, source_target_pairs={{0,16},{16,0},{1,17},{17,1},{2,18},{18,2},{3,19},{19,3},{4,20},{20... | collective-permute-start | bytes 270344 | tf_op jit(solution)/shard_map/ppermute | solution.py:56
  22.0 3.6 %collective-permute-done.6.other.frames = f32[22,8,128]{2,1,0:T(8,128)S(1)} collective-permute-done((f32[22,8,128]{2,1,0:T(8,128)S(1)}, f32[22,8,128]{2,1,0:T(8,128)S(1)}, u32[]{:S(2)}, u32[]{:S(2)}) %collective-permute-start.6) | collective-permute-done | bytes 90144 | tf_op jit(solution)/shard_map/ppermute | solution.py:56
  25.7 2.1 %collective-permute-start.8 = (f32[21,8,128]{2,1,0:T(8,128)S(1)}, f32[21,8,128]{2,1,0:T(8,128)S(1)}, u32[]{:S(2)}, u32[]{:S(2)}) collective-permute-start(f32[21,8,128]{2,1,0:T(8,128)S(1)} %get-tuple-element.131), channel_id=1, source_target_pairs={{0,4},{1,2},{2,1},{3,7},{4,0},{5,6},{6,5},{7,3},{8,12},{9,10},{10,... | collective-permute-start | bytes 258056 | tf_op jit(solution)/shard_map/ppermute | solution.py:51
  27.8 0.2 shard_map.67
  28.0 1.0 %collective-permute-start.11 = (f32[1,8,32,128]{3,2,1,0:T(8,128)S(1)}, f32[1,8,32,128]{3,2,1,0:T(8,128)S(1)}, u32[]{:S(2)}, u32[]{:S(2)}) collective-permute-start(f32[1,8,32,128]{3,2,1,0:T(8,128)S(1)} %get-tuple-element.137), channel_id=1, source_target_pairs={{0,16},{16,0},{1,17},{17,1},{2,18},{18,2},{3,19},{19,3},{4,20},{20... | collective-permute-start | bytes 393224 | tf_op jit(solution)/shard_map/ppermute | solution.py:56
  29.0 1.3 %collective-permute-done.8.z_b = f32[21,8,128]{2,1,0:T(8,128)S(1)} collective-permute-done((f32[21,8,128]{2,1,0:T(8,128)S(1)}, f32[21,8,128]{2,1,0:T(8,128)S(1)}, u32[]{:S(2)}, u32[]{:S(2)}) %collective-permute-start.8) | collective-permute-done | bytes 86048 | tf_op jit(solution)/shard_map/ppermute | solution.py:51
  30.3 0.3 shard_map.68
  30.6 2.1 %collective-permute-start.9 = (f32[11,8,128]{2,1,0:T(8,128)S(1)}, f32[11,8,128]{2,1,0:T(8,128)S(1)}, u32[]{:S(2)}, u32[]{:S(2)}) collective-permute-start(f32[11,8,128]{2,1,0:T(8,128)S(1)} %get-tuple-element.134), channel_id=1, source_target_pairs={{0,4},{4,0},{8,12},{12,8},{1,5},{5,1},{9,13},{13,9},{2,6},{6,2},{1... | collective-permute-start | bytes 135176 | tf_op jit(solution)/shard_map/ppermute | solution.py:56
  32.7 2.0 %collective-permute-done.9.y_a.refs_2_ = f32[11,8,128]{2,1,0:T(8,128)S(1)} collective-permute-done((f32[11,8,128]{2,1,0:T(8,128)S(1)}, f32[11,8,128]{2,1,0:T(8,128)S(1)}, u32[]{:S(2)}, u32[]{:S(2)}) %collective-permute-start.9) | collective-permute-done | bytes 45088 | tf_op jit(solution)/shard_map/ppermute | solution.py:56
  34.8 1.8 %shard_map.70 = (f32[4,6,40,128]{3,2,1,0:T(8,128)S(1)}, f32[4,40,128]{2,1,0:T(8,128)S(1)}) custom-call(f32[4,4,24,128]{3,2,1,0:T(8,128)S(1)} %get-tuple-element.140.refs_0_, f32[4,32,128]{2,1,0:T(8,128)S(1)} %get-tuple-element.141.refs_1_, f32[11,8,128]{2,1,0:T(8,128)S(1)} %collective-permute-done.9.y_a.refs_2_, ...), custom_call_target="tpu_custom_call" | custom-call | flops 4000000 | bytes 4000000 | tf_op jit(solution)/shard_map/pallas_call | solution.py:21
  36.6 2.7 %shard_map.71 = (f32[3,8,32,128]{3,2,1,0:T(8,128)}, f32[8,32,128]{2,1,0:T(8,128)}) custom-call(f32[14,40,128]{2,1,0:T(8,128)S(1)} %get-tuple-element.116.refs_0_, f32[40,128]{1,0:T(8,128)S(1)} %get-tuple-element.117.refs_1_, f32[3,14,40,128]{3,2,1,0:T(8,128)S(1)} %get-tuple-element.118.refs_2_, f32[3,40,128]{2,1,0:T(8,128)S(1)} %get-tuple-element.119.refs_3_, ...), custom_call_target="tpu_custom_call" | custom-call | flops 8000000 | bytes 8000000 | tf_op jit(solution)/shard_map/pallas_call | solution.py:21
  (13 shorter events, 0.3 us)
Async XLA Ops:
  2.5 13.2 %collective-permute-start.5 = (f32[1,21,32,128]{3,2,1,0:T(8,128)S(1)}, f32[1,21,32,128]{3,2,1,0:T(8,128)S(1)}, u32[]{:S(2)}, u32[]{:S(2)}) collective-permute-start(f32[1,21,32,128]{3,2,1,0:T(8,128)S(1)} %get-tuple-element.98), channel_id=1, source_target_pairs={{0,16},{16,0},{1,17},{17,1},{2,18},{18,2},{3,19},{19,3},{4,20},{20... | collective-permute-start | bytes 1032200 | tf_op jit(solution)/shard_map/ppermute | solution.py:56
  5.6 3.9 %collective-permute-start = (f32[2,32,128]{2,1,0:T(8,128)S(1)}, f32[2,32,128]{2,1,0:T(8,128)S(1)}, u32[]{:S(2)}, u32[]{:S(2)}) collective-permute-start(f32[2,32,128]{2,1,0:T(8,128)S(1)} %get-tuple-element.91), channel_id=1, source_target_pairs={{0,4},{4,0},{8,12},{12,8},{1,5},{5,1},{9,13},{13,9},{2,6},{6,2},{1... | collective-permute-start | bytes 98312 | tf_op jit(solution)/shard_map/ppermute | solution.py:56
  7.1 2.3 %collective-permute-start.1 = (f32[2,32,128]{2,1,0:T(8,128)S(1)}, f32[2,32,128]{2,1,0:T(8,128)S(1)}, u32[]{:S(2)}, u32[]{:S(2)}) collective-permute-start(f32[2,32,128]{2,1,0:T(8,128)S(1)} %get-tuple-element.92), channel_id=1, source_target_pairs={{0,1},{1,0},{2,3},{3,2},{4,8},{5,9},{6,10},{7,11},{8,4},{9,5},{10,... | collective-permute-start | bytes 98312 | tf_op jit(solution)/shard_map/ppermute | solution.py:51
  9.6 2.8 %collective-permute-start.2 = (f32[24,8,128]{2,1,0:T(8,128)S(1)}, f32[24,8,128]{2,1,0:T(8,128)S(1)}, u32[]{:S(2)}, u32[]{:S(2)}) collective-permute-start(f32[24,8,128]{2,1,0:T(8,128)S(1)} %shard_map.62), channel_id=1, source_target_pairs={{0,1},{1,0},{2,3},{3,2},{4,5},{5,4},{6,7},{7,6},{8,9},{9,8},{10,11... | collective-permute-start | bytes 294920 | tf_op jit(solution)/shard_map/ppermute | solution.py:56
  9.7 5.4 %collective-permute-start.3 = (f32[24,8,128]{2,1,0:T(8,128)S(1)}, f32[24,8,128]{2,1,0:T(8,128)S(1)}, u32[]{:S(2)}, u32[]{:S(2)}) collective-permute-start(f32[24,8,128]{2,1,0:T(8,128)S(1)} %get-tuple-element.94), channel_id=1, source_target_pairs={{0,4},{1,2},{2,1},{3,7},{4,0},{5,6},{6,5},{7,3},{8,12},{9,10},{10,... | collective-permute-start | bytes 294920 | tf_op jit(solution)/shard_map/ppermute | solution.py:51
  15.2 4.1 %collective-permute-start.4 = (f32[1,11,8,128]{3,2,1,0:T(8,128)S(1)}, f32[1,11,8,128]{3,2,1,0:T(8,128)S(1)}, u32[]{:S(2)}, u32[]{:S(2)}) collective-permute-start(f32[1,11,8,128]{3,2,1,0:T(8,128)S(1)} %get-tuple-element.95), channel_id=1, source_target_pairs={{0,16},{16,0},{1,17},{17,1},{2,18},{18,2},{3,19},{19,3},{4,20},{20... | collective-permute-start | bytes 135176 | tf_op jit(solution)/shard_map/ppermute | solution.py:56
  21.0 4.6 %collective-permute-start.6 = (f32[22,8,128]{2,1,0:T(8,128)S(1)}, f32[22,8,128]{2,1,0:T(8,128)S(1)}, u32[]{:S(2)}, u32[]{:S(2)}) collective-permute-start(f32[22,8,128]{2,1,0:T(8,128)S(1)} %get-tuple-element.128.own), channel_id=1, source_target_pairs={{0,16},{16,0},{1,17},{17,1},{2,18},{18,2},{3,19},{19,3},{4,20},{20... | collective-permute-start | bytes 270344 | tf_op jit(solution)/shard_map/ppermute | solution.py:56
  25.7 3.3 %collective-permute-start.7 = (f32[21,8,128]{2,1,0:T(8,128)S(1)}, f32[21,8,128]{2,1,0:T(8,128)S(1)}, u32[]{:S(2)}, u32[]{:S(2)}) collective-permute-start(f32[21,8,128]{2,1,0:T(8,128)S(1)} %get-tuple-element.130), channel_id=1, source_target_pairs={{0,1},{1,0},{2,3},{3,2},{4,5},{5,4},{6,7},{7,6},{8,9},{9,8},{10,11... | collective-permute-start | bytes 258056 | tf_op jit(solution)/shard_map/ppermute | solution.py:56
  25.7 4.6 %collective-permute-start.8 = (f32[21,8,128]{2,1,0:T(8,128)S(1)}, f32[21,8,128]{2,1,0:T(8,128)S(1)}, u32[]{:S(2)}, u32[]{:S(2)}) collective-permute-start(f32[21,8,128]{2,1,0:T(8,128)S(1)} %get-tuple-element.131), channel_id=1, source_target_pairs={{0,4},{1,2},{2,1},{3,7},{4,0},{5,6},{6,5},{7,3},{8,12},{9,10},{10,... | collective-permute-start | bytes 258056 | tf_op jit(solution)/shard_map/ppermute | solution.py:51
  28.0 8.6 %collective-permute-start.11 = (f32[1,8,32,128]{3,2,1,0:T(8,128)S(1)}, f32[1,8,32,128]{3,2,1,0:T(8,128)S(1)}, u32[]{:S(2)}, u32[]{:S(2)}) collective-permute-start(f32[1,8,32,128]{3,2,1,0:T(8,128)S(1)} %get-tuple-element.137), channel_id=1, source_target_pairs={{0,16},{16,0},{1,17},{17,1},{2,18},{18,2},{3,19},{19,3},{4,20},{20... | collective-permute-start | bytes 393224 | tf_op jit(solution)/shard_map/ppermute | solution.py:56
  30.6 4.1 %collective-permute-start.9 = (f32[11,8,128]{2,1,0:T(8,128)S(1)}, f32[11,8,128]{2,1,0:T(8,128)S(1)}, u32[]{:S(2)}, u32[]{:S(2)}) collective-permute-start(f32[11,8,128]{2,1,0:T(8,128)S(1)} %get-tuple-element.134), channel_id=1, source_target_pairs={{0,4},{4,0},{8,12},{12,8},{1,5},{5,1},{9,13},{13,9},{2,6},{6,2},{1... | collective-permute-start | bytes 135176 | tf_op jit(solution)/shard_map/ppermute | solution.py:56
  32.7 2.0 %collective-permute-start.10 = (f32[11,8,128]{2,1,0:T(8,128)S(1)}, f32[11,8,128]{2,1,0:T(8,128)S(1)}, u32[]{:S(2)}, u32[]{:S(2)}) collective-permute-start(f32[11,8,128]{2,1,0:T(8,128)S(1)} %get-tuple-element.135), channel_id=1, source_target_pairs={{0,1},{1,0},{2,3},{3,2},{4,8},{5,9},{6,10},{7,11},{8,4},{9,5},{10,... | collective-permute-start | bytes 135176 | tf_op jit(solution)/shard_map/ppermute | solution.py:51

commit v8 on v7

--- a/solution.py
+++ b/solution.py
@@ -57,6 +57,19 @@
 
 
 FIXED = []
+
+
+def choose(x, chosen):
+    parts = []
+    for _ in range(3):
+        parts.append(x.astype(jnp.bfloat16))
+        x = x - parts[-1].astype(F32)
+    chosen = jnp.where(chosen, 1.0, 0.0).astype(jnp.bfloat16)
+    return jnp.dot(
+        jnp.concatenate(parts, axis=1),
+        jnp.concatenate([chosen] * 3, axis=0),
+        preferred_element_type=F32,
+    )
 
 
 def by_sides(body):
@@ -679,9 +692,7 @@
             left.append(jnp.concatenate(halves, axis=1))
     left = jnp.concatenate(left, axis=0)
     pick = iota((2 * LANES, LANES), 0) // 2 == iota((2 * LANES, LANES), 1)
-    out = jnp.dot(
-        left, pick.astype(F32), precision=lax.Precision.HIGHEST, preferred_element_type=F32
-    )
+    out = choose(left, pick)
     for k in range(5):
         for r in range(nx // 4):
             at = (k * (nx // 4) + r) * cz
@@ -1013,8 +1024,7 @@
     for i in range(own + 2):
         x = jnp.concatenate([cb[k, first + i] for k in range(4)], axis=0)
         here = (lane >= LANES) & ((slot + 1) // 2 - 1 == i) & (cell == wanted)
-        chosen = (here | ((lane < LANES) & (lane // 2 == cell))).astype(F32)
-        wide = jnp.dot(x, chosen, precision=lax.Precision.HIGHEST, preferred_element_type=F32)
+        wide = choose(x, here | ((lane < LANES) & (lane // 2 == cell)))
         for k in range(4):
             grow(main, (k, i), wide[k * rows : (k + 1) * rows, :LANES])
         column += wide[:, LANES:]
@@ -1090,6 +1100,17 @@
     last_sweep(ub, hb, beside, w, e, force, None, store)
 
 
+def finish(*refs):
+    coarse, operator, rest = refs[:4], refs[4:15], refs[15:]
+    fields, z_halo, x_fine, z_rim, v_out, p_out, halo_full, y_rim, main, column = rest[:10]
+    sixth_pack(*coarse[2:], halo_full, y_rim)
+    coarse_solve(*coarse, main, column, *rest[10:22])
+    post_smooth(
+        *operator, fields, z_halo, halo_full, x_fine, z_rim, y_rim, main, column, v_out, p_out,
+        *rest[22:],
+    )
+
+
 def local(velocity, pressure, viscosity, body_force):
     nx, nz, ny = pressure.shape
     if ny != LANES or nx * SLOT * 2 != LANES or nz % 16:
@@ -1166,24 +1187,16 @@
         [whole, z_a, z_b, edges, frames],
     )
     y_a, y_b = swap(y_a, "gy", 0), swap(y_b, "gy", 1)
-    halo_full, y_rim = call(sixth_pack, [(2, rows, LANES), rim], [y_a, y_b])
     planes = 2 * pairs
     plane = (shallow, LANES)
-    grown, beside = call(
-        by_sides(coarse_solve),
-        [(4, nx // 2 + 2, rows, LANES), (4, rows, LANES)],
-        [full, full_e, y_a, y_b],
-        [(4, planes + 2) + plane] * 2
-        + [(4, planes) + plane]
-        + [(planes + 2,) + plane] * 7
-        + [(planes + 2, deep, LANES), (16, LANES)],
-        cost=4,
-    )
+    coarse_scratch = [(4, nx // 2 + 2, rows, LANES), (4, rows, LANES)]
+    coarse_scratch += [(4, planes + 2) + plane] * 2 + [(4, planes) + plane]
+    coarse_scratch += [(planes + 2,) + plane] * 7 + [(planes + 2, deep, LANES), (16, LANES)]
     v_out, p_out = call(
-        by_sides(post_smooth),
+        by_sides(finish),
         [(3, nx) + block, (nx,) + block],
-        operator + [fields, z_halo, halo_full, x_fine, z_rim, y_rim, grown, beside],
-        [spread] * 2 + [column] * 3 + [spread],
+        [full, full_e, y_a, y_b] + operator + [fields, z_halo, x_fine, z_rim],
+        [(2, rows, LANES), rim] + coarse_scratch + [spread] * 2 + [column] * 3 + [spread],
         cost=8,
     )
     return v_out, p_out

time: 39.4 us -> 38.8 us (0.985)
  Pallas kernels: 11.7 us -> 11.1 us
    pallas_call x13 -> x11, Pallas kernels: 11.7 us -> 11.1 us  [call(): pl.pallas_call(body, out_shape=[jax.ShapeDtypeStruct(shape, F32) for shap...]
  transfers between devices with their start and end apart: 12 -> 12, of which waited for: 6 -> 7; matrix products, arithmetic and copies ran while one was open for 0% -> 0% of each run, Pallas kernels for 14% -> 9%
where the time goes in v8:
time: 38.8 us; the launch traced here: 38.6 us
  starting transfers between devices  14.1 us (36%)
  waiting for transfers between devices  12.7 us (33%)
  Pallas kernels  11.1 us (29%)
  between operations  0.73 us (2%)
    pallas_call x11, Pallas kernels, call(): pl.pallas_call(body, out_shape=[jax.ShapeDtypeStruct(shape, F32) for shap...  11.1 us
    ppermute x8, starting transfers between devices, swap(): return lax.ppermute(array, axis, pairs)  9.19 us
    ppermute x8, waiting for transfers between devices, swap(): return lax.ppermute(array, axis, pairs)  8.76 us
    ppermute x4, starting transfers between devices, swap(): return lax.ppermute(array, ('gy', 'gz'), pairs)  4.86 us
    ppermute x4, waiting for transfers between devices, swap(): return lax.ppermute(array, ('gy', 'gz'), pairs)  3.97 us
  transfers between devices with their start and end apart: 12, of which 7 were waited for; matrix products, arithmetic and copies ran while one was open for 0% of the time, Pallas kernels for 9%

profile of v8, /device:TPU:0, one launch (start us, length us, event | category | flops | bytes accessed | tf_op | source)
XLA Modules:
  0.0 38.6 jit_solution(7868659110109028223)
XLA Ops:
  0.6 1.8 %shard_map.59 = (f32[4,32,128]{2,1,0:T(8,128)S(1)}, f32[4,32,128]{2,1,0:T(8,128)S(1)}, f32[4,32,128]{2,1,0:T(8,128)S(1)}, f32[4,32,128]{2,1,0:T(8,128)S(1)}, f32...) custom-call(f32[3,8,32,128]{3,2,1,0:T(8,128)} %v_in.1, ...), custom_call_target="tpu_custom_call" | custom-call | flops 1000000 | bytes 1000000 | tf_op jit(solution)/shard_map/pallas_call | solution.py:21
  2.4 0.1 shard_map.60
  2.5 3.0 %collective-permute-start.5 = (f32[1,21,32,128]{3,2,1,0:T(8,128)S(1)}, f32[1,21,32,128]{3,2,1,0:T(8,128)S(1)}, u32[]{:S(2)}, u32[]{:S(2)}) collective-permute-start(f32[1,21,32,128]{3,2,1,0:T(8,128)S(1)} %get-tuple-element.94), channel_id=1, source_target_pairs={{0,16},{16,0},{1,17},{17,1},{2,18},{18,2},{3,19},{19,3},{4,20},{20... | collective-permute-start | bytes 1032200 | tf_op jit(solution)/shard_map/ppermute | solution.py:56
  5.6 1.6 %collective-permute-start = (f32[2,32,128]{2,1,0:T(8,128)S(1)}, f32[2,32,128]{2,1,0:T(8,128)S(1)}, u32[]{:S(2)}, u32[]{:S(2)}) collective-permute-start(f32[2,32,128]{2,1,0:T(8,128)S(1)} %get-tuple-element.87), channel_id=1, source_target_pairs={{0,4},{4,0},{8,12},{12,8},{1,5},{5,1},{9,13},{13,9},{2,6},{6,2},{1... | collective-permute-start | bytes 98312 | tf_op jit(solution)/shard_map/ppermute | solution.py:56
  7.1 2.3 %collective-permute-done.y_a = f32[2,32,128]{2,1,0:T(8,128)S(1)} collective-permute-done((f32[2,32,128]{2,1,0:T(8,128)S(1)}, f32[2,32,128]{2,1,0:T(8,128)S(1)}, u32[]{:S(2)}, u32[]{:S(2)}) %collective-permute-start) | collective-permute-done | bytes 32800 | tf_op jit(solution)/shard_map/ppermute | solution.py:56
  9.5 0.1 shard_map.61
  9.7 2.8 %collective-permute-start.3 = (f32[24,8,128]{2,1,0:T(8,128)S(1)}, f32[24,8,128]{2,1,0:T(8,128)S(1)}, u32[]{:S(2)}, u32[]{:S(2)}) collective-permute-start(f32[24,8,128]{2,1,0:T(8,128)S(1)} %get-tuple-element.90), channel_id=1, source_target_pairs={{0,4},{1,2},{2,1},{3,7},{4,0},{5,6},{6,5},{7,3},{8,12},{9,10},{10,... | collective-permute-start | bytes 294920 | tf_op jit(solution)/shard_map/ppermute | solution.py:51
  12.5 2.6 %collective-permute-done.3.z_b = f32[24,8,128]{2,1,0:T(8,128)S(1)} collective-permute-done((f32[24,8,128]{2,1,0:T(8,128)S(1)}, f32[24,8,128]{2,1,0:T(8,128)S(1)}, u32[]{:S(2)}, u32[]{:S(2)}) %collective-permute-start.3) | collective-permute-done | bytes 98336 | tf_op jit(solution)/shard_map/ppermute | solution.py:51
  15.1 0.1 shard_map.63
  15.2 0.6 %collective-permute-start.4 = (f32[1,11,8,128]{3,2,1,0:T(8,128)S(1)}, f32[1,11,8,128]{3,2,1,0:T(8,128)S(1)}, u32[]{:S(2)}, u32[]{:S(2)}) collective-permute-start(f32[1,11,8,128]{3,2,1,0:T(8,128)S(1)} %get-tuple-element.91), channel_id=1, source_target_pairs={{0,16},{16,0},{1,17},{17,1},{2,18},{18,2},{3,19},{19,3},{4,20},{20... | collective-permute-start | bytes 135176 | tf_op jit(solution)/shard_map/ppermute | solution.py:56
  15.8 2.8 %shard_map.64 = (f32[14,40,128]{2,1,0:T(8,128)S(1)}, f32[40,128]{1,0:T(8,128)S(1)}, f32[3,14,40,128]{3,2,1,0:T(8,128)S(1)}, f32[3,40,128]{2,1,0:T(8,128)S(1)}, f...) custom-call(f32[4,32,128]{2,1,0:T(8,128)S(1)} %get-tuple-element.69., ...), custom_call_target="tpu_custom_call" | custom-call | flops 4000000 | bytes 4000000 | tf_op jit(solution)/shard_map/pallas_call | solution.py:21
  18.6 0.7 %collective-permute-done.4.refs_0_ = f32[1,11,8,128]{3,2,1,0:T(8,128)S(1)} collective-permute-done((f32[1,11,8,128]{3,2,1,0:T(8,128)S(1)}, f32[1,11,8,128]{3,2,1,0:T(8,128)S(1)}, u32[]{:S(2)}, u32[]{:S(2)}) %collective-permute-start.4) | collective-permute-done | bytes 45088 | tf_op jit(solution)/shard_map/ppermute | solution.py:56
  19.3 1.6 %shard_map.65 = (f32[14,40,128]{2,1,0:T(8,128)S(1)}, f32[40,128]{1,0:T(8,128)S(1)}, f32[3,14,40,128]{3,2,1,0:T(8,128)S(1)}, f32[3,40,128]{2,1,0:T(8,128)S(1)}, f...) custom-call(f32[1,11,8,128]{3,2,1,0:T(8,128)S(1)} %collective-permut, ...), custom_call_target="tpu_custom_call", output_to_operand_aliasing={{0}: (1, {}), {1}: (2, {}), {2}: (3, {}), {3}: (4, {}), {4}... | custom-call | flops 8000000 | bytes 8000000 | tf_op jit(solution)/shard_map/pallas_call | solution.py:21
  21.0 0.9 %collective-permute-start.6 = (f32[22,8,128]{2,1,0:T(8,128)S(1)}, f32[22,8,128]{2,1,0:T(8,128)S(1)}, u32[]{:S(2)}, u32[]{:S(2)}) collective-permute-start(f32[22,8,128]{2,1,0:T(8,128)S(1)} %get-tuple-element.112.own), channel_id=1, source_target_pairs={{0,16},{16,0},{1,17},{17,1},{2,18},{18,2},{3,19},{19,3},{4,20},{20... | collective-permute-start | bytes 270344 | tf_op jit(solution)/shard_map/ppermute | solution.py:56
  21.9 3.7 %collective-permute-done.6.other.frames = f32[22,8,128]{2,1,0:T(8,128)S(1)} collective-permute-done((f32[22,8,128]{2,1,0:T(8,128)S(1)}, f32[22,8,128]{2,1,0:T(8,128)S(1)}, u32[]{:S(2)}, u32[]{:S(2)}) %collective-permute-start.6) | collective-permute-done | bytes 90144 | tf_op jit(solution)/shard_map/ppermute | solution.py:56
  25.7 2.1 %collective-permute-start.8 = (f32[21,8,128]{2,1,0:T(8,128)S(1)}, f32[21,8,128]{2,1,0:T(8,128)S(1)}, u32[]{:S(2)}, u32[]{:S(2)}) collective-permute-start(f32[21,8,128]{2,1,0:T(8,128)S(1)} %get-tuple-element.116), channel_id=1, source_target_pairs={{0,4},{1,2},{2,1},{3,7},{4,0},{5,6},{6,5},{7,3},{8,12},{9,10},{10,... | collective-permute-start | bytes 258056 | tf_op jit(solution)/shard_map/ppermute | solution.py:51
  27.8 0.2 shard_map.67
  28.0 0.9 %collective-permute-start.11 = (f32[1,8,32,128]{3,2,1,0:T(8,128)S(1)}, f32[1,8,32,128]{3,2,1,0:T(8,128)S(1)}, u32[]{:S(2)}, u32[]{:S(2)}) collective-permute-start(f32[1,8,32,128]{3,2,1,0:T(8,128)S(1)} %get-tuple-element.134), channel_id=1, source_target_pairs={{0,16},{16,0},{1,17},{17,1},{2,18},{18,2},{3,19},{19,3},{4,20},{20... | collective-permute-start | bytes 393224 | tf_op jit(solution)/shard_map/ppermute | solution.py:56
  28.9 1.4 %collective-permute-done.8.z_b = f32[21,8,128]{2,1,0:T(8,128)S(1)} collective-permute-done((f32[21,8,128]{2,1,0:T(8,128)S(1)}, f32[21,8,128]{2,1,0:T(8,128)S(1)}, u32[]{:S(2)}, u32[]{:S(2)}) %collective-permute-start.8) | collective-permute-done | bytes 86048 | tf_op jit(solution)/shard_map/ppermute | solution.py:51
  30.3 0.3 shard_map.68
  30.6 2.1 %collective-permute-start.9 = (f32[11,8,128]{2,1,0:T(8,128)S(1)}, f32[11,8,128]{2,1,0:T(8,128)S(1)}, u32[]{:S(2)}, u32[]{:S(2)}) collective-permute-start(f32[11,8,128]{2,1,0:T(8,128)S(1)} %get-tuple-element.120), channel_id=1, source_target_pairs={{0,4},{4,0},{8,12},{12,8},{1,5},{5,1},{9,13},{13,9},{2,6},{6,2},{1... | collective-permute-start | bytes 135176 | tf_op jit(solution)/shard_map/ppermute | solution.py:56
  32.7 0.3 collective-permute-done.11.refs_17_
  33.0 1.7 %collective-permute-done.9.refs_2_ = f32[11,8,128]{2,1,0:T(8,128)S(1)} collective-permute-done((f32[11,8,128]{2,1,0:T(8,128)S(1)}, f32[11,8,128]{2,1,0:T(8,128)S(1)}, u32[]{:S(2)}, u32[]{:S(2)}) %collective-permute-start.9) | collective-permute-done | bytes 45088 | tf_op jit(solution)/shard_map/ppermute | solution.py:56
  34.7 3.9 %shard_map.69 = (f32[3,8,32,128]{3,2,1,0:T(8,128)}, f32[8,32,128]{2,1,0:T(8,128)}) custom-call(f32[4,4,24,128]{3,2,1,0:T(8,128)S(1)} %get-tuple-element.118.refs_0_, f32[4,32,128]{2,1,0:T(8,128)S(1)} %get-tuple-element.119.refs_1_, f32[11,8,128]{2,1,0:T(8,128)S(1)} %collective-permute-done.9.refs_2_, f32[11,8,128]{2,1,0:T(8,128)S(1)} %collective-permute-done.10.refs_3_, ...), custom_call_target="tpu_custom_call" | custom-call | flops 8000000 | bytes 8000000 | tf_op jit(solution)/shard_map/pallas_call | solution.py:21
  (11 shorter events, 0.3 us)
Async XLA Ops:
  2.5 13.2 %collective-permute-start.5 = (f32[1,21,32,128]{3,2,1,0:T(8,128)S(1)}, f32[1,21,32,128]{3,2,1,0:T(8,128)S(1)}, u32[]{:S(2)}, u32[]{:S(2)}) collective-permute-start(f32[1,21,32,128]{3,2,1,0:T(8,128)S(1)} %get-tuple-element.94), channel_id=1, source_target_pairs={{0,16},{16,0},{1,17},{17,1},{2,18},{18,2},{3,19},{19,3},{4,20},{20... | collective-permute-start | bytes 1032200 | tf_op jit(solution)/shard_map/ppermute | solution.py:56
  5.6 3.9 %collective-permute-start = (f32[2,32,128]{2,1,0:T(8,128)S(1)}, f32[2,32,128]{2,1,0:T(8,128)S(1)}, u32[]{:S(2)}, u32[]{:S(2)}) collective-permute-start(f32[2,32,128]{2,1,0:T(8,128)S(1)} %get-tuple-element.87), channel_id=1, source_target_pairs={{0,4},{4,0},{8,12},{12,8},{1,5},{5,1},{9,13},{13,9},{2,6},{6,2},{1... | collective-permute-start | bytes 98312 | tf_op jit(solution)/shard_map/ppermute | solution.py:56
  7.1 2.3 %collective-permute-start.1 = (f32[2,32,128]{2,1,0:T(8,128)S(1)}, f32[2,32,128]{2,1,0:T(8,128)S(1)}, u32[]{:S(2)}, u32[]{:S(2)}) collective-permute-start(f32[2,32,128]{2,1,0:T(8,128)S(1)} %get-tuple-element.88), channel_id=1, source_target_pairs={{0,1},{1,0},{2,3},{3,2},{4,8},{5,9},{6,10},{7,11},{8,4},{9,5},{10,... | collective-permute-start | bytes 98312 | tf_op jit(solution)/shard_map/ppermute | solution.py:51
  9.6 2.8 %collective-permute-start.2 = (f32[24,8,128]{2,1,0:T(8,128)S(1)}, f32[24,8,128]{2,1,0:T(8,128)S(1)}, u32[]{:S(2)}, u32[]{:S(2)}) collective-permute-start(f32[24,8,128]{2,1,0:T(8,128)S(1)} %shard_map.62), channel_id=1, source_target_pairs={{0,1},{1,0},{2,3},{3,2},{4,5},{5,4},{6,7},{7,6},{8,9},{9,8},{10,11... | collective-permute-start | bytes 294920 | tf_op jit(solution)/shard_map/ppermute | solution.py:56
  9.7 5.4 %collective-permute-start.3 = (f32[24,8,128]{2,1,0:T(8,128)S(1)}, f32[24,8,128]{2,1,0:T(8,128)S(1)}, u32[]{:S(2)}, u32[]{:S(2)}) collective-permute-start(f32[24,8,128]{2,1,0:T(8,128)S(1)} %get-tuple-element.90), channel_id=1, source_target_pairs={{0,4},{1,2},{2,1},{3,7},{4,0},{5,6},{6,5},{7,3},{8,12},{9,10},{10,... | collective-permute-start | bytes 294920 | tf_op jit(solution)/shard_map/ppermute | solution.py:51
  15.2 4.1 %collective-permute-start.4 = (f32[1,11,8,128]{3,2,1,0:T(8,128)S(1)}, f32[1,11,8,128]{3,2,1,0:T(8,128)S(1)}, u32[]{:S(2)}, u32[]{:S(2)}) collective-permute-start(f32[1,11,8,128]{3,2,1,0:T(8,128)S(1)} %get-tuple-element.91), channel_id=1, source_target_pairs={{0,16},{16,0},{1,17},{17,1},{2,18},{18,2},{3,19},{19,3},{4,20},{20... | collective-permute-start | bytes 135176 | tf_op jit(solution)/shard_map/ppermute | solution.py:56
  21.0 4.6 %collective-permute-start.6 = (f32[22,8,128]{2,1,0:T(8,128)S(1)}, f32[22,8,128]{2,1,0:T(8,128)S(1)}, u32[]{:S(2)}, u32[]{:S(2)}) collective-permute-start(f32[22,8,128]{2,1,0:T(8,128)S(1)} %get-tuple-element.112.own), channel_id=1, source_target_pairs={{0,16},{16,0},{1,17},{17,1},{2,18},{18,2},{3,19},{19,3},{4,20},{20... | collective-permute-start | bytes 270344 | tf_op jit(solution)/shard_map/ppermute | solution.py:56
  25.6 3.3 %collective-permute-start.7 = (f32[21,8,128]{2,1,0:T(8,128)S(1)}, f32[21,8,128]{2,1,0:T(8,128)S(1)}, u32[]{:S(2)}, u32[]{:S(2)}) collective-permute-start(f32[21,8,128]{2,1,0:T(8,128)S(1)} %get-tuple-element.115), channel_id=1, source_target_pairs={{0,1},{1,0},{2,3},{3,2},{4,5},{5,4},{6,7},{7,6},{8,9},{9,8},{10,11... | collective-permute-start | bytes 258056 | tf_op jit(solution)/shard_map/ppermute | solution.py:56
  25.7 4.6 %collective-permute-start.8 = (f32[21,8,128]{2,1,0:T(8,128)S(1)}, f32[21,8,128]{2,1,0:T(8,128)S(1)}, u32[]{:S(2)}, u32[]{:S(2)}) collective-permute-start(f32[21,8,128]{2,1,0:T(8,128)S(1)} %get-tuple-element.116), channel_id=1, source_target_pairs={{0,4},{1,2},{2,1},{3,7},{4,0},{5,6},{6,5},{7,3},{8,12},{9,10},{10,... | collective-permute-start | bytes 258056 | tf_op jit(solution)/shard_map/ppermute | solution.py:51
  28.0 5.0 %collective-permute-start.11 = (f32[1,8,32,128]{3,2,1,0:T(8,128)S(1)}, f32[1,8,32,128]{3,2,1,0:T(8,128)S(1)}, u32[]{:S(2)}, u32[]{:S(2)}) collective-permute-start(f32[1,8,32,128]{3,2,1,0:T(8,128)S(1)} %get-tuple-element.134), channel_id=1, source_target_pairs={{0,16},{16,0},{1,17},{17,1},{2,18},{18,2},{3,19},{19,3},{4,20},{20... | collective-permute-start | bytes 393224 | tf_op jit(solution)/shard_map/ppermute | solution.py:56
  30.6 4.1 %collective-permute-start.9 = (f32[11,8,128]{2,1,0:T(8,128)S(1)}, f32[11,8,128]{2,1,0:T(8,128)S(1)}, u32[]{:S(2)}, u32[]{:S(2)}) collective-permute-start(f32[11,8,128]{2,1,0:T(8,128)S(1)} %get-tuple-element.120), channel_id=1, source_target_pairs={{0,4},{4,0},{8,12},{12,8},{1,5},{5,1},{9,13},{13,9},{2,6},{6,2},{1... | collective-permute-start | bytes 135176 | tf_op jit(solution)/shard_map/ppermute | solution.py:56
  32.7 2.0 %collective-permute-start.10 = (f32[11,8,128]{2,1,0:T(8,128)S(1)}, f32[11,8,128]{2,1,0:T(8,128)S(1)}, u32[]{:S(2)}, u32[]{:S(2)}) collective-permute-start(f32[11,8,128]{2,1,0:T(8,128)S(1)} %get-tuple-element.121), channel_id=1, source_target_pairs={{0,1},{1,0},{2,3},{3,2},{4,8},{5,9},{6,10},{7,11},{8,4},{9,5},{10,... | collective-permute-start | bytes 135176 | tf_op jit(solution)/shard_map/ppermute | solution.py:51

commit v9 on v8

--- a/solution.py
+++ b/solution.py
@@ -238,14 +238,11 @@
         out[3 * j + 2] = jnp.where(row < 5, first[3 * j + 2], x)
 
 
-def second_pack(z_first, y_a, y_b, halo, z_b):
+def second_pack(z_first_a, z_first_b, y_a, y_b, halo, z_a, z_b):
     for j in range(2):
         halo[j], halo[j + 2] = merge_y(y_a[j], y_b[j])
-    z_tail(halo, z_first, z_b, 1)
-
-
-def second_pack_near(z_first, halo, z_a):
-    z_tail(halo, z_first, z_a, 0)
+    z_tail(halo, z_first_a, z_a, 0)
+    z_tail(halo, z_first_b, z_b, 1)
 
 
 def z_tile(a, b, at, rows):
@@ -611,7 +608,7 @@
 
 
 def residuals(u, halo, beside, w, force, e, summed, chosen):
-    _, blocks, nz, _ = summed.shape
+    blocks, nz = summed.shape[1], summed.shape[2] - 8
     slots = u.shape[1]
     spread_halo(halo, beside, slots, 0, lambda p: chosen((p - 3) // 2), False)
 
@@ -626,7 +623,7 @@
             totals[3] += spread
             totals[4] += e[p, pl.ds(0, nz)]
         for k in range(5):
-            summed[k, q] = totals[k]
+            summed[k, q, pl.ds(0, nz)] = totals[k]
 
     for q in range(blocks):
         if chosen(q):
@@ -1128,8 +1125,9 @@
     x_main, z_a, z_b = call(side_pack, [(sides, 21) + block, z_shape, z_shape], staged)
     y_a, y_b = swap(y_a, "gy", 0), swap(y_b, "gy", 1)
     x_main = swap_x(x_main)
-    halo, z_b = call(second_pack, [(4,) + block, z_shape], [z_b, y_a, y_b])
-    (z_a,) = call(second_pack_near, [z_shape], [z_a, halo])
+    halo, z_a, z_b = call(
+        second_pack, [(4,) + block, z_shape, z_shape], [z_a, z_b, y_a, y_b]
+    )
     z_a, z_b = swap(z_a, "gz", 0), swap(z_b, "gz", 1)
     tiles = rows // 8
     z_first, halo_first, x_first = call(
@@ -1142,7 +1140,7 @@
     spread, column = (4, slots, rows, LANES), (4, rows, LANES)
     started = [(slots, rows, LANES), (rows, LANES), (3, slots, rows, LANES), (3, rows, LANES)]
     started += [(slots, rows, LANES)] * 6 + [spread, spread] + [column] * 3 + [(rows, LANES)]
-    started += [(5, nx // 2, nz, LANES)]
+    started += [(5, nx // 2, rows, LANES)]
     tiles_c = 5 * (nx // 4) * (nz // 16)
     state = call(
         by_sides(pre_start),
@@ -1191,7 +1189,7 @@
     plane = (shallow, LANES)
     coarse_scratch = [(4, nx // 2 + 2, rows, LANES), (4, rows, LANES)]
     coarse_scratch += [(4, planes + 2) + plane] * 2 + [(4, planes) + plane]
-    coarse_scratch += [(planes + 2,) + plane] * 7 + [(planes + 2, deep, LANES), (16, LANES)]
+    coarse_scratch += [(planes + 2,) + plane] * 7 + [(planes + 2, deep, LANES), (24, LANES)]
     v_out, p_out = call(
         by_sides(finish),
         [(3, nx) + block, (nx,) + block],

time: 38.8 us -> 38.8 us (level)
    pallas_call x11 -> x10, Pallas kernels: 11.1 us -> 11.1 us  [call(): pl.pallas_call(body, out_shape=[jax.ShapeDtypeStruct(shape, F32) for shap...]
where the time goes in v9:
time: 38.8 us; the launch traced here: 38.6 us
  starting transfers between devices  14.1 us (36%)
  waiting for transfers between devices  12.7 us (33%)
  Pallas kernels  11.1 us (29%)
  between operations  0.72 us (2%)
    pallas_call x10, Pallas kernels, call(): pl.pallas_call(body, out_shape=[jax.ShapeDtypeStruct(shape, F32) for shap...  11.1 us
    ppermute x8, starting transfers between devices, swap(): return lax.ppermute(array, axis, pairs)  9.21 us
    ppermute x8, waiting for transfers between devices, swap(): return lax.ppermute(array, axis, pairs)  8.75 us
    ppermute x4, starting transfers between devices, swap(): return lax.ppermute(array, ('gy', 'gz'), pairs)  4.86 us
    ppermute x4, waiting for transfers between devices, swap(): return lax.ppermute(array, ('gy', 'gz'), pairs)  3.96 us
  transfers between devices with their start and end apart: 12, of which 7 were waited for; matrix products, arithmetic and copies ran while one was open for 0% of the time, Pallas kernels for 9%

profile of v9, /device:TPU:0, one launch (start us, length us, event | category | flops | bytes accessed | tf_op | source)
XLA Modules:
  0.0 38.6 jit_solution(5368235507129531674)
XLA Ops:
  0.6 1.8 %shard_map.59 = (f32[4,32,128]{2,1,0:T(8,128)S(1)}, f32[4,32,128]{2,1,0:T(8,128)S(1)}, f32[4,32,128]{2,1,0:T(8,128)S(1)}, f32[4,32,128]{2,1,0:T(8,128)S(1)}, f32...) custom-call(f32[3,8,32,128]{3,2,1,0:T(8,128)} %v_in.1, ...), custom_call_target="tpu_custom_call" | custom-call | flops 1000000 | bytes 1000000 | tf_op jit(solution)/shard_map/pallas_call | solution.py:21
  2.4 0.1 shard_map.60
  2.5 3.0 %collective-permute-start.5 = (f32[1,21,32,128]{3,2,1,0:T(8,128)S(1)}, f32[1,21,32,128]{3,2,1,0:T(8,128)S(1)}, u32[]{:S(2)}, u32[]{:S(2)}) collective-permute-start(f32[1,21,32,128]{3,2,1,0:T(8,128)S(1)} %get-tuple-element.96), channel_id=1, source_target_pairs={{0,16},{16,0},{1,17},{17,1},{2,18},{18,2},{3,19},{19,3},{4,20},{20... | collective-permute-start | bytes 1032200 | tf_op jit(solution)/shard_map/ppermute | solution.py:56
  5.6 1.6 %collective-permute-start = (f32[2,32,128]{2,1,0:T(8,128)S(1)}, f32[2,32,128]{2,1,0:T(8,128)S(1)}, u32[]{:S(2)}, u32[]{:S(2)}) collective-permute-start(f32[2,32,128]{2,1,0:T(8,128)S(1)} %get-tuple-element.88), channel_id=1, source_target_pairs={{0,4},{4,0},{8,12},{12,8},{1,5},{5,1},{9,13},{13,9},{2,6},{6,2},{1... | collective-permute-start | bytes 98312 | tf_op jit(solution)/shard_map/ppermute | solution.py:56
  7.1 2.3 %collective-permute-done.y_a = f32[2,32,128]{2,1,0:T(8,128)S(1)} collective-permute-done((f32[2,32,128]{2,1,0:T(8,128)S(1)}, f32[2,32,128]{2,1,0:T(8,128)S(1)}, u32[]{:S(2)}, u32[]{:S(2)}) %collective-permute-start) | collective-permute-done | bytes 32800 | tf_op jit(solution)/shard_map/ppermute | solution.py:56
  9.5 0.1 shard_map.61
  9.7 2.8 %collective-permute-start.3 = (f32[24,8,128]{2,1,0:T(8,128)S(1)}, f32[24,8,128]{2,1,0:T(8,128)S(1)}, u32[]{:S(2)}, u32[]{:S(2)}) collective-permute-start(f32[24,8,128]{2,1,0:T(8,128)S(1)} %get-tuple-element.91), channel_id=1, source_target_pairs={{0,4},{1,2},{2,1},{3,7},{4,0},{5,6},{6,5},{7,3},{8,12},{9,10},{10,... | collective-permute-start | bytes 294920 | tf_op jit(solution)/shard_map/ppermute | solution.py:51
  12.4 2.6 %collective-permute-done.3.z_b = f32[24,8,128]{2,1,0:T(8,128)S(1)} collective-permute-done((f32[24,8,128]{2,1,0:T(8,128)S(1)}, f32[24,8,128]{2,1,0:T(8,128)S(1)}, u32[]{:S(2)}, u32[]{:S(2)}) %collective-permute-start.3) | collective-permute-done | bytes 98336 | tf_op jit(solution)/shard_map/ppermute | solution.py:51
  15.0 0.1 shard_map.62
  15.2 0.6 %collective-permute-start.4 = (f32[1,11,8,128]{3,2,1,0:T(8,128)S(1)}, f32[1,11,8,128]{3,2,1,0:T(8,128)S(1)}, u32[]{:S(2)}, u32[]{:S(2)}) collective-permute-start(f32[1,11,8,128]{3,2,1,0:T(8,128)S(1)} %get-tuple-element.93), channel_id=1, source_target_pairs={{0,16},{16,0},{1,17},{17,1},{2,18},{18,2},{3,19},{19,3},{4,20},{20... | collective-permute-start | bytes 135176 | tf_op jit(solution)/shard_map/ppermute | solution.py:56
  15.7 2.8 %shard_map.63 = (f32[14,40,128]{2,1,0:T(8,128)S(1)}, f32[40,128]{1,0:T(8,128)S(1)}, f32[3,14,40,128]{3,2,1,0:T(8,128)S(1)}, f32[3,40,128]{2,1,0:T(8,128)S(1)}, f...) custom-call(f32[4,32,128]{2,1,0:T(8,128)S(1)} %get-tuple-element.70., ...), custom_call_target="tpu_custom_call" | custom-call | flops 4000000 | bytes 4000000 | tf_op jit(solution)/shard_map/pallas_call | solution.py:21
  18.6 0.7 %collective-permute-done.4.refs_0_ = f32[1,11,8,128]{3,2,1,0:T(8,128)S(1)} collective-permute-done((f32[1,11,8,128]{3,2,1,0:T(8,128)S(1)}, f32[1,11,8,128]{3,2,1,0:T(8,128)S(1)}, u32[]{:S(2)}, u32[]{:S(2)}) %collective-permute-start.4) | collective-permute-done | bytes 45088 | tf_op jit(solution)/shard_map/ppermute | solution.py:56
  19.3 1.6 %shard_map.64 = (f32[14,40,128]{2,1,0:T(8,128)S(1)}, f32[40,128]{1,0:T(8,128)S(1)}, f32[3,14,40,128]{3,2,1,0:T(8,128)S(1)}, f32[3,40,128]{2,1,0:T(8,128)S(1)}, f...) custom-call(f32[1,11,8,128]{3,2,1,0:T(8,128)S(1)} %collective-permut, ...), custom_call_target="tpu_custom_call", output_to_operand_aliasing={{0}: (1, {}), {1}: (2, {}), {2}: (3, {}), {3}: (4, {}), {4}... | custom-call | flops 8000000 | bytes 8000000 | tf_op jit(solution)/shard_map/pallas_call | solution.py:21
  20.9 0.9 %collective-permute-start.6 = (f32[22,8,128]{2,1,0:T(8,128)S(1)}, f32[22,8,128]{2,1,0:T(8,128)S(1)}, u32[]{:S(2)}, u32[]{:S(2)}) collective-permute-start(f32[22,8,128]{2,1,0:T(8,128)S(1)} %get-tuple-element.114.own), channel_id=1, source_target_pairs={{0,16},{16,0},{1,17},{17,1},{2,18},{18,2},{3,19},{19,3},{4,20},{20... | collective-permute-start | bytes 270344 | tf_op jit(solution)/shard_map/ppermute | solution.py:56
  21.8 3.7 %collective-permute-done.6.other.frames = f32[22,8,128]{2,1,0:T(8,128)S(1)} collective-permute-done((f32[22,8,128]{2,1,0:T(8,128)S(1)}, f32[22,8,128]{2,1,0:T(8,128)S(1)}, u32[]{:S(2)}, u32[]{:S(2)}) %collective-permute-start.6) | collective-permute-done | bytes 90144 | tf_op jit(solution)/shard_map/ppermute | solution.py:56
  25.7 2.1 %collective-permute-start.8 = (f32[21,8,128]{2,1,0:T(8,128)S(1)}, f32[21,8,128]{2,1,0:T(8,128)S(1)}, u32[]{:S(2)}, u32[]{:S(2)}) collective-permute-start(f32[21,8,128]{2,1,0:T(8,128)S(1)} %get-tuple-element.118), channel_id=1, source_target_pairs={{0,4},{1,2},{2,1},{3,7},{4,0},{5,6},{6,5},{7,3},{8,12},{9,10},{10,... | collective-permute-start | bytes 258056 | tf_op jit(solution)/shard_map/ppermute | solution.py:51
  27.8 0.2 shard_map.66
  28.0 0.9 %collective-permute-start.11 = (f32[1,8,32,128]{3,2,1,0:T(8,128)S(1)}, f32[1,8,32,128]{3,2,1,0:T(8,128)S(1)}, u32[]{:S(2)}, u32[]{:S(2)}) collective-permute-start(f32[1,8,32,128]{3,2,1,0:T(8,128)S(1)} %get-tuple-element.136), channel_id=1, source_target_pairs={{0,16},{16,0},{1,17},{17,1},{2,18},{18,2},{3,19},{19,3},{4,20},{20... | collective-permute-start | bytes 393224 | tf_op jit(solution)/shard_map/ppermute | solution.py:56
  28.9 1.4 %collective-permute-done.8.z_b = f32[21,8,128]{2,1,0:T(8,128)S(1)} collective-permute-done((f32[21,8,128]{2,1,0:T(8,128)S(1)}, f32[21,8,128]{2,1,0:T(8,128)S(1)}, u32[]{:S(2)}, u32[]{:S(2)}) %collective-permute-start.8) | collective-permute-done | bytes 86048 | tf_op jit(solution)/shard_map/ppermute | solution.py:51
  30.2 0.3 shard_map.67
  30.6 2.1 %collective-permute-start.9 = (f32[11,8,128]{2,1,0:T(8,128)S(1)}, f32[11,8,128]{2,1,0:T(8,128)S(1)}, u32[]{:S(2)}, u32[]{:S(2)}) collective-permute-start(f32[11,8,128]{2,1,0:T(8,128)S(1)} %get-tuple-element.122), channel_id=1, source_target_pairs={{0,4},{4,0},{8,12},{12,8},{1,5},{5,1},{9,13},{13,9},{2,6},{6,2},{1... | collective-permute-start | bytes 135176 | tf_op jit(solution)/shard_map/ppermute | solution.py:56
  32.7 0.3 collective-permute-done.11.refs_17_
  33.0 1.7 %collective-permute-done.9.refs_2_ = f32[11,8,128]{2,1,0:T(8,128)S(1)} collective-permute-done((f32[11,8,128]{2,1,0:T(8,128)S(1)}, f32[11,8,128]{2,1,0:T(8,128)S(1)}, u32[]{:S(2)}, u32[]{:S(2)}) %collective-permute-start.9) | collective-permute-done | bytes 45088 | tf_op jit(solution)/shard_map/ppermute | solution.py:56
  34.7 3.9 %shard_map.68 = (f32[3,8,32,128]{3,2,1,0:T(8,128)}, f32[8,32,128]{2,1,0:T(8,128)}) custom-call(f32[4,4,24,128]{3,2,1,0:T(8,128)S(1)} %get-tuple-element.120.refs_0_, f32[4,32,128]{2,1,0:T(8,128)S(1)} %get-tuple-element.121.refs_1_, f32[11,8,128]{2,1,0:T(8,128)S(1)} %collective-permute-done.9.refs_2_, f32[11,8,128]{2,1,0:T(8,128)S(1)} %collective-permute-done.10.refs_3_, ...), custom_call_target="tpu_custom_call" | custom-call | flops 8000000 | bytes 8000000 | tf_op jit(solution)/shard_map/pallas_call | solution.py:21
  (10 shorter events, 0.2 us)
Async XLA Ops:
  2.5 13.2 %collective-permute-start.5 = (f32[1,21,32,128]{3,2,1,0:T(8,128)S(1)}, f32[1,21,32,128]{3,2,1,0:T(8,128)S(1)}, u32[]{:S(2)}, u32[]{:S(2)}) collective-permute-start(f32[1,21,32,128]{3,2,1,0:T(8,128)S(1)} %get-tuple-element.96), channel_id=1, source_target_pairs={{0,16},{16,0},{1,17},{17,1},{2,18},{18,2},{3,19},{19,3},{4,20},{20... | collective-permute-start | bytes 1032200 | tf_op jit(solution)/shard_map/ppermute | solution.py:56
  5.6 3.9 %collective-permute-start = (f32[2,32,128]{2,1,0:T(8,128)S(1)}, f32[2,32,128]{2,1,0:T(8,128)S(1)}, u32[]{:S(2)}, u32[]{:S(2)}) collective-permute-start(f32[2,32,128]{2,1,0:T(8,128)S(1)} %get-tuple-element.88), channel_id=1, source_target_pairs={{0,4},{4,0},{8,12},{12,8},{1,5},{5,1},{9,13},{13,9},{2,6},{6,2},{1... | collective-permute-start | bytes 98312 | tf_op jit(solution)/shard_map/ppermute | solution.py:56
  7.1 2.3 %collective-permute-start.1 = (f32[2,32,128]{2,1,0:T(8,128)S(1)}, f32[2,32,128]{2,1,0:T(8,128)S(1)}, u32[]{:S(2)}, u32[]{:S(2)}) collective-permute-start(f32[2,32,128]{2,1,0:T(8,128)S(1)} %get-tuple-element.89), channel_id=1, source_target_pairs={{0,1},{1,0},{2,3},{3,2},{4,8},{5,9},{6,10},{7,11},{8,4},{9,5},{10,... | collective-permute-start | bytes 98312 | tf_op jit(solution)/shard_map/ppermute | solution.py:51
  9.6 2.8 %collective-permute-start.2 = (f32[24,8,128]{2,1,0:T(8,128)S(1)}, f32[24,8,128]{2,1,0:T(8,128)S(1)}, u32[]{:S(2)}, u32[]{:S(2)}) collective-permute-start(f32[24,8,128]{2,1,0:T(8,128)S(1)} %get-tuple-element.90), channel_id=1, source_target_pairs={{0,1},{1,0},{2,3},{3,2},{4,5},{5,4},{6,7},{7,6},{8,9},{9,8},{10,11... | collective-permute-start | bytes 294920 | tf_op jit(solution)/shard_map/ppermute | solution.py:56
  9.7 5.4 %collective-permute-start.3 = (f32[24,8,128]{2,1,0:T(8,128)S(1)}, f32[24,8,128]{2,1,0:T(8,128)S(1)}, u32[]{:S(2)}, u32[]{:S(2)}) collective-permute-start(f32[24,8,128]{2,1,0:T(8,128)S(1)} %get-tuple-element.91), channel_id=1, source_target_pairs={{0,4},{1,2},{2,1},{3,7},{4,0},{5,6},{6,5},{7,3},{8,12},{9,10},{10,... | collective-permute-start | bytes 294920 | tf_op jit(solution)/shard_map/ppermute | solution.py:51
  15.2 4.1 %collective-permute-start.4 = (f32[1,11,8,128]{3,2,1,0:T(8,128)S(1)}, f32[1,11,8,128]{3,2,1,0:T(8,128)S(1)}, u32[]{:S(2)}, u32[]{:S(2)}) collective-permute-start(f32[1,11,8,128]{3,2,1,0:T(8,128)S(1)} %get-tuple-element.93), channel_id=1, source_target_pairs={{0,16},{16,0},{1,17},{17,1},{2,18},{18,2},{3,19},{19,3},{4,20},{20... | collective-permute-start | bytes 135176 | tf_op jit(solution)/shard_map/ppermute | solution.py:56
  20.9 4.6 %collective-permute-start.6 = (f32[22,8,128]{2,1,0:T(8,128)S(1)}, f32[22,8,128]{2,1,0:T(8,128)S(1)}, u32[]{:S(2)}, u32[]{:S(2)}) collective-permute-start(f32[22,8,128]{2,1,0:T(8,128)S(1)} %get-tuple-element.114.own), channel_id=1, source_target_pairs={{0,16},{16,0},{1,17},{17,1},{2,18},{18,2},{3,19},{19,3},{4,20},{20... | collective-permute-start | bytes 270344 | tf_op jit(solution)/shard_map/ppermute | solution.py:56
  25.6 3.3 %collective-permute-start.7 = (f32[21,8,128]{2,1,0:T(8,128)S(1)}, f32[21,8,128]{2,1,0:T(8,128)S(1)}, u32[]{:S(2)}, u32[]{:S(2)}) collective-permute-start(f32[21,8,128]{2,1,0:T(8,128)S(1)} %get-tuple-element.117), channel_id=1, source_target_pairs={{0,1},{1,0},{2,3},{3,2},{4,5},{5,4},{6,7},{7,6},{8,9},{9,8},{10,11... | collective-permute-start | bytes 258056 | tf_op jit(solution)/shard_map/ppermute | solution.py:56
  25.7 4.6 %collective-permute-start.8 = (f32[21,8,128]{2,1,0:T(8,128)S(1)}, f32[21,8,128]{2,1,0:T(8,128)S(1)}, u32[]{:S(2)}, u32[]{:S(2)}) collective-permute-start(f32[21,8,128]{2,1,0:T(8,128)S(1)} %get-tuple-element.118), channel_id=1, source_target_pairs={{0,4},{1,2},{2,1},{3,7},{4,0},{5,6},{6,5},{7,3},{8,12},{9,10},{10,... | collective-permute-start | bytes 258056 | tf_op jit(solution)/shard_map/ppermute | solution.py:51
  28.0 5.0 %collective-permute-start.11 = (f32[1,8,32,128]{3,2,1,0:T(8,128)S(1)}, f32[1,8,32,128]{3,2,1,0:T(8,128)S(1)}, u32[]{:S(2)}, u32[]{:S(2)}) collective-permute-start(f32[1,8,32,128]{3,2,1,0:T(8,128)S(1)} %get-tuple-element.136), channel_id=1, source_target_pairs={{0,16},{16,0},{1,17},{17,1},{2,18},{18,2},{3,19},{19,3},{4,20},{20... | collective-permute-start | bytes 393224 | tf_op jit(solution)/shard_map/ppermute | solution.py:56
  30.6 4.1 %collective-permute-start.9 = (f32[11,8,128]{2,1,0:T(8,128)S(1)}, f32[11,8,128]{2,1,0:T(8,128)S(1)}, u32[]{:S(2)}, u32[]{:S(2)}) collective-permute-start(f32[11,8,128]{2,1,0:T(8,128)S(1)} %get-tuple-element.122), channel_id=1, source_target_pairs={{0,4},{4,0},{8,12},{12,8},{1,5},{5,1},{9,13},{13,9},{2,6},{6,2},{1... | collective-permute-start | bytes 135176 | tf_op jit(solution)/shard_map/ppermute | solution.py:56
  32.7 2.0 %collective-permute-start.10 = (f32[11,8,128]{2,1,0:T(8,128)S(1)}, f32[11,8,128]{2,1,0:T(8,128)S(1)}, u32[]{:S(2)}, u32[]{:S(2)}) collective-permute-start(f32[11,8,128]{2,1,0:T(8,128)S(1)} %get-tuple-element.123), channel_id=1, source_target_pairs={{0,1},{1,0},{2,3},{3,2},{4,8},{5,9},{6,10},{7,11},{8,4},{9,5},{10,... | collective-permute-start | bytes 135176 | tf_op jit(solution)/shard_map/ppermute | solution.py:51
